TPU v7x, 32 devices: a whole 2x2x4 slice. The times are simulated.
32 devices in a mesh: fsdp: 32 (over z, y, x, core).
Axes of the slice: x: 2, y: 2, z: 4, core: 2. Of those that a mesh axis runs over, the one named last changes fastest.
Arguments:
- images: float32 [64, 32, 32, 3], P('fsdp'), may hold values from -1 to 1
- noise_draws: float32 [64, 32, 32, 3], P('fsdp'), may hold values from -5 to 5
- labels: int32 [64], P('fsdp'), may hold values from 0 to 999
- step_index: int32 [64], P('fsdp'), may hold values from 0 to 38
- valid_rows: int32 [64], P('fsdp'), may hold values from 16 to 32
- counts: int32 [32], P('fsdp'), may hold values from 1 to 2, as said below
- master_weights: float32 [9273344], P('fsdp'), as said below
- momentum: float32 [9273344], P('fsdp'), may hold values from -0.00048828125 to 0.00048828125
- ema_weights: float32 [9273344], P('fsdp'), as said below
Outputs:
- loss: float32 [], replicated
- new_momentum: float32 [9273344], P('fsdp')
- new_master: float32 [9273344], P('fsdp')
- new_ema: float32 [9273344], P('fsdp')
- bias_gradient: float32 [3], replicated
Inputs may be any that keep to these rules, and one draw needn't show every extreme that they name: `counts`: some device holds 2 images. `master_weights`: weights of the layout above: matrices of spread one over the root of their rows (attn_out four times that), gains near one, shifts and biases small, zeros past 9272451. `ema_weights`: weights of the same kind as master_weights, drawn apart.
All inputs are finite; a program needn't handle non-finite values.
Results may differ from a plain program's by a relative error of at most 0.0095.
Values may be sent and summed in bfloat16 or wider, within the bound.
No kernel may reach another device: no remote copies, remote signals or barrier semaphores. Data moves between devices by JAX's collectives and lax.ppermute only.
A program may use at most 256 MiB of HBM per device.

v0:
```python
from functools import partial
import math

import jax
import jax.numpy as jnp
from jax import lax
from jax.sharding import PartitionSpec as P

CH_BASE = 192
CH_MID = 384
EMB_DIM = 768
HEADS = 6
HEAD_DIM = 64
CLASSES = 1000
GROUPS = 32
RES = 32
MB_DEV = 2
DISCRETE = 40


EPSILON = 1e-05
SIGMA_DATA = 0.5
SIGMA_LOW = 0.002
SIGMA_HIGH = 80.0
RHO_POWER = 7.0
MOMENTUM = 0.9
EMA_DECAY = 0.9
LEARN_RATE = 2000.0
HIGHEST = lax.Precision.HIGHEST
CONTRACT_ROWS = (((0,), (0,)), ((), ()))
CONTRACT_COLS = (((1,), (1,)), ((), ()))


def layout():
    shapes = [
        ("conv_in", (27, CH_BASE)),
        ("bias_in", (CH_BASE,)),
        ("conv_down", (9 * CH_BASE, CH_MID)),
        ("bias_down", (CH_MID,)),
        ("time_one", (CH_BASE, EMB_DIM)),
        ("time_bias_one", (EMB_DIM,)),
        ("time_two", (EMB_DIM, EMB_DIM)),
        ("time_bias_two", (EMB_DIM,)),
        ("class_table", (CLASSES, EMB_DIM)),
    ]
    for parameter_prefix in ("first", "second"):
        shapes += [
            (parameter_prefix + "_gains", (4, CH_MID)),
            (parameter_prefix + "_conv_one", (9 * CH_MID, CH_MID)),
            (parameter_prefix + "_bias_one", (CH_MID,)),
            (parameter_prefix + "_embed", (EMB_DIM, 2 * CH_MID)),
            (parameter_prefix + "_embed_bias", (2 * CH_MID,)),
            (parameter_prefix + "_conv_two", (9 * CH_MID, CH_MID)),
            (parameter_prefix + "_bias_two", (CH_MID,)),
        ]
    shapes += [
        ("attn_gains", (2, CH_MID)),
        ("attn_qkv", (CH_MID, 3 * CH_MID)),
        ("attn_out", (CH_MID, CH_MID)),
        ("attn_bias", (CH_MID,)),
        ("final_gains", (2, CH_MID)),
        ("conv_out", (9 * CH_MID, 3)),
        ("bias_out", (3,)),
    ]
    return shapes


def unflatten(flat_vec):
    network_parameters = {}
    offset = 0
    for key_name, seg_shape in layout():
        length = math.prod(seg_shape)
        network_parameters[key_name] = flat_vec[offset : offset + length].reshape(seg_shape)
        offset += length
    return network_parameters


def flatten(grad_map, length):
    flat_vec = jnp.concatenate([grad_map[key_name].reshape(-1) for key_name, seg_shape in layout()])
    return jnp.pad(flat_vec, (0, length - flat_vec.shape[0]))


def karras(index):
    ramp_frac = index.astype(jnp.float32) / (DISCRETE - 1)
    low_root = SIGMA_LOW ** (1.0 / RHO_POWER)
    high_root = SIGMA_HIGH ** (1.0 / RHO_POWER)
    return (low_root + ramp_frac * (high_root - low_root)) ** RHO_POWER


def preconditioning_factors(noise_sigma_level):
    variance_sum = noise_sigma_level * noise_sigma_level + SIGMA_DATA**2
    skip_scaling_factor = SIGMA_DATA**2 / ((noise_sigma_level - SIGMA_LOW) ** 2 + SIGMA_DATA**2)
    output_scaling_factor = (noise_sigma_level - SIGMA_LOW) * SIGMA_DATA * lax.rsqrt(variance_sum)
    return (skip_scaling_factor, output_scaling_factor, lax.rsqrt(variance_sum))


def noise_features(noise_sigma_level):
    half_width = CH_BASE // 2
    frequency = jnp.exp(-math.log(10000.0) * jnp.arange(half_width, dtype=jnp.float32) / half_width)
    phases = 250.0 * jnp.log(noise_sigma_level) * frequency
    return jnp.concatenate([jnp.cos(phases), jnp.sin(phases)])


def group_norm(values, gain_row, shift_row):
    grouped = values.reshape(-1, GROUPS, values.shape[-1] // GROUPS)
    center = jnp.mean(grouped, axis=(0, 2), keepdims=True)
    spread = jnp.mean(jnp.square(grouped - center), axis=(0, 2), keepdims=True)
    normed = ((grouped - center) * lax.rsqrt(spread + EPSILON)).reshape(values.shape)
    return normed * gain_row + shift_row


def norm_act(values, gain_row, shift_row):
    return jax.nn.silu(group_norm(values, gain_row, shift_row))


def norm_modulate(values, gain_row, shift_row, modulation):
    normed = group_norm(values, gain_row, shift_row)
    return jax.nn.silu(normed * (1.0 + modulation[:CH_MID]) + modulation[CH_MID:])


def modulate_piece(condition_embedding, weight, bias_vec):
    return jnp.dot(jax.nn.silu(condition_embedding), weight, precision=HIGHEST) + bias_vec


def embed_piece(features, onehot, time_one, time_bias_one, time_two, time_bias_two, class_table):
    inner_out = jax.nn.silu(jnp.dot(features, time_one, precision=HIGHEST) + time_bias_one)
    second_activation = jnp.dot(inner_out, time_two, precision=HIGHEST) + time_bias_two
    return second_activation + jnp.dot(onehot, class_table, precision=HIGHEST)


def small_weights(network_parameters):
    return tuple(
        (
            network_parameters[key_name].astype(jnp.float32)
            for key_name in (
                "time_one",
                "time_bias_one",
                "time_two",
                "time_bias_two",
                "class_table",
            )
        )
    )


def patches(image_low, stride):
    height, breadth, channels = image_low.shape
    out_height, out_breadth = (height // stride, breadth // stride)
    padded = jnp.pad(image_low, ((1, 1), (1, 1), (0, 0)))
    pieces = [
        padded[
            tap_index // 3 : tap_index // 3 + stride * out_height : stride,
            tap_index % 3 : tap_index % 3 + stride * out_breadth : stride,
        ]
        for tap_index in range(9)
    ]
    return jnp.concatenate(pieces, axis=2).reshape(out_height * out_breadth, 9 * channels)


def unpatch(columns, image_shape, stride):
    height, breadth, channels = image_shape
    out_height, out_breadth = (height // stride, breadth // stride)
    pieces = columns.reshape(out_height, out_breadth, 9, channels)
    padded = jnp.zeros((height + 2, breadth + 2, channels), jnp.float32)
    for tap_index in range(9):
        row_start, col_start = (tap_index // 3, tap_index % 3)
        padded = padded.at[
            row_start : row_start + stride * out_height : stride,
            col_start : col_start + stride * out_breadth : stride,
        ].add(pieces[:, :, tap_index])
    return padded[1:-1, 1:-1].reshape(height * breadth, channels)


def conv_apply(image_low, weight, stride):
    return jnp.dot(patches(image_low, stride), weight, preferred_element_type=jnp.float32)


def conv_grads(image_low, weight, grad_low, stride, need_input):
    weight_grad = lax.dot_general(
        patches(image_low, stride), grad_low, CONTRACT_ROWS, preferred_element_type=jnp.float32
    )
    if not need_input:
        return (weight_grad, None)
    columns = lax.dot_general(grad_low, weight, CONTRACT_COLS, preferred_element_type=jnp.float32)
    return (weight_grad, unpatch(columns, image_low.shape, stride))


def res_forward(hidden_activation, condition_embedding, network_parameters, parameter_prefix):
    half_res = RES // 2
    gain_rows = network_parameters[parameter_prefix + "_gains"].astype(jnp.float32)
    act_one = norm_act(hidden_activation, gain_rows[0], gain_rows[1]).astype(jnp.bfloat16)
    inner_out = (
        conv_apply(
            act_one.reshape(half_res, half_res, CH_MID),
            network_parameters[parameter_prefix + "_conv_one"],
            1,
        )
        + network_parameters[parameter_prefix + "_bias_one"]
    )
    modulation = modulate_piece(
        condition_embedding,
        network_parameters[parameter_prefix + "_embed"].astype(jnp.float32),
        network_parameters[parameter_prefix + "_embed_bias"].astype(jnp.float32),
    )
    act_two = norm_modulate(inner_out, gain_rows[2], gain_rows[3], modulation).astype(jnp.bfloat16)
    output = (
        hidden_activation
        + conv_apply(
            act_two.reshape(half_res, half_res, CH_MID),
            network_parameters[parameter_prefix + "_conv_two"],
            1,
        )
        + network_parameters[parameter_prefix + "_bias_two"]
    )
    return (output, (hidden_activation, inner_out))


def res_backward(grad_out, saved_state, condition_embedding, network_parameters, parameter_prefix):
    half_res = RES // 2
    hidden_activation, inner_out = saved_state
    gain_rows = network_parameters[parameter_prefix + "_gains"].astype(jnp.float32)
    modulation, modulate_pull = jax.vjp(
        modulate_piece,
        condition_embedding,
        network_parameters[parameter_prefix + "_embed"].astype(jnp.float32),
        network_parameters[parameter_prefix + "_embed_bias"].astype(jnp.float32),
    )
    act_two, second_pull = jax.vjp(norm_modulate, inner_out, gain_rows[2], gain_rows[3], modulation)
    grad_map = {parameter_prefix + "_bias_two": jnp.sum(grad_out, axis=0)}
    grad_map[parameter_prefix + "_conv_two"], grad_act = conv_grads(
        act_two.astype(jnp.bfloat16).reshape(half_res, half_res, CH_MID),
        network_parameters[parameter_prefix + "_conv_two"],
        grad_out.astype(jnp.bfloat16),
        1,
        True,
    )
    grad_inner, grad_gain_two, grad_shift_two, grad_mod = second_pull(grad_act)
    grad_emb, grad_map[parameter_prefix + "_embed"], grad_map[parameter_prefix + "_embed_bias"] = (
        modulate_pull(grad_mod)
    )
    grad_map[parameter_prefix + "_bias_one"] = jnp.sum(grad_inner, axis=0)
    act_one, first_pull = jax.vjp(norm_act, hidden_activation, gain_rows[0], gain_rows[1])
    grad_map[parameter_prefix + "_conv_one"], grad_act = conv_grads(
        act_one.astype(jnp.bfloat16).reshape(half_res, half_res, CH_MID),
        network_parameters[parameter_prefix + "_conv_one"],
        grad_inner.astype(jnp.bfloat16),
        1,
        True,
    )
    grad_hidden, grad_gain_one, grad_shift_one = first_pull(grad_act)
    grad_map[parameter_prefix + "_gains"] = jnp.stack(
        [grad_gain_one, grad_shift_one, grad_gain_two, grad_shift_two]
    )
    return (grad_out + grad_hidden, grad_emb, grad_map)


def attn_scores(query_block, key_vals):
    return jnp.einsum(
        "qhd,khd->hqk", query_block, key_vals, preferred_element_type=jnp.float32
    ) * HEAD_DIM ** (-0.5)


def split_triple(triple):
    tokens = triple.shape[0]
    block_rows = min(512, tokens)
    queries = triple[:, :CH_MID].reshape(tokens // block_rows, block_rows, HEADS, HEAD_DIM)
    key_vals = triple[:, CH_MID : 2 * CH_MID].reshape(tokens, HEADS, HEAD_DIM)
    values_v = triple[:, 2 * CH_MID :].reshape(tokens, HEADS, HEAD_DIM)
    return (queries, key_vals, values_v)


def attn_forward(hidden_activation, network_parameters):
    tokens = hidden_activation.shape[0]
    gain_rows = network_parameters["attn_gains"].astype(jnp.float32)
    normed = group_norm(hidden_activation, gain_rows[0], gain_rows[1]).astype(jnp.bfloat16)
    triple = jnp.dot(
        normed, network_parameters["attn_qkv"], preferred_element_type=jnp.float32
    ).astype(jnp.bfloat16)
    queries, key_vals, values_v = split_triple(triple)

    def one_block(query_block):
        scores = attn_scores(query_block, key_vals)
        row_max = jnp.max(scores, axis=-1, keepdims=True)
        weights = jnp.exp(scores - row_max)
        totals = jnp.sum(weights, axis=-1, keepdims=True)
        prob_vals = (weights / totals).astype(jnp.bfloat16)
        mixed_out = jnp.einsum(
            "hqk,khd->qhd", prob_vals, values_v, preferred_element_type=jnp.float32
        )
        return (mixed_out, row_max[..., 0] + jnp.log(totals[..., 0]))

    mixed_out, logsum = lax.map(one_block, queries)
    mixed_low = mixed_out.reshape(tokens, CH_MID).astype(jnp.bfloat16)
    output = (
        hidden_activation
        + jnp.dot(mixed_low, network_parameters["attn_out"], preferred_element_type=jnp.float32)
        + network_parameters["attn_bias"]
    )
    return (output, (hidden_activation, triple, logsum, mixed_low))


def attn_backward(grad_out, saved_state, network_parameters):
    hidden_activation, triple, logsum, mixed_low = saved_state
    tokens = hidden_activation.shape[0]
    scale_factor = HEAD_DIM ** (-0.5)
    grad_map = {"attn_bias": jnp.sum(grad_out, axis=0)}
    grad_low = grad_out.astype(jnp.bfloat16)
    grad_map["attn_out"] = lax.dot_general(
        mixed_low, grad_low, CONTRACT_ROWS, preferred_element_type=jnp.float32
    )
    grad_mixed = lax.dot_general(
        grad_low, network_parameters["attn_out"], CONTRACT_COLS, preferred_element_type=jnp.float32
    ).astype(jnp.bfloat16)
    queries, key_vals, values_v = split_triple(triple)
    grad_blocks = grad_mixed.reshape(queries.shape)

    def one_block(carried, inputs):
        query_block, grad_block, logsum_block = inputs
        prob_vals = jnp.exp(attn_scores(query_block, key_vals) - logsum_block[..., None])
        grad_values = carried[1] + jnp.einsum(
            "hqk,qhd->khd",
            prob_vals.astype(jnp.bfloat16),
            grad_block,
            preferred_element_type=jnp.float32,
        )
        grad_probs = jnp.einsum(
            "qhd,khd->hqk", grad_block, values_v, preferred_element_type=jnp.float32
        )
        grad_scores = (
            prob_vals * (grad_probs - jnp.sum(grad_probs * prob_vals, axis=-1, keepdims=True))
        ).astype(jnp.bfloat16)
        grad_query = (
            jnp.einsum("hqk,khd->qhd", grad_scores, key_vals, preferred_element_type=jnp.float32)
            * scale_factor
        )
        grad_keys = (
            carried[0]
            + jnp.einsum(
                "hqk,qhd->khd", grad_scores, query_block, preferred_element_type=jnp.float32
            )
            * scale_factor
        )
        return ((grad_keys, grad_values), grad_query)

    zero_acc = jnp.zeros((tokens, HEADS, HEAD_DIM), jnp.float32)
    (grad_keys, grad_values), grad_queries = lax.scan(
        one_block, (zero_acc, zero_acc), (queries, grad_blocks, logsum)
    )
    grad_triple = jnp.concatenate(
        [
            grad_queries.reshape(tokens, CH_MID),
            grad_keys.reshape(tokens, CH_MID),
            grad_values.reshape(tokens, CH_MID),
        ],
        axis=1,
    ).astype(jnp.bfloat16)
    gain_rows = network_parameters["attn_gains"].astype(jnp.float32)
    normed, norm_pull = jax.vjp(group_norm, hidden_activation, gain_rows[0], gain_rows[1])
    grad_map["attn_qkv"] = lax.dot_general(
        normed.astype(jnp.bfloat16), grad_triple, CONTRACT_ROWS, preferred_element_type=jnp.float32
    )
    grad_normed = lax.dot_general(
        grad_triple,
        network_parameters["attn_qkv"],
        CONTRACT_COLS,
        preferred_element_type=jnp.float32,
    )
    grad_hidden, grad_gain, grad_shift = norm_pull(grad_normed)
    grad_map["attn_gains"] = jnp.stack([grad_gain, grad_shift])
    return (grad_out + grad_hidden, grad_map)


def upsampled_act(hidden_activation, network_parameters):
    half_res = RES // 2
    gain_rows = network_parameters["final_gains"].astype(jnp.float32)
    act_full, act_pull = jax.vjp(norm_act, hidden_activation, gain_rows[0], gain_rows[1])
    act_low = act_full.astype(jnp.bfloat16).reshape(half_res, half_res, CH_MID)
    return (jnp.repeat(jnp.repeat(act_low, 2, axis=0), 2, axis=1), act_pull)


def denoise_forward(network_parameters, noisy, noise_sigma_level, onehot):
    skip_scaling_factor, output_scaling_factor, input_scaling_factor = preconditioning_factors(
        noise_sigma_level
    )
    input_low = (input_scaling_factor * noisy).astype(jnp.bfloat16)
    first_low = (
        (conv_apply(input_low, network_parameters["conv_in"], 1) + network_parameters["bias_in"])
        .astype(jnp.bfloat16)
        .reshape(RES, RES, CH_BASE)
    )
    hidden_activation = (
        conv_apply(first_low, network_parameters["conv_down"], 2) + network_parameters["bias_down"]
    )
    condition_embedding = embed_piece(
        noise_features(noise_sigma_level), onehot, *small_weights(network_parameters)
    )
    hidden_activation, saved_one = res_forward(
        hidden_activation, condition_embedding, network_parameters, "first"
    )
    hidden_activation, saved_attn = attn_forward(hidden_activation, network_parameters)
    hidden_activation, saved_two = res_forward(
        hidden_activation, condition_embedding, network_parameters, "second"
    )
    upsampled, act_pull = upsampled_act(hidden_activation, network_parameters)
    model_out = (
        conv_apply(upsampled, network_parameters["conv_out"], 1) + network_parameters["bias_out"]
    )
    denoised = skip_scaling_factor * noisy + output_scaling_factor * model_out.reshape(RES, RES, 3)
    return (
        denoised,
        (
            input_low,
            first_low,
            condition_embedding,
            saved_one,
            saved_attn,
            saved_two,
            hidden_activation,
        ),
    )


def denoise_backward(grad_denoised, saved_state, network_parameters, noise_sigma_level, onehot):
    half_res = RES // 2
    input_low, first_low, condition_embedding, saved_one, saved_attn, saved_two, last_hidden = (
        saved_state
    )
    skip_scaling_factor, output_scaling_factor, input_scaling_factor = preconditioning_factors(
        noise_sigma_level
    )
    grad_model = (output_scaling_factor * grad_denoised).reshape(RES * RES, 3)
    upsampled, act_pull = upsampled_act(last_hidden, network_parameters)
    grad_map = {"bias_out": jnp.sum(grad_model, axis=0)}
    grad_map["conv_out"], grad_up = conv_grads(
        upsampled, network_parameters["conv_out"], grad_model.astype(jnp.bfloat16), 1, True
    )
    grad_act = (
        grad_up.reshape(half_res, 2, half_res, 2, CH_MID).sum(axis=(1, 3)).reshape(-1, CH_MID)
    )
    grad_hidden, grad_gain, grad_shift = act_pull(grad_act)
    grad_map["final_gains"] = jnp.stack([grad_gain, grad_shift])
    grad_hidden, grad_emb_two, more_grads = res_backward(
        grad_hidden, saved_two, condition_embedding, network_parameters, "second"
    )
    grad_map.update(more_grads)
    grad_hidden, more_grads = attn_backward(grad_hidden, saved_attn, network_parameters)
    grad_map.update(more_grads)
    grad_hidden, grad_emb_one, more_grads = res_backward(
        grad_hidden, saved_one, condition_embedding, network_parameters, "first"
    )
    grad_map.update(more_grads)
    embedding_again, embed_pull = jax.vjp(
        partial(embed_piece, noise_features(noise_sigma_level), onehot),
        *small_weights(network_parameters)
    )
    small_names = ("time_one", "time_bias_one", "time_two", "time_bias_two", "class_table")
    for key_name, grad_value in zip(small_names, embed_pull(grad_emb_one + grad_emb_two)):
        grad_map[key_name] = grad_value
    grad_map["bias_down"] = jnp.sum(grad_hidden, axis=0)
    grad_map["conv_down"], grad_first = conv_grads(
        first_low, network_parameters["conv_down"], grad_hidden.astype(jnp.bfloat16), 2, True
    )
    grad_map["bias_in"] = jnp.sum(grad_first, axis=0)
    grad_map["conv_in"], unused_grad = conv_grads(
        input_low, network_parameters["conv_in"], grad_first.astype(jnp.bfloat16), 1, False
    )
    return grad_map


def per_device(
    images,
    noise_draws,
    labels,
    step_index,
    valid_rows,
    counts,
    master_weights,
    momentum,
    ema_weights,
):
    online_low, target_low = (
        lax.all_gather(master_weights.astype(jnp.bfloat16), "fsdp", axis=0, tiled=True),
        lax.all_gather(ema_weights.astype(jnp.bfloat16), "fsdp", axis=0, tiled=True),
    )
    online = unflatten(online_low)
    target = unflatten(target_low)
    flat_length = online_low.shape[0]
    slot_live = (jnp.arange(MB_DEV) < counts[0]).astype(jnp.float32)
    row_live = (jnp.arange(RES)[None, :] < valid_rows[:, None]).astype(jnp.float32)
    pixel_mask = slot_live[:, None] * row_live
    pixel_total = 3.0 * RES * lax.psum(jnp.sum(pixel_mask), "fsdp")
    local_loss = jnp.zeros((), jnp.float32)
    pending = []
    for slot_index in range(MB_DEV):
        sigma_lo = karras(step_index[slot_index])
        sigma_hi = karras(step_index[slot_index] + 1)
        onehot = (jnp.arange(CLASSES) == labels[slot_index]).astype(jnp.float32)
        clean_img = images[slot_index]
        noise_img = noise_draws[slot_index]
        target_out, unused_state = denoise_forward(
            target, clean_img + sigma_lo * noise_img, sigma_lo, onehot
        )
        online_out, saved_state = denoise_forward(
            online, clean_img + sigma_hi * noise_img, sigma_hi, onehot
        )
        residual_gap = online_out - target_out
        weighted = pixel_mask[slot_index][:, None, None]
        local_loss = local_loss + jnp.sum(weighted * jnp.square(residual_gap))
        pending.append((2.0 * weighted * residual_gap / pixel_total, saved_state, sigma_hi, onehot))
    back_params = unflatten(
        lax.all_gather(master_weights.astype(jnp.bfloat16), "fsdp", axis=0, tiled=True)
    )
    total_grads = None
    for grad_denoised, saved_state, sigma_hi, onehot in pending:
        slot_grads = denoise_backward(grad_denoised, saved_state, back_params, sigma_hi, onehot)
        total_grads = (
            slot_grads if total_grads is None else jax.tree.map(jnp.add, total_grads, slot_grads)
        )
    reduced = lax.psum_scatter(
        flatten(total_grads, flat_length), "fsdp", scatter_dimension=0, tiled=True
    )
    new_momentum = MOMENTUM * momentum + reduced
    new_master = master_weights - LEARN_RATE * (reduced + MOMENTUM * new_momentum)
    new_ema = EMA_DECAY * ema_weights + (1.0 - EMA_DECAY) * new_master
    loss_sum, bias_gradient = lax.psum((local_loss, total_grads["bias_out"]), "fsdp")
    loss = loss_sum / pixel_total
    return (loss, new_momentum, new_master, new_ema, bias_gradient)


def solution(mesh):
    placed = (
        P("fsdp", None, None, None),
        P("fsdp", None, None, None),
        P("fsdp"),
        P("fsdp"),
        P("fsdp"),
        P("fsdp"),
        P("fsdp"),
        P("fsdp"),
        P("fsdp"),
    )
    return jax.shard_map(
        per_device,
        mesh=mesh,
        in_specs=placed,
        out_specs=(P(), P("fsdp"), P("fsdp"), P("fsdp"), P()),
        check_vma=False,
    )
```

profile of v0, /device:TPU:0, one launch (start us, length us, event | category | flops | bytes accessed | tf_op | source)
XLA Modules:
  0.0 2700.8 jit_solution(3443541189295662057)
XLA Ops:
  11.8 43.0 %psum.22 = f32[]{:T(128)} all-reduce(f32[]{:T(128)} %get-tuple-element.1717), channel_id=1, replica_groups=mesh['fsdp'=32] {'fsdp'}, use_global_device_ids=true, to_apply=%region_108.109 | all-reduce | flops 1 | bytes 8 | tf_op jit(solution)/shard_map/psum | solution.py:491
  80.8 57.8 %all-gather.3.cloned.1.call-done = bf16[9273344]{0:T(1024)(128)(2,1)} async-done(((bf16[289792]{0:T(1024)(128)(2,1)}), bf16[9273344]{0:T(1024)(128)(2,1)}) %all-gather.3.cloned.1.call-update) | async-done | bytes 18546704 | tf_op jit(solution)/shard_map/all_gather | solution.py:482
  230.9 32.3 %all-gather.5.cloned.1.call-done = bf16[9273344]{0:T(1024)(128)(2,1)} async-done(((bf16[289792]{0:T(1024)(128)(2,1)}), bf16[9273344]{0:T(1024)(128)(2,1)}) %all-gather.5.cloned.1.call-update) | async-done | bytes 18546704 | tf_op jit(solution)/shard_map/all_gather | solution.py:483
  816.7 15.4 scatter-add.421
  836.7 15.4 scatter-add.424
  856.7 13.9 scatter-add.426
  873.4 14.1 scatter-add.429
  892.1 13.6 scatter-add.431
  908.5 13.6 scatter-add.434
  934.4 15.4 scatter-add.511
  954.4 15.4 scatter-add.514
  974.4 13.9 scatter-add.516
  991.1 13.9 scatter-add.519
  1009.6 13.6 scatter-add.521
  1026.1 13.6 scatter-add.524
  1446.0 18.9 scatter_fusion.9
  1464.9 18.9 scatter_fusion.10
  1483.8 18.8 scatter_fusion.11
  1570.5 13.7 scatter_fusion.17
  1631.8 18.9 scatter_fusion
  1817.5 301.6 %concatenate.903 = f32[9272451]{0:T(1024)} concatenate(f32[5184]{0:T(1024)S(1)} %reshape.5061, f32[192]{0:T(256)S(1)} %add.2401, f32[663552]{0:T(1024)} %reshape.5062, f32[384]{0:T(512)S(1)} %add.2403, f32[147456]{0:T(1024)} %reshape.5063, f32[768]{0:T(1024)S(1)} %get-tuple-element.1299, f32[589824]{0:T(1024)} %reshape.5064, f32[768]{0:T(1024)S(1)} %copy-done.356, ...), dimensions={0} | concatenate | bytes 74179608 | tf_op jit(solution)/shard_map/concatenate | solution.py:79
  2119.2 27.8 %pad.536 = f32[9273344]{0:T(1024)} pad(f32[9272451]{0:T(1024)} %concatenate.903, f32[]{:T(128)} %constant.2245.clone.1), padding=0_893 | pad | bytes 74183184 | tf_op jit(solution)/shard_map/jit(_pad)/pad | solution.py:80
  2148.7 40.5 %all-reduce.48 = (f32[]{:T(128)}, f32[3]{0:T(128)}) all-reduce(f32[]{:T(128)S(6)} %add.2295, f32[3]{0:T(128)S(1)} %copy-done.431), channel_id=1, replica_groups=mesh['fsdp'=32] {'fsdp'}, use_global_device_ids=true, to_apply=%region_106.107 | all-reduce | flops 4 | bytes 32 | tf_op jit(solution)/shard_map/psum | solution.py:525
  2189.9 499.5 %all-reduce.51.cloned.1.call-done = f32[9273344]{0:T(1024)} async-done(((f32[9273344]{0:T(1024)}), f32[9273344]{0:T(1024)}) %all-reduce.51.cloned.1.call-update) | async-done | bytes 37093392
  (2195 shorter events, 1405.3 us)
Async XLA Ops:
  7.2 131.4 %all-gather.3.cloned.1.call-start = ((), (), s32[]{:S(2)}) async-start(), calls=%async_computation | async-start | bytes 19126272 | tf_op jit(solution)/shard_map/all_gather | solution.py:482
  9.4 45.4 %copy-start.428 = (s32[2]{0:T(128)S(1)}, s32[2]{0:T(128)}, u32[]{:S(2)}) copy-start(s32[2]{0:T(128)} %param.192) | copy-start | bytes 28
  9.4 49.3 %copy-start.429 = (s32[2]{0:T(128)S(1)}, s32[2]{0:T(128)}, u32[]{:S(2)}) copy-start(s32[2]{0:T(128)} %param.191) | copy-start | bytes 28
  9.4 58.7 %copy-start.241 = (f32[2,32,32,3]{2,1,3,0:T(8,128)S(1)}, f32[2,32,32,3]{2,1,3,0:T(8,128)}, u32[]{:S(2)}) copy-start(f32[2,32,32,3]{2,1,3,0:T(8,128)} %param.189) | copy-start | bytes 73732
  9.5 58.7 %copy-start.242 = (f32[2,32,32,3]{2,1,3,0:T(8,128)S(1)}, f32[2,32,32,3]{2,1,3,0:T(8,128)}, u32[]{:S(2)}) copy-start(f32[2,32,32,3]{2,1,3,0:T(8,128)} %param.190) | copy-start | bytes 73732
  9.5 253.7 %all-gather.5.cloned.1.call-start = ((), (), s32[]{:S(2)}) async-start(), calls=%async_computation.1 | async-start | bytes 19126272 | tf_op jit(solution)/shard_map/all_gather | solution.py:483
  10.4 2678.9 %all-reduce.51.cloned.1.call-start = ((), (), s32[]{:S(2)}) async-start(), calls=%async_computation.2 | async-start | bytes 74186752
  72.2 68.5 %copy-start.141 = (bf16[32,32,27]{1,2,0:T(8,128)(2,1)}, bf16[32,32,27]{1,2,0:T(8,128)(2,1)S(1)}, u32[]{:S(2)}) copy-start(bf16[32,32,27]{1,2,0:T(8,128)(2,1)S(1)} %concatenate.793) | copy-start | bytes 165892
  654.0 37.2 %copy-start.257 = (f32[384]{0:T(512)}, f32[384]{0:T(512)S(1)}, u32[]{:S(2)}) copy-start(f32[384]{0:T(512)S(1)} %get-tuple-element.1683) | copy-start | bytes 4612
  665.5 21.2 copy-start.50
  674.3 64.5 %copy-start.320 = (f32[384]{0:T(512)}, f32[384]{0:T(512)S(1)}, u32[]{:S(2)}) copy-start(f32[384]{0:T(512)S(1)} %get-tuple-element.1654) | copy-start | bytes 4612
  674.3 64.5 %copy-start.348 = (f32[384]{0:T(512)}, f32[384]{0:T(512)S(1)}, u32[]{:S(2)}) copy-start(f32[384]{0:T(512)S(1)} %get-tuple-element.1655) | copy-start | bytes 4612
  675.8 63.1 %copy-start.322 = (f32[384]{0:T(512)}, f32[384]{0:T(512)S(1)}, u32[]{:S(2)}) copy-start(f32[384]{0:T(512)S(1)} %get-tuple-element.1680) | copy-start | bytes 4612
  699.1 42.9 %copy-start.38 = (f32[256,384]{1,0:T(8,128)}, f32[256,384]{1,0:T(8,128)S(1)}, u32[]{:S(2)}) copy-start(f32[256,384]{1,0:T(8,128)S(1)} %get-tuple-element.1770) | copy-start | bytes 1179652
  700.1 21.9 copy-start.305
  751.1 297.2 %copy-start.315 = (f32[384]{0:T(512)}, f32[384]{0:T(512)S(1)}, u32[]{:S(2)}) copy-start(f32[384]{0:T(512)S(1)} %mul.2126) | copy-start | bytes 4612
  1054.8 47.0 %copy-start.159 = (bf16[256,384]{1,0:T(8,128)(2,1)}, bf16[256,384]{1,0:T(8,128)(2,1)S(1)}, u32[]{:S(2)}) copy-start(bf16[256,384]{1,0:T(8,128)(2,1)S(1)} %convert_element_type.617) | copy-start | bytes 589828
  1260.5 47.3 %copy-start.163 = (bf16[256,384]{1,0:T(8,128)(2,1)}, bf16[256,384]{1,0:T(8,128)(2,1)S(1)}, u32[]{:S(2)}) copy-start(bf16[256,384]{1,0:T(8,128)(2,1)S(1)} %convert_element_type.623) | copy-start | bytes 589828
  1350.4 49.0 %copy-start.169 = (bf16[256,384]{1,0:T(8,128)(2,1)}, bf16[256,384]{1,0:T(8,128)(2,1)S(1)}, u32[]{:S(2)}) copy-start(bf16[256,384]{1,0:T(8,128)(2,1)S(1)} %get-tuple-element.1395) | copy-start | bytes 589828
  1446.0 18.9 copy-start.7
  1817.3 301.9 %copy-start.430 = (f32[3]{0:T(128)}, f32[3]{0:T(128)S(1)}, u32[]{:S(2)}) copy-start(f32[3]{0:T(128)S(1)} %add.2435) | copy-start | bytes 40
  2147.0 542.4 %copy-start.87 = (f32[289792]{0:T(1024)S(1)}, f32[289792]{0:T(1024)}, u32[]{:S(2)}) copy-start(f32[289792]{0:T(1024)} %param.195) | copy-start | bytes 3477508
  2147.0 542.4 %copy-start.89 = (f32[289792]{0:T(1024)S(1)}, f32[289792]{0:T(1024)}, u32[]{:S(2)}) copy-start(f32[289792]{0:T(1024)} %param.197) | copy-start | bytes 3477508
  2147.0 542.4 %copy-start.184 = (f32[289792]{0:T(1024)S(1)}, f32[289792]{0:T(1024)}, u32[]{:S(2)}) copy-start(f32[289792]{0:T(1024)} %param.196) | copy-start | bytes 3477508
  (435 other events, 1784.6 us)
Sparse Core Ops, SparseCore 0:
  11.5 127.0 all-gather.2
  142.1 121.1 all-gather.4
  2147.1 542.1 all-reduce.50
where the time goes:
time: 2740 us; the launch traced here: 2700 us
  local copies, waits for them, and re-layouts  1310 us (48%)
  waiting for transfers between devices  590 us (22%)
  other arithmetic  525 us (19%)
  matrix products  163 us (6%)
  blocking collectives  83.6 us (3%)
  between operations  32 us (1%)
    unnamed x4, waiting for transfers between devices  500 us
    scatter-add x70, local copies, waits for them, and re-layouts, unpatch(): padded = padded.at[row_start:row_start + stride * out_height:stride, col_...  392 us
    concatenate x1, local copies, waits for them, and re-layouts, flatten(): jnp.concatenate([grad_map[key_name].reshape(-1) for key_name, seg_shape i...  302 us
    scatter-add x38, other arithmetic, unpatch(): padded = padded.at[row_start:row_start + stride * out_height:stride, col_...  289 us
    slice x60, local copies, waits for them, and re-layouts, patches(): padded[tap_index // 3:tap_index // 3 + stride * out_height:stride, tap_in...  201 us
    unnamed x1072, local copies, waits for them, and re-layouts  96.2 us
    add x50, other arithmetic, unpatch(): padded = padded.at[row_start:row_start + stride * out_height:stride, col_...  84.7 us
    reshape x28, local copies, waits for them, and re-layouts, unflatten(): flat_vec[offset:offset + length].reshape(seg_shape)  64.8 us
  transfers between devices with their start and end apart: 3, of which 3 were waited for; matrix products, arithmetic and copies ran while one was open for 4% of the time, Pallas kernels for 0%

commit v1 on v0

v1 whole, which is shorter than its diff:
```python
import math

import jax
import jax.numpy as jnp
import numpy as np
from jax import lax
from jax.experimental import pallas as pl
from jax.experimental.pallas import tpu as pltpu
from jax.sharding import PartitionSpec as P

CH_BASE = 192
CH_MID = 384
EMB_DIM = 768
HEADS = 6
HEAD_DIM = 64
CLASSES = 1000
GROUPS = 32
RES = 32
MB_DEV = 2
DISCRETE = 40

EPSILON = 1e-05
SIGMA_DATA = 0.5
SIGMA_LOW = 0.002
SIGMA_HIGH = 80.0
RHO_POWER = 7.0
MOMENTUM = 0.9
EMA_DECAY = 0.9
LEARN_RATE = 2000.0

F32 = jnp.float32
BF16 = jnp.bfloat16
LINE = 128
HALF = RES // 2
PIX = HALF * HALF
ROWS = MB_DEV * PIX
GROUP_SIZE = PIX * (CH_MID // GROUPS)
CHUNK = 64
PADDED = 16 + MB_DEV * (PIX + 16)
NN = (((1,), (0,)), ((), ()))
NT = (((1,), (1,)), ((), ()))
TN = (((0,), (0,)), ((), ()))


class Place:
    pass


class Cut:
    def __init__(self):
        self.offset = 0

    def take(self, *shape):
        at = self.offset
        self.offset += math.prod(shape)
        return at // LINE


def block_place(cut):
    at = Place()
    at.gains = cut.take(4, CH_MID)
    at.conv_one = cut.take(9 * CH_MID, CH_MID)
    at.bias_one = cut.take(CH_MID)
    at.embed = cut.take(EMB_DIM, 2 * CH_MID)
    at.embed_bias = cut.take(2 * CH_MID)
    at.conv_two = cut.take(9 * CH_MID, CH_MID)
    at.bias_two = cut.take(CH_MID)
    return at


def places():
    cut, at = Cut(), Place()
    at.conv_in = cut.take(27, CH_BASE)
    at.bias_in = cut.take(CH_BASE)
    at.conv_down = cut.take(9 * CH_BASE, CH_MID)
    at.bias_down = cut.take(CH_MID)
    at.time_one = cut.take(CH_BASE, EMB_DIM)
    at.time_bias_one = cut.take(EMB_DIM)
    at.time_two = cut.take(EMB_DIM, EMB_DIM)
    at.time_bias_two = cut.take(EMB_DIM)
    at.class_table = cut.take(CLASSES, EMB_DIM)
    at.first = block_place(cut)
    at.second = block_place(cut)
    at.attn_gains = cut.take(2, CH_MID)
    at.attn_qkv = cut.take(CH_MID, 3 * CH_MID)
    at.attn_out = cut.take(CH_MID, CH_MID)
    at.attn_bias = cut.take(CH_MID)
    at.final_gains = cut.take(2, CH_MID)
    at.conv_out = cut.take(9 * CH_MID, 3)
    at.bias_out = cut.take(3)
    return at


AT = places()
TAIL = AT.conv_out
SHARDS, PLANE = 32, 8
SHARD = 2264
ROOM = 2272
ALL_LINES = SHARDS * SHARD
MIDDLE = ALL_LINES // 2
SPLIT = AT.first.conv_two // 16 * 16

V_DOWN, V_G1, V_B11, V_B12, V_AG, V_AB, V_FG, V_G2, V_B21, V_B22 = 0, 1, 5, 6, 7, 9, 10, 12, 16, 17
VEC_ROWS = 24


def group_table():
    at = np.arange(CH_MID) // (CH_MID // GROUPS)
    return (at[:, None] == at[None, :]).astype(np.float32)


def spread_tables():
    select = np.zeros((LINE, LINE), np.float32)
    gather = np.zeros((LINE, LINE), np.float32)
    for ky in range(3):
        for kx in range(3):
            for a in range(2):
                for b in range(2):
                    dy, dx = (a + ky - 1) // 2, (b + kx - 1) // 2
                    shift = (dy + 1) * 3 + dx + 1
                    for c in range(3):
                        out = (a * 2 + b) * 3 + c
                        select[(ky * 3 + kx) * 3 + c, shift * 12 + out] = 1.0
                        gather[shift * 12 + out, out] = 1.0
    return select, gather


def split3(v):
    hi = v.astype(BF16)
    rest = v - hi.astype(F32)
    mid = rest.astype(BF16)
    low = (rest - mid.astype(F32)).astype(BF16)
    return hi, mid, low


def dot(a, b, dims=NN):
    return lax.dot_general(a, b, dims, preferred_element_type=F32)


def dot3(a, b, dims=NN):
    rows = a.shape[0]
    hi, mid, low = split3(a)
    if rows % 16:
        out = dot(jnp.concatenate([p.astype(F32) for p in (hi, mid, low)], 0).astype(BF16), b, dims)
    else:
        out = dot(jnp.concatenate([hi, mid, low], 0), b, dims)
    return out[:rows] + out[rows : 2 * rows] + out[2 * rows :]


def outer(a, b):
    pa, pb = split3(a), split3(b)
    pairs = [(0, 0), (0, 1), (1, 0), (1, 1), (0, 2), (2, 0)]
    left = jnp.concatenate([pa[i].astype(F32) for i, _ in pairs], 0).astype(BF16)
    right = jnp.concatenate([pb[j].astype(F32) for _, j in pairs], 0).astype(BF16)
    return dot(left, right, TN)


def sigmoid(z):
    return 1.0 / (1.0 + jnp.exp(-z))


def silu(z):
    return z * sigmoid(z)


def silu_slope(z):
    s = sigmoid(z)
    return s * (1.0 + z * (1.0 - s))


def colsum(ref, base, count=PIX):
    def body(c, acc):
        return acc + jnp.sum(ref[pl.ds(pl.multiple_of(base + c * CHUNK, 8), CHUNK), :], 0, keepdims=True)

    return lax.fori_loop(0, count // CHUNK, body, jnp.zeros((1, ref.shape[1]), F32))


def eight(v):
    return jnp.broadcast_to(v, (8, v.shape[1]))


def group_mean(v, gm_ref):
    return dot3(eight(v), gm_ref[...])[:1] * (1.0 / GROUP_SIZE)


def group_stats(x_ref, img, gm_ref):
    mean = group_mean(colsum(x_ref, img * PIX), gm_ref)

    def body(c, acc):
        gap = x_ref[pl.ds(pl.multiple_of(img * PIX + c * CHUNK, 8), CHUNK), :] - mean
        return acc + jnp.sum(gap * gap, 0, keepdims=True)

    square = lax.fori_loop(0, PIX // CHUNK, body, jnp.zeros((1, CH_MID), F32))
    return mean, lax.rsqrt(group_mean(square, gm_ref) + EPSILON)


def norm_to(pbuf, x_ref, stats, scales, act):
    for img in range(MB_DEV):
        (mean, rstd), (k, o) = stats[img], scales[img]

        def body(c, carry):
            r = pl.multiple_of(img * PIX + c * CHUNK, 8)
            z = (x_ref[pl.ds(r, CHUNK), :] - mean) * rstd * k + o
            pbuf[pl.ds(r + 8, CHUNK), :] = silu(z) if act else z
            return carry

        lax.fori_loop(0, PIX // CHUNK, body, 0)


def norm_back(x_ref, d_ref, stats, scales, act, gm_ref, emit):
    sums = []
    for img in range(MB_DEV):
        (mean, rstd), (k, o) = stats[img], scales[img]

        def one(c, carry):
            r = pl.multiple_of(img * PIX + c * CHUNK, 8)
            xhat = (x_ref[pl.ds(r, CHUNK), :] - mean) * rstd
            dz = d_ref[pl.ds(r, CHUNK), :]
            if act:
                dz = dz * silu_slope(xhat * k + o)
                d_ref[pl.ds(r, CHUNK), :] = dz
            return (carry[0] + jnp.sum(dz, 0, keepdims=True), carry[1] + jnp.sum(dz * xhat, 0, keepdims=True))

        zero = jnp.zeros((1, CH_MID), F32)
        a, b = lax.fori_loop(0, PIX // CHUNK, one, (zero, zero))
        m1, m2 = group_mean(a * k, gm_ref), group_mean(b * k, gm_ref)

        def two(c, carry):
            r = pl.multiple_of(img * PIX + c * CHUNK, 8)
            xhat = (x_ref[pl.ds(r, CHUNK), :] - mean) * rstd
            emit(r, rstd * (d_ref[pl.ds(r, CHUNK), :] * k - m1 - xhat * m2))
            return carry

        lax.fori_loop(0, PIX // CHUNK, two, 0)
        sums.append((a, b))
    return sums


def clear_pads(sbuf):
    for k in range(3):
        for r in range(0, PADDED, PIX + 16):
            sbuf[k, pl.ds(r, 16), :] = jnp.zeros((16, sbuf.shape[2]), BF16)


def shift_to(sbuf, pbuf):
    column = lax.rem(lax.broadcasted_iota(jnp.int32, (CHUNK, CH_MID), 0), HALF)
    for r in range(0, ROWS, CHUNK):
        for k in range(3):
            v = pbuf[r + 7 + k : r + 7 + k + CHUNK, :]
            if k == 0:
                v = jnp.where(column == 0, 0.0, v)
            if k == 2:
                v = jnp.where(column == HALF - 1, 0.0, v)
            start = r + 16 * (r // PIX + 1)
            sbuf[k, start : start + CHUNK, :] = v.astype(BF16)


def shifted(sbuf, k, row):
    first = sbuf[k, pl.ds(pl.multiple_of(row, 16), PIX), :]
    second = sbuf[k, pl.ds(pl.multiple_of(row + PIX + 16, 16), PIX), :]
    return jnp.concatenate([first, second], 0)


def conv_forward(sbuf, w_ref, out_ref):
    def body(t, carry):
        lhs = shifted(sbuf, lax.rem(t, 3), lax.div(t, 3) * 16)
        out_ref[...] += dot(lhs, w_ref[pl.ds(pl.multiple_of(t * CH_MID, CH_MID), CH_MID), :])
        return carry

    lax.fori_loop(0, 9, body, 0)


def put_lines(g_ref, at, value, step, more=None):
    n = value.shape[0]
    low = at // 8 * 8
    start = low if more is None else pl.multiple_of(low + more, 8)
    view = g_ref.at[pl.ds(start, min(n * step + 8, g_ref.shape[0] - low)), :] if more is None else g_ref.at[pl.ds(start, n * step + 8), :]
    for j in range(step):
        view[pl.ds(at - low + j, n, stride=step), :] = value[:, j * LINE : (j + 1) * LINE]


def put_row(g_ref, at, row):
    for j in range(row.shape[1] // LINE):
        g_ref[pl.ds(at + j, 1), :] = row[:, j * LINE : (j + 1) * LINE]


def conv_back(sbuf, at_ref, w_ref, dx_ref, g_ref, at):
    dx_ref[...] = jnp.zeros_like(dx_ref)

    def body(s, carry):
        t = 8 - s
        d = shifted(sbuf, lax.rem(s, 3), lax.div(s, 3) * 16)
        w = w_ref[pl.ds(pl.multiple_of(t * CH_MID, CH_MID), CH_MID), :]
        dx_ref[...] += dot(d, w, NT)
        put_lines(g_ref, at, dot(at_ref[...], d), 3, t * (3 * CH_MID))
        return carry

    lax.fori_loop(0, 9, body, 0)


def transpose_to(at_ref, pbuf):
    for c in range(ROWS // LINE):
        at_ref[:, c * LINE : (c + 1) * LINE] = pbuf[8 + c * LINE : 8 + (c + 1) * LINE, :].T.astype(BF16)


class Lines:
    def __init__(self, lines, stage, wide, sem):
        self.lines, self.stage, self.wide, self.sem = lines, stage, wide, sem

    def copy(self, l0, l1):
        low, top = l0 // 16 * 16, -(-l1 // 16) * 16
        return pltpu.make_async_copy(
            self.lines.at[pl.ds(low, top - low), :], self.stage.at[pl.ds(0, top - low), :], self.sem
        )

    def start(self, span):
        self.copy(*span).start()

    def take(self, span, then=None):
        l0, l1 = span
        self.copy(l0, l1).wait()
        self.low = l0 // 16 * 16
        count = -(-l1 // 16) * 16 - self.low
        whole, rest = divmod(count, 256)

        def body(c, carry):
            r = pl.multiple_of(c * 256, 256)
            self.wide[pl.ds(r, 256), :] = self.stage[pl.ds(r, 256), :].astype(F32)
            return carry

        lax.fori_loop(0, whole, body, 0)
        if rest:
            self.wide[whole * 256 : count, :] = self.stage[whole * 256 : count, :].astype(F32)
        if then is not None:
            self.start(then)

    def matrix(self, w_ref, at, rows, step):
        block = 128 if rows % 192 else 192
        base = at - self.low
        low = base // 8 * 8

        def body(c, carry):
            r = pl.multiple_of(c * block, block)
            view = self.wide.at[pl.ds(pl.multiple_of(low + r * step, 8), block * step + 8), :]
            for j in range(step):
                v = view[pl.ds(base - low + j, block, stride=step), :]
                w_ref[pl.ds(r, block), j * LINE : (j + 1) * LINE] = v.astype(BF16)
            return carry

        lax.fori_loop(0, rows // block, body, 0)

    def row(self, at, step):
        base = at - self.low
        return jnp.concatenate([self.wide[pl.ds(base + j, 1), :] for j in range(step)], 1)


def attention_pair(qkv_ref, img, pair):
    rows = pl.ds(pl.multiple_of(img * PIX, PIX), PIX)
    return [qkv_ref[rows, part * CH_MID + pair * LINE : part * CH_MID + (pair + 1) * LINE] for part in range(3)]


def lane_half():
    return lax.broadcasted_iota(jnp.int32, (1, LINE), 1) < HEAD_DIM


def keep_half(v, half, side):
    mine = half if side == 0 else jnp.logical_not(half)
    return jnp.where(mine, v.astype(F32), 0.0).astype(BF16)


SPAN_TIME = (AT.time_one, AT.class_table)
SPAN_EMB1 = (AT.first.embed, AT.first.conv_two)
SPAN_EMB2 = (AT.second.embed, AT.second.conv_two)
SPAN_DOWN = (AT.conv_down, AT.time_one)
SPAN_ONE1 = (AT.first.gains, AT.first.embed)
SPAN_TWO1 = (AT.first.conv_two, AT.second.gains)
SPAN_ATTN = (AT.attn_gains, AT.conv_out)
SPAN_ONE2 = (AT.second.gains, AT.second.embed)
SPAN_TWO2 = (AT.second.conv_two, AT.attn_gains)


def block_scales(vec, row, mod_ref=None, mod_row=0):
    gain, shift = vec[row : row + 1, :], vec[row + 1 : row + 2, :]
    if mod_ref is None:
        return [(gain, shift)] * MB_DEV
    out = []
    for img in range(MB_DEV):
        scale = 1.0 + mod_ref[mod_row + img : mod_row + img + 1, :CH_MID]
        out.append((gain * scale, shift * scale + mod_ref[mod_row + img : mod_row + img + 1, CH_MID:]))
    return out


def upsample_masks(shift):
    dy, dx = shift // 3 - 1, shift % 3 - 1
    p = lax.broadcasted_iota(jnp.int32, (ROWS, 1), 0)
    i, j = lax.rem(lax.div(p, HALF), HALF), lax.rem(p, HALF)
    inside = (i + dy >= 0) & (i + dy < HALF) & (j + dx >= 0) & (j + dx < HALF)
    lane = lax.broadcasted_iota(jnp.int32, (1, LINE), 1)
    return inside & (lane >= shift * 12) & (lane < shift * 12 + 12), dy * HALF + dx


def forward_kernel(save, *refs):
    labels, lines, xp, win, bin_, wz, bz, phi, gm, sel, gat = refs[:11]
    f_out = refs[11]
    (h0s, h1, u1, h2, qkv, mixed, h3, u2, h4, vec, mod, emb, pre) = refs[12:25]
    if save:
        sw_time, sw_emb1, sw_emb2, sw_down, sw_11, sw_12, sw_attn, sw_21, sw_22 = refs[25:34]
    stage, wide, w_ref, w_sq, sbuf, pbuf, h0p, table, sem, save_sem, tab_sem = refs[34 if save else 25 :]
    src = Lines(lines, stage, wide, sem)
    pending = []

    def keep(source, target):
        if save:
            cp = pltpu.make_async_copy(source, target, save_sem)
            cp.start()
            pending.append(cp)

    def free():
        while pending:
            pending.pop().wait()

    tabs = []
    for n in range(MB_DEV):
        at = AT.class_table + labels[n] * (EMB_DIM // LINE)
        low = pl.multiple_of(lax.div(at, 16) * 16, 16)
        cp = pltpu.make_async_copy(lines.at[pl.ds(low, 32), :], table.at[pl.ds(n * 32, 32), :], tab_sem.at[n])
        cp.start()
        tabs.append((cp, at - low))
    src.start(SPAN_TIME)
    clear_pads(sbuf)
    pbuf[0:8, :] = jnp.zeros((8, CH_MID), F32)
    pbuf[ROWS + 8 : ROWS + 16, :] = jnp.zeros((8, CH_MID), F32)
    src.take(SPAN_TIME, SPAN_EMB1)
    src.matrix(w_sq.at[0], AT.time_one, CH_BASE, 6)
    src.matrix(w_sq.at[1], AT.time_two, EMB_DIM, 6)
    pre[...] = dot3(phi[...], w_sq[0, :CH_BASE, :]) + src.row(AT.time_bias_one, 6)
    emb[...] = dot3(silu(pre[...]), w_sq[1]) + src.row(AT.time_bias_two, 6)
    for n in range(MB_DEV):
        tabs[n][0].wait()
    wide[0 : 32 * MB_DEV, :] = table[...].astype(F32)
    for n in range(MB_DEV):
        for j in range(6):
            cols = slice(j * LINE, (j + 1) * LINE)
            emb[n : n + 1, cols] += wide[pl.ds(n * 32 + tabs[n][1] + j, 1), :]
    keep(w_sq.at[1], sw_time if save else None)
    se = silu(emb[...])
    src.take(SPAN_EMB1, SPAN_EMB2)
    src.matrix(w_sq.at[0], AT.first.embed, EMB_DIM, 6)
    m1 = dot3(se, w_sq[0]) + src.row(AT.first.embed_bias, 6)
    free()
    keep(w_sq.at[0], sw_emb1 if save else None)
    src.take(SPAN_EMB2, SPAN_DOWN)
    src.matrix(w_sq.at[1], AT.second.embed, EMB_DIM, 6)
    m2 = dot3(se, w_sq[1]) + src.row(AT.second.embed_bias, 6)
    free()
    keep(w_sq.at[1], sw_emb2 if save else None)
    mod[0:2, :] = m1[0:2]
    mod[2:4, :] = m2[0:2]
    mod[4:8, :] = jnp.zeros((4, EMB_DIM), F32)

    for ph in range(4):
        v = dot(xp[ph * ROWS : (ph + 1) * ROWS, :], win[...]) + bin_[...]
        h0s[ph * ROWS : (ph + 1) * ROWS, :] = v.astype(BF16)
    src.take(SPAN_DOWN, SPAN_ONE1)
    for j in range(3):
        vec[V_DOWN : V_DOWN + 1, j * LINE : (j + 1) * LINE] = src.row(AT.bias_down + j, 1)
    src.matrix(w_ref, AT.conv_down, 9 * CH_BASE, 3)
    free()
    keep(w_ref.at[pl.ds(0, 9 * CH_BASE), :], sw_down if save else None)
    h1[...] = jnp.broadcast_to(vec[V_DOWN : V_DOWN + 1, :], (ROWS, CH_MID))
    p = lax.broadcasted_iota(jnp.int32, (ROWS, 1), 0)
    has_left, has_up = lax.rem(p, HALF) > 0, lax.rem(lax.div(p, HALF), HALF) > 0
    for ph in range(4):
        h0p[0:32, :] = jnp.zeros((32, h0p.shape[1]), F32)
        h0p[32 : 32 + ROWS, :] = h0s[ph * ROWS : (ph + 1) * ROWS, :].astype(F32)
        for ky in ((0, 2) if ph // 2 else (1,)):
            for kx in ((0, 2) if ph % 2 else (1,)):
                back = (16 if ky == 0 else 0) + (1 if kx == 0 else 0)
                v = h0p[32 - back : 32 - back + ROWS, :]
                if ky == 0:
                    v = jnp.where(has_up, v, 0.0)
                if kx == 0:
                    v = jnp.where(has_left, v, 0.0)
                t = 3 * ky + kx
                h1[...] += dot(v[:, :CH_BASE].astype(BF16), w_ref[t * CH_BASE : (t + 1) * CH_BASE, :])

    def vectors(row, at, count):
        for n in range(count):
            for j in range(3):
                vec[row + n : row + n + 1, j * LINE : (j + 1) * LINE] = src.row(at + 3 * n + j, 1)

    def half_block(x_ref, scales, bias_row, add_ref, out_ref, at, target):
        src.matrix(w_ref, at, 9 * CH_MID, 3)
        keep(w_ref, target)
        stats = [group_stats(x_ref, img, gm) for img in range(MB_DEV)]
        norm_to(pbuf, x_ref, stats, scales, True)
        shift_to(sbuf, pbuf)
        bias = jnp.broadcast_to(vec[bias_row : bias_row + 1, :], (ROWS, CH_MID))
        out_ref[...] = bias if add_ref is None else add_ref[...] + bias
        conv_forward(sbuf, w_ref, out_ref)

    def block(h_in, u, h_out, prefix, g_row, b1_row, b2_row, mod_row, spans, nxt, targets):
        src.take(spans[0], spans[1])
        free()
        vectors(g_row, prefix.gains, 4)
        vectors(b1_row, prefix.bias_one, 1)
        half_block(h_in, block_scales(vec, g_row), b1_row, None, u, prefix.conv_one, targets[0])
        src.take(spans[1], nxt)
        free()
        vectors(b2_row, prefix.bias_two, 1)
        half_block(u, block_scales(vec, g_row + 2, mod, mod_row), b2_row, h_in, h_out, prefix.conv_two, targets[1])

    saved = (sw_11, sw_12, sw_21, sw_22) if save else (None,) * 4
    block(h1, u1, h2, AT.first, V_G1, V_B11, V_B12, 0, (SPAN_ONE1, SPAN_TWO1), SPAN_ATTN, saved[:2])

    src.take(SPAN_ATTN, SPAN_ONE2)
    free()
    vectors(V_AG, AT.attn_gains, 2)
    vectors(V_AB, AT.attn_bias, 1)
    vectors(V_FG, AT.final_gains, 2)
    for part in range(3):
        base = AT.attn_qkv - src.low
        for j in range(3):
            v = wide[pl.ds(base + part * 3 + j, CH_MID, stride=9), :]
            w_ref[part * CH_MID : (part + 1) * CH_MID, j * LINE : (j + 1) * LINE] = v.astype(BF16)
    src.matrix(w_ref.at[pl.ds(3 * CH_MID, CH_MID), :], AT.attn_out, CH_MID, 3)
    keep(w_ref.at[pl.ds(0, 4 * CH_MID), :], sw_attn if save else None)
    stats = [group_stats(h2, img, gm) for img in range(MB_DEV)]
    norm_to(pbuf, h2, stats, block_scales(vec, V_AG), False)
    n_low = pbuf[8 : 8 + ROWS, :].astype(BF16)
    for part in range(3):
        v = dot(n_low, w_ref[part * CH_MID : (part + 1) * CH_MID, :])
        qkv[:, part * CH_MID : (part + 1) * CH_MID] = v.astype(BF16)
    half = lane_half()

    def heads(img, carry):
        for pair in range(HEADS // 2):
            q, k, v = attention_pair(qkv, img, pair)
            outs = []
            for side in range(2):
                s = dot(keep_half(q, half, side), k, NT) * HEAD_DIM ** (-0.5)
                e = jnp.exp(s - jnp.max(s, 1, keepdims=True))
                prob = (e / jnp.sum(e, 1, keepdims=True)).astype(BF16)
                outs.append(dot(prob, v))
            mixed[pl.ds(pl.multiple_of(img * PIX, PIX), PIX), pair * LINE : (pair + 1) * LINE] = jnp.where(
                half, outs[0], outs[1]
            ).astype(BF16)
        return carry

    lax.fori_loop(0, MB_DEV, heads, 0)
    h3[...] = h2[...] + dot(mixed[...], w_ref[3 * CH_MID : 4 * CH_MID, :]) + vec[V_AB : V_AB + 1, :]

    block(h3, u2, h4, AT.second, V_G2, V_B21, V_B22, 2, (SPAN_ONE2, SPAN_TWO2), None, saved[2:])

    stats = [group_stats(h4, img, gm) for img in range(MB_DEV)]
    norm_to(pbuf, h4, stats, block_scales(vec, V_FG), True)
    z = dot(pbuf[8 : 8 + ROWS, :].astype(BF16), wz[...])
    t_all = dot3(z, sel[...])
    u_all = jnp.zeros((ROWS, LINE), F32)
    for shift in range(9):
        inside, by = upsample_masks(shift)
        moved = t_all if by == 0 else pltpu.roll(t_all, (-by) % ROWS, 0)
        u_all = u_all + jnp.where(inside, moved, 0.0)
    f_out[...] = dot3(u_all, gat[...]) + bz[...]
    free()


def vmem(*shape_dtype):
    return pltpu.VMEM(*shape_dtype)


VM = pl.BlockSpec(memory_space=pltpu.VMEM)
HB = pl.BlockSpec(memory_space=pl.ANY)
SM = pl.BlockSpec(memory_space=pltpu.SMEM)


def state_shapes():
    act = ((ROWS, CH_MID), F32)
    return [
        ((4 * ROWS, 256), BF16),
        act, act, act,
        ((ROWS, 3 * CH_MID), BF16),
        ((ROWS, CH_MID), BF16),
        act, act, act,
        ((VEC_ROWS, CH_MID), F32),
        ((8, EMB_DIM), F32),
        ((8, EMB_DIM), F32),
        ((8, EMB_DIM), F32),
    ]


def weight_shapes():
    sq = ((EMB_DIM, EMB_DIM), BF16)
    conv = ((9 * CH_MID, CH_MID), BF16)
    return [sq, sq, sq, ((9 * CH_BASE, CH_MID), BF16), conv, conv, ((4 * CH_MID, CH_MID), BF16), conv, conv]


def forward_call(save, labels, lines, xp, win, bin_, wz, bz, phi, tables):
    sds = lambda s: jax.ShapeDtypeStruct(*s)
    outs = [sds(((ROWS, LINE), F32))]
    out_specs = [VM]
    state = state_shapes()
    scratch = []
    if save:
        outs += [sds(s) for s in state] + [sds(s) for s in weight_shapes()]
        out_specs += [VM] * len(state) + [HB] * len(weight_shapes())
    else:
        scratch += [vmem(*s) for s in state]
    stage_rows = 10416
    scratch += [
        vmem((stage_rows, LINE), BF16),
        vmem((stage_rows, LINE), F32),
        vmem((9 * CH_MID, CH_MID), BF16),
        vmem((2, EMB_DIM, EMB_DIM), BF16),
        vmem((3, PADDED, CH_MID), BF16),
        vmem((ROWS + 16, CH_MID), F32),
        vmem((ROWS + 32, 256), F32),
        vmem((32 * MB_DEV, LINE), BF16),
        pltpu.SemaphoreType.DMA,
        pltpu.SemaphoreType.DMA,
        pltpu.SemaphoreType.DMA((MB_DEV,)),
    ]

    def body(*refs):
        forward_kernel(save, *refs)

    return pl.pallas_call(
        body,
        out_shape=outs,
        in_specs=[SM, HB] + [VM] * 9,
        out_specs=out_specs,
        scratch_shapes=scratch,
        compiler_params=pltpu.CompilerParams(vmem_limit_bytes=60 * 1024 * 1024),
        cost_estimate=pl.CostEstimate(flops=8 * 10**9, bytes_accessed=4 * 10**7, transcendentals=10**6),
        name="forward_save" if save else "forward_plain",
    )(labels, lines, xp, win, bin_, wz, bz, phi, *tables)


def column_sum(pbuf):
    def body(c, acc):
        return acc + jnp.sum(pbuf[pl.ds(pl.multiple_of(c * CHUNK + 8, 8), CHUNK), :], 0, keepdims=True)

    return lax.fori_loop(0, ROWS // CHUNK, body, jnp.zeros((1, CH_MID), F32))


def refill(pbuf, source):
    for c in range(0, ROWS, CHUNK):
        pbuf[8 + c : 8 + c + CHUNK, :] = source[c : c + CHUNK, :]


def block_back_two(dh, u_ref, at, base, rows, vec, mod, mod_row, weights, tools, g, dm):
    g_row, b1_row, b2_row = rows
    sbuf, pbuf, dx, at_ref, gm = tools
    put_row(g, at.bias_two - base, colsum(dh, 0, ROWS))
    u_stats = [group_stats(u_ref, img, gm) for img in range(MB_DEV)]
    scales = block_scales(vec, g_row + 2, mod, mod_row)
    norm_to(pbuf, u_ref, u_stats, scales, True)
    transpose_to(at_ref, pbuf)
    refill(pbuf, dh)
    shift_to(sbuf, pbuf)
    conv_back(sbuf, at_ref, weights.take(), dx, g, at.conv_two - base)
    weights.begin()

    def emit_inner(r, v):
        pbuf[pl.ds(r + 8, CHUNK), :] = v

    sums = norm_back(u_ref, dx, u_stats, scales, True, gm, emit_inner)
    gain, shift = vec[g_row + 2 : g_row + 3, :], vec[g_row + 3 : g_row + 4, :]
    d_gain = d_shift = 0.0
    dm[...] = jnp.zeros_like(dm)
    for img, (a, b) in enumerate(sums):
        scale = 1.0 + mod[mod_row + img : mod_row + img + 1, :CH_MID]
        d_gain, d_shift = d_gain + scale * b, d_shift + scale * a
        dm[img : img + 1, :CH_MID] = gain * b + shift * a
        dm[img : img + 1, CH_MID:] = a
    return d_gain, d_shift


def block_back_one(dh, x_ref, at, base, rows, vec, weights, tools, g):
    g_row, b1_row, b2_row = rows
    sbuf, pbuf, dx, at_ref, gm = tools
    put_row(g, at.bias_one - base, column_sum(pbuf))
    shift_to(sbuf, pbuf)
    stats = [group_stats(x_ref, img, gm) for img in range(MB_DEV)]
    scales = block_scales(vec, g_row)
    norm_to(pbuf, x_ref, stats, scales, True)
    transpose_to(at_ref, pbuf)
    conv_back(sbuf, at_ref, weights.take(), dx, g, at.conv_one - base)
    weights.begin()

    def emit_outer(r, v):
        dh[pl.ds(r, CHUNK), :] += v

    sums = norm_back(x_ref, dx, stats, scales, True, gm, emit_outer)
    put_row(g, at.gains - base, sums[0][1] + sums[1][1])
    put_row(g, at.gains + 3 - base, sums[0][0] + sums[1][0])


def rowsum(v):
    return jnp.sum(v, 0, keepdims=True)


def put_outer(g, at, left, right):
    for c in range(-(-left.shape[1] // LINE)):
        piece = outer(left[:, c * LINE : (c + 1) * LINE], right)
        put_lines(g, at + c * LINE * (EMB_DIM // LINE), piece, EMB_DIM // LINE)


class Weights:
    def __init__(self, sources, slots, sems):
        self.copies = []
        for n, source in enumerate(sources):
            target = slots.at[n % 2, pl.ds(0, source.shape[0]), :]
            self.copies.append((pltpu.make_async_copy(source, target, sems.at[n % 2]), target))
        self.begun = self.done = 0

    def begin(self):
        if self.begun < len(self.copies):
            self.copies[self.begun][0].start()
            self.begun += 1

    def take(self):
        copy, target = self.copies[self.done]
        copy.wait()
        self.done += 1
        return target


class Leave:
    def __init__(self, me, g, base, keep, send, stage, sems):
        self.core, self.place = lax.rem(me[0], 2), lax.div(me[0], 2)
        self.g, self.base, self.keep, self.send, self.stage, self.sems = g, base, keep, send, stage, sems
        self.copies = []

    def plane(self, plane, slot):
        pairs = PLANE // 2
        for q in range(pairs):
            at = q ^ self.place
            first = (plane * PLANE + 2 * q) * SHARD - self.base
            mine = pl.multiple_of(first + self.core * SHARD, 8)
            other = pl.multiple_of(first + (1 - self.core) * SHARD, 8)
            kept = pltpu.make_async_copy(self.g.at[pl.ds(mine, ROOM), :], self.keep.at[slot, at], self.sems.at[0])
            kept.start()
            stage = self.stage.at[slot * pairs + q]
            block = ROOM // 8

            def body(c, carry):
                stage[pl.ds(pl.multiple_of(c * 288, 16), 288), :] = self.g[
                    pl.ds(pl.multiple_of(other + c * 288, 8), 288), :
                ].astype(BF16)
                return carry

            whole = ROOM // 288
            lax.fori_loop(0, whole, body, 0)
            rest = ROOM - whole * 288
            stage[whole * 288 :, :] = self.g[pl.ds(pl.multiple_of(other + whole * 288, 8), rest), :].astype(BF16)
            sent = pltpu.make_async_copy(stage, self.send.at[slot, at], self.sems.at[1])
            sent.start()
            self.copies += [kept, sent]

    def wait(self):
        for copy in self.copies:
            copy.wait()


def clear_lines(g, first, count):
    if count:
        g[first : first + count, :] = jnp.zeros((count, LINE), F32)


def back_two_kernel(*refs):
    me, df, wz, gm, sel, gat, vec, mod, emb, h4, u2, h3, qkv, mixed, h2, u1, s22, s21, s_attn, s12, s_emb = refs[:21]
    keep, send, rest, dh, du, dm_first, extra, dse, dwz = refs[21:30]
    g, slots, w_sq, sbuf, pbuf, dx, at_ref, dqkv, dm, stage, sems, sq_sem, out_sems = refs[30:]
    weights = Weights([s22, s21, s_attn, s12], slots, sems)
    weights.begin()
    weights.begin()
    sq_copy = pltpu.make_async_copy(s_emb, w_sq, sq_sem)
    sq_copy.start()
    clear_pads(sbuf)
    clear_lines(g, TAIL - SPLIT, g.shape[0] - (TAIL - SPLIT))
    pbuf[0:8, :] = jnp.zeros((8, CH_MID), F32)
    pbuf[ROWS + 8 : ROWS + 16, :] = jnp.zeros((8, CH_MID), F32)
    tools = (sbuf, pbuf, dx, at_ref, gm)

    stats = [group_stats(h4, img, gm) for img in range(MB_DEV)]
    scales = block_scales(vec, V_FG)
    norm_to(pbuf, h4, stats, scales, True)
    transpose_to(at_ref, pbuf)
    spread = dot(df[...].astype(BF16), gat[...], NT)
    dt = jnp.zeros((ROWS, LINE), F32)
    for shift in range(9):
        inside, by = upsample_masks(shift)
        part = jnp.where(inside, spread, 0.0)
        dt = dt + (part if by == 0 else pltpu.roll(part, by % ROWS, 0))
    dz = dot(dt.astype(BF16), sel[...], NT)
    parts = split3(dz)
    dwz[...] = dot(at_ref[...], parts[0]) + dot(at_ref[...], parts[1]) + dot(at_ref[...], parts[2])
    dx[...] = dot(parts[0], wz[...], NT) + dot(parts[1], wz[...], NT) + dot(parts[2], wz[...], NT)

    def emit_first(r, v):
        dh[pl.ds(r, CHUNK), :] = v

    sums = norm_back(h4, dx, stats, scales, True, gm, emit_first)
    put_row(g, AT.final_gains - SPLIT, sums[0][1] + sums[1][1])
    put_row(g, AT.final_gains + 3 - SPLIT, sums[0][0] + sums[1][0])

    rows = (V_G2, V_B21, V_B22)
    d_gain, d_shift = block_back_two(dh, u2, AT.second, SPLIT, rows, vec, mod, 2, weights, tools, g, dm)
    put_row(g, AT.second.gains + 6 - SPLIT, d_gain)
    put_row(g, AT.second.gains + 9 - SPLIT, d_shift)
    block_back_one(dh, h3, AT.second, SPLIT, rows, vec, weights, tools, g)
    se = silu(emb[...])
    put_outer(g, AT.second.embed - SPLIT, se, dm[...])
    put_row(g, AT.second.embed_bias - SPLIT, rowsum(dm[...]))
    sq_copy.wait()
    dse[...] = dot3(dm[...], w_sq[...], NT)

    put_row(g, AT.attn_bias - SPLIT, colsum(dh, 0, ROWS))
    w = weights.take()
    d_low = dh[...].astype(BF16)
    for c in range(ROWS // LINE):
        at_ref[:, c * LINE : (c + 1) * LINE] = mixed[c * LINE : (c + 1) * LINE, :].astype(F32).T.astype(BF16)
    put_lines(g, AT.attn_out - SPLIT, dot(at_ref[...], d_low), 3)
    pbuf[8 : 8 + ROWS, :] = dot(d_low, w[3 * CH_MID : 4 * CH_MID, :], NT)
    half = lane_half()
    scale = HEAD_DIM ** (-0.5)

    def heads(img, carry):
        rows = pl.ds(pl.multiple_of(img * PIX, PIX), PIX)
        for pair in range(HEADS // 2):
            q, k, v = attention_pair(qkv, img, pair)
            cols = slice(pair * LINE, (pair + 1) * LINE)
            do = pbuf[pl.ds(pl.multiple_of(img * PIX + 8, 8), PIX), cols].astype(BF16)
            dqs, dks, dvs = [], [], []
            for side in range(2):
                s = dot(keep_half(k, half, side), q, NT) * scale
                e = jnp.exp(s - jnp.max(s, 0, keepdims=True))
                prob = e / jnp.sum(e, 0, keepdims=True)
                dvs.append(dot(prob.astype(BF16), do))
                dp = dot(keep_half(v, half, side), do, NT)
                ds = prob * (dp - jnp.sum(dp * prob, 0, keepdims=True))
                dks.append(dot(ds.astype(BF16), q))
                dqs.append(dot(ds.T.astype(BF16), k))
            for part, pieces in enumerate((dqs, dks, dvs)):
                value = jnp.where(half, pieces[0], pieces[1])
                if part < 2:
                    value = value * scale
                dqkv[rows, part * CH_MID + pair * LINE : part * CH_MID + (pair + 1) * LINE] = value.astype(BF16)
        return carry

    lax.fori_loop(0, MB_DEV, heads, 0)
    stats = [group_stats(h2, img, gm) for img in range(MB_DEV)]
    scales = block_scales(vec, V_AG)
    norm_to(pbuf, h2, stats, scales, False)
    transpose_to(at_ref, pbuf)
    dx[...] = jnp.zeros_like(dx)
    for part in range(3):
        d = dqkv[:, part * CH_MID : (part + 1) * CH_MID]
        dw = dot(at_ref[...], d)
        for j in range(3):
            g[pl.ds(AT.attn_qkv - SPLIT + part * 3 + j, CH_MID, stride=9), :] = dw[:, j * LINE : (j + 1) * LINE]
        dx[...] += dot(d, w[part * CH_MID : (part + 1) * CH_MID, :], NT)
    weights.begin()

    def emit(r, v):
        dh[pl.ds(r, CHUNK), :] += v

    sums = norm_back(h2, dx, stats, scales, False, gm, emit)
    put_row(g, AT.attn_gains - SPLIT, sums[0][1] + sums[1][1])
    put_row(g, AT.attn_gains + 3 - SPLIT, sums[0][0] + sums[1][0])

    leave = Leave(me, g, SPLIT, keep, send, stage, out_sems)
    leave.plane(3, 1)
    rows = (V_G1, V_B11, V_B12)
    d_gain, d_shift = block_back_two(dh, u1, AT.first, SPLIT, rows, vec, mod, 0, weights, tools, g, dm_first)
    extra[...] = jnp.zeros_like(extra)
    extra[0:1, :] = d_gain
    extra[1:2, :] = d_shift
    for c in range(0, ROWS, CHUNK):
        du[c : c + CHUNK, :] = pbuf[8 + c : 8 + c + CHUNK, :]
    leave.plane(2, 0)
    below = pltpu.make_async_copy(g.at[pl.ds(0, MIDDLE - SPLIT), :], rest, out_sems.at[2])
    below.start()
    below.wait()
    leave.wait()


def back_one_kernel(*refs):
    (me, labels, dh_in, du, dm, extra, dse_in, gm, vec, emb, pre, phi, h1, h0s, xpt) = refs[:15]
    s11, s_down, s_emb, s_time, rest = refs[15:20]
    keep, send, dwin, dbin = refs[20:24]
    g, slots, w_sq, sbuf, pbuf, dx, at_ref, dh, h0t, demb_ref, stage, sems, sq_sem, out_sems = refs[24:]
    above = pltpu.make_async_copy(rest, g.at[pl.ds(SPLIT, MIDDLE - SPLIT), :], out_sems.at[2])
    above.start()
    weights = Weights([s11, s_down], slots, sems)
    weights.begin()
    weights.begin()
    sq_copies = [pltpu.make_async_copy(s, w_sq.at[n], sq_sem.at[n]) for n, s in enumerate((s_emb, s_time))]
    for copy in sq_copies:
        copy.start()
    clear_pads(sbuf)
    clear_lines(g, 0, AT.conv_down)
    clear_lines(g, MIDDLE, g.shape[0] - MIDDLE)
    pbuf[0:8, :] = jnp.zeros((8, CH_MID), F32)
    pbuf[ROWS + 8 : ROWS + 16, :] = jnp.zeros((8, CH_MID), F32)
    refill(pbuf, du)
    for c in range(0, ROWS, CHUNK):
        dh[c : c + CHUNK, :] = dh_in[c : c + CHUNK, :]
    above.wait()
    tools = (sbuf, pbuf, dx, at_ref, gm)
    block_back_one(dh, h1, AT.first, 0, (V_G1, V_B11, V_B12), vec, weights, tools, g)
    put_row(g, AT.first.gains + 6, extra[0:1, :])
    put_row(g, AT.first.gains + 9, extra[1:2, :])
    se = silu(emb[...])
    put_outer(g, AT.first.embed, se, dm[...])
    put_row(g, AT.first.embed_bias, rowsum(dm[...]))
    leave = Leave(me, g, 0, keep, send, stage, out_sems)
    for copy in sq_copies:
        copy.wait()
    demb = (dse_in[...] + dot3(dm[...], w_sq[0], NT)) * silu_slope(emb[...])
    put_row(g, AT.time_bias_two, rowsum(demb))
    put_outer(g, AT.time_two, silu(pre[...]), demb)
    dpre = dot3(demb, w_sq[1], NT) * silu_slope(pre[...])
    put_row(g, AT.time_bias_one, rowsum(dpre))
    put_outer(g, AT.time_one, phi[...], dpre)
    clear = 240
    first, lines = AT.class_table, CLASSES * (EMB_DIM // LINE)

    def wipe(c, carry):
        g[pl.ds(first + c * clear, clear), :] = jnp.zeros((clear, LINE), F32)
        return carry

    lax.fori_loop(0, lines // clear, wipe, 0)
    demb_ref[...] = demb
    for n in range(MB_DEV):
        for j in range(EMB_DIM // LINE):
            at = first + labels[n] * (EMB_DIM // LINE) + j
            g[pl.ds(at, 1), :] += demb_ref[n : n + 1, j * LINE : (j + 1) * LINE]
    leave.plane(1, 1)

    put_row(g, AT.bias_down, colsum(dh, 0, ROWS))
    refill(pbuf, dh)
    shift_to(sbuf, pbuf)
    w = weights.take()
    dwin[...] = jnp.zeros_like(dwin)
    dbin[...] = jnp.zeros_like(dbin)
    for ph in range(4):
        for c in range(ROWS // LINE):
            rows = slice(ph * ROWS + c * LINE, ph * ROWS + (c + 1) * LINE)
            h0t[:, c * LINE : (c + 1) * LINE] = h0s[rows, :].astype(F32).T.astype(BF16)
        d0 = jnp.zeros((ROWS, CH_BASE), F32)
        for ky in ((0, 2) if ph // 2 else (1,)):
            for kx in ((0, 2) if ph % 2 else (1,)):
                d = shifted(sbuf, 2 if kx == 0 else 1, 32 if ky == 0 else 16)
                t = 3 * ky + kx
                d0 = d0 + dot(d, w[t * CH_BASE : (t + 1) * CH_BASE, :], NT)
                put_lines(g, AT.conv_down + t * CH_BASE * 3, dot(h0t[0:CH_BASE, :], d), 3)
        dbin[:, :CH_BASE] += rowsum(d0)
        dwin[:, :CH_BASE] += dot(xpt[:, ph * ROWS : (ph + 1) * ROWS], d0.astype(BF16))
    leave.plane(0, 0)
    leave.wait()


def kernel_params():
    return dict(
        compiler_params=pltpu.CompilerParams(vmem_limit_bytes=60 * 1024 * 1024),
        cost_estimate=pl.CostEstimate(flops=8 * 10**9, bytes_accessed=4 * 10**7, transcendentals=10**6),
    )


def back_scratch(lines):
    return [
        vmem((lines + 8, LINE), F32),
        vmem((2, 9 * CH_MID, CH_MID), BF16),
        vmem((2, EMB_DIM, EMB_DIM), BF16),
        vmem((3, PADDED, CH_MID), BF16),
        vmem((ROWS + 16, CH_MID), F32),
        vmem((ROWS, CH_MID), F32),
        vmem((CH_MID, ROWS), BF16),
    ]


def plane_shapes():
    pairs = PLANE // 2
    return [
        jax.ShapeDtypeStruct((2, pairs, ROOM, LINE), F32),
        jax.ShapeDtypeStruct((2, pairs, ROOM, LINE), BF16),
    ]


def back_two_call(args):
    sds = lambda *s: jax.ShapeDtypeStruct(*s)
    act = sds((ROWS, CH_MID), F32)
    scratch = back_scratch(ALL_LINES - SPLIT)
    scratch[2] = vmem((EMB_DIM, EMB_DIM), BF16)
    return pl.pallas_call(
        back_two_kernel,
        out_shape=plane_shapes()
        + [
            sds((MIDDLE - SPLIT, LINE), F32),
            act,
            act,
            sds((8, EMB_DIM), F32),
            sds((8, CH_MID), F32),
            sds((8, EMB_DIM), F32),
            sds((CH_MID, LINE), F32),
        ],
        in_specs=[SM] + [VM] * 15 + [HB] * 5,
        out_specs=[HB] * 3 + [VM] * 6,
        scratch_shapes=scratch
        + [
            vmem((ROWS, 3 * CH_MID), BF16),
            vmem((8, EMB_DIM), F32),
            vmem((PLANE, ROOM, LINE), BF16),
            pltpu.SemaphoreType.DMA((2,)),
            pltpu.SemaphoreType.DMA,
            pltpu.SemaphoreType.DMA((3,)),
        ],
        name="back_two",
        **kernel_params(),
    )(*args)


def back_one_call(args):
    sds = lambda *s: jax.ShapeDtypeStruct(*s)
    return pl.pallas_call(
        back_one_kernel,
        out_shape=plane_shapes() + [sds((32, 256), F32), sds((1, 256), F32)],
        in_specs=[SM] * 2 + [VM] * 13 + [HB] * 5,
        out_specs=[HB] * 2 + [VM] * 2,
        scratch_shapes=back_scratch(MIDDLE)
        + [
            vmem((ROWS, CH_MID), F32),
            vmem((256, ROWS), BF16),
            vmem((8, EMB_DIM), F32),
            vmem((PLANE, ROOM, LINE), BF16),
            pltpu.SemaphoreType.DMA((2,)),
            pltpu.SemaphoreType.DMA((2,)),
            pltpu.SemaphoreType.DMA((3,)),
        ],
        name="back_one",
        **kernel_params(),
    )(*args)


def karras(index):
    ramp_frac = index.astype(F32) / (DISCRETE - 1)
    low_root = SIGMA_LOW ** (1.0 / RHO_POWER)
    high_root = SIGMA_HIGH ** (1.0 / RHO_POWER)
    return (low_root + ramp_frac * (high_root - low_root)) ** RHO_POWER


def preconditioning_factors(sigma):
    variance_sum = sigma * sigma + SIGMA_DATA**2
    skip = SIGMA_DATA**2 / ((sigma - SIGMA_LOW) ** 2 + SIGMA_DATA**2)
    out = (sigma - SIGMA_LOW) * SIGMA_DATA * lax.rsqrt(variance_sum)
    return (skip, out, lax.rsqrt(variance_sum))


def noise_features(sigma):
    half_width = CH_BASE // 2
    frequency = jnp.exp(-math.log(10000.0) * jnp.arange(half_width, dtype=F32) / half_width)
    phases = 250.0 * jnp.log(sigma)[:, None] * frequency
    return jnp.pad(jnp.concatenate([jnp.cos(phases), jnp.sin(phases)], 1), ((0, 8 - MB_DEV), (0, 0)))


def by_parity(image):
    channels = image.shape[-1]
    split = image.reshape(MB_DEV, HALF, 2, HALF, 2, channels)
    return split.transpose(2, 4, 0, 1, 3, 5).reshape(4, ROWS, channels)


def pixels(image):
    return by_parity(image).transpose(1, 0, 2).reshape(ROWS, 12)


def input_patches(noisy, scale):
    low = (scale[:, None, None, None] * noisy).astype(BF16)
    padded = jnp.pad(low, ((0, 0), (1, 1), (1, 1), (0, 0)))
    taps = [padded[:, t // 3 : t // 3 + RES, t % 3 : t % 3 + RES] for t in range(9)]
    flat = by_parity(jnp.concatenate(taps, 3)).reshape(4 * ROWS, 27)
    return jnp.pad(flat, ((0, 0), (0, 5)))


def small_weights(lines):
    front = lines[: AT.conv_down].reshape(-1)
    size = 27 * CH_BASE
    win = jnp.pad(front[:size].reshape(27, CH_BASE), ((0, 5), (0, 64)))
    bin_ = jnp.pad(front[size : size + CH_BASE].astype(F32)[None], ((0, 0), (0, 64)))
    tail = lines[TAIL:].reshape(-1)
    size = 27 * CH_MID
    wz = tail[:size].reshape(9, CH_MID, 3).transpose(1, 0, 2).reshape(CH_MID, 27)
    bz = jnp.tile(tail[size : size + 3].astype(F32), 4)
    return win, bin_, jnp.pad(wz, ((0, 0), (0, LINE - 27))), jnp.pad(bz, (0, LINE - 12))[None]


def per_part(labels, lines, noisy, sigma, save, tables):
    skip, out_scale, in_scale = preconditioning_factors(sigma)
    xp = input_patches(noisy, in_scale)
    phi = noise_features(sigma)
    win, bin_, wz, bz = small_weights(lines)
    results = forward_call(save, labels, lines, xp, win, bin_, wz, bz, phi, tables)
    model = results[0][:, :12]
    per_row = lambda v: jnp.repeat(v, PIX)[:, None]
    denoised = per_row(skip) * pixels(noisy) + per_row(out_scale) * model
    return denoised, (xp, phi, wz, out_scale, results[1:])


AXIS = "fsdp"
CORE, EAST, SOUTH, UP = 1, 2, 4, 8
CUT_ROWS = ROOM // 2


def swap(values, hop):
    return lax.ppermute(values, AXIS, [(i, i ^ hop) for i in range(SHARDS)])


def total_of(values, n):
    hop = 1
    while hop < n:
        values = values + lax.ppermute(values, AXIS, [(i, i ^ hop) for i in range(n)])
        hop *= 2
    return values


def reduce_planes(keep, send):
    planes = keep.shape[0]
    got = swap(send, CORE)
    low = lambda v: v.astype(BF16)
    wide = lambda v: v.astype(F32)
    a, b = slice(0, CUT_ROWS), slice(CUT_ROWS, ROOM)
    quarter = lambda i, rows: keep[:, i, rows] + wide(got[:, i, rows])
    send_a = low(jnp.stack([quarter(1, a), quarter(3, a)], 1))
    send_b = low(jnp.stack([quarter(2, b), quarter(3, b)], 1))
    got_a, got_b = swap(send_a, EAST), swap(send_b, SOUTH)
    last_a = low(quarter(2, a) + wide(got_a[:, 1]))
    last_b = low(quarter(1, b) + wide(got_b[:, 1]))
    end_a, end_b = swap(last_a, SOUTH), swap(last_b, EAST)
    sum_a = quarter(0, a) + wide(got_a[:, 0]) + wide(end_a)
    sum_b = quarter(0, b) + wide(got_b[:, 0]) + wide(end_b)
    return jnp.concatenate([sum_a, sum_b], 1)


def reduce_column(part, z):
    planes = part.shape[0]
    pick = lambda p: lax.dynamic_index_in_dim(part, jnp.clip(p, 0, planes - 1), 0, keepdims=False)
    total = pick(z)
    for way in (1, -1):
        run = None
        for far in range(planes - 1, 0, -1):
            value = pick(z + way * far)
            if run is not None:
                value = value + run
            holders = [q for q in range(planes) if 0 <= q + way * far < planes]
            pairs = [(q * PLANE + i, (q + way) * PLANE + i) for q in holders for i in range(PLANE)]
            run = lax.ppermute(value.astype(BF16), AXIS, pairs).astype(F32)
        total = total + run
    return total


def per_device(n, images, noise_draws, labels, step_index, valid_rows, counts, master, momentum, ema):
    direct = n == SHARDS
    index = lax.axis_index(AXIS)
    me = jnp.where(direct, lax.rem(index, PLANE), 0).astype(jnp.int32)[None]
    gather = lambda v: lax.all_gather(v.astype(BF16).reshape(-1, LINE), AXIS, axis=0, tiled=True)
    online, target = gather(master), gather(ema)
    select, collect = spread_tables()
    tables = (jnp.asarray(group_table(), BF16), jnp.asarray(select, BF16), jnp.asarray(collect, BF16))
    slot_live = (jnp.arange(MB_DEV) < counts[0]).astype(F32)
    row_live = (jnp.arange(RES)[None, :] < valid_rows[:, None]).astype(F32)
    pixel_mask = slot_live[:, None] * row_live
    pixel_total = 3.0 * RES * total_of(jnp.sum(pixel_mask), n)
    mask = pixels(jnp.broadcast_to(pixel_mask[:, :, None, None], images.shape))
    sigma_lo, sigma_hi = karras(step_index), karras(step_index + 1)
    add_noise = lambda sigma: images + sigma[:, None, None, None] * noise_draws
    online_out, (xp, phi, wz, out_scale, saved) = per_part(labels, online, add_noise(sigma_hi), sigma_hi, True, tables)
    target_out, _ = per_part(labels, target, add_noise(sigma_lo), sigma_lo, False, tables)
    gap = online_out - target_out
    local_loss = jnp.sum(mask * jnp.square(gap))
    grad_model = jnp.repeat(out_scale, PIX)[:, None] * 2.0 * mask * gap / pixel_total
    bias_out = jnp.sum(grad_model.reshape(ROWS, 4, 3), axis=(0, 1))
    (h0s, h1, u1, h2, qkv, mixed, h3, u2, h4, vec, mod, emb, pre) = saved[:13]
    s_time, s_emb1, s_emb2, s_down, s11, s12, s_attn, s21, s22 = saved[13:]
    gm, sel, gat = tables
    df = jnp.pad(grad_model, ((0, 0), (0, LINE - 12)))
    keep_top, send_top, rest, dh, du, dm, extra, dse, dwz = back_two_call(
        (me, df, wz, gm, sel, gat, vec, mod, emb, h4, u2, h3, qkv, mixed, h2, u1, s22, s21, s_attn, s12, s_emb2)
    )
    keep_low, send_low, dwin, dbin = back_one_call(
        (me, labels, dh, du, dm, extra, dse, gm, vec, emb, pre, phi, h1, h0s, xp.T, s11, s_down, s_emb1, s_time, rest)
    )
    tail = dwz[:, :27].reshape(CH_MID, 9, 3).transpose(1, 0, 2).reshape(-1)
    small = jnp.concatenate([dwin[:27, :CH_BASE].reshape(-1), dbin[0, :CH_BASE], tail, bias_out, local_loss[None]])
    front_size, tail_size = AT.conv_down * LINE, tail.shape[0] + 3
    small = jnp.pad(small, (0, LINE * LINE - small.shape[0])).reshape(LINE, LINE)
    small = total_of(small, n).reshape(-1)
    if direct:
        part = jnp.concatenate([reduce_planes(keep_low, send_low), reduce_planes(keep_top, send_top)])
        reduced = reduce_column(part, lax.div(index, PLANE))[:SHARD].reshape(-1)
    else:
        both = [jnp.stack([k, s.astype(F32)], 2) for k, s in ((keep_low, send_low), (keep_top, send_top))]
        lines = jnp.concatenate(both).reshape(SHARDS, ROOM, LINE)[:, :SHARD].reshape(n, -1)
        reduced = lax.psum_scatter(lines, AXIS, scatter_dimension=0, tiled=True).reshape(-1)
    size = master.shape[0]
    start = TAIL * LINE - (n - 1) * size
    first = jnp.where(index == 0, small[:front_size], 0.0)
    last = jnp.where(index == n - 1, small[front_size : front_size + tail_size], 0.0)
    reduced = reduced + jnp.pad(first, (0, size - front_size)) + jnp.pad(last, (start, size - start - tail_size))
    new_momentum = MOMENTUM * momentum + reduced
    new_master = master - LEARN_RATE * (reduced + MOMENTUM * new_momentum)
    new_ema = EMA_DECAY * ema + (1.0 - EMA_DECAY) * new_master
    end = front_size + tail_size
    return (small[end] / pixel_total, new_momentum, new_master, new_ema, small[end - 3 : end])


def solution(mesh):
    n = mesh.shape[AXIS]

    def step(*args):
        return per_device(n, *args)

    return jax.shard_map(
        step,
        mesh=mesh,
        in_specs=(P(AXIS, None, None, None),) * 2 + (P(AXIS),) * 7,
        out_specs=(P(), P(AXIS), P(AXIS), P(AXIS), P()),
        check_vma=False,
    )
```

time: 2740 us -> 620 us (0.23); the launches traced: 2700 us -> 615 us
  local copies, waits for them, and re-layouts: 1310 us -> 47.2 us
  other arithmetic: 525 us -> 34.2 us
  waiting for transfers between devices: 590 us -> 305 us
  matrix products: 163 us -> 0 us
  Pallas kernels: 0 us -> 163 us
  blocking collectives: 83.6 us -> 0 us
  starting transfers between devices: 0.12 us -> 44.7 us
    unnamed x4 -> x2, waiting for transfers between devices: 500 us -> 0.03 us
    scatter-add x70 -> x0, local copies, waits for them, and re-layouts: 392 us -> none  [unpatch(): padded = padded.at[row_start:row_start + stride * out_height:stride, col_...]
    concatenate x46 -> x5, local copies, waits for them, and re-layouts: 329 us -> 2.93 us  [the longest x4 1.47 us: input_patches(): flat = by_parity(jnp.concatenate(taps, 3)).reshape(4 * ROWS, 27)]
    scatter-add x38 -> x0, other arithmetic: 289 us -> none  [unpatch(): padded = padded.at[row_start:row_start + stride * out_height:stride, col_...]
    slice x116 -> x9, local copies, waits for them, and re-layouts: 269 us -> 2.99 us  [the longest x2 1.47 us: small_weights(): tail[:size].reshape(9, CH_MID, 3).transpose(1, 0, 2).reshape(CH_MID, 27)]
    pallas_call x0 -> x4, Pallas kernels: none -> 163 us  [the longest x2 90 us: forward_call(): pl.pallas_call(body, out_shape=outs, in_specs=[SM, HB] + [VM] * 9, out_sp...]
    dot_general x110 -> x0, matrix products: 158 us -> none  [the longest x14 48.9 us: conv_grads(): lax.dot_general(patches(image_low, stride), grad_low, CONTRACT_ROWS, pref...]
    all_gather x2, waiting for transfers between devices: 90.1 us -> 202 us  [per_device(): lax.all_gather(v.astype(BF16).reshape(-1, LINE), AXIS, axis=0, tiled=True)]
  transfers between devices with their start and end apart: 3 -> 28, of which waited for: 3 -> 21; matrix products, arithmetic and copies ran while one was open for 4% -> 10% of each run, Pallas kernels for 0% -> 0%
where the time goes in v1:
time: 620 us; the launch traced here: 615 us
  waiting for transfers between devices  305 us (49%)
  Pallas kernels  163 us (26%)
  local copies, waits for them, and re-layouts  47.2 us (8%)
  starting transfers between devices  44.7 us (7%)
  other arithmetic  34.2 us (6%)
  between operations  21.4 us (3%)
    all_gather x2, waiting for transfers between devices, per_device(): lax.all_gather(v.astype(BF16).reshape(-1, LINE), AXIS, axis=0, tiled=True)  202 us
    pallas_call x2, Pallas kernels, forward_call(): pl.pallas_call(body, out_shape=outs, in_specs=[SM, HB] + [VM] * 9, out_sp...  90 us
    ppermute x10, waiting for transfers between devices, swap(): return lax.ppermute(values, AXIS, [(i, i ^ hop) for i in range(SHARDS)])  68.6 us
    pallas_call x1, Pallas kernels, back_two_call(): pl.pallas_call(back_two_kernel, out_shape=plane_shapes() + [sds((MIDDLE -...  50.5 us
    ppermute x10, starting transfers between devices, total_of(): lax.ppermute(values, AXIS, [(i, i ^ hop) for i in range(n)])  23.5 us
    pallas_call x1, Pallas kernels, back_one_call(): pl.pallas_call(back_one_kernel, out_shape=plane_shapes() + [sds((32, 256)...  22.4 us
    ppermute x10, waiting for transfers between devices, total_of(): lax.ppermute(values, AXIS, [(i, i ^ hop) for i in range(n)])  19 us
    ppermute x6, waiting for transfers between devices, reduce_column(): run = lax.ppermute(value.astype(BF16), AXIS, pairs).astype(F32)  15.5 us
  transfers between devices with their start and end apart: 28, of which 21 were waited for; matrix products, arithmetic and copies ran while one was open for 10% of the time, Pallas kernels for 0%

profile of v1, /device:TPU:0, one launch (start us, length us, event | category | flops | bytes accessed | tf_op | source)
XLA Modules:
  0.0 615.1 jit_solution(9801065399231665195)
XLA Ops:
  34.7 3.9 collective-permute-start.1
  39.4 3.4 collective-permute-start.2
  43.6 3.4 collective-permute-start.3
  47.8 4.4 collective-permute-start.4
  53.0 84.2 %all-gather.5.cloned.1.call-done.refs_1_ = bf16[72448,128]{1,0:T(8,128)(2,1)} async-done(((bf16[2264,128]{1,0:T(8,128)(2,1)}), bf16[72448,128]{1,0:T(8,128)(2,1)}) %all-gather.5.cloned.1.call-update) | async-done | bytes 18546704 | tf_op jit(solution)/shard_map/all_gather | solution.py:1166
  144.3 117.4 %all-gather.3.cloned.1.call-done.refs_1_ = bf16[72448,128]{1,0:T(8,128)(2,1)} async-done(((bf16[2264,128]{1,0:T(8,128)(2,1)}), bf16[72448,128]{1,0:T(8,128)(2,1)}) %all-gather.3.cloned.1.call-update) | async-done | bytes 18546704 | tf_op jit(solution)/shard_map/all_gather | solution.py:1166
  269.0 43.7 %forward_plain.1 = f32[512,128]{1,0:T(8,128)} custom-call(s32[2]{0:T(128)} %refs_1_.1, bf16[72448,128]{1,0:T(8,128)(2,1)} %all-gather.5.cloned.1.call-done.refs_1_, bf16[2048,32]{1,0:T(8,128)(2,1)} %pad.78.refs_2_, bf16[32,256]{1,0:T(8,128)(2,1)} %pad.79.refs_3_, f32[1,256]{1,0:T(1,128)} %pad_convert_fusion.refs_4_, bf16[384,128]{1,0:T(8,128)(2,1)} %pad.82.refs_5_, ...), custom_call_target="tpu_custom_call" | custom-call | flops 8000000000 | bytes 40000000 | tf_op jit(solution)/shard_map/forward_plain/pallas_call | solution.py:627
  312.7 46.3 %forward_save.1 = (f32[512,128]{1,0:T(8,128)}, bf16[2048,256]{1,0:T(8,128)(2,1)}, f32[512,384]{1,0:T(8,128)}, f32[512,384]{1,0:T(8,128)}, f32[512,384]{1,0:T(8,1...) custom-call(s32[2]{0:T(128)} %refs_1_.1, ...), custom_call_target="tpu_custom_call" | custom-call | flops 8000000000 | bytes 40000000 | tf_op jit(solution)/shard_map/forward_save/pallas_call | solution.py:627
  362.4 50.5 %back_two.1 = (f32[2,4,2272,128]{3,2,1,0:T(8,128)}, bf16[2,4,2272,128]{3,2,1,0:T(8,128)(2,1)}, f32[4240,128]{1,0:T(8,128)}, f32[512,384]{1,0:T(8,128)}, f32[512,...) custom-call(s32[1]{0:T(128)} %bitcast.refs_0_, ...), custom_call_target="tpu_custom_call" | custom-call | flops 8000000000 | bytes 40000000 | tf_op jit(solution)/shard_map/back_two/pallas_call | solution.py:997
  412.9 22.4 %back_one.1 = (f32[2,4,2272,128]{3,2,1,0:T(8,128)}, bf16[2,4,2272,128]{3,2,1,0:T(8,128)(2,1)}, f32[32,256]{1,0:T(8,128)}, f32[1,256]{1,0:T(1,128)}) custom-call(s32[1]{0:T(128)} %bitcast.refs_0_, s32[2]{0:T(128)} %refs_1_.1, f32[512,384]{1,0:T(8,128)} %get-tuple-element.57.refs_2_, f32[512,384]{1,0:T(8,128)} %get-tuple-element.58.refs_3_, ...), custom_call_target="tpu_custom_call" | custom-call | flops 8000000000 | bytes 40000000 | tf_op jit(solution)/shard_map/back_one/pallas_call | solution.py:1027
  438.8 4.7 collective-permute-done.10
  443.5 3.6 fusion.22
  452.7 23.0 %collective-permute-done.11 = bf16[2,2,1136,128]{3,2,0,1:T(8,128)(2,1)S(1)} collective-permute-done((bf16[2,2,1136,128]{3,2,0,1:T(8,128)(2,1)S(1)}, bf16[2,2,1136,128]{3,2,0,1:T(8,128)(2,1)S(1)}, u32[]{:S(2)}, u32[]{:S(2)}) %collective-permute-start.11) | collective-permute-done | bytes 1163296 | tf_op jit(solution)/shard_map/ppermute | solution.py:1116
  480.1 19.9 %collective-permute-done.16 = bf16[2,2,1136,128]{3,2,0,1:T(8,128)(2,1)S(1)} collective-permute-done((bf16[2,2,1136,128]{3,2,0,1:T(8,128)(2,1)S(1)}, bf16[2,2,1136,128]{3,2,0,1:T(8,128)(2,1)S(1)}, u32[]{:S(2)}, u32[]{:S(2)}) %collective-permute-start.16) | collective-permute-done | bytes 1163296 | tf_op jit(solution)/shard_map/ppermute | solution.py:1116
  509.2 9.5 %collective-permute-done.17 = bf16[2,1136,128]{2,1,0:T(8,128)(2,1)} collective-permute-done((bf16[2,1136,128]{2,1,0:T(8,128)(2,1)}, bf16[2,1136,128]{2,1,0:T(8,128)(2,1)}, u32[]{:S(2)}, u32[]{:S(2)}) %collective-permute-start.17) | collective-permute-done | bytes 581664 | tf_op jit(solution)/shard_map/ppermute | solution.py:1116
  522.0 8.0 %collective-permute-done.12 = bf16[2,1136,128]{2,1,0:T(8,128)(2,1)S(1)} collective-permute-done((bf16[2,1136,128]{2,1,0:T(8,128)(2,1)S(1)}, bf16[2,1136,128]{2,1,0:T(8,128)(2,1)S(1)}, u32[]{:S(2)}, u32[]{:S(2)}) %collective-permute-start.12) | collective-permute-done | bytes 581664 | tf_op jit(solution)/shard_map/ppermute | solution.py:1116
  546.0 3.8 collective-permute-done.20
  551.3 4.5 collective-permute-start.21
  557.1 3.1 collective-permute-done.6
  561.6 2.9 collective-permute-done.7
  569.8 5.2 collective-permute-start.9
  575.0 12.2 %collective-permute-done.9 = f32[128,128]{1,0:T(8,128)S(1)} collective-permute-done((f32[128,128]{1,0:T(8,128)S(1)}, f32[128,128]{1,0:T(8,128)S(1)}, u32[]{:S(2)}, u32[]{:S(2)}) %collective-permute-start.9) | collective-permute-done | bytes 65568 | tf_op jit(solution)/shard_map/ppermute | solution.py:1122
  595.3 3.6 collective-permute-done.22
  598.9 5.6 collective-permute-done.25
  (231 shorter events, 104.5 us)
Async XLA Ops:
  7.2 130.0 %all-gather.5.cloned.1.call-start = ((), (), s32[]{:S(2)}) async-start(), calls=%async_computation.1 | async-start | bytes 19126272 | tf_op jit(solution)/shard_map/all_gather | solution.py:1166
  9.5 252.3 %all-gather.3.cloned.1.call-start = ((), (), s32[]{:S(2)}) async-start(), calls=%async_computation | async-start | bytes 19126272 | tf_op jit(solution)/shard_map/all_gather | solution.py:1166
  11.8 21.6 %collective-permute-start = (f32[]{:T(128)}, f32[]{:T(128)}, u32[]{:S(2)}, u32[]{:S(2)}) collective-permute-start(f32[]{:T(128)} %fusion.60), channel_id=1, source_target_pairs={{0,1},{1,0},{2,3},{3,2},{4,5},{5,4},{6,7},{7,6},{8,9},{9,8},{10,11... | collective-permute-start | bytes 20 | tf_op jit(solution)/shard_map/ppermute | solution.py:1122
  47.8 4.6 collective-permute-start.4
  435.4 8.1 %collective-permute-start.10 = (bf16[2,4,2272,128]{3,2,1,0:T(8,128)(2,1)}, bf16[2,4,2272,128]{3,2,1,0:T(8,128)(2,1)S(1)}, u32[]{:S(2)}, u32[]{:S(2)}) collective-permute-start(bf16[2,4,2272,128]{3,2,1,0:T(8,128)(2,1)} %get-tuple-element.74), channel_id=1, source_target_pairs={{0,1},{1,0},{2,3},{3,2},{4,5},{5,4},{6,7},{7,6},{8,9},{9,8},{10,11... | collective-permute-start | bytes 13959176 | tf_op jit(solution)/shard_map/ppermute | solution.py:1116
  438.5 11.4 %collective-permute-start.15 = (bf16[2,4,2272,128]{3,2,0,1:T(8,128)(2,1)S(1)}, bf16[2,4,2272,128]{3,2,0,1:T(8,128)(2,1)S(1)}, u32[]{:S(2)}, u32[]{:S(2)}) collective-permute-start(bf16[2,4,2272,128]{3,2,0,1:T(8,128)(2,1)S(1)} %copy.230), channel_id=1, source_target_pairs={{0,1},{1,0},{2,3},{3,2},{4,5},{5,4},{6,7},{7,6},{8,9},{9,8},{10,11... | collective-permute-start | bytes 13959176 | tf_op jit(solution)/shard_map/ppermute | solution.py:1116
  447.2 28.5 %collective-permute-start.11 = (bf16[2,2,1136,128]{3,2,0,1:T(8,128)(2,1)S(1)}, bf16[2,2,1136,128]{3,2,0,1:T(8,128)(2,1)S(1)}, u32[]{:S(2)}, u32[]{:S(2)}) collective-permute-start(bf16[2,2,1136,128]{3,2,0,1:T(8,128)(2,1)S(1)} %pad_maximum_fusion), channel_id=1, source_target_pairs={{0,2},{1,3},{2,0},{3,1},{4,6},{5,7},{6,4},{7,5},{8,10},{9,11},{10,... | collective-permute-start | bytes 3489800 | tf_op jit(solution)/shard_map/ppermute | solution.py:1116
  450.5 49.4 %collective-permute-start.16 = (bf16[2,2,1136,128]{3,2,0,1:T(8,128)(2,1)S(1)}, bf16[2,2,1136,128]{3,2,0,1:T(8,128)(2,1)S(1)}, u32[]{:S(2)}, u32[]{:S(2)}) collective-permute-start(bf16[2,2,1136,128]{3,2,0,1:T(8,128)(2,1)S(1)} %pad_maximum_fusion.2), channel_id=1, source_target_pairs={{0,2},{1,3},{2,0},{3,1},{4,6},{5,7},{6,4},{7,5},{8,10},{9,11},{10,... | collective-permute-start | bytes 3489800 | tf_op jit(solution)/shard_map/ppermute | solution.py:1116
  451.9 48.1 %collective-permute-start.18 = (bf16[2,2,1136,128]{3,2,0,1:T(8,128)(2,1)S(1)}, bf16[2,2,1136,128]{3,2,0,1:T(8,128)(2,1)S(1)}, u32[]{:S(2)}, u32[]{:S(2)}) collective-permute-start(bf16[2,2,1136,128]{3,2,0,1:T(8,128)(2,1)S(1)} %pad_maximum_fusion.3), channel_id=1, source_target_pairs={{0,4},{1,5},{2,6},{3,7},{4,0},{5,1},{6,2},{7,3},{8,12},{9,13},{10,... | collective-permute-start | bytes 3489800 | tf_op jit(solution)/shard_map/ppermute | solution.py:1116
  478.7 27.6 %collective-permute-start.13 = (bf16[2,2,1136,128]{3,2,0,1:T(8,128)(2,1)S(1)}, bf16[2,2,1136,128]{3,2,0,1:T(8,128)(2,1)}, u32[]{:S(2)}, u32[]{:S(2)}) collective-permute-start(bf16[2,2,1136,128]{3,2,0,1:T(8,128)(2,1)S(1)} %pad_maximum_fusion.1), channel_id=1, source_target_pairs={{0,4},{1,5},{2,6},{3,7},{4,0},{5,1},{6,2},{7,3},{8,12},{9,13},{10,... | collective-permute-start | bytes 3489800 | tf_op jit(solution)/shard_map/ppermute | solution.py:1116
  501.5 17.2 %collective-permute-start.17 = (bf16[2,1136,128]{2,1,0:T(8,128)(2,1)}, bf16[2,1136,128]{2,1,0:T(8,128)(2,1)}, u32[]{:S(2)}, u32[]{:S(2)}) collective-permute-start(bf16[2,1136,128]{2,1,0:T(8,128)(2,1)} %get-tuple-element.105), channel_id=1, source_target_pairs={{0,4},{1,5},{2,6},{3,7},{4,0},{5,1},{6,2},{7,3},{8,12},{9,13},{10,... | collective-permute-start | bytes 1744904 | tf_op jit(solution)/shard_map/ppermute | solution.py:1116
  503.0 16.2 %collective-permute-start.19 = (bf16[2,1136,128]{2,1,0:T(8,128)(2,1)S(1)}, bf16[2,1136,128]{2,1,0:T(8,128)(2,1)}, u32[]{:S(2)}, u32[]{:S(2)}) collective-permute-start(bf16[2,1136,128]{2,1,0:T(8,128)(2,1)S(1)} %get-tuple-element.106), channel_id=1, source_target_pairs={{0,2},{1,3},{2,0},{3,1},{4,6},{5,7},{6,4},{7,5},{8,10},{9,11},{10,... | collective-permute-start | bytes 1744904 | tf_op jit(solution)/shard_map/ppermute | solution.py:1116
  503.4 26.5 %collective-permute-start.12 = (bf16[2,1136,128]{2,1,0:T(8,128)(2,1)S(1)}, bf16[2,1136,128]{2,1,0:T(8,128)(2,1)S(1)}, u32[]{:S(2)}, u32[]{:S(2)}) collective-permute-start(bf16[2,1136,128]{2,1,0:T(8,128)(2,1)S(1)} %get-tuple-element.98), channel_id=1, source_target_pairs={{0,4},{1,5},{2,6},{3,7},{4,0},{5,1},{6,2},{7,3},{8,12},{9,13},{10,... | collective-permute-start | bytes 1744904 | tf_op jit(solution)/shard_map/ppermute | solution.py:1116
  508.0 21.9 %collective-permute-start.14 = (bf16[2,1136,128]{2,1,0:T(8,128)(2,1)S(1)}, bf16[2,1136,128]{2,1,0:T(8,128)(2,1)S(1)}, u32[]{:S(2)}, u32[]{:S(2)}) collective-permute-start(bf16[2,1136,128]{2,1,0:T(8,128)(2,1)S(1)} %fusion.37), channel_id=1, source_target_pairs={{0,2},{1,3},{2,0},{3,1},{4,6},{5,7},{6,4},{7,5},{8,10},{9,11},{10,... | collective-permute-start | bytes 1744904 | tf_op jit(solution)/shard_map/ppermute | solution.py:1116
  536.1 13.7 %collective-permute-start.20 = (bf16[2272,128]{1,0:T(8,128)(2,1)S(1)}, bf16[2272,128]{1,0:T(8,128)(2,1)}, u32[]{:S(2)}, u32[]{:S(2)}) collective-permute-start(bf16[2272,128]{1,0:T(8,128)(2,1)S(1)} %get-tuple-element.113), channel_id=1, source_target_pairs={{0,8},{1,9},{2,10},{3,11},{4,12},{5,13},{6,14},{7,15}} | collective-permute-start | bytes 1744904 | tf_op jit(solution)/shard_map/ppermute | solution.py:1157
  545.2 10.7 %collective-permute-start.5 = (f32[128,128]{1,0:T(8,128)S(1)}, f32[128,128]{1,0:T(8,128)S(1)}, u32[]{:S(2)}, u32[]{:S(2)}) collective-permute-start(f32[128,128]{1,0:T(8,128)S(1)} %pad_bitcast_fusion), channel_id=1, source_target_pairs={{0,1},{1,0},{2,3},{3,2},{4,5},{5,4},{6,7},{7,6},{8,9},{9,8},{10,11... | collective-permute-start | bytes 196616 | tf_op jit(solution)/shard_map/ppermute | solution.py:1122
  545.3 19.4 %collective-permute-start.23 = (bf16[2272,128]{1,0:T(8,128)(2,1)}, bf16[2272,128]{1,0:T(8,128)(2,1)S(1)}, u32[]{:S(2)}, u32[]{:S(2)}) collective-permute-start(bf16[2272,128]{1,0:T(8,128)(2,1)} %get-tuple-element.114), channel_id=1, source_target_pairs={{24,16},{25,17},{26,18},{27,19},{28,20},{29,21},{30,22},{31,23}} | collective-permute-start | bytes 1744904 | tf_op jit(solution)/shard_map/ppermute | solution.py:1157
  551.3 15.9 %collective-permute-start.21 = (bf16[2272,128]{1,0:T(8,128)(2,1)S(1)}, bf16[2272,128]{1,0:T(8,128)(2,1)S(1)}, u32[]{:S(2)}, u32[]{:S(2)}) collective-permute-start(bf16[2272,128]{1,0:T(8,128)(2,1)S(1)} %fusion.29), channel_id=1, source_target_pairs={{0,8},{1,9},{2,10},{3,11},{4,12},{5,13},{6,14},{7,15},{8,16},{9,17... | collective-permute-start | bytes 1744904 | tf_op jit(solution)/shard_map/ppermute | solution.py:1157
  555.9 4.3 collective-permute-start.6
  564.6 5.2 collective-permute-start.8
  569.0 21.3 %collective-permute-start.24 = (bf16[2272,128]{1,0:T(8,128)(2,1)S(1)}, bf16[2272,128]{1,0:T(8,128)(2,1)S(1)}, u32[]{:S(2)}, u32[]{:S(2)}) collective-permute-start(bf16[2272,128]{1,0:T(8,128)(2,1)S(1)} %get-tuple-element.112), channel_id=1, source_target_pairs={{16,8},{17,9},{18,10},{19,11},{20,12},{21,13},{22,14},{23,15},{24,... | collective-permute-start | bytes 1744904 | tf_op jit(solution)/shard_map/ppermute | solution.py:1157
  569.8 17.4 %collective-permute-start.9 = (f32[128,128]{1,0:T(8,128)S(1)}, f32[128,128]{1,0:T(8,128)S(1)}, u32[]{:S(2)}, u32[]{:S(2)}) collective-permute-start(f32[128,128]{1,0:T(8,128)S(1)} %add.296), channel_id=1, source_target_pairs={{0,16},{1,17},{2,18},{3,19},{4,20},{5,21},{6,22},{7,23},{8,24},{9,... | collective-permute-start | bytes 196616 | tf_op jit(solution)/shard_map/ppermute | solution.py:1122
  589.0 9.9 %collective-permute-start.22 = (bf16[2272,128]{1,0:T(8,128)(2,1)S(1)}, bf16[2272,128]{1,0:T(8,128)(2,1)S(1)}, u32[]{:S(2)}, u32[]{:S(2)}) collective-permute-start(bf16[2272,128]{1,0:T(8,128)(2,1)S(1)} %get-tuple-element.111), channel_id=1, source_target_pairs={{0,8},{1,9},{2,10},{3,11},{4,12},{5,13},{6,14},{7,15},{8,16},{9,17... | collective-permute-start | bytes 1744904 | tf_op jit(solution)/shard_map/ppermute | solution.py:1157
  591.7 12.7 %collective-permute-start.25 = (bf16[2272,128]{1,0:T(8,128)(2,1)S(1)}, bf16[2272,128]{1,0:T(8,128)(2,1)S(1)}, u32[]{:S(2)}, u32[]{:S(2)}) collective-permute-start(bf16[2272,128]{1,0:T(8,128)(2,1)S(1)} %fusion.28), channel_id=1, source_target_pairs={{8,0},{9,1},{10,2},{11,3},{12,4},{13,5},{14,6},{15,7},{16,8},{17,9... | collective-permute-start | bytes 1744904 | tf_op jit(solution)/shard_map/ppermute | solution.py:1157
  (31 other events, 370.5 us)
Sparse Core Ops, SparseCore 0:
  11.5 125.6 all-gather.4
  140.6 121.1 all-gather.2

commit v2 on v1

--- a/solution.py
+++ b/solution.py
@@ -109,9 +109,13 @@
     return (at[:, None] == at[None, :]).astype(np.float32)
 
 
+TAPS = 16
+
+
 def spread_tables():
     select = np.zeros((LINE, LINE), np.float32)
     gather = np.zeros((LINE, LINE), np.float32)
+    tile = np.zeros((LINE, LINE), np.float32)
     for ky in range(3):
         for kx in range(3):
             for a in range(2):
@@ -120,9 +124,37 @@
                     shift = (dy + 1) * 3 + dx + 1
                     for c in range(3):
                         out = (a * 2 + b) * 3 + c
-                        select[(ky * 3 + kx) * 3 + c, shift * 12 + out] = 1.0
-                        gather[shift * 12 + out, out] = 1.0
-    return select, gather
+                        select[c * TAPS + ky * 3 + kx, shift * 12 + out] = 1.0
+                        gather[out::12, out][:9] = 1.0
+                        tile[c, out] = 1.0
+    return select, gather, tile
+
+
+def patch_table():
+    pick = np.zeros((4, LINE, 32), np.float32)
+    for a in range(2):
+        for b in range(2):
+            for ky in range(3):
+                for kx in range(3):
+                    (dy, ya), (dx, xb) = divmod(a + ky - 1, 2), divmod(b + kx - 1, 2)
+                    shift = (dy + 1) * 3 + dx + 1
+                    for c in range(3):
+                        k = (ky * 3 + kx) * 3 + c
+                        pick[a * 2 + b, shift * 12 + (ya * 2 + xb) * 3 + c, k // 2 + 16 * (k % 2)] = 1.0
+    return pick
+
+
+def expand_table():
+    return (np.arange(3 * CH_MID)[None, :] // 3 == np.arange(CH_MID)[:, None]).astype(np.float32)
+
+
+def colour(c):
+    lane = lax.broadcasted_iota(jnp.int32, (1, 3 * CH_MID), 1)
+    return lax.rem(lane, 3) == c
+
+
+def first_lanes():
+    return lax.broadcasted_iota(jnp.int32, (1, LINE), 1) < LINE // 2
 
 
 def split3(v):
@@ -304,35 +336,37 @@
 
 
 class Lines:
-    def __init__(self, lines, stage, wide, sem):
-        self.lines, self.stage, self.wide, self.sem = lines, stage, wide, sem
-
-    def copy(self, l0, l1):
-        low, top = l0 // 16 * 16, -(-l1 // 16) * 16
-        return pltpu.make_async_copy(
-            self.lines.at[pl.ds(low, top - low), :], self.stage.at[pl.ds(0, top - low), :], self.sem
-        )
-
-    def start(self, span):
-        self.copy(*span).start()
-
-    def take(self, span, then=None):
+    def __init__(self, held, wide):
+        self.held, self.wide = held, wide
+
+    def take(self, span):
         l0, l1 = span
-        self.copy(l0, l1).wait()
-        self.low = l0 // 16 * 16
-        count = -(-l1 // 16) * 16 - self.low
-        whole, rest = divmod(count, 256)
-
-        def body(c, carry):
-            r = pl.multiple_of(c * 256, 256)
-            self.wide[pl.ds(r, 256), :] = self.stage[pl.ds(r, 256), :].astype(F32)
-            return carry
-
-        lax.fori_loop(0, whole, body, 0)
-        if rest:
-            self.wide[whole * 256 : count, :] = self.stage[whole * 256 : count, :].astype(F32)
-        if then is not None:
-            self.start(then)
+        first = l0 // SHARD
+        self.low = first * SHARD + (l0 - first * SHARD) // 16 * 16
+        for s in range(first, (l1 - 1) // SHARD + 1):
+            start = max(l0 - s * SHARD, 0) // 16 * 16
+            count = -(-min(l1 - s * SHARD, SHARD) // 16) * 16 - start
+            to = s * SHARD + start - self.low
+            block = self.held.at[s // PLANE, s % PLANE]
+            whole, rest = divmod(count, 256)
+
+            def body(c, carry):
+                self.wide[pl.ds(pl.multiple_of(to + c * 256, 8), 256), :] = block[
+                    pl.ds(pl.multiple_of(start + c * 256, 16), 256), :
+                ].astype(F32)
+                return carry
+
+            lax.fori_loop(0, whole, body, 0)
+            if rest:
+                done = whole * 256
+                self.wide[to + done : to + count, :] = block[start + done : start + count, :].astype(F32)
+
+    def line(self, at, scratch):
+        shard = lax.div(at, SHARD)
+        row = at - shard * SHARD
+        low = pl.multiple_of(lax.div(row, 16) * 16, 16)
+        scratch[...] = self.held[lax.div(shard, PLANE), lax.rem(shard, PLANE), pl.ds(low, 16), :].astype(F32)
+        return scratch[pl.ds(row - low, 1), :]
 
     def matrix(self, w_ref, at, rows, step):
         block = 128 if rows % 192 else 192
@@ -371,10 +405,10 @@
 SPAN_TIME = (AT.time_one, AT.class_table)
 SPAN_EMB1 = (AT.first.embed, AT.first.conv_two)
 SPAN_EMB2 = (AT.second.embed, AT.second.conv_two)
-SPAN_DOWN = (AT.conv_down, AT.time_one)
+SPAN_DOWN = (AT.conv_in, AT.time_one)
 SPAN_ONE1 = (AT.first.gains, AT.first.embed)
 SPAN_TWO1 = (AT.first.conv_two, AT.second.gains)
-SPAN_ATTN = (AT.attn_gains, AT.conv_out)
+SPAN_ATTN = (AT.attn_gains, ALL_LINES)
 SPAN_ONE2 = (AT.second.gains, AT.second.embed)
 SPAN_TWO2 = (AT.second.conv_two, AT.attn_gains)
 
@@ -399,14 +433,31 @@
     return inside & (lane >= shift * 12) & (lane < shift * 12 + 12), dy * HALF + dx
 
 
-def forward_kernel(save, *refs):
-    labels, lines, xp, win, bin_, wz, bz, phi, gm, sel, gat = refs[:11]
-    f_out = refs[11]
-    (h0s, h1, u1, h2, qkv, mixed, h3, u2, h4, vec, mod, emb, pre) = refs[12:25]
+def forward_kernel(save, moves, flip, *refs):
+    me, labels, x_in, phi, gm, sel, gat, tile, expand, pick = refs[:10]
+    sources = max(move[0] for move in moves) + 1
+    pieces, refs = refs[10 : 10 + sources], refs[10 + sources :]
+    f_out = refs[0]
+    (h0s, h1, u1, h2, qkv, mixed, h3, u2, h4, vec, mod, emb, pre, wz, xp) = refs[1:16]
     if save:
-        sw_time, sw_emb1, sw_emb2, sw_down, sw_11, sw_12, sw_attn, sw_21, sw_22 = refs[25:34]
-    stage, wide, w_ref, w_sq, sbuf, pbuf, h0p, table, sem, save_sem, tab_sem = refs[34 if save else 25 :]
-    src = Lines(lines, stage, wide, sem)
+        sw_time, sw_emb1, sw_emb2, sw_down, sw_11, sw_12, sw_attn, sw_21, sw_22 = refs[16:25]
+    held, wide, w_ref, w_sq, sbuf, pbuf, h0p, table, w_in, b_out, sems, save_sem = refs[25 if save else 16 :]
+    src = Lines(held, wide)
+    arriving = []
+    for plane in range(SHARDS // PLANE):
+        copies = []
+        for n, lead, r, row, rows in moves:
+            target = held.at[plane, r ^ me[0], pl.ds(row, rows), :]
+            source = pieces[n].at[plane, lead] if flip[n] else pieces[n].at[lead, plane]
+            copies.append(pltpu.make_async_copy(source, target, sems.at[plane]))
+        for copy in copies:
+            copy.start()
+        arriving.append(copies)
+
+    def arrive(plane):
+        for copy in arriving[plane]:
+            copy.wait()
+
     pending = []
 
     def keep(source, target):
@@ -419,49 +470,49 @@
         while pending:
             pending.pop().wait()
 
-    tabs = []
-    for n in range(MB_DEV):
-        at = AT.class_table + labels[n] * (EMB_DIM // LINE)
-        low = pl.multiple_of(lax.div(at, 16) * 16, 16)
-        cp = pltpu.make_async_copy(lines.at[pl.ds(low, 32), :], table.at[pl.ds(n * 32, 32), :], tab_sem.at[n])
-        cp.start()
-        tabs.append((cp, at - low))
-    src.start(SPAN_TIME)
     clear_pads(sbuf)
     pbuf[0:8, :] = jnp.zeros((8, CH_MID), F32)
     pbuf[ROWS + 8 : ROWS + 16, :] = jnp.zeros((8, CH_MID), F32)
-    src.take(SPAN_TIME, SPAN_EMB1)
+    arrive(0)
+    src.take(SPAN_TIME)
     src.matrix(w_sq.at[0], AT.time_one, CH_BASE, 6)
     src.matrix(w_sq.at[1], AT.time_two, EMB_DIM, 6)
     pre[...] = dot3(phi[...], w_sq[0, :CH_BASE, :]) + src.row(AT.time_bias_one, 6)
     emb[...] = dot3(silu(pre[...]), w_sq[1]) + src.row(AT.time_bias_two, 6)
     for n in range(MB_DEV):
-        tabs[n][0].wait()
-    wide[0 : 32 * MB_DEV, :] = table[...].astype(F32)
-    for n in range(MB_DEV):
         for j in range(6):
             cols = slice(j * LINE, (j + 1) * LINE)
-            emb[n : n + 1, cols] += wide[pl.ds(n * 32 + tabs[n][1] + j, 1), :]
+            emb[n : n + 1, cols] += src.line(AT.class_table + labels[n] * 6 + j, table)
     keep(w_sq.at[1], sw_time if save else None)
     se = silu(emb[...])
-    src.take(SPAN_EMB1, SPAN_EMB2)
+    arrive(1)
+    src.take(SPAN_EMB1)
     src.matrix(w_sq.at[0], AT.first.embed, EMB_DIM, 6)
     m1 = dot3(se, w_sq[0]) + src.row(AT.first.embed_bias, 6)
     free()
     keep(w_sq.at[0], sw_emb1 if save else None)
-    src.take(SPAN_EMB2, SPAN_DOWN)
-    src.matrix(w_sq.at[1], AT.second.embed, EMB_DIM, 6)
-    m2 = dot3(se, w_sq[1]) + src.row(AT.second.embed_bias, 6)
-    free()
-    keep(w_sq.at[1], sw_emb2 if save else None)
     mod[0:2, :] = m1[0:2]
-    mod[2:4, :] = m2[0:2]
     mod[4:8, :] = jnp.zeros((4, EMB_DIM), F32)
 
+    src.take(SPAN_DOWN)
+    trio = [wide[pl.ds(j, 16, stride=3), :] for j in range(3)]
+    turned = [pltpu.roll(v, LINE // 2, 1) for v in trio[1:]]
+    w_in[0:16, 0:LINE] = trio[0]
+    w_in[0:16, LINE : 2 * LINE] = trio[1]
+    w_in[16:32, 0:LINE] = jnp.where(first_lanes(), turned[0], turned[1])
+    w_in[16:32, LINE : 2 * LINE] = turned[1]
+    w_low = w_in[...].astype(BF16)
+    spread = dot(x_in[...], gat[...], NT)
+    around = jnp.zeros((ROWS, LINE), F32)
+    for shift in range(9):
+        inside, by = upsample_masks(shift)
+        around = around + jnp.where(inside, spread if by == 0 else pltpu.roll(spread, (-by) % ROWS, 0), 0.0)
+    around = around.astype(BF16)
+    one = (lax.broadcasted_iota(jnp.int32, (1, 32), 1) == 29).astype(F32)
     for ph in range(4):
-        v = dot(xp[ph * ROWS : (ph + 1) * ROWS, :], win[...]) + bin_[...]
-        h0s[ph * ROWS : (ph + 1) * ROWS, :] = v.astype(BF16)
-    src.take(SPAN_DOWN, SPAN_ONE1)
+        patch = (dot(around, pick[ph]) + one).astype(BF16)
+        xp[ph * ROWS : (ph + 1) * ROWS, :] = patch
+        h0s[ph * ROWS : (ph + 1) * ROWS, :] = dot(patch, w_low).astype(BF16)
     for j in range(3):
         vec[V_DOWN : V_DOWN + 1, j * LINE : (j + 1) * LINE] = src.row(AT.bias_down + j, 1)
     src.matrix(w_ref, AT.conv_down, 9 * CH_BASE, 3)
@@ -499,25 +550,36 @@
         out_ref[...] = bias if add_ref is None else add_ref[...] + bias
         conv_forward(sbuf, w_ref, out_ref)
 
-    def block(h_in, u, h_out, prefix, g_row, b1_row, b2_row, mod_row, spans, nxt, targets):
-        src.take(spans[0], spans[1])
+    def block(h_in, u, h_out, prefix, g_row, b1_row, b2_row, mod_row, spans, targets):
+        src.take(spans[0])
         free()
         vectors(g_row, prefix.gains, 4)
         vectors(b1_row, prefix.bias_one, 1)
         half_block(h_in, block_scales(vec, g_row), b1_row, None, u, prefix.conv_one, targets[0])
-        src.take(spans[1], nxt)
+        src.take(spans[1])
         free()
         vectors(b2_row, prefix.bias_two, 1)
         half_block(u, block_scales(vec, g_row + 2, mod, mod_row), b2_row, h_in, h_out, prefix.conv_two, targets[1])
 
     saved = (sw_11, sw_12, sw_21, sw_22) if save else (None,) * 4
-    block(h1, u1, h2, AT.first, V_G1, V_B11, V_B12, 0, (SPAN_ONE1, SPAN_TWO1), SPAN_ATTN, saved[:2])
-
-    src.take(SPAN_ATTN, SPAN_ONE2)
+    arrive(2)
+    block(h1, u1, h2, AT.first, V_G1, V_B11, V_B12, 0, (SPAN_ONE1, SPAN_TWO1), saved[:2])
+
+    arrive(3)
+    src.take(SPAN_ATTN)
     free()
     vectors(V_AG, AT.attn_gains, 2)
     vectors(V_AB, AT.attn_bias, 1)
     vectors(V_FG, AT.final_gains, 2)
+    base = AT.conv_out - src.low
+    tap_row = lax.broadcasted_iota(jnp.int32, (TAPS, 1), 0) < 9
+    taps = [jnp.where(tap_row, wide[pl.ds(base + j, TAPS, stride=9), :], 0.0) for j in range(9)]
+    taps = jnp.concatenate(taps, 1)
+    rows_out = jnp.concatenate([jnp.where(colour(c), taps, 0.0) for c in range(3)], 0).astype(BF16)
+    wz[...] = jnp.zeros_like(wz)
+    wz[0 : 3 * TAPS, :] = dot(rows_out, expand[...], NT).astype(BF16)
+    last = AT.bias_out - src.low
+    b_out[...] = dot(eight(wide[last : last + 1, :]).astype(BF16), tile[...])
     for part in range(3):
         base = AT.attn_qkv - src.low
         for j in range(3):
@@ -550,18 +612,24 @@
     lax.fori_loop(0, MB_DEV, heads, 0)
     h3[...] = h2[...] + dot(mixed[...], w_ref[3 * CH_MID : 4 * CH_MID, :]) + vec[V_AB : V_AB + 1, :]
 
-    block(h3, u2, h4, AT.second, V_G2, V_B21, V_B22, 2, (SPAN_ONE2, SPAN_TWO2), None, saved[2:])
+    src.take(SPAN_EMB2)
+    src.matrix(w_sq.at[1], AT.second.embed, EMB_DIM, 6)
+    m2 = dot3(silu(emb[...]), w_sq[1]) + src.row(AT.second.embed_bias, 6)
+    mod[2:4, :] = m2[0:2]
+    free()
+    keep(w_sq.at[1], sw_emb2 if save else None)
+    block(h3, u2, h4, AT.second, V_G2, V_B21, V_B22, 2, (SPAN_ONE2, SPAN_TWO2), saved[2:])
 
     stats = [group_stats(h4, img, gm) for img in range(MB_DEV)]
     norm_to(pbuf, h4, stats, block_scales(vec, V_FG), True)
-    z = dot(pbuf[8 : 8 + ROWS, :].astype(BF16), wz[...])
+    z = dot(pbuf[8 : 8 + ROWS, :].astype(BF16), wz[...], NT)
     t_all = dot3(z, sel[...])
     u_all = jnp.zeros((ROWS, LINE), F32)
     for shift in range(9):
         inside, by = upsample_masks(shift)
         moved = t_all if by == 0 else pltpu.roll(t_all, (-by) % ROWS, 0)
         u_all = u_all + jnp.where(inside, moved, 0.0)
-    f_out[...] = dot3(u_all, gat[...]) + bz[...]
+    f_out[...] = dot3(u_all, gat[...]) + b_out[0:1, :]
     free()
 
 
@@ -586,6 +654,8 @@
         ((8, EMB_DIM), F32),
         ((8, EMB_DIM), F32),
         ((8, EMB_DIM), F32),
+        ((LINE, CH_MID), BF16),
+        ((4 * ROWS, 32), BF16),
     ]
 
 
@@ -595,7 +665,8 @@
     return [sq, sq, sq, ((9 * CH_BASE, CH_MID), BF16), conv, conv, ((4 * CH_MID, CH_MID), BF16), conv, conv]
 
 
-def forward_call(save, labels, lines, xp, win, bin_, wz, bz, phi, tables):
+def forward_call(save, me, labels, lines, x_in, phi, tables):
+    pieces, moves, flip = lines
     sds = lambda s: jax.ShapeDtypeStruct(*s)
     outs = [sds(((ROWS, LINE), F32))]
     out_specs = [VM]
@@ -606,34 +677,33 @@
         out_specs += [VM] * len(state) + [HB] * len(weight_shapes())
     else:
         scratch += [vmem(*s) for s in state]
-    stage_rows = 10416
     scratch += [
-        vmem((stage_rows, LINE), BF16),
-        vmem((stage_rows, LINE), F32),
+        vmem((SHARDS // PLANE, PLANE, ROOM, LINE), BF16),
+        vmem((10432, LINE), F32),
         vmem((9 * CH_MID, CH_MID), BF16),
         vmem((2, EMB_DIM, EMB_DIM), BF16),
         vmem((3, PADDED, CH_MID), BF16),
         vmem((ROWS + 16, CH_MID), F32),
-        vmem((ROWS + 32, 256), F32),
-        vmem((32 * MB_DEV, LINE), BF16),
+        vmem((ROWS + 48, 256), F32),
+        vmem((16, LINE), F32),
+        vmem((32, 2 * LINE), F32),
+        vmem((8, LINE), F32),
+        pltpu.SemaphoreType.DMA((SHARDS // PLANE,)),
         pltpu.SemaphoreType.DMA,
-        pltpu.SemaphoreType.DMA,
-        pltpu.SemaphoreType.DMA((MB_DEV,)),
     ]
 
     def body(*refs):
-        forward_kernel(save, *refs)
+        forward_kernel(save, moves, flip, *refs)
 
     return pl.pallas_call(
         body,
         out_shape=outs,
-        in_specs=[SM, HB] + [VM] * 9,
+        in_specs=[SM] * 2 + [VM] * 8 + [HB] * len(pieces),
         out_specs=out_specs,
         scratch_shapes=scratch,
-        compiler_params=pltpu.CompilerParams(vmem_limit_bytes=60 * 1024 * 1024),
-        cost_estimate=pl.CostEstimate(flops=8 * 10**9, bytes_accessed=4 * 10**7, transcendentals=10**6),
         name="forward_save" if save else "forward_plain",
-    )(labels, lines, xp, win, bin_, wz, bz, phi, *tables)
+        **kernel_params(),
+    )(me, labels, x_in, phi, *tables, *pieces)
 
 
 def column_sum(pbuf):
@@ -769,9 +839,9 @@
 
 
 def back_two_kernel(*refs):
-    me, df, wz, gm, sel, gat, vec, mod, emb, h4, u2, h3, qkv, mixed, h2, u1, s22, s21, s_attn, s12, s_emb = refs[:21]
-    keep, send, rest, dh, du, dm_first, extra, dse, dwz = refs[21:30]
-    g, slots, w_sq, sbuf, pbuf, dx, at_ref, dqkv, dm, stage, sems, sq_sem, out_sems = refs[30:]
+    me, df, wz, gm, sel, gat, tile, expand, vec, mod, emb, h4, u2, h3, qkv, mixed, h2, u1, s22, s21, s_attn, s12, s_emb = refs[:23]
+    keep, send, rest, dh, du, dm_first, extra, dse = refs[23:31]
+    g, slots, w_sq, sbuf, pbuf, dx, at_ref, dqkv, dm, stage, sems, sq_sem, out_sems = refs[31:]
     weights = Weights([s22, s21, s_attn, s12], slots, sems)
     weights.begin()
     weights.begin()
@@ -795,8 +865,16 @@
         dt = dt + (part if by == 0 else pltpu.roll(part, by % ROWS, 0))
     dz = dot(dt.astype(BF16), sel[...], NT)
     parts = split3(dz)
-    dwz[...] = dot(at_ref[...], parts[0]) + dot(at_ref[...], parts[1]) + dot(at_ref[...], parts[2])
-    dx[...] = dot(parts[0], wz[...], NT) + dot(parts[1], wz[...], NT) + dot(parts[2], wz[...], NT)
+    dwz = dot(at_ref[...], parts[0]) + dot(at_ref[...], parts[1]) + dot(at_ref[...], parts[2])
+    dx[...] = dot(parts[0], wz[...]) + dot(parts[1], wz[...]) + dot(parts[2], wz[...])
+    d_rows = dot3(dwz.T[0 : 3 * TAPS, :], expand[...])
+    d_taps = jnp.zeros((TAPS, 3 * CH_MID), F32)
+    for c in range(3):
+        d_taps = d_taps + jnp.where(colour(c), d_rows[c * TAPS : (c + 1) * TAPS, :], 0.0)
+    for j in range(9):
+        g[pl.ds(TAIL - SPLIT + j, 9, stride=9), :] = d_taps[0:9, j * LINE : (j + 1) * LINE]
+    b_row = AT.bias_out - SPLIT
+    g[b_row : b_row + 1, :] = dot3(eight(colsum(df, 0, ROWS)), tile[...], NT)[0:1]
 
     def emit_first(r, v):
         dh[pl.ds(r, CHUNK), :] = v
@@ -887,10 +965,10 @@
 
 
 def back_one_kernel(*refs):
-    (me, labels, dh_in, du, dm, extra, dse_in, gm, vec, emb, pre, phi, h1, h0s, xpt) = refs[:15]
+    (me, labels, dh_in, du, dm, extra, dse_in, gm, vec, emb, pre, phi, h1, h0s, xp) = refs[:15]
     s11, s_down, s_emb, s_time, rest = refs[15:20]
-    keep, send, dwin, dbin = refs[20:24]
-    g, slots, w_sq, sbuf, pbuf, dx, at_ref, dh, h0t, demb_ref, stage, sems, sq_sem, out_sems = refs[24:]
+    keep, send = refs[20:22]
+    g, slots, w_sq, sbuf, pbuf, dx, at_ref, dh, h0t, demb_ref, stage, dwin, dbin, sems, sq_sem, out_sems = refs[22:]
     above = pltpu.make_async_copy(rest, g.at[pl.ds(SPLIT, MIDDLE - SPLIT), :], out_sems.at[2])
     above.start()
     weights = Weights([s11, s_down], slots, sems)
@@ -900,7 +978,6 @@
     for copy in sq_copies:
         copy.start()
     clear_pads(sbuf)
-    clear_lines(g, 0, AT.conv_down)
     clear_lines(g, MIDDLE, g.shape[0] - MIDDLE)
     pbuf[0:8, :] = jnp.zeros((8, CH_MID), F32)
     pbuf[ROWS + 8 : ROWS + 16, :] = jnp.zeros((8, CH_MID), F32)
@@ -956,8 +1033,14 @@
                 t = 3 * ky + kx
                 d0 = d0 + dot(d, w[t * CH_BASE : (t + 1) * CH_BASE, :], NT)
                 put_lines(g, AT.conv_down + t * CH_BASE * 3, dot(h0t[0:CH_BASE, :], d), 3)
-        dbin[:, :CH_BASE] += rowsum(d0)
-        dwin[:, :CH_BASE] += dot(xpt[:, ph * ROWS : (ph + 1) * ROWS], d0.astype(BF16))
+        dbin[0:1, :CH_BASE] += rowsum(d0)
+        dwin[:, :CH_BASE] += dot(xp[ph * ROWS : (ph + 1) * ROWS, :], d0.astype(BF16), TN)
+    dwin[29:30, :] = dbin[0:1, :]
+    even, odd = dwin[0:16, :], dwin[16:32, :]
+    turned = pltpu.roll(odd[:, :LINE], LINE // 2, 1), pltpu.roll(odd[:, LINE:], LINE // 2, 1)
+    g[pl.ds(0, 14, stride=3), :] = even[0:14, :LINE]
+    g[pl.ds(1, 14, stride=3), :] = jnp.where(first_lanes(), even[:, LINE:], turned[0])[0:14]
+    g[pl.ds(2, 14, stride=3), :] = jnp.where(first_lanes(), turned[0], turned[1])[0:14]
     leave.plane(0, 0)
     leave.wait()
 
@@ -1004,10 +1087,9 @@
             sds((8, EMB_DIM), F32),
             sds((8, CH_MID), F32),
             sds((8, EMB_DIM), F32),
-            sds((CH_MID, LINE), F32),
         ],
-        in_specs=[SM] + [VM] * 15 + [HB] * 5,
-        out_specs=[HB] * 3 + [VM] * 6,
+        in_specs=[SM] + [VM] * 17 + [HB] * 5,
+        out_specs=[HB] * 3 + [VM] * 5,
         scratch_shapes=scratch
         + [
             vmem((ROWS, 3 * CH_MID), BF16),
@@ -1023,18 +1105,19 @@
 
 
 def back_one_call(args):
-    sds = lambda *s: jax.ShapeDtypeStruct(*s)
     return pl.pallas_call(
         back_one_kernel,
-        out_shape=plane_shapes() + [sds((32, 256), F32), sds((1, 256), F32)],
+        out_shape=plane_shapes(),
         in_specs=[SM] * 2 + [VM] * 13 + [HB] * 5,
-        out_specs=[HB] * 2 + [VM] * 2,
+        out_specs=[HB] * 2,
         scratch_shapes=back_scratch(MIDDLE)
         + [
             vmem((ROWS, CH_MID), F32),
             vmem((256, ROWS), BF16),
             vmem((8, EMB_DIM), F32),
             vmem((PLANE, ROOM, LINE), BF16),
+            vmem((32, 2 * LINE), F32),
+            vmem((8, 2 * LINE), F32),
             pltpu.SemaphoreType.DMA((2,)),
             pltpu.SemaphoreType.DMA((2,)),
             pltpu.SemaphoreType.DMA((3,)),
@@ -1065,46 +1148,25 @@
     return jnp.pad(jnp.concatenate([jnp.cos(phases), jnp.sin(phases)], 1), ((0, 8 - MB_DEV), (0, 0)))
 
 
-def by_parity(image):
-    channels = image.shape[-1]
-    split = image.reshape(MB_DEV, HALF, 2, HALF, 2, channels)
-    return split.transpose(2, 4, 0, 1, 3, 5).reshape(4, ROWS, channels)
-
-
-def pixels(image):
-    return by_parity(image).transpose(1, 0, 2).reshape(ROWS, 12)
-
-
-def input_patches(noisy, scale):
-    low = (scale[:, None, None, None] * noisy).astype(BF16)
-    padded = jnp.pad(low, ((0, 0), (1, 1), (1, 1), (0, 0)))
-    taps = [padded[:, t // 3 : t // 3 + RES, t % 3 : t % 3 + RES] for t in range(9)]
-    flat = by_parity(jnp.concatenate(taps, 3)).reshape(4 * ROWS, 27)
-    return jnp.pad(flat, ((0, 0), (0, 5)))
-
-
-def small_weights(lines):
-    front = lines[: AT.conv_down].reshape(-1)
-    size = 27 * CH_BASE
-    win = jnp.pad(front[:size].reshape(27, CH_BASE), ((0, 5), (0, 64)))
-    bin_ = jnp.pad(front[size : size + CH_BASE].astype(F32)[None], ((0, 0), (0, 64)))
-    tail = lines[TAIL:].reshape(-1)
-    size = 27 * CH_MID
-    wz = tail[:size].reshape(9, CH_MID, 3).transpose(1, 0, 2).reshape(CH_MID, 27)
-    bz = jnp.tile(tail[size : size + 3].astype(F32), 4)
-    return win, bin_, jnp.pad(wz, ((0, 0), (0, LINE - 27))), jnp.pad(bz, (0, LINE - 12))[None]
-
-
-def per_part(labels, lines, noisy, sigma, save, tables):
-    skip, out_scale, in_scale = preconditioning_factors(sigma)
-    xp = input_patches(noisy, in_scale)
-    phi = noise_features(sigma)
-    win, bin_, wz, bz = small_weights(lines)
-    results = forward_call(save, labels, lines, xp, win, bin_, wz, bz, phi, tables)
-    model = results[0][:, :12]
-    per_row = lambda v: jnp.repeat(v, PIX)[:, None]
-    denoised = per_row(skip) * pixels(noisy) + per_row(out_scale) * model
-    return denoised, (xp, phi, wz, out_scale, results[1:])
+def pixels(images):
+    lead = images.shape[0]
+    split = images.reshape(lead, MB_DEV, HALF, 2, HALF, 2, 3)
+    return split.transpose(0, 1, 2, 4, 3, 5, 6).reshape(lead, ROWS, 12)
+
+
+def pixel_live(counts, valid_rows):
+    row = lax.broadcasted_iota(jnp.int32, (ROWS, 12), 0)
+    lane = lax.broadcasted_iota(jnp.int32, (ROWS, 12), 1)
+    slot = row // PIX
+    line = 2 * ((row // HALF) % HALF) + lane // 6
+    top = jnp.where(slot == 0, valid_rows[0], valid_rows[1])
+    return ((slot < counts[0]) & (line < top)).astype(F32)
+
+
+def per_part(me, labels, lines, inputs, save, tables):
+    _, x_in, phi, _ = inputs
+    results = forward_call(save, me, labels, lines, x_in, phi, tables)
+    return results[0], results[1:]
 
 
 AXIS = "fsdp"
@@ -1122,6 +1184,115 @@
         values = values + lax.ppermute(values, AXIS, [(i, i ^ hop) for i in range(n)])
         hop *= 2
     return values
+
+
+CUTS = (0, 864, 1728, ROOM)
+TALL = SHARDS // PLANE
+
+
+def gate(values, after):
+    count = len(values)
+
+    def body(*refs):
+        pass
+
+    return pl.pallas_call(
+        body,
+        out_shape=[jax.ShapeDtypeStruct(v.shape, v.dtype) for v in values],
+        in_specs=[HB] * (count + len(after)),
+        out_specs=[HB] * count,
+        input_output_aliases={i: i for i in range(count)},
+        name="gate",
+    )(*values, *after)
+
+
+def climb(values, way, far, first=0):
+    planes = range(first, TALL - far) if way == 1 else range(TALL - 1 - first, far - 1, -1)
+    pairs = [(q * PLANE + i, (q + way * far) * PLANE + i) for q in planes for i in range(PLANE)]
+    return lax.ppermute(values, AXIS, pairs)
+
+
+def column_window(slots, z):
+    rows = []
+    for p in range(TALL):
+        value = slots[TALL - 1 + p]
+        for q in range(1, TALL):
+            value = jnp.where(z == q, slots[TALL - 1 - q + p], value)
+        rows.append(value)
+    return jnp.stack(rows)
+
+
+def column_one(own):
+    return climb(own, 1, 1), climb(own, -1, 1)
+
+
+def column_two(own, one):
+    below, above = one
+    return climb(below, 1, 1, 1), climb(above, -1, 1, 1), climb(own, 1, 3), climb(own, -1, 3)
+
+
+def column_all(own, one, two, z):
+    return column_window([two[2], two[0], one[0], own, one[1], two[1], two[3]], z)
+
+
+def gather_both(online, target, z, early):
+    ab_o, ab_t = online[: CUTS[2]], target[: CUTS[2]]
+    c_own = jnp.stack([online[CUTS[2] :], target[CUTS[2] :]])
+    one = column_one(ab_o)
+    c_two = jnp.stack([c_own, swap(c_own, SOUTH)])
+    c_four = jnp.concatenate([c_two, swap(c_two, EAST)])
+    two = column_two(ab_o, one)
+    column = column_all(ab_o, one, two, z)
+    za, zb = column[:, : CUTS[1]], column[:, CUTS[1] :]
+    done = early([two[0][:16], two[1][:16]])
+    a_two, b_two = jnp.stack([za, swap(za, EAST)]), jnp.stack([zb, swap(zb, SOUTH)])
+    a_far, b_far = swap(a_two, SOUTH), swap(b_two, EAST)
+    (ab_t,) = gate([ab_t], two)
+    one = column_one(ab_t)
+    two = column_two(ab_t, one)
+    column = column_all(ab_t, one, two, z)
+    za, zb = column[:, : CUTS[1]], column[:, CUTS[1] :]
+    co_four, ct_four = c_four[:, 0], c_four[:, 1]
+    (co_four,) = gate([co_four], two)
+    c_one = column_one(co_four)
+    c_next = column_two(co_four, c_one)
+    c_all = column_all(co_four, c_one, c_next, z)
+    first = [a_two, a_far, b_two, b_far, c_all]
+    first = first + [swap(v, CORE) for v in first]
+    za, zb = gate([za, zb], [a_far, b_far])
+    a_east, b_south = swap(za, EAST), swap(zb, SOUTH)
+    at_two, bt_two = jnp.stack([za, a_east]), jnp.stack([zb, b_south])
+    (ct_four,) = gate([ct_four], c_next)
+    ct_one = column_one(ct_four)
+    ct_next = column_two(ct_four, ct_one)
+    at_far, bt_far = swap(at_two, SOUTH), swap(bt_two, EAST)
+    at_core, bt_core = swap(at_two, CORE), swap(bt_two, CORE)
+
+    def second(model):
+        af, bf, c0, c1, c2, c3 = gate([at_far, bt_far, *ct_next], [model])
+        ct_all = column_all(ct_four, ct_one, (c0, c1, c2, c3), z)
+        rest = [swap(v, CORE) for v in (af, bf, ct_all)]
+        return [at_two, af, bt_two, bf, ct_all, at_core, rest[0], bt_core, rest[1], rest[2]]
+
+    return done, first, [a_east, b_south, *ct_one], second
+
+
+def gather_moves():
+    places = [(0, 1), (2, 3), (0, 2), (1, 3), (0, 2, 1, 3)]
+    part = (0, 0, 1, 1, 2)
+    moves = []
+    for core in range(2):
+        for n in range(5):
+            row, end = CUTS[part[n]], CUTS[part[n] + 1]
+            for lead, place in enumerate(places[n]):
+                moves.append((core * 5 + n, lead, 2 * place + core, row, end - row))
+    return moves
+
+
+def gather_plain(shard):
+    lines = lax.all_gather(shard, AXIS, axis=0, tiled=True).reshape(SHARDS // PLANE, PLANE, SHARD, LINE)
+    lines = jnp.pad(lines, ((0, 0), (0, 0), (0, ROOM - SHARD), (0, 0)))
+    return [lines], [(0, r, r, 0, ROOM) for r in range(PLANE)], (True,)
 
 
 def reduce_planes(keep, send):
@@ -1163,55 +1334,72 @@
     direct = n == SHARDS
     index = lax.axis_index(AXIS)
     me = jnp.where(direct, lax.rem(index, PLANE), 0).astype(jnp.int32)[None]
-    gather = lambda v: lax.all_gather(v.astype(BF16).reshape(-1, LINE), AXIS, axis=0, tiled=True)
-    online, target = gather(master), gather(ema)
-    select, collect = spread_tables()
-    tables = (jnp.asarray(group_table(), BF16), jnp.asarray(select, BF16), jnp.asarray(collect, BF16))
-    slot_live = (jnp.arange(MB_DEV) < counts[0]).astype(F32)
-    row_live = (jnp.arange(RES)[None, :] < valid_rows[:, None]).astype(F32)
-    pixel_mask = slot_live[:, None] * row_live
-    pixel_total = 3.0 * RES * total_of(jnp.sum(pixel_mask), n)
-    mask = pixels(jnp.broadcast_to(pixel_mask[:, :, None, None], images.shape))
-    sigma_lo, sigma_hi = karras(step_index), karras(step_index + 1)
-    add_noise = lambda sigma: images + sigma[:, None, None, None] * noise_draws
-    online_out, (xp, phi, wz, out_scale, saved) = per_part(labels, online, add_noise(sigma_hi), sigma_hi, True, tables)
-    target_out, _ = per_part(labels, target, add_noise(sigma_lo), sigma_lo, False, tables)
+    z = lax.div(index, PLANE)
+    shards = [v.astype(BF16).reshape(-1, LINE) for v in (master, ema)]
+    tables = tuple(jnp.asarray(v, BF16) for v in (group_table(), *spread_tables(), expand_table(), patch_table()))
+    live = (jnp.arange(MB_DEV) < counts[0]).astype(jnp.int32)
+    local_rows = jnp.sum(live * jnp.clip(valid_rows, 0, RES)).astype(F32)
+
+    def early(after):
+        clean, noise = gate([images, noise_draws], after) if after else (images, noise_draws)
+        clean, noise = pixels(jnp.stack([clean, noise]))
+        per_row = lambda v: jnp.repeat(v, PIX)[:, None]
+
+        def inputs_of(sigma):
+            noisy = clean + per_row(sigma) * noise
+            skip, out_scale, in_scale = preconditioning_factors(sigma)
+            x_in = jnp.pad((per_row(in_scale) * noisy).astype(BF16), ((0, 0), (0, LINE - 12)))
+            return per_row(skip) * noisy, x_in, noise_features(sigma), per_row(out_scale)
+
+        mask = pixel_live(counts, valid_rows)
+        return inputs_of(karras(step_index)), inputs_of(karras(step_index + 1)), mask
+
+    total = total_of(jnp.broadcast_to(local_rows, (8, LINE)), n)
+    pixel_total = 3.0 * RES * total[0, 0]
+    if direct:
+        rooms = [jnp.pad(v, ((0, ROOM - SHARD), (0, 0))) for v in shards]
+        (in_lo, in_hi, mask), pieces, before, second = gather_both(rooms[0], rooms[1], z, early)
+        moves, flip = gather_moves(), (False,) * 4 + (True,) + (False,) * 4 + (True,)
+        online = (pieces, moves, flip)
+        (x_in,) = gate([in_hi[1]], [*before, in_lo[0], in_lo[1], in_lo[2], in_hi[0], in_hi[2], total])
+        in_hi = (in_hi[0], x_in, *in_hi[2:])
+    else:
+        online, target = gather_plain(shards[0]), gather_plain(shards[1])
+        in_lo, in_hi, mask = early(())
+    model_o, saved = per_part(me, labels, online, in_hi, True, tables)
+    if direct:
+        target = (second(model_o), moves, flip)
+    model_t, _ = per_part(me, labels, target, in_lo, False, tables)
+    online_out = in_hi[0] + in_hi[3] * model_o[:, :12]
+    target_out = in_lo[0] + in_lo[3] * model_t[:, :12]
+    phi, out_scale = in_hi[2], in_hi[3]
     gap = online_out - target_out
     local_loss = jnp.sum(mask * jnp.square(gap))
-    grad_model = jnp.repeat(out_scale, PIX)[:, None] * 2.0 * mask * gap / pixel_total
+    grad_model = out_scale * 2.0 * mask * gap / pixel_total
     bias_out = jnp.sum(grad_model.reshape(ROWS, 4, 3), axis=(0, 1))
-    (h0s, h1, u1, h2, qkv, mixed, h3, u2, h4, vec, mod, emb, pre) = saved[:13]
-    s_time, s_emb1, s_emb2, s_down, s11, s12, s_attn, s21, s22 = saved[13:]
-    gm, sel, gat = tables
+    (h0s, h1, u1, h2, qkv, mixed, h3, u2, h4, vec, mod, emb, pre, wz, xp) = saved[:15]
+    s_time, s_emb1, s_emb2, s_down, s11, s12, s_attn, s21, s22 = saved[15:]
+    gm = tables[0]
     df = jnp.pad(grad_model, ((0, 0), (0, LINE - 12)))
-    keep_top, send_top, rest, dh, du, dm, extra, dse, dwz = back_two_call(
-        (me, df, wz, gm, sel, gat, vec, mod, emb, h4, u2, h3, qkv, mixed, h2, u1, s22, s21, s_attn, s12, s_emb2)
+    keep_top, send_top, rest, dh, du, dm, extra, dse = back_two_call(
+        (me, df, wz, *tables[:5], vec, mod, emb, h4, u2, h3, qkv, mixed, h2, u1, s22, s21, s_attn, s12, s_emb2)
     )
-    keep_low, send_low, dwin, dbin = back_one_call(
-        (me, labels, dh, du, dm, extra, dse, gm, vec, emb, pre, phi, h1, h0s, xp.T, s11, s_down, s_emb1, s_time, rest)
+    keep_low, send_low = back_one_call(
+        (me, labels, dh, du, dm, extra, dse, gm, vec, emb, pre, phi, h1, h0s, xp, s11, s_down, s_emb1, s_time, rest)
     )
-    tail = dwz[:, :27].reshape(CH_MID, 9, 3).transpose(1, 0, 2).reshape(-1)
-    small = jnp.concatenate([dwin[:27, :CH_BASE].reshape(-1), dbin[0, :CH_BASE], tail, bias_out, local_loss[None]])
-    front_size, tail_size = AT.conv_down * LINE, tail.shape[0] + 3
-    small = jnp.pad(small, (0, LINE * LINE - small.shape[0])).reshape(LINE, LINE)
-    small = total_of(small, n).reshape(-1)
+    small = jnp.concatenate([local_loss[None], bias_out])
+    small = total_of(jnp.broadcast_to(small, (8, 4)), n)[0]
     if direct:
         part = jnp.concatenate([reduce_planes(keep_low, send_low), reduce_planes(keep_top, send_top)])
-        reduced = reduce_column(part, lax.div(index, PLANE))[:SHARD].reshape(-1)
+        reduced = reduce_column(part, z)[:SHARD].reshape(-1)
     else:
         both = [jnp.stack([k, s.astype(F32)], 2) for k, s in ((keep_low, send_low), (keep_top, send_top))]
         lines = jnp.concatenate(both).reshape(SHARDS, ROOM, LINE)[:, :SHARD].reshape(n, -1)
         reduced = lax.psum_scatter(lines, AXIS, scatter_dimension=0, tiled=True).reshape(-1)
-    size = master.shape[0]
-    start = TAIL * LINE - (n - 1) * size
-    first = jnp.where(index == 0, small[:front_size], 0.0)
-    last = jnp.where(index == n - 1, small[front_size : front_size + tail_size], 0.0)
-    reduced = reduced + jnp.pad(first, (0, size - front_size)) + jnp.pad(last, (start, size - start - tail_size))
     new_momentum = MOMENTUM * momentum + reduced
     new_master = master - LEARN_RATE * (reduced + MOMENTUM * new_momentum)
     new_ema = EMA_DECAY * ema + (1.0 - EMA_DECAY) * new_master
-    end = front_size + tail_size
-    return (small[end] / pixel_total, new_momentum, new_master, new_ema, small[end - 3 : end])
+    return (small[0] / pixel_total, new_momentum, new_master, new_ema, small[1:])
 
 
 def solution(mesh):

time: 620 us -> 574 us (0.926)
  waiting for transfers between devices: 305 us -> 167 us
  starting transfers between devices: 44.7 us -> 127 us
  other arithmetic: 34.2 us -> 62.1 us
  between operations: 21.4 us -> 5.76 us
  local copies, waits for them, and re-layouts: 47.2 us -> 36.7 us
    all_gather x2 -> x0, waiting for transfers between devices: 202 us -> none  [per_device(): lax.all_gather(v.astype(BF16).reshape(-1, LINE), AXIS, axis=0, tiled=True)]
    ppermute x0 -> x24, starting transfers between devices: none -> 62.9 us  [climb(): return lax.ppermute(values, AXIS, pairs)]
    ppermute x10 -> x30, waiting for transfers between devices: 68.6 us -> 99.8 us  [swap(): return lax.ppermute(values, AXIS, [(i, i ^ hop) for i in range(SHARDS)])]
    ppermute x0 -> x24, waiting for transfers between devices: none -> 27.4 us  [climb(): return lax.ppermute(values, AXIS, pairs)]
    another operation x2 -> x16, other arithmetic: 4.11 us -> 27.3 us  [the longest x8 12 us: column_window(): return jnp.stack(rows)]
    ppermute x10 -> x30, starting transfers between devices: 9.64 us -> 26.4 us  [swap(): return lax.ppermute(values, AXIS, [(i, i ^ hop) for i in range(SHARDS)])]
    reshape x25 -> x0, local copies, waits for them, and re-layouts: 12.9 us -> none  [the longest x6 3.94 us: small_weights(): tail[:size].reshape(9, CH_MID, 3).transpose(1, 0, 2).reshape(CH_MID, 27)]
    ppermute x6, waiting for transfers between devices: 15.5 us -> 27.7 us  [reduce_column(): run = lax.ppermute(value.astype(BF16), AXIS, pairs).astype(F32)]
  transfers between devices with their start and end apart: 28 -> 70, of which waited for: 21 -> 33; matrix products, arithmetic and copies ran while one was open for 10% -> 12% of each run, Pallas kernels for 0% -> 9%
where the time goes in v2:
time: 574 us; the launch traced here: 565 us
  waiting for transfers between devices  167 us (29%)
  Pallas kernels  167 us (29%)
  starting transfers between devices  127 us (22%)
  other arithmetic  62.1 us (11%)
  local copies, waits for them, and re-layouts  36.7 us (6%)
  between operations  5.76 us (1%)
    ppermute x30, waiting for transfers between devices, swap(): return lax.ppermute(values, AXIS, [(i, i ^ hop) for i in range(SHARDS)])  99.8 us
    pallas_call x2, Pallas kernels, forward_call(): pl.pallas_call(body, out_shape=outs, in_specs=[SM] * 2 + [VM] * 8 + [HB]...  92.8 us
    ppermute x24, starting transfers between devices, climb(): return lax.ppermute(values, AXIS, pairs)  62.9 us
    pallas_call x1, Pallas kernels, back_two_call(): pl.pallas_call(back_two_kernel, out_shape=plane_shapes() + [sds((MIDDLE -...  51.5 us
    ppermute x6, waiting for transfers between devices, reduce_column(): run = lax.ppermute(value.astype(BF16), AXIS, pairs).astype(F32)  27.7 us
    ppermute x24, waiting for transfers between devices, climb(): return lax.ppermute(values, AXIS, pairs)  27.4 us
    ppermute x30, starting transfers between devices, swap(): return lax.ppermute(values, AXIS, [(i, i ^ hop) for i in range(SHARDS)])  26.4 us
    pallas_call x1, Pallas kernels, back_one_call(): pl.pallas_call(back_one_kernel, out_shape=plane_shapes(), in_specs=[SM] *...  22.2 us
  transfers between devices with their start and end apart: 70, of which 33 were waited for; matrix products, arithmetic and copies ran while one was open for 12% of the time, Pallas kernels for 9%

profile of v2, /device:TPU:0, one launch (start us, length us, event | category | flops | bytes accessed | tf_op | source)
XLA Modules:
  0.0 564.7 jit_solution(18118798605479914783)
XLA Ops:
  2.9 5.7 %collective-permute-start = (bf16[1728,128]{1,0:T(8,128)(2,1)}, bf16[1728,128]{1,0:T(8,128)(2,1)}, u32[]{:S(2)}, u32[]{:S(2)}) collective-permute-start(bf16[1728,128]{1,0:T(8,128)(2,1)} %slice_bitcast_fusion.11), channel_id=1, source_target_pairs={{0,8},{1,9},{2,10},{3,11},{4,12},{5,13},{6,14},{7,15},{8,16},{9,17... | collective-permute-start | bytes 1327112 | tf_op jit(solution)/shard_map/ppermute | solution.py:1212
  9.9 7.3 %collective-permute-start.4 = (bf16[1728,128]{1,0:T(8,128)(2,1)}, bf16[1728,128]{1,0:T(8,128)(2,1)}, u32[]{:S(2)}, u32[]{:S(2)}) collective-permute-start(bf16[1728,128]{1,0:T(8,128)(2,1)} %slice_bitcast_fusion.11), channel_id=1, source_target_pairs={{0,24},{1,25},{2,26},{3,27},{4,28},{5,29},{6,30},{7,31}} | collective-permute-start | bytes 1327112 | tf_op jit(solution)/shard_map/ppermute | solution.py:1212
  37.0 5.7 %collective-permute-done.3.refs_2_ = bf16[1728,128]{1,0:T(8,128)(2,1)} collective-permute-done((bf16[1728,128]{1,0:T(8,128)(2,1)}, bf16[1728,128]{1,0:T(8,128)(2,1)}, u32[]{:S(2)}, u32[]{:S(2)}) %collective-permute-start.3) | collective-permute-done | bytes 442400 | tf_op jit(solution)/shard_map/ppermute | solution.py:1212
  43.9 5.8 %collective-permute-start.7 = (bf16[1728,128]{1,0:T(8,128)(2,1)}, bf16[1728,128]{1,0:T(8,128)(2,1)S(1)}, u32[]{:S(2)}, u32[]{:S(2)}) collective-permute-start(bf16[1728,128]{1,0:T(8,128)(2,1)} %gate.8), channel_id=1, source_target_pairs={{0,8},{1,9},{2,10},{3,11},{4,12},{5,13},{6,14},{7,15},{8,16},{9,17... | collective-permute-start | bytes 1327112 | tf_op jit(solution)/shard_map/ppermute | solution.py:1212
  57.5 6.1 %collective-permute-start.6 = (bf16[1728,128]{1,0:T(8,128)(2,1)S(1)}, bf16[1728,128]{1,0:T(8,128)(2,1)S(1)}, u32[]{:S(2)}, u32[]{:S(2)}) collective-permute-start(bf16[1728,128]{1,0:T(8,128)(2,1)S(1)} %copy-done.12), channel_id=1, source_target_pairs={{0,24},{1,25},{2,26},{3,27},{4,28},{5,29},{6,30},{7,31}} | collective-permute-start | bytes 1327112 | tf_op jit(solution)/shard_map/ppermute | solution.py:1212
  70.2 8.2 %collective-permute-start.31 = (f32[8,128]{1,0:T(8,128)S(1)}, f32[8,128]{1,0:T(8,128)S(1)}, u32[]{:S(2)}, u32[]{:S(2)}) collective-permute-start(f32[8,128]{1,0:T(8,128)S(1)} %add.276), channel_id=1, source_target_pairs={{0,8},{1,9},{2,10},{3,11},{4,12},{5,13},{6,14},{7,15},{8,0},{9,1},... | collective-permute-start | bytes 12296 | tf_op jit(solution)/shard_map/ppermute | solution.py:1184
  84.4 6.2 %collective-permute-start.24 = (bf16[4,544,128]{2,1,0:T(8,128)(2,1)}, bf16[4,544,128]{2,1,0:T(8,128)(2,1)S(1)}, u32[]{:S(2)}, u32[]{:S(2)}) collective-permute-start(bf16[4,544,128]{2,1,0:T(8,128)(2,1)} %gate.10), channel_id=1, source_target_pairs={{0,24},{1,25},{2,26},{3,27},{4,28},{5,29},{6,30},{7,31}} | collective-permute-start | bytes 1671176 | tf_op jit(solution)/shard_map/ppermute | solution.py:1212
  106.3 10.6 %collective-permute-done.25.refs_4_ = bf16[4,544,128]{2,1,0:T(8,128)(2,1)S(1)} collective-permute-done((bf16[4,544,128]{2,1,0:T(8,128)(2,1)S(1)}, bf16[4,544,128]{2,1,0:T(8,128)(2,1)S(1)}, u32[]{:S(2)}, u32[]{:S(2)}) %collective-permute-start.25) | collective-permute-done | bytes 557088 | tf_op jit(solution)/shard_map/ppermute | solution.py:1212
  119.3 6.2 %collective-permute-done.23.refs_2_ = bf16[4,544,128]{2,1,0:T(8,128)(2,1)} collective-permute-done((bf16[4,544,128]{2,1,0:T(8,128)(2,1)S(1)}, bf16[4,544,128]{2,1,0:T(8,128)(2,1)}, u32[]{:S(2)}, u32[]{:S(2)}) %collective-permute-start.23) | collective-permute-done | bytes 557088 | tf_op jit(solution)/shard_map/ppermute | solution.py:1212
  142.2 6.8 %collective-permute-start.17 = (bf16[4,864,128]{2,1,0:T(8,128)(2,1)}, bf16[4,864,128]{2,1,0:T(8,128)(2,1)S(1)}, u32[]{:S(2)}, u32[]{:S(2)}) collective-permute-start(bf16[4,864,128]{2,1,0:T(8,128)(2,1)} %get-tuple-element.53), channel_id=1, source_target_pairs={{0,4},{1,5},{2,6},{3,7},{4,0},{5,1},{6,2},{7,3},{8,12},{9,13},{10,... | collective-permute-start | bytes 2654216 | tf_op jit(solution)/shard_map/ppermute | solution.py:1178
  152.8 6.5 %collective-permute-done.16.refs_1_ = bf16[4,864,128]{2,1,0:T(8,128)(2,1)S(1)} collective-permute-done((bf16[4,864,128]{2,1,0:T(8,128)(2,1)}, bf16[4,864,128]{2,1,0:T(8,128)(2,1)S(1)}, u32[]{:S(2)}, u32[]{:S(2)}) %collective-permute-start.16) | collective-permute-done | bytes 884768 | tf_op jit(solution)/shard_map/ppermute | solution.py:1178
  159.3 6.5 %collective-permute-done.17.refs_2_ = bf16[4,864,128]{2,1,0:T(8,128)(2,1)S(1)} collective-permute-done((bf16[4,864,128]{2,1,0:T(8,128)(2,1)}, bf16[4,864,128]{2,1,0:T(8,128)(2,1)S(1)}, u32[]{:S(2)}, u32[]{:S(2)}) %collective-permute-start.17) | collective-permute-done | bytes 884768 | tf_op jit(solution)/shard_map/ppermute | solution.py:1178
  195.9 48.2 %forward_save.1 = (f32[512,128]{1,0:T(8,128)}, bf16[2048,256]{1,0:T(8,128)(2,1)}, f32[512,384]{1,0:T(8,128)}, f32[512,384]{1,0:T(8,128)}, f32[512,384]{1,0:T(8,1...) custom-call(s32[1]{0:T(128)} %bitcast.7.refs_0_, ...), custom_call_target="tpu_custom_call" | custom-call | flops 8000000000 | bytes 40000000 | tf_op jit(solution)/shard_map/forward_save/pallas_call | solution.py:698
  262.2 44.6 %forward_plain.1 = f32[512,128]{1,0:T(8,128)} custom-call(s32[1]{0:T(128)} %bitcast.7.refs_0_, s32[2]{0:T(128)} %refs_1_.6, bf16[512,128]{1,0:T(8,128)(2,1)} %pad.28.refs_6_.refs_2_, f32[8,192]{1,0:T(8,128)} %select_maximum_fusion.1.refs_7_.refs_3_, bf16[384,384]{1,0:T(8,128)(2,1)} %constant.166.clone.refs_4_.refs_3_.refs_7_, ...), custom_call_target="tpu_custom_call" | custom-call | flops 8000000000 | bytes 40000000 | tf_op jit(solution)/shard_map/forward_plain/pallas_call | solution.py:698
  313.0 51.5 %back_two.1 = (f32[2,4,2272,128]{3,2,1,0:T(8,128)}, bf16[2,4,2272,128]{3,2,1,0:T(8,128)(2,1)}, f32[4240,128]{1,0:T(8,128)}, f32[512,384]{1,0:T(8,128)}, f32[512,...) custom-call(s32[1]{0:T(128)} %bitcast.7.refs_0_, f32[512,128]{1,0:T(8,128)} %pad.31.refs_1_, ...), custom_call_target="tpu_custom_call" | custom-call | flops 8000000000 | bytes 40000000 | tf_op jit(solution)/shard_map/back_two/pallas_call | solution.py:1080
  364.5 22.2 %back_one.1 = (f32[2,4,2272,128]{3,2,1,0:T(8,128)}, bf16[2,4,2272,128]{3,2,1,0:T(8,128)(2,1)}) custom-call(s32[1]{0:T(128)} %bitcast.7.refs_0_, s32[2]{0:T(128)} %refs_1_.6, f32[512,384]{1,0:T(8,128)} %get-tuple-element.77.refs_2_, f32[512,384]{1,0:T(8,128)} %get-tuple-element.78.refs_3_, f32[8,768]{1,0:T(8,128)} %get-tuple-element.79.refs_4_, ...), custom_call_target="tpu_custom_call" | custom-call | flops 8000000000 | bytes 40000000 | tf_op jit(solution)/shard_map/back_one/pallas_call | solution.py:1108
  402.9 24.2 %collective-permute-done.55 = bf16[2,2,1136,128]{3,2,0,1:T(8,128)(2,1)S(1)} collective-permute-done((bf16[2,2,1136,128]{3,2,0,1:T(8,128)(2,1)S(1)}, bf16[2,2,1136,128]{3,2,0,1:T(8,128)(2,1)S(1)}, u32[]{:S(2)}, u32[]{:S(2)}) %collective-permute-start.55) | collective-permute-done | bytes 1163296 | tf_op jit(solution)/shard_map/ppermute | solution.py:1178
  431.3 19.9 %collective-permute-done.60 = bf16[2,2,1136,128]{3,2,0,1:T(8,128)(2,1)S(1)} collective-permute-done((bf16[2,2,1136,128]{3,2,0,1:T(8,128)(2,1)S(1)}, bf16[2,2,1136,128]{3,2,0,1:T(8,128)(2,1)S(1)}, u32[]{:S(2)}, u32[]{:S(2)}) %collective-permute-start.60) | collective-permute-done | bytes 1163296 | tf_op jit(solution)/shard_map/ppermute | solution.py:1178
  461.5 10.0 %collective-permute-done.61 = bf16[2,1136,128]{2,1,0:T(8,128)(2,1)} collective-permute-done((bf16[2,1136,128]{2,1,0:T(8,128)(2,1)}, bf16[2,1136,128]{2,1,0:T(8,128)(2,1)}, u32[]{:S(2)}, u32[]{:S(2)}) %collective-permute-start.61) | collective-permute-done | bytes 581664 | tf_op jit(solution)/shard_map/ppermute | solution.py:1178
  474.4 7.4 %collective-permute-done.56 = bf16[2,1136,128]{2,1,0:T(8,128)(2,1)S(1)} collective-permute-done((bf16[2,1136,128]{2,1,0:T(8,128)(2,1)}, bf16[2,1136,128]{2,1,0:T(8,128)(2,1)S(1)}, u32[]{:S(2)}, u32[]{:S(2)}) %collective-permute-start.56) | collective-permute-done | bytes 581664 | tf_op jit(solution)/shard_map/ppermute | solution.py:1178
  493.9 9.2 %collective-permute-done.64 = bf16[2272,128]{1,0:T(8,128)(2,1)} collective-permute-done((bf16[2272,128]{1,0:T(8,128)(2,1)S(1)}, bf16[2272,128]{1,0:T(8,128)(2,1)}, u32[]{:S(2)}, u32[]{:S(2)}) %collective-permute-start.64) | collective-permute-done | bytes 581664 | tf_op jit(solution)/shard_map/ppermute | solution.py:1328
  504.6 5.3 collective-permute-start.65
  510.8 8.1 %collective-permute-done.65 = bf16[2272,128]{1,0:T(8,128)(2,1)} collective-permute-done((bf16[2272,128]{1,0:T(8,128)(2,1)S(1)}, bf16[2272,128]{1,0:T(8,128)(2,1)}, u32[]{:S(2)}, u32[]{:S(2)}) %collective-permute-start.65) | collective-permute-done | bytes 581664 | tf_op jit(solution)/shard_map/ppermute | solution.py:1328
  554.7 6.2 %collective-permute-done.69 = bf16[2272,128]{1,0:T(8,128)(2,1)S(1)} collective-permute-done((bf16[2272,128]{1,0:T(8,128)(2,1)S(1)}, bf16[2272,128]{1,0:T(8,128)(2,1)S(1)}, u32[]{:S(2)}, u32[]{:S(2)}) %collective-permute-start.69) | collective-permute-done | bytes 581664 | tf_op jit(solution)/shard_map/ppermute | solution.py:1328
  (332 shorter events, 220.5 us)
Async XLA Ops:
  2.9 24.1 %collective-permute-start = (bf16[1728,128]{1,0:T(8,128)(2,1)}, bf16[1728,128]{1,0:T(8,128)(2,1)}, u32[]{:S(2)}, u32[]{:S(2)}) collective-permute-start(bf16[1728,128]{1,0:T(8,128)(2,1)} %slice_bitcast_fusion.11), channel_id=1, source_target_pairs={{0,8},{1,9},{2,10},{3,11},{4,12},{5,13},{6,14},{7,15},{8,16},{9,17... | collective-permute-start | bytes 1327112 | tf_op jit(solution)/shard_map/ppermute | solution.py:1212
  9.9 25.6 %collective-permute-start.4 = (bf16[1728,128]{1,0:T(8,128)(2,1)}, bf16[1728,128]{1,0:T(8,128)(2,1)}, u32[]{:S(2)}, u32[]{:S(2)}) collective-permute-start(bf16[1728,128]{1,0:T(8,128)(2,1)} %slice_bitcast_fusion.11), channel_id=1, source_target_pairs={{0,24},{1,25},{2,26},{3,27},{4,28},{5,29},{6,30},{7,31}} | collective-permute-start | bytes 1327112 | tf_op jit(solution)/shard_map/ppermute | solution.py:1212
  55.1 29.3 %collective-permute-start.14 = (bf16[4,864,128]{2,1,0:T(8,128)(2,1)}, bf16[4,864,128]{2,1,0:T(8,128)(2,1)}, u32[]{:S(2)}, u32[]{:S(2)}) collective-permute-start(bf16[4,864,128]{2,1,0:T(8,128)(2,1)} %get-tuple-element.127), channel_id=1, source_target_pairs={{0,4},{1,5},{2,6},{3,7},{4,0},{5,1},{6,2},{7,3},{8,12},{9,13},{10,... | collective-permute-start | bytes 2654216 | tf_op jit(solution)/shard_map/ppermute | solution.py:1178
  55.6 37.9 %collective-permute-start.12 = (bf16[4,864,128]{2,1,0:T(8,128)(2,1)}, bf16[4,864,128]{2,1,0:T(8,128)(2,1)}, u32[]{:S(2)}, u32[]{:S(2)}) collective-permute-start(bf16[4,864,128]{2,1,0:T(8,128)(2,1)} %get-tuple-element.128), channel_id=1, source_target_pairs={{0,2},{1,3},{2,0},{3,1},{4,6},{5,7},{6,4},{7,5},{8,10},{9,11},{10,... | collective-permute-start | bytes 2654216 | tf_op jit(solution)/shard_map/ppermute | solution.py:1178
  70.2 28.3 %collective-permute-start.31 = (f32[8,128]{1,0:T(8,128)S(1)}, f32[8,128]{1,0:T(8,128)S(1)}, u32[]{:S(2)}, u32[]{:S(2)}) collective-permute-start(f32[8,128]{1,0:T(8,128)S(1)} %add.276), channel_id=1, source_target_pairs={{0,8},{1,9},{2,10},{3,11},{4,12},{5,13},{6,14},{7,15},{8,0},{9,1},... | collective-permute-start | bytes 12296 | tf_op jit(solution)/shard_map/ppermute | solution.py:1184
  93.5 39.7 %collective-permute-start.15 = (bf16[2,4,864,128]{3,2,1,0:T(8,128)(2,1)}, bf16[2,4,864,128]{3,2,1,0:T(8,128)(2,1)}, u32[]{:S(2)}, u32[]{:S(2)}) collective-permute-start(bf16[2,4,864,128]{3,2,1,0:T(8,128)(2,1)} %pad_maximum_fusion.5.refs_12_), channel_id=1, source_target_pairs={{0,2},{1,3},{2,0},{3,1},{4,6},{5,7},{6,4},{7,5},{8,10},{9,11},{10,... | collective-permute-start | bytes 5308424 | tf_op jit(solution)/shard_map/ppermute | solution.py:1178
  98.5 35.9 %collective-permute-start.13 = (bf16[2,4,864,128]{3,2,1,0:T(8,128)(2,1)}, bf16[2,4,864,128]{3,2,1,0:T(8,128)(2,1)}, u32[]{:S(2)}, u32[]{:S(2)}) collective-permute-start(bf16[2,4,864,128]{3,2,1,0:T(8,128)(2,1)} %pad_maximum_fusion.4.refs_10_), channel_id=1, source_target_pairs={{0,4},{1,5},{2,6},{3,7},{4,0},{5,1},{6,2},{7,3},{8,12},{9,13},{10,... | collective-permute-start | bytes 5308424 | tf_op jit(solution)/shard_map/ppermute | solution.py:1178
  133.2 40.7 %collective-permute-start.35 = (bf16[2,4,864,128]{3,2,1,0:T(8,128)(2,1)}, bf16[2,4,864,128]{3,2,1,0:T(8,128)(2,1)}, u32[]{:S(2)}, u32[]{:S(2)}) collective-permute-start(bf16[2,4,864,128]{3,2,1,0:T(8,128)(2,1)} %pad_maximum_fusion.5.refs_12_), channel_id=1, source_target_pairs={{0,1},{1,0},{2,3},{3,2},{4,5},{5,4},{6,7},{7,6},{8,9},{9,8},{10,11... | collective-permute-start | bytes 5308424 | tf_op jit(solution)/shard_map/ppermute | solution.py:1178
  134.4 41.2 %collective-permute-start.33 = (bf16[2,4,864,128]{3,2,1,0:T(8,128)(2,1)}, bf16[2,4,864,128]{3,2,1,0:T(8,128)(2,1)}, u32[]{:S(2)}, u32[]{:S(2)}) collective-permute-start(bf16[2,4,864,128]{3,2,1,0:T(8,128)(2,1)} %pad_maximum_fusion.4.refs_10_), channel_id=1, source_target_pairs={{0,1},{1,0},{2,3},{3,2},{4,5},{5,4},{6,7},{7,6},{8,9},{9,8},{10,11... | collective-permute-start | bytes 5308424 | tf_op jit(solution)/shard_map/ppermute | solution.py:1178
  142.2 23.6 %collective-permute-start.17 = (bf16[4,864,128]{2,1,0:T(8,128)(2,1)}, bf16[4,864,128]{2,1,0:T(8,128)(2,1)S(1)}, u32[]{:S(2)}, u32[]{:S(2)}) collective-permute-start(bf16[4,864,128]{2,1,0:T(8,128)(2,1)} %get-tuple-element.53), channel_id=1, source_target_pairs={{0,4},{1,5},{2,6},{3,7},{4,0},{5,1},{6,2},{7,3},{8,12},{9,13},{10,... | collective-permute-start | bytes 2654216 | tf_op jit(solution)/shard_map/ppermute | solution.py:1178
  152.7 37.9 %collective-permute-start.37 = (bf16[4,4,544,128]{3,2,1,0:T(8,128)(2,1)}, bf16[4,4,544,128]{3,2,1,0:T(8,128)(2,1)}, u32[]{:S(2)}, u32[]{:S(2)}) collective-permute-start(bf16[4,4,544,128]{3,2,1,0:T(8,128)(2,1)} %pad_maximum_fusion.refs_14_), channel_id=1, source_target_pairs={{0,1},{1,0},{2,3},{3,2},{4,5},{5,4},{6,7},{7,6},{8,9},{9,8},{10,11... | collective-permute-start | bytes 6684680 | tf_op jit(solution)/shard_map/ppermute | solution.py:1178
  159.3 33.7 %collective-permute-start.36 = (bf16[2,4,864,128]{3,2,1,0:T(8,128)(2,1)}, bf16[2,4,864,128]{3,2,1,0:T(8,128)(2,1)}, u32[]{:S(2)}, u32[]{:S(2)}) collective-permute-start(bf16[2,4,864,128]{3,2,1,0:T(8,128)(2,1)} %collective-permute-done.15.refs_3_.refs_13_), channel_id=1, source_target_pairs={{0,1},{1,0},{2,3},{3,2},{4,5},{5,4},{6,7},{7,6},{8,9},{9,8},{10,11... | collective-permute-start | bytes 5308424 | tf_op jit(solution)/shard_map/ppermute | solution.py:1178
  165.8 28.6 %collective-permute-start.34 = (bf16[2,4,864,128]{3,2,1,0:T(8,128)(2,1)}, bf16[2,4,864,128]{3,2,1,0:T(8,128)(2,1)}, u32[]{:S(2)}, u32[]{:S(2)}) collective-permute-start(bf16[2,4,864,128]{3,2,1,0:T(8,128)(2,1)} %collective-permute-done.13.refs_2_.refs_11_), channel_id=1, source_target_pairs={{0,1},{1,0},{2,3},{3,2},{4,5},{5,4},{6,7},{7,6},{8,9},{9,8},{10,11... | collective-permute-start | bytes 5308424 | tf_op jit(solution)/shard_map/ppermute | solution.py:1178
  173.9 70.3 %collective-permute-start.39 = (bf16[2,4,864,128]{3,2,1,0:T(8,128)(2,1)}, bf16[2,4,864,128]{3,2,1,0:T(8,128)(2,1)}, u32[]{:S(2)}, u32[]{:S(2)}) collective-permute-start(bf16[2,4,864,128]{3,2,1,0:T(8,128)(2,1)} %pad_maximum_fusion.7.refs_12_), channel_id=1, source_target_pairs={{0,2},{1,3},{2,0},{3,1},{4,6},{5,7},{6,4},{7,5},{8,10},{9,11},{10,... | collective-permute-start | bytes 5308424 | tf_op jit(solution)/shard_map/ppermute | solution.py:1178
  175.6 68.7 %collective-permute-start.38 = (bf16[2,4,864,128]{3,2,1,0:T(8,128)(2,1)}, bf16[2,4,864,128]{3,2,1,0:T(8,128)(2,1)}, u32[]{:S(2)}, u32[]{:S(2)}) collective-permute-start(bf16[2,4,864,128]{3,2,1,0:T(8,128)(2,1)} %pad_maximum_fusion.6.refs_10_), channel_id=1, source_target_pairs={{0,4},{1,5},{2,6},{3,7},{4,0},{5,1},{6,2},{7,3},{8,12},{9,13},{10,... | collective-permute-start | bytes 5308424 | tf_op jit(solution)/shard_map/ppermute | solution.py:1178
  191.7 52.5 %collective-permute-start.43 = (bf16[4,544,128]{2,1,0:T(8,128)(2,1)S(1)}, bf16[4,544,128]{2,1,0:T(8,128)(2,1)S(1)}, u32[]{:S(2)}, u32[]{:S(2)}) collective-permute-start(bf16[4,544,128]{2,1,0:T(8,128)(2,1)S(1)} %copy-done.8), channel_id=1, source_target_pairs={{24,0},{25,1},{26,2},{27,3},{28,4},{29,5},{30,6},{31,7}} | collective-permute-start | bytes 1671176 | tf_op jit(solution)/shard_map/ppermute | solution.py:1212
  193.0 51.2 %collective-permute-start.40 = (bf16[4,544,128]{2,1,0:T(8,128)(2,1)}, bf16[4,544,128]{2,1,0:T(8,128)(2,1)}, u32[]{:S(2)}, u32[]{:S(2)}) collective-permute-start(bf16[4,544,128]{2,1,0:T(8,128)(2,1)} %collective-permute-done.26.refs_3_), channel_id=1, source_target_pairs={{8,16},{9,17},{10,18},{11,19},{12,20},{13,21},{14,22},{15,23},{16,... | collective-permute-start | bytes 1671176 | tf_op jit(solution)/shard_map/ppermute | solution.py:1212
  194.4 49.8 %collective-permute-start.41 = (bf16[4,544,128]{2,1,0:T(8,128)(2,1)}, bf16[4,544,128]{2,1,0:T(8,128)(2,1)}, u32[]{:S(2)}, u32[]{:S(2)}) collective-permute-start(bf16[4,544,128]{2,1,0:T(8,128)(2,1)} %collective-permute-done.27.refs_4_), channel_id=1, source_target_pairs={{16,8},{17,9},{18,10},{19,11},{20,12},{21,13},{22,14},{23,15},{8,0... | collective-permute-start | bytes 1671176 | tf_op jit(solution)/shard_map/ppermute | solution.py:1212
  398.5 28.5 %collective-permute-start.55 = (bf16[2,2,1136,128]{3,2,0,1:T(8,128)(2,1)S(1)}, bf16[2,2,1136,128]{3,2,0,1:T(8,128)(2,1)S(1)}, u32[]{:S(2)}, u32[]{:S(2)}) collective-permute-start(bf16[2,2,1136,128]{3,2,0,1:T(8,128)(2,1)S(1)} %pad_maximum_fusion.8), channel_id=1, source_target_pairs={{0,2},{1,3},{2,0},{3,1},{4,6},{5,7},{6,4},{7,5},{8,10},{9,11},{10,... | collective-permute-start | bytes 3489800 | tf_op jit(solution)/shard_map/ppermute | solution.py:1178
  401.9 29.3 %collective-permute-start.62 = (bf16[2,2,1136,128]{3,2,0,1:T(8,128)(2,1)S(1)}, bf16[2,2,1136,128]{3,2,0,1:T(8,128)(2,1)S(1)}, u32[]{:S(2)}, u32[]{:S(2)}) collective-permute-start(bf16[2,2,1136,128]{3,2,0,1:T(8,128)(2,1)S(1)} %pad_maximum_fusion.11), channel_id=1, source_target_pairs={{0,4},{1,5},{2,6},{3,7},{4,0},{5,1},{6,2},{7,3},{8,12},{9,13},{10,... | collective-permute-start | bytes 3489800 | tf_op jit(solution)/shard_map/ppermute | solution.py:1178
  402.4 48.8 %collective-permute-start.60 = (bf16[2,2,1136,128]{3,2,0,1:T(8,128)(2,1)S(1)}, bf16[2,2,1136,128]{3,2,0,1:T(8,128)(2,1)S(1)}, u32[]{:S(2)}, u32[]{:S(2)}) collective-permute-start(bf16[2,2,1136,128]{3,2,0,1:T(8,128)(2,1)S(1)} %pad_maximum_fusion.10), channel_id=1, source_target_pairs={{0,2},{1,3},{2,0},{3,1},{4,6},{5,7},{6,4},{7,5},{8,10},{9,11},{10,... | collective-permute-start | bytes 3489800 | tf_op jit(solution)/shard_map/ppermute | solution.py:1178
  430.9 28.2 %collective-permute-start.57 = (bf16[2,2,1136,128]{3,2,0,1:T(8,128)(2,1)S(1)}, bf16[2,2,1136,128]{3,2,0,1:T(8,128)(2,1)}, u32[]{:S(2)}, u32[]{:S(2)}) collective-permute-start(bf16[2,2,1136,128]{3,2,0,1:T(8,128)(2,1)S(1)} %pad_maximum_fusion.9), channel_id=1, source_target_pairs={{0,4},{1,5},{2,6},{3,7},{4,0},{5,1},{6,2},{7,3},{8,12},{9,13},{10,... | collective-permute-start | bytes 3489800 | tf_op jit(solution)/shard_map/ppermute | solution.py:1178
  453.4 28.5 %collective-permute-start.56 = (bf16[2,1136,128]{2,1,0:T(8,128)(2,1)}, bf16[2,1136,128]{2,1,0:T(8,128)(2,1)S(1)}, u32[]{:S(2)}, u32[]{:S(2)}) collective-permute-start(bf16[2,1136,128]{2,1,0:T(8,128)(2,1)} %get-tuple-element.108), channel_id=1, source_target_pairs={{0,4},{1,5},{2,6},{3,7},{4,0},{5,1},{6,2},{7,3},{8,12},{9,13},{10,... | collective-permute-start | bytes 1744904 | tf_op jit(solution)/shard_map/ppermute | solution.py:1178
  521.1 24.6 %collective-permute-start.68 = (bf16[2272,128]{1,0:T(8,128)(2,1)S(1)}, bf16[2272,128]{1,0:T(8,128)(2,1)}, u32[]{:S(2)}, u32[]{:S(2)}) collective-permute-start(bf16[2272,128]{1,0:T(8,128)(2,1)S(1)} %get-tuple-element.122), channel_id=1, source_target_pairs={{16,8},{17,9},{18,10},{19,11},{20,12},{21,13},{22,14},{23,15},{24,... | collective-permute-start | bytes 1744904 | tf_op jit(solution)/shard_map/ppermute | solution.py:1328
  (94 other events, 1203.0 us)

commit v3 on v2

--- a/solution.py
+++ b/solution.py
@@ -97,8 +97,10 @@
 SHARD = 2264
 ROOM = 2272
 ALL_LINES = SHARDS * SHARD
-MIDDLE = ALL_LINES // 2
-SPLIT = AT.first.conv_two // 16 * 16
+PLANES = [p * PLANE * SHARD for p in range(SHARDS // PLANE)]
+BASE_ONE = AT.second.gains // 16 * 16
+BASE_TWO = AT.first.conv_two // 16 * 16
+BASE_THREE = AT.first.gains // 16 * 16
 
 V_DOWN, V_G1, V_B11, V_B12, V_AG, V_AB, V_FG, V_G2, V_B21, V_B22 = 0, 1, 5, 6, 7, 9, 10, 12, 16, 17
 VEC_ROWS = 24
@@ -799,34 +801,35 @@
 class Leave:
     def __init__(self, me, g, base, keep, send, stage, sems):
         self.core, self.place = lax.rem(me[0], 2), lax.div(me[0], 2)
-        self.g, self.base, self.keep, self.send, self.stage, self.sems = g, base, keep, send, stage, sems
+        self.g, self.base, self.outs, self.stage, self.sems = g, base, (keep, send), stage, sems
         self.copies = []
 
-    def plane(self, plane, slot):
-        pairs = PLANE // 2
-        for q in range(pairs):
+    def plane(self, plane):
+        for q in range(PLANE // 2):
             at = q ^ self.place
-            first = (plane * PLANE + 2 * q) * SHARD - self.base
-            mine = pl.multiple_of(first + self.core * SHARD, 8)
-            other = pl.multiple_of(first + (1 - self.core) * SHARD, 8)
-            kept = pltpu.make_async_copy(self.g.at[pl.ds(mine, ROOM), :], self.keep.at[slot, at], self.sems.at[0])
-            kept.start()
-            stage = self.stage.at[slot * pairs + q]
-            block = ROOM // 8
-
-            def body(c, carry):
-                stage[pl.ds(pl.multiple_of(c * 288, 16), 288), :] = self.g[
-                    pl.ds(pl.multiple_of(other + c * 288, 8), 288), :
-                ].astype(BF16)
-                return carry
-
-            whole = ROOM // 288
-            lax.fori_loop(0, whole, body, 0)
-            rest = ROOM - whole * 288
-            stage[whole * 288 :, :] = self.g[pl.ds(pl.multiple_of(other + whole * 288, 8), rest), :].astype(BF16)
-            sent = pltpu.make_async_copy(stage, self.send.at[slot, at], self.sems.at[1])
-            sent.start()
-            self.copies += [kept, sent]
+            first = PLANES[plane] + 2 * q * SHARD - self.base
+            for side in range(2):
+                core = 1 - self.core if side else self.core
+                start = first + core * SHARD
+                stage = self.stage.at[2 * q + side]
+                whole, rest = divmod(ROOM, 288)
+
+                def body(c, carry):
+                    lines = self.g[pl.ds(pl.multiple_of(start + c * 288, 8), 288), :]
+                    stage[pl.ds(pl.multiple_of(c * 288, 16), 288), :] = lines.astype(BF16)
+                    return carry
+
+                lax.fori_loop(0, whole, body, 0)
+                lines = self.g[pl.ds(pl.multiple_of(start + whole * 288, 8), rest), :]
+                stage[whole * 288 :, :] = lines.astype(BF16)
+                copy = pltpu.make_async_copy(stage, self.outs[side].at[at], self.sems.at[side])
+                copy.start()
+                self.copies.append(copy)
+
+    def below(self, count, rest):
+        copy = pltpu.make_async_copy(self.g.at[pl.ds(0, count), :], rest, self.sems.at[2])
+        copy.start()
+        self.copies.append(copy)
 
     def wait(self):
         for copy in self.copies:
@@ -838,19 +841,24 @@
         g[first : first + count, :] = jnp.zeros((count, LINE), F32)
 
 
-def back_two_kernel(*refs):
-    me, df, wz, gm, sel, gat, tile, expand, vec, mod, emb, h4, u2, h3, qkv, mixed, h2, u1, s22, s21, s_attn, s12, s_emb = refs[:23]
-    keep, send, rest, dh, du, dm_first, extra, dse = refs[23:31]
-    g, slots, w_sq, sbuf, pbuf, dx, at_ref, dqkv, dm, stage, sems, sq_sem, out_sems = refs[31:]
-    weights = Weights([s22, s21, s_attn, s12], slots, sems)
+def prepare(sbuf, pbuf):
+    clear_pads(sbuf)
+    pbuf[0:8, :] = jnp.zeros((8, CH_MID), F32)
+    pbuf[ROWS + 8 : ROWS + 16, :] = jnp.zeros((8, CH_MID), F32)
+
+
+def back_top_kernel(*refs):
+    me, df, wz, gm, sel, gat, tile, expand, vec, mod, emb, h4, u2, h3, qkv, mixed, h2, s22, s21, s_attn, s_emb = refs[:21]
+    keep, send, rest, dh, dse = refs[21:26]
+    g, slots, sbuf, pbuf, dx, at_ref, stage, sems, out_sems, w_sq, dqkv, dm, sq_sem = refs[26:]
+    base = BASE_ONE
+    weights = Weights([s22, s21, s_attn], slots, sems)
     weights.begin()
     weights.begin()
     sq_copy = pltpu.make_async_copy(s_emb, w_sq, sq_sem)
     sq_copy.start()
-    clear_pads(sbuf)
-    clear_lines(g, TAIL - SPLIT, g.shape[0] - (TAIL - SPLIT))
-    pbuf[0:8, :] = jnp.zeros((8, CH_MID), F32)
-    pbuf[ROWS + 8 : ROWS + 16, :] = jnp.zeros((8, CH_MID), F32)
+    prepare(sbuf, pbuf)
+    clear_lines(g, TAIL - base, g.shape[0] - (TAIL - base))
     tools = (sbuf, pbuf, dx, at_ref, gm)
 
     stats = [group_stats(h4, img, gm) for img in range(MB_DEV)]
@@ -872,34 +880,34 @@
     for c in range(3):
         d_taps = d_taps + jnp.where(colour(c), d_rows[c * TAPS : (c + 1) * TAPS, :], 0.0)
     for j in range(9):
-        g[pl.ds(TAIL - SPLIT + j, 9, stride=9), :] = d_taps[0:9, j * LINE : (j + 1) * LINE]
-    b_row = AT.bias_out - SPLIT
+        g[pl.ds(TAIL - base + j, 9, stride=9), :] = d_taps[0:9, j * LINE : (j + 1) * LINE]
+    b_row = AT.bias_out - base
     g[b_row : b_row + 1, :] = dot3(eight(colsum(df, 0, ROWS)), tile[...], NT)[0:1]
 
     def emit_first(r, v):
         dh[pl.ds(r, CHUNK), :] = v
 
     sums = norm_back(h4, dx, stats, scales, True, gm, emit_first)
-    put_row(g, AT.final_gains - SPLIT, sums[0][1] + sums[1][1])
-    put_row(g, AT.final_gains + 3 - SPLIT, sums[0][0] + sums[1][0])
+    put_row(g, AT.final_gains - base, sums[0][1] + sums[1][1])
+    put_row(g, AT.final_gains + 3 - base, sums[0][0] + sums[1][0])
 
     rows = (V_G2, V_B21, V_B22)
-    d_gain, d_shift = block_back_two(dh, u2, AT.second, SPLIT, rows, vec, mod, 2, weights, tools, g, dm)
-    put_row(g, AT.second.gains + 6 - SPLIT, d_gain)
-    put_row(g, AT.second.gains + 9 - SPLIT, d_shift)
-    block_back_one(dh, h3, AT.second, SPLIT, rows, vec, weights, tools, g)
+    d_gain, d_shift = block_back_two(dh, u2, AT.second, base, rows, vec, mod, 2, weights, tools, g, dm)
+    put_row(g, AT.second.gains + 6 - base, d_gain)
+    put_row(g, AT.second.gains + 9 - base, d_shift)
+    block_back_one(dh, h3, AT.second, base, rows, vec, weights, tools, g)
     se = silu(emb[...])
-    put_outer(g, AT.second.embed - SPLIT, se, dm[...])
-    put_row(g, AT.second.embed_bias - SPLIT, rowsum(dm[...]))
+    put_outer(g, AT.second.embed - base, se, dm[...])
+    put_row(g, AT.second.embed_bias - base, rowsum(dm[...]))
     sq_copy.wait()
     dse[...] = dot3(dm[...], w_sq[...], NT)
 
-    put_row(g, AT.attn_bias - SPLIT, colsum(dh, 0, ROWS))
+    put_row(g, AT.attn_bias - base, colsum(dh, 0, ROWS))
     w = weights.take()
     d_low = dh[...].astype(BF16)
     for c in range(ROWS // LINE):
         at_ref[:, c * LINE : (c + 1) * LINE] = mixed[c * LINE : (c + 1) * LINE, :].astype(F32).T.astype(BF16)
-    put_lines(g, AT.attn_out - SPLIT, dot(at_ref[...], d_low), 3)
+    put_lines(g, AT.attn_out - base, dot(at_ref[...], d_low), 3)
     pbuf[8 : 8 + ROWS, :] = dot(d_low, w[3 * CH_MID : 4 * CH_MID, :], NT)
     half = lane_half()
     scale = HEAD_DIM ** (-0.5)
@@ -937,7 +945,7 @@
         d = dqkv[:, part * CH_MID : (part + 1) * CH_MID]
         dw = dot(at_ref[...], d)
         for j in range(3):
-            g[pl.ds(AT.attn_qkv - SPLIT + part * 3 + j, CH_MID, stride=9), :] = dw[:, j * LINE : (j + 1) * LINE]
+            g[pl.ds(AT.attn_qkv - base + part * 3 + j, CH_MID, stride=9), :] = dw[:, j * LINE : (j + 1) * LINE]
         dx[...] += dot(d, w[part * CH_MID : (part + 1) * CH_MID, :], NT)
     weights.begin()
 
@@ -945,60 +953,90 @@
         dh[pl.ds(r, CHUNK), :] += v
 
     sums = norm_back(h2, dx, stats, scales, False, gm, emit)
-    put_row(g, AT.attn_gains - SPLIT, sums[0][1] + sums[1][1])
-    put_row(g, AT.attn_gains + 3 - SPLIT, sums[0][0] + sums[1][0])
-
-    leave = Leave(me, g, SPLIT, keep, send, stage, out_sems)
-    leave.plane(3, 1)
+    put_row(g, AT.attn_gains - base, sums[0][1] + sums[1][1])
+    put_row(g, AT.attn_gains + 3 - base, sums[0][0] + sums[1][0])
+
+    leave = Leave(me, g, base, keep, send, stage, out_sems)
+    leave.plane(3)
+    leave.below(PLANES[3] - base, rest)
+    leave.wait()
+
+
+def back_second_half_kernel(*refs):
+    me, dh, gm, vec, mod, u1, s12, rest_in = refs[:8]
+    keep, send, rest, du, dm, extra = refs[8:14]
+    g, slots, sbuf, pbuf, dx, at_ref, stage, sems, out_sems, in_sem = refs[14:]
+    base = BASE_TWO
+    weights = Weights([s12], slots, sems)
+    weights.begin()
+    above = pltpu.make_async_copy(rest_in, g.at[pl.ds(BASE_ONE - base, PLANES[3] - BASE_ONE), :], in_sem)
+    above.start()
+    prepare(sbuf, pbuf)
+    clear_lines(g, PLANES[3] - base, g.shape[0] - (PLANES[3] - base))
+    above.wait()
     rows = (V_G1, V_B11, V_B12)
-    d_gain, d_shift = block_back_two(dh, u1, AT.first, SPLIT, rows, vec, mod, 0, weights, tools, g, dm_first)
+    tools = (sbuf, pbuf, dx, at_ref, gm)
+    d_gain, d_shift = block_back_two(dh, u1, AT.first, base, rows, vec, mod, 0, weights, tools, g, dm)
     extra[...] = jnp.zeros_like(extra)
     extra[0:1, :] = d_gain
     extra[1:2, :] = d_shift
     for c in range(0, ROWS, CHUNK):
         du[c : c + CHUNK, :] = pbuf[8 + c : 8 + c + CHUNK, :]
-    leave.plane(2, 0)
-    below = pltpu.make_async_copy(g.at[pl.ds(0, MIDDLE - SPLIT), :], rest, out_sems.at[2])
-    below.start()
-    below.wait()
+    leave = Leave(me, g, base, keep, send, stage, out_sems)
+    leave.plane(2)
+    leave.below(PLANES[2] - base, rest)
     leave.wait()
 
 
-def back_one_kernel(*refs):
-    (me, labels, dh_in, du, dm, extra, dse_in, gm, vec, emb, pre, phi, h1, h0s, xp) = refs[:15]
-    s11, s_down, s_emb, s_time, rest = refs[15:20]
-    keep, send = refs[20:22]
-    g, slots, w_sq, sbuf, pbuf, dx, at_ref, dh, h0t, demb_ref, stage, dwin, dbin, sems, sq_sem, out_sems = refs[22:]
-    above = pltpu.make_async_copy(rest, g.at[pl.ds(SPLIT, MIDDLE - SPLIT), :], out_sems.at[2])
+def back_first_half_kernel(*refs):
+    me, dh_in, du, dm, extra, dse_in, gm, vec, emb, h1, s11, s_emb, rest_in = refs[:13]
+    keep, send, rest, dh, dse = refs[13:18]
+    g, slots, sbuf, pbuf, dx, at_ref, stage, sems, out_sems, w_sq, in_sem, sq_sem = refs[18:]
+    base = BASE_THREE
+    weights = Weights([s11], slots, sems)
+    weights.begin()
+    sq_copy = pltpu.make_async_copy(s_emb, w_sq, sq_sem)
+    sq_copy.start()
+    above = pltpu.make_async_copy(rest_in, g.at[pl.ds(BASE_TWO - base, PLANES[2] - BASE_TWO), :], in_sem)
     above.start()
-    weights = Weights([s11, s_down], slots, sems)
-    weights.begin()
-    weights.begin()
-    sq_copies = [pltpu.make_async_copy(s, w_sq.at[n], sq_sem.at[n]) for n, s in enumerate((s_emb, s_time))]
-    for copy in sq_copies:
-        copy.start()
-    clear_pads(sbuf)
-    clear_lines(g, MIDDLE, g.shape[0] - MIDDLE)
-    pbuf[0:8, :] = jnp.zeros((8, CH_MID), F32)
-    pbuf[ROWS + 8 : ROWS + 16, :] = jnp.zeros((8, CH_MID), F32)
+    prepare(sbuf, pbuf)
+    clear_lines(g, PLANES[2] - base, g.shape[0] - (PLANES[2] - base))
     refill(pbuf, du)
     for c in range(0, ROWS, CHUNK):
         dh[c : c + CHUNK, :] = dh_in[c : c + CHUNK, :]
     above.wait()
     tools = (sbuf, pbuf, dx, at_ref, gm)
-    block_back_one(dh, h1, AT.first, 0, (V_G1, V_B11, V_B12), vec, weights, tools, g)
-    put_row(g, AT.first.gains + 6, extra[0:1, :])
-    put_row(g, AT.first.gains + 9, extra[1:2, :])
-    se = silu(emb[...])
-    put_outer(g, AT.first.embed, se, dm[...])
-    put_row(g, AT.first.embed_bias, rowsum(dm[...]))
-    leave = Leave(me, g, 0, keep, send, stage, out_sems)
-    for copy in sq_copies:
-        copy.wait()
-    demb = (dse_in[...] + dot3(dm[...], w_sq[0], NT)) * silu_slope(emb[...])
+    put_outer(g, AT.first.embed - base, silu(emb[...]), dm[...])
+    put_row(g, AT.first.embed_bias - base, rowsum(dm[...]))
+    block_back_one(dh, h1, AT.first, base, (V_G1, V_B11, V_B12), vec, weights, tools, g)
+    put_row(g, AT.first.gains + 6 - base, extra[0:1, :])
+    put_row(g, AT.first.gains + 9 - base, extra[1:2, :])
+    leave = Leave(me, g, base, keep, send, stage, out_sems)
+    leave.plane(1)
+    leave.below(PLANES[1] - base, rest)
+    sq_copy.wait()
+    dse[...] = dse_in[...] + dot3(dm[...], w_sq[...], NT)
+    leave.wait()
+
+
+def back_low_kernel(*refs):
+    me, labels, dh, dse, emb, pre, phi, h0s, xp, s_down, s_time, rest_in = refs[:12]
+    keep, send = refs[12:14]
+    g, slots, sbuf, pbuf, h0t, stage, sems, out_sems, w_sq, demb_ref, dwin, dbin, in_sem, sq_sem = refs[14:]
+    weights = Weights([s_down], slots, sems)
+    weights.begin()
+    sq_copy = pltpu.make_async_copy(s_time, w_sq, sq_sem)
+    sq_copy.start()
+    above = pltpu.make_async_copy(rest_in, g.at[pl.ds(BASE_THREE, PLANES[1] - BASE_THREE), :], in_sem)
+    above.start()
+    prepare(sbuf, pbuf)
+    clear_lines(g, PLANES[1], g.shape[0] - PLANES[1])
+    above.wait()
+    demb = dse[...] * silu_slope(emb[...])
     put_row(g, AT.time_bias_two, rowsum(demb))
     put_outer(g, AT.time_two, silu(pre[...]), demb)
-    dpre = dot3(demb, w_sq[1], NT) * silu_slope(pre[...])
+    sq_copy.wait()
+    dpre = dot3(demb, w_sq[...], NT) * silu_slope(pre[...])
     put_row(g, AT.time_bias_one, rowsum(dpre))
     put_outer(g, AT.time_one, phi[...], dpre)
     clear = 240
@@ -1014,7 +1052,6 @@
         for j in range(EMB_DIM // LINE):
             at = first + labels[n] * (EMB_DIM // LINE) + j
             g[pl.ds(at, 1), :] += demb_ref[n : n + 1, j * LINE : (j + 1) * LINE]
-    leave.plane(1, 1)
 
     put_row(g, AT.bias_down, colsum(dh, 0, ROWS))
     refill(pbuf, dh)
@@ -1041,7 +1078,8 @@
     g[pl.ds(0, 14, stride=3), :] = even[0:14, :LINE]
     g[pl.ds(1, 14, stride=3), :] = jnp.where(first_lanes(), even[:, LINE:], turned[0])[0:14]
     g[pl.ds(2, 14, stride=3), :] = jnp.where(first_lanes(), turned[0], turned[1])[0:14]
-    leave.plane(0, 0)
+    leave = Leave(me, g, 0, keep, send, stage, out_sems)
+    leave.plane(0)
     leave.wait()
 
 
@@ -1052,79 +1090,73 @@
     )
 
 
-def back_scratch(lines):
-    return [
+def back_call(kernel, name, lines, slots, args, smem, hbm, rest, outs, scratch, norms=True):
+    sds = lambda *s: jax.ShapeDtypeStruct(*s)
+    plane = sds((PLANE // 2, ROOM, LINE), BF16)
+    rest = [sds((rest, LINE), F32)] if rest else []
+    common = [
         vmem((lines + 8, LINE), F32),
-        vmem((2, 9 * CH_MID, CH_MID), BF16),
-        vmem((2, EMB_DIM, EMB_DIM), BF16),
+        vmem((slots, 9 * CH_MID, CH_MID), BF16),
         vmem((3, PADDED, CH_MID), BF16),
         vmem((ROWS + 16, CH_MID), F32),
-        vmem((ROWS, CH_MID), F32),
-        vmem((CH_MID, ROWS), BF16),
     ]
-
-
-def plane_shapes():
-    pairs = PLANE // 2
-    return [
-        jax.ShapeDtypeStruct((2, pairs, ROOM, LINE), F32),
-        jax.ShapeDtypeStruct((2, pairs, ROOM, LINE), BF16),
+    if norms:
+        common += [vmem((ROWS, CH_MID), F32), vmem((CH_MID, ROWS), BF16)]
+    else:
+        common += [vmem((256, ROWS), BF16)]
+    common += [
+        vmem((PLANE, ROOM, LINE), BF16),
+        pltpu.SemaphoreType.DMA((2,)),
+        pltpu.SemaphoreType.DMA((3,)),
     ]
-
-
-def back_two_call(args):
-    sds = lambda *s: jax.ShapeDtypeStruct(*s)
-    act = sds((ROWS, CH_MID), F32)
-    scratch = back_scratch(ALL_LINES - SPLIT)
-    scratch[2] = vmem((EMB_DIM, EMB_DIM), BF16)
     return pl.pallas_call(
-        back_two_kernel,
-        out_shape=plane_shapes()
-        + [
-            sds((MIDDLE - SPLIT, LINE), F32),
-            act,
-            act,
-            sds((8, EMB_DIM), F32),
-            sds((8, CH_MID), F32),
-            sds((8, EMB_DIM), F32),
-        ],
-        in_specs=[SM] + [VM] * 17 + [HB] * 5,
-        out_specs=[HB] * 3 + [VM] * 5,
-        scratch_shapes=scratch
-        + [
-            vmem((ROWS, 3 * CH_MID), BF16),
-            vmem((8, EMB_DIM), F32),
-            vmem((PLANE, ROOM, LINE), BF16),
-            pltpu.SemaphoreType.DMA((2,)),
-            pltpu.SemaphoreType.DMA,
-            pltpu.SemaphoreType.DMA((3,)),
-        ],
-        name="back_two",
+        kernel,
+        out_shape=[plane, plane, *rest, *(sds(*o) for o in outs)],
+        in_specs=[SM] * smem + [VM] * (len(args) - smem - hbm) + [HB] * hbm,
+        out_specs=[HB] * (2 + len(rest)) + [VM] * len(outs),
+        scratch_shapes=common + scratch,
+        name=name,
         **kernel_params(),
     )(*args)
 
 
-def back_one_call(args):
-    return pl.pallas_call(
-        back_one_kernel,
-        out_shape=plane_shapes(),
-        in_specs=[SM] * 2 + [VM] * 13 + [HB] * 5,
-        out_specs=[HB] * 2,
-        scratch_shapes=back_scratch(MIDDLE)
-        + [
-            vmem((ROWS, CH_MID), F32),
-            vmem((256, ROWS), BF16),
-            vmem((8, EMB_DIM), F32),
-            vmem((PLANE, ROOM, LINE), BF16),
-            vmem((32, 2 * LINE), F32),
-            vmem((8, 2 * LINE), F32),
-            pltpu.SemaphoreType.DMA((2,)),
-            pltpu.SemaphoreType.DMA((2,)),
-            pltpu.SemaphoreType.DMA((3,)),
-        ],
-        name="back_one",
-        **kernel_params(),
-    )(*args)
+ACT = ((ROWS, CH_MID), F32)
+WIDE_ROW = ((8, EMB_DIM), F32)
+DMA = pltpu.SemaphoreType.DMA
+
+
+def back_top(args):
+    scratch = [vmem((EMB_DIM, EMB_DIM), BF16), vmem((ROWS, 3 * CH_MID), BF16), vmem(*WIDE_ROW), DMA]
+    lines = ALL_LINES - BASE_ONE
+    return back_call(
+        back_top_kernel, "back_top", lines, 2, args, 1, 4, PLANES[3] - BASE_ONE, [ACT, WIDE_ROW], scratch
+    )
+
+
+def back_second_half(args):
+    outs = [ACT, WIDE_ROW, ((8, CH_MID), F32)]
+    lines = PLANES[3] - BASE_TWO
+    return back_call(back_second_half_kernel, "back_b", lines, 1, args, 1, 2, PLANES[2] - BASE_TWO, outs, [DMA])
+
+
+def back_first_half(args):
+    scratch = [vmem((EMB_DIM, EMB_DIM), BF16), DMA, DMA]
+    lines = PLANES[2] - BASE_THREE
+    return back_call(
+        back_first_half_kernel, "back_c", lines, 1, args, 1, 3, PLANES[1] - BASE_THREE, [ACT, WIDE_ROW], scratch
+    )
+
+
+def back_low(args):
+    scratch = [
+        vmem((EMB_DIM, EMB_DIM), BF16),
+        vmem(*WIDE_ROW),
+        vmem((32, 2 * LINE), F32),
+        vmem((8, 2 * LINE), F32),
+        DMA,
+        DMA,
+    ]
+    return back_call(back_low_kernel, "back_low", PLANES[1], 1, args, 2, 3, 0, [], scratch, False)
 
 
 def karras(index):
@@ -1186,7 +1218,7 @@
     return values
 
 
-CUTS = (0, 864, 1728, ROOM)
+CUTS = (0, 880, 1760, ROOM)
 TALL = SHARDS // PLANE
 
 
@@ -1222,59 +1254,27 @@
     return jnp.stack(rows)
 
 
-def column_one(own):
-    return climb(own, 1, 1), climb(own, -1, 1)
-
-
-def column_two(own, one):
-    below, above = one
-    return climb(below, 1, 1, 1), climb(above, -1, 1, 1), climb(own, 1, 3), climb(own, -1, 3)
-
-
-def column_all(own, one, two, z):
-    return column_window([two[2], two[0], one[0], own, one[1], two[1], two[3]], z)
-
-
-def gather_both(online, target, z, early):
-    ab_o, ab_t = online[: CUTS[2]], target[: CUTS[2]]
-    c_own = jnp.stack([online[CUTS[2] :], target[CUTS[2] :]])
-    one = column_one(ab_o)
-    c_two = jnp.stack([c_own, swap(c_own, SOUTH)])
+def column_gather(own, z):
+    below, above = [climb(own, 1, 1)], [climb(own, -1, 1)]
+    for step in range(1, TALL - 1):
+        below.append(climb(below[-1], 1, 1, step))
+        above.append(climb(above[-1], -1, 1, step))
+    return column_window([*below[::-1], own, *above], z), [below[0], above[0]], [below[-1], above[-1]]
+
+
+def gather_lines(shard, z, early):
+    ab, c = shard[: CUTS[2]], shard[CUTS[2] :]
+    c_two = jnp.stack([c, swap(c, SOUTH)])
     c_four = jnp.concatenate([c_two, swap(c_two, EAST)])
-    two = column_two(ab_o, one)
-    column = column_all(ab_o, one, two, z)
+    column, step, last = column_gather(ab, z)
     za, zb = column[:, : CUTS[1]], column[:, CUTS[1] :]
-    done = early([two[0][:16], two[1][:16]])
+    done, ready = early(step)
     a_two, b_two = jnp.stack([za, swap(za, EAST)]), jnp.stack([zb, swap(zb, SOUTH)])
     a_far, b_far = swap(a_two, SOUTH), swap(b_two, EAST)
-    (ab_t,) = gate([ab_t], two)
-    one = column_one(ab_t)
-    two = column_two(ab_t, one)
-    column = column_all(ab_t, one, two, z)
-    za, zb = column[:, : CUTS[1]], column[:, CUTS[1] :]
-    co_four, ct_four = c_four[:, 0], c_four[:, 1]
-    (co_four,) = gate([co_four], two)
-    c_one = column_one(co_four)
-    c_next = column_two(co_four, c_one)
-    c_all = column_all(co_four, c_one, c_next, z)
-    first = [a_two, a_far, b_two, b_far, c_all]
-    first = first + [swap(v, CORE) for v in first]
-    za, zb = gate([za, zb], [a_far, b_far])
-    a_east, b_south = swap(za, EAST), swap(zb, SOUTH)
-    at_two, bt_two = jnp.stack([za, a_east]), jnp.stack([zb, b_south])
-    (ct_four,) = gate([ct_four], c_next)
-    ct_one = column_one(ct_four)
-    ct_next = column_two(ct_four, ct_one)
-    at_far, bt_far = swap(at_two, SOUTH), swap(bt_two, EAST)
-    at_core, bt_core = swap(at_two, CORE), swap(bt_two, CORE)
-
-    def second(model):
-        af, bf, c0, c1, c2, c3 = gate([at_far, bt_far, *ct_next], [model])
-        ct_all = column_all(ct_four, ct_one, (c0, c1, c2, c3), z)
-        rest = [swap(v, CORE) for v in (af, bf, ct_all)]
-        return [at_two, af, bt_two, bf, ct_all, at_core, rest[0], bt_core, rest[1], rest[2]]
-
-    return done, first, [a_east, b_south, *ct_one], second
+    (c_four,) = gate([c_four], [*last, *ready])
+    c_all, _, _ = column_gather(c_four, z)
+    pieces = [a_two, a_far, b_two, b_far, c_all]
+    return done, pieces + [swap(v, CORE) for v in pieces]
 
 
 def gather_moves():
@@ -1290,42 +1290,64 @@
 
 
 def gather_plain(shard):
-    lines = lax.all_gather(shard, AXIS, axis=0, tiled=True).reshape(SHARDS // PLANE, PLANE, SHARD, LINE)
-    lines = jnp.pad(lines, ((0, 0), (0, 0), (0, ROOM - SHARD), (0, 0)))
+    rows = shard.shape[0]
+    lines = lax.all_gather(shard, AXIS, axis=0, tiled=True)
+    if rows != ROOM:
+        lines = jnp.pad(lines.reshape(SHARDS, SHARD, LINE), ((0, 0), (0, ROOM - SHARD), (0, 0)))
+    lines = lines.reshape(TALL, PLANE, ROOM, LINE)
     return [lines], [(0, r, r, 0, ROOM) for r in range(PLANE)], (True,)
 
 
-def reduce_planes(keep, send):
-    planes = keep.shape[0]
-    got = swap(send, CORE)
-    low = lambda v: v.astype(BF16)
-    wide = lambda v: v.astype(F32)
-    a, b = slice(0, CUT_ROWS), slice(CUT_ROWS, ROOM)
-    quarter = lambda i, rows: keep[:, i, rows] + wide(got[:, i, rows])
-    send_a = low(jnp.stack([quarter(1, a), quarter(3, a)], 1))
-    send_b = low(jnp.stack([quarter(2, b), quarter(3, b)], 1))
-    got_a, got_b = swap(send_a, EAST), swap(send_b, SOUTH)
-    last_a = low(quarter(2, a) + wide(got_a[:, 1]))
-    last_b = low(quarter(1, b) + wide(got_b[:, 1]))
-    end_a, end_b = swap(last_a, SOUTH), swap(last_b, EAST)
-    sum_a = quarter(0, a) + wide(got_a[:, 0]) + wide(end_a)
-    sum_b = quarter(0, b) + wide(got_b[:, 0]) + wide(end_b)
-    return jnp.concatenate([sum_a, sum_b], 1)
-
-
-def reduce_column(part, z):
-    planes = part.shape[0]
-    pick = lambda p: lax.dynamic_index_in_dim(part, jnp.clip(p, 0, planes - 1), 0, keepdims=False)
-    total = pick(z)
+def low(v):
+    return v.astype(BF16)
+
+
+def wide(v):
+    return v.astype(F32)
+
+
+class PlaneSum:
+    def __init__(self, keep, send):
+        self.keep, self.got = keep, swap(send, CORE)
+        self.a, self.b = slice(0, CUT_ROWS), slice(CUT_ROWS, ROOM)
+
+    def quarter(self, i, rows):
+        return wide(self.keep[i, rows]) + wide(self.got[i, rows])
+
+    def first(self):
+        a = low(jnp.stack([self.quarter(1, self.a), self.quarter(3, self.a)]))
+        b = low(jnp.stack([self.quarter(2, self.b), self.quarter(3, self.b)]))
+        return a, b
+
+    def send_first(self, a, b):
+        self.got_a, self.got_b = swap(a, EAST), swap(b, SOUTH)
+
+    def last(self):
+        return low(self.quarter(2, self.a) + wide(self.got_a[1])), low(self.quarter(1, self.b) + wide(self.got_b[1]))
+
+    def send_last(self, a, b):
+        self.end_a, self.end_b = swap(a, SOUTH), swap(b, EAST)
+
+    def total(self):
+        a = self.quarter(0, self.a) + wide(self.got_a[0]) + wide(self.end_a)
+        b = self.quarter(0, self.b) + wide(self.got_b[0]) + wide(self.end_b)
+        return jnp.concatenate([a, b])
+
+
+def column_sums(parts, first, z):
+    pick = lambda p: jnp.where(p == first, parts[0], parts[1])
+    total = 0.0
     for way in (1, -1):
         run = None
-        for far in range(planes - 1, 0, -1):
+        for far in range(TALL - 1, 0, -1):
+            holders = [q for q in range(TALL) if q + way * far in (first, first + 1)]
+            if not holders:
+                continue
             value = pick(z + way * far)
             if run is not None:
                 value = value + run
-            holders = [q for q in range(planes) if 0 <= q + way * far < planes]
             pairs = [(q * PLANE + i, (q + way) * PLANE + i) for q in holders for i in range(PLANE)]
-            run = lax.ppermute(value.astype(BF16), AXIS, pairs).astype(F32)
+            run = wide(lax.ppermute(low(value), AXIS, pairs))
         total = total + run
     return total
 
@@ -1340,6 +1362,9 @@
     live = (jnp.arange(MB_DEV) < counts[0]).astype(jnp.int32)
     local_rows = jnp.sum(live * jnp.clip(valid_rows, 0, RES)).astype(F32)
 
+    total = total_of(jnp.broadcast_to(local_rows, (8, LINE)), n)
+    pixel_total = 3.0 * RES * total[0, 0]
+
     def early(after):
         clean, noise = gate([images, noise_draws], after) if after else (images, noise_draws)
         clean, noise = pixels(jnp.stack([clean, noise]))
@@ -1352,24 +1377,19 @@
             return per_row(skip) * noisy, x_in, noise_features(sigma), per_row(out_scale)
 
         mask = pixel_live(counts, valid_rows)
-        return inputs_of(karras(step_index)), inputs_of(karras(step_index + 1)), mask
-
-    total = total_of(jnp.broadcast_to(local_rows, (8, LINE)), n)
-    pixel_total = 3.0 * RES * total[0, 0]
+        both = inputs_of(karras(step_index)), inputs_of(karras(step_index + 1))
+        return (*both, mask), [v for part in both for v in part[:3]] + [mask, total]
+
     if direct:
         rooms = [jnp.pad(v, ((0, ROOM - SHARD), (0, 0))) for v in shards]
-        (in_lo, in_hi, mask), pieces, before, second = gather_both(rooms[0], rooms[1], z, early)
-        moves, flip = gather_moves(), (False,) * 4 + (True,) + (False,) * 4 + (True,)
-        online = (pieces, moves, flip)
-        (x_in,) = gate([in_hi[1]], [*before, in_lo[0], in_lo[1], in_lo[2], in_hi[0], in_hi[2], total])
-        in_hi = (in_hi[0], x_in, *in_hi[2:])
+        target = gather_plain(rooms[1])
+        (in_lo, in_hi, mask), pieces = gather_lines(rooms[0], z, early)
+        online = (pieces, gather_moves(), (False,) * 4 + (True,) + (False,) * 4 + (True,))
     else:
         online, target = gather_plain(shards[0]), gather_plain(shards[1])
-        in_lo, in_hi, mask = early(())
+        in_lo, in_hi, mask = early(())[0]
     model_o, saved = per_part(me, labels, online, in_hi, True, tables)
-    if direct:
-        target = (second(model_o), moves, flip)
-    model_t, _ = per_part(me, labels, target, in_lo, False, tables)
+    model_t, _ = per_part(jnp.zeros_like(me), labels, target, in_lo, False, tables)
     online_out = in_hi[0] + in_hi[3] * model_o[:, :12]
     target_out = in_lo[0] + in_lo[3] * model_t[:, :12]
     phi, out_scale = in_hi[2], in_hi[3]
@@ -1381,25 +1401,52 @@
     s_time, s_emb1, s_emb2, s_down, s11, s12, s_attn, s21, s22 = saved[15:]
     gm = tables[0]
     df = jnp.pad(grad_model, ((0, 0), (0, LINE - 12)))
-    keep_top, send_top, rest, dh, du, dm, extra, dse = back_two_call(
-        (me, df, wz, *tables[:5], vec, mod, emb, h4, u2, h3, qkv, mixed, h2, u1, s22, s21, s_attn, s12, s_emb2)
+    small = jnp.concatenate([local_loss[None], bias_out])
+    small = jnp.broadcast_to(small, (8, 4))
+    keep3, send3, rest, dh, dse = back_top(
+        (me, df, wz, *tables[:5], vec, mod, emb, h4, u2, h3, qkv, mixed, h2, s22, s21, s_attn, s_emb2)
     )
-    keep_low, send_low = back_one_call(
-        (me, labels, dh, du, dm, extra, dse, gm, vec, emb, pre, phi, h1, h0s, xp, s11, s_down, s_emb1, s_time, rest)
-    )
-    small = jnp.concatenate([local_loss[None], bias_out])
-    small = total_of(jnp.broadcast_to(small, (8, 4)), n)[0]
     if direct:
-        part = jnp.concatenate([reduce_planes(keep_low, send_low), reduce_planes(keep_top, send_top)])
-        reduced = reduce_column(part, z)[:SHARD].reshape(-1)
+        three = PlaneSum(keep3, send3)
+    keep2, send2, rest, du, dm, extra = back_second_half((me, dh, gm, vec, mod, u1, s12, rest))
+    if direct:
+        first3 = three.first()
+        (du,) = gate([du], first3)
+        three.send_first(*first3)
+        two = PlaneSum(keep2, send2)
+    keep1, send1, rest, dh, dse = back_first_half((me, dh, du, dm, extra, dse, gm, vec, emb, h1, s11, s_emb1, rest))
+    if direct:
+        last3, first2 = three.last(), two.first()
+        (dh,) = gate([dh], [*last3, *first2])
+        three.send_last(*last3)
+        two.send_first(*first2)
+        one = PlaneSum(keep1, send1)
+    keep0, send0 = back_low((me, labels, dh, dse, emb, pre, phi, h0s, xp, s_down, s_time, rest))
+    if direct:
+        zero = PlaneSum(keep0, send0)
+        one.send_first(*one.first())
+        two.send_last(*two.last())
+        first0 = zero.first()
+        zero.send_first(*first0)
+        (small,) = gate([small], first0)
+        small = total_of(small, n)
+        top = [two.total(), three.total()]
+        high = column_sums(top, 2, z)
+        one.send_last(*one.last())
+        zero.send_last(*zero.last())
+        bottom = gate([zero.total(), one.total()], [small])
+        reduced = column_sums(bottom, 0, z) + high
+        own = jnp.where(z < 2, jnp.where(z == 0, bottom[0], bottom[1]), jnp.where(z == 2, top[0], top[1]))
+        reduced = (reduced + own)[:SHARD].reshape(-1)
     else:
-        both = [jnp.stack([k, s.astype(F32)], 2) for k, s in ((keep_low, send_low), (keep_top, send_top))]
-        lines = jnp.concatenate(both).reshape(SHARDS, ROOM, LINE)[:, :SHARD].reshape(n, -1)
+        small = total_of(small, n)
+        both = [jnp.stack([wide(k), wide(s)], 1) for k, s in ((keep0, send0), (keep1, send1), (keep2, send2), (keep3, send3))]
+        lines = jnp.stack(both).reshape(SHARDS, ROOM, LINE)[:, :SHARD].reshape(n, -1)
         reduced = lax.psum_scatter(lines, AXIS, scatter_dimension=0, tiled=True).reshape(-1)
     new_momentum = MOMENTUM * momentum + reduced
     new_master = master - LEARN_RATE * (reduced + MOMENTUM * new_momentum)
     new_ema = EMA_DECAY * ema + (1.0 - EMA_DECAY) * new_master
-    return (small[0] / pixel_total, new_momentum, new_master, new_ema, small[1:])
+    return (small[0, 0] / pixel_total, new_momentum, new_master, new_ema, small[0, 1:])
 
 
 def solution(mesh):

time: 574 us -> 528 us (0.920)
  starting transfers between devices: 127 us -> 75 us
  between operations: 5.76 us -> 19.3 us
  local copies, waits for them, and re-layouts: 36.7 us -> 24.6 us
  Pallas kernels: 167 us -> 179 us
  waiting for transfers between devices: 167 us -> 161 us
    ppermute x24 -> x12, waiting for transfers between devices: 27.4 us -> 100 us  [climb(): return lax.ppermute(values, AXIS, pairs)]
    ppermute x30 -> x31, waiting for transfers between devices: 99.8 us -> 31.1 us  [swap(): return lax.ppermute(values, AXIS, [(i, i ^ hop) for i in range(SHARDS)])]
    ppermute x24 -> x12, starting transfers between devices: 62.9 us -> 17.7 us  [climb(): return lax.ppermute(values, AXIS, pairs)]
    ppermute x6 -> x8, waiting for transfers between devices: 27.7 us -> 14.8 us  [column_sums(): run = wide(lax.ppermute(low(value), AXIS, pairs))]
    pallas_call x2 -> x4, Pallas kernels: 73.7 us -> 86.3 us  [back_call(): pl.pallas_call(kernel, out_shape=[plane, plane, *rest, *(sds(*o) for o in...]
    ppermute x10, starting transfers between devices: 20.5 us -> 9.82 us  [total_of(): lax.ppermute(values, AXIS, [(i, i ^ hop) for i in range(n)])]
    another operation x8 -> x4, other arithmetic: 12 us -> 2.26 us  [column_window(): return jnp.stack(rows)]
    convert_element_type x6 -> x12, other arithmetic: 12.2 us -> 17 us  [the longest x10 13.1 us: low(): return v.astype(BF16)]
  transfers between devices with their start and end apart: 70 -> 62, of which waited for: 33 -> 27; matrix products, arithmetic and copies ran while one was open for 12% -> 13% of each run, Pallas kernels for 9% -> 18%
where the time goes in v3:
time: 528 us; the launch traced here: 519 us
  Pallas kernels  179 us (34%)
  waiting for transfers between devices  161 us (30%)
  starting transfers between devices  75 us (14%)
  other arithmetic  60.9 us (12%)
  local copies, waits for them, and re-layouts  24.6 us (5%)
  between operations  19.3 us (4%)
    ppermute x12, waiting for transfers between devices, climb(): return lax.ppermute(values, AXIS, pairs)  100 us
    pallas_call x2, Pallas kernels, forward_call(): pl.pallas_call(body, out_shape=outs, in_specs=[SM] * 2 + [VM] * 8 + [HB]...  92.7 us
    pallas_call x4, Pallas kernels, back_call(): pl.pallas_call(kernel, out_shape=[plane, plane, *rest, *(sds(*o) for o in...  86.3 us
    ppermute x31, waiting for transfers between devices, swap(): return lax.ppermute(values, AXIS, [(i, i ^ hop) for i in range(SHARDS)])  31.1 us
    ppermute x31, starting transfers between devices, swap(): return lax.ppermute(values, AXIS, [(i, i ^ hop) for i in range(SHARDS)])  29.2 us
    ppermute x8, starting transfers between devices, column_sums(): run = wide(lax.ppermute(low(value), AXIS, pairs))  18.2 us
    ppermute x12, starting transfers between devices, climb(): return lax.ppermute(values, AXIS, pairs)  17.7 us
    ppermute x8, waiting for transfers between devices, column_sums(): run = wide(lax.ppermute(low(value), AXIS, pairs))  14.8 us
  transfers between devices with their start and end apart: 62, of which 27 were waited for; matrix products, arithmetic and copies ran while one was open for 13% of the time, Pallas kernels for 18%

profile of v3, /device:TPU:0, one launch (start us, length us, event | category | flops | bytes accessed | tf_op | source)
XLA Modules:
  0.0 519.2 jit_solution(4612459633936943259)
XLA Ops:
  10.1 5.0 collective-permute-start
  28.6 7.5 %collective-permute-done.1.refs_3_ = bf16[1760,128]{1,0:T(8,128)(2,1)S(1)} collective-permute-done((bf16[1760,128]{1,0:T(8,128)(2,1)S(1)}, bf16[1760,128]{1,0:T(8,128)(2,1)S(1)}, u32[]{:S(2)}, u32[]{:S(2)}) %collective-permute-start.1) | collective-permute-done | bytes 450592 | tf_op jit(solution)/shard_map/ppermute | solution.py:1244
  44.4 6.6 %collective-permute-done.4 = bf16[1760,128]{1,0:T(8,128)(2,1)} collective-permute-done((bf16[1760,128]{1,0:T(8,128)(2,1)S(1)}, bf16[1760,128]{1,0:T(8,128)(2,1)}, u32[]{:S(2)}, u32[]{:S(2)}) %collective-permute-start.4) | collective-permute-done | bytes 450592 | tf_op jit(solution)/shard_map/ppermute | solution.py:1244
  69.3 16.3 %collective-permute-done.5.refs_2_ = bf16[1760,128]{1,0:T(8,128)(2,1)S(1)} collective-permute-done((bf16[1760,128]{1,0:T(8,128)(2,1)}, bf16[1760,128]{1,0:T(8,128)(2,1)S(1)}, u32[]{:S(2)}, u32[]{:S(2)}) %collective-permute-start.5) | collective-permute-done | bytes 450592 | tf_op jit(solution)/shard_map/ppermute | solution.py:1244
  98.3 21.7 %collective-permute-done.17 = bf16[4,512,128]{2,1,0:T(8,128)(2,1)S(1)} collective-permute-done((bf16[4,512,128]{2,1,0:T(8,128)(2,1)}, bf16[4,512,128]{2,1,0:T(8,128)(2,1)S(1)}, u32[]{:S(2)}, u32[]{:S(2)}) %collective-permute-start.17) | collective-permute-done | bytes 524320 | tf_op jit(solution)/shard_map/ppermute | solution.py:1244
  120.7 12.0 %collective-permute-done.20 = bf16[4,512,128]{2,1,0:T(8,128)(2,1)S(1)} collective-permute-done((bf16[4,512,128]{2,1,0:T(8,128)(2,1)}, bf16[4,512,128]{2,1,0:T(8,128)(2,1)S(1)}, u32[]{:S(2)}, u32[]{:S(2)}) %collective-permute-start.20) | collective-permute-done | bytes 524320 | tf_op jit(solution)/shard_map/ppermute | solution.py:1244
  142.1 14.7 %collective-permute-done.21 = bf16[4,512,128]{2,1,0:T(8,128)(2,1)S(1)} collective-permute-done((bf16[4,512,128]{2,1,0:T(8,128)(2,1)S(1)}, bf16[4,512,128]{2,1,0:T(8,128)(2,1)S(1)}, u32[]{:S(2)}, u32[]{:S(2)}) %collective-permute-start.21) | collective-permute-done | bytes 524320 | tf_op jit(solution)/shard_map/ppermute | solution.py:1244
  158.1 20.8 %collective-permute-done.22 = bf16[4,512,128]{2,1,0:T(8,128)(2,1)S(1)} collective-permute-done((bf16[4,512,128]{2,1,0:T(8,128)(2,1)S(1)}, bf16[4,512,128]{2,1,0:T(8,128)(2,1)S(1)}, u32[]{:S(2)}, u32[]{:S(2)}) %collective-permute-start.22) | collective-permute-done | bytes 524320 | tf_op jit(solution)/shard_map/ppermute | solution.py:1244
  180.1 4.0 collective-permute-done.7.refs_11_
  194.3 48.1 %forward_save.1 = (f32[512,128]{1,0:T(8,128)}, bf16[2048,256]{1,0:T(8,128)(2,1)}, f32[512,384]{1,0:T(8,128)}, f32[512,384]{1,0:T(8,128)}, f32[512,384]{1,0:T(8,1...) custom-call(s32[1]{0:T(128)} %bitcast.7.refs_0_, ...), custom_call_target="tpu_custom_call" | custom-call | flops 8000000000 | bytes 40000000 | tf_op jit(solution)/shard_map/forward_save/pallas_call | solution.py:700
  242.6 44.6 %forward_plain.1 = f32[512,128]{1,0:T(8,128)} custom-call(s32[1]{0:T(128)} %constant.137.clone.1.refs_0_, s32[2]{0:T(128)} %refs_1_.6, bf16[512,128]{1,0:T(8,128)(2,1)} %pad.28.refs_4_.refs_2_, f32[8,192]{1,0:T(8,128)} %select_maximum_fusion.refs_5_.refs_3_, bf16[384,384]{1,0:T(8,128)(2,1)} %constant.145.clone.refs_4_.refs_3_.refs_2_.refs_6_, ...), custom_call_target="tpu_custom_call" | custom-call | flops 8000000000 | bytes 40000000 | tf_op jit(solution)/shard_map/forward_plain/pallas_call | solution.py:700
  287.3 3.6 select_reduce_fusion
  293.5 42.4 %back_top.1 = (bf16[4,2272,128]{2,1,0:T(8,128)(2,1)}, bf16[4,2272,128]{2,1,0:T(8,128)(2,1)}, f32[11968,128]{1,0:T(8,128)}, f32[512,384]{1,0:T(8,128)}, f32[8,768]{1,0:T(8,128)}) custom-call(s32[1]{0:T(128)} %bitcast.7.refs_0_, f32[512,128]{1,0:T(8,128)} %pad.31.refs_1_, bf16[128,384]{1,0:T(8,128)(2,1)} %get-tuple-element.55.refs_2_, ...), custom_call_target="tpu_custom_call" | custom-call | flops 8000000000 | bytes 40000000 | tf_op jit(solution)/shard_map/back_top/pallas_call | solution.py:1112
  336.1 17.0 %back_b.1 = (bf16[4,2272,128]{2,1,0:T(8,128)(2,1)}, bf16[4,2272,128]{2,1,0:T(8,128)(2,1)}, f32[4240,128]{1,0:T(8,128)}, f32[512,384]{1,0:T(8,128)}, f32[8,768]{1,0:T(8,128)}, /*index=5*/f32[8,384]{1,0:T(8,128)}) custom-call(s32[1]{0:T(128)} %bitcast.7.refs_0_, f32[512,384]{1,0:T(8,128)} %get-tuple-element.69.refs_1_, ...), custom_call_target="tpu_custom_call" | custom-call | flops 8000000000 | bytes 40000000 | tf_op jit(solution)/shard_map/back_b/pallas_call | solution.py:1112
  364.0 16.1 %back_c.1 = (bf16[4,2272,128]{2,1,0:T(8,128)(2,1)}, bf16[4,2272,128]{2,1,0:T(8,128)(2,1)}, f32[1120,128]{1,0:T(8,128)}, f32[512,384]{1,0:T(8,128)}, f32[8,768]{1,0:T(8,128)}) custom-call(s32[1]{0:T(128)} %bitcast.7.refs_0_, f32[512,384]{1,0:T(8,128)} %get-tuple-element.69.refs_1_, f32[512,384]{1,0:T(8,128)} %gate.8.refs_2_, ...), custom_call_target="tpu_custom_call" | custom-call | flops 8000000000 | bytes 40000000 | tf_op jit(solution)/shard_map/back_c/pallas_call | solution.py:1112
  386.2 10.9 %back_low.1 = (bf16[4,2272,128]{2,1,0:T(8,128)(2,1)}, bf16[4,2272,128]{2,1,0:T(8,128)(2,1)}) custom-call(s32[1]{0:T(128)} %bitcast.7.refs_0_, s32[2]{0:T(128)} %refs_1_.6, f32[512,384]{1,0:T(8,128)} %gate.9.refs_2_, f32[8,768]{1,0:T(8,128)} %get-tuple-element.86.refs_3_, f32[8,768]{1,0:T(8,128)} %get-tuple-element.58.refs_10_.refs_8_.refs_4_, ...), custom_call_target="tpu_custom_call" | custom-call | flops 8000000000 | bytes 40000000 | tf_op jit(solution)/shard_map/back_low/pallas_call | solution.py:1112
  401.1 7.1 %collective-permute-done.54 = bf16[1136,128]{1,0:T(8,128)(2,1)S(1)} collective-permute-done((bf16[1136,128]{1,0:T(8,128)(2,1)S(1)}, bf16[1136,128]{1,0:T(8,128)(2,1)S(1)}, u32[]{:S(2)}, u32[]{:S(2)}) %collective-permute-start.54) | collective-permute-done | bytes 290848 | tf_op jit(solution)/shard_map/ppermute | solution.py:1210
  423.8 5.4 %collective-permute-done.43 = bf16[2,1136,128]{2,1,0:T(8,128)(2,1)} collective-permute-done((bf16[2,1136,128]{2,1,0:T(8,128)(2,1)}, bf16[2,1136,128]{2,1,0:T(8,128)(2,1)}, u32[]{:S(2)}, u32[]{:S(2)}) %collective-permute-start.43) | collective-permute-done | bytes 581664 | tf_op jit(solution)/shard_map/ppermute | solution.py:1210
  433.4 6.9 %collective-permute-done.34 = f32[8,4]{1,0:T(8,128)S(1)} collective-permute-done((f32[8,4]{1,0:T(8,128)S(1)}, f32[8,4]{1,0:T(8,128)S(1)}, u32[]{:S(2)}, u32[]{:S(2)}) %collective-permute-start.34) | collective-permute-done | bytes 160 | tf_op jit(solution)/shard_map/ppermute | solution.py:1216
  462.0 3.9 collective-permute-done.39
  474.5 6.5 %collective-permute-done.58 = bf16[2272,128]{1,0:T(8,128)(2,1)S(1)} collective-permute-done((bf16[2272,128]{1,0:T(8,128)(2,1)S(1)}, bf16[2272,128]{1,0:T(8,128)(2,1)S(1)}, u32[]{:S(2)}, u32[]{:S(2)}) %collective-permute-start.58) | collective-permute-done | bytes 581664 | tf_op jit(solution)/shard_map/ppermute | solution.py:1350
  483.5 8.3 %collective-permute-start.47 = (bf16[2272,128]{1,0:T(8,128)(2,1)}, bf16[2272,128]{1,0:T(8,128)(2,1)}, u32[]{:S(2)}, u32[]{:S(2)}) collective-permute-start(bf16[2272,128]{1,0:T(8,128)(2,1)} %get-tuple-element.142), channel_id=1, source_target_pairs={{0,8},{1,9},{2,10},{3,11},{4,12},{5,13},{6,14},{7,15}} | collective-permute-start | bytes 1744904 | tf_op jit(solution)/shard_map/ppermute | solution.py:1350
  498.6 6.8 %collective-permute-done.50 = bf16[2272,128]{1,0:T(8,128)(2,1)} collective-permute-done((bf16[2272,128]{1,0:T(8,128)(2,1)}, bf16[2272,128]{1,0:T(8,128)(2,1)}, u32[]{:S(2)}, u32[]{:S(2)}) %collective-permute-start.50) | collective-permute-done | bytes 581664 | tf_op jit(solution)/shard_map/ppermute | solution.py:1350
  505.4 5.4 %multiply_add_fusion = (f32[289792]{0:T(1024)}, f32[289792]{0:T(1024)}, f32[289792]{0:T(1024)}) fusion(f32[289792]{0:T(1024)} %param.23, f32[289792]{0:T(1024)} %param.21, f32[289792]{0:T(1024)} %param.22, f32[1136,128]{1,0:T(8,128)S(1)} %get-tuple-element.126, f32[1136,128]{1,0:T(8,128)S(1)} %get-tuple-element.127, f32[1136,128]{1,0:T(8,128)} %copy-done.2, ...), kind=kLoop, calls=%fused_computation.27 | loop fusion | flops 6375424 | bytes 13918211 | tf_op jit(solution)/shard_map/add | solution.py:1448
  (326 shorter events, 158.3 us)
Async XLA Ops:
  7.2 235.3 %all-gather.2.cloned.1.call-start = ((), (), s32[]{:S(2)}) async-start(), calls=%async_computation | async-start | bytes 19193856 | tf_op jit(solution)/shard_map/all_gather | solution.py:1294
  15.1 21.0 %collective-permute-start.1 = (bf16[1760,128]{1,0:T(8,128)(2,1)S(1)}, bf16[1760,128]{1,0:T(8,128)(2,1)S(1)}, u32[]{:S(2)}, u32[]{:S(2)}) collective-permute-start(bf16[1760,128]{1,0:T(8,128)(2,1)S(1)} %slice_bitcast_fusion), channel_id=1, source_target_pairs={{24,16},{25,17},{26,18},{27,19},{28,20},{29,21},{30,22},{31,23},{1... | collective-permute-start | bytes 1351688 | tf_op jit(solution)/shard_map/ppermute | solution.py:1244
  18.5 20.5 %collective-permute-start.10 = (bf16[512,128]{1,0:T(8,128)(2,1)S(1)}, bf16[512,128]{1,0:T(8,128)(2,1)S(1)}, u32[]{:S(2)}, u32[]{:S(2)}) collective-permute-start(bf16[512,128]{1,0:T(8,128)(2,1)S(1)} %get-tuple-element.159), channel_id=1, source_target_pairs={{0,4},{1,5},{2,6},{3,7},{4,0},{5,1},{6,2},{7,3},{8,12},{9,13},{10,... | collective-permute-start | bytes 393224 | tf_op jit(solution)/shard_map/ppermute | solution.py:1210
  39.1 23.8 %collective-permute-start.11 = (bf16[2,512,128]{2,1,0:T(8,128)(2,1)S(1)}, bf16[2,512,128]{2,1,0:T(8,128)(2,1)S(1)}, u32[]{:S(2)}, u32[]{:S(2)}) collective-permute-start(bf16[2,512,128]{2,1,0:T(8,128)(2,1)S(1)} %pad_maximum_fusion.17), channel_id=1, source_target_pairs={{0,2},{1,3},{2,0},{3,1},{4,6},{5,7},{6,4},{7,5},{8,10},{9,11},{10,... | collective-permute-start | bytes 786440 | tf_op jit(solution)/shard_map/ppermute | solution.py:1210
  43.8 25.5 %collective-permute-start.3 = (bf16[1760,128]{1,0:T(8,128)(2,1)}, bf16[1760,128]{1,0:T(8,128)(2,1)S(1)}, u32[]{:S(2)}, u32[]{:S(2)}) collective-permute-start(bf16[1760,128]{1,0:T(8,128)(2,1)} %collective-permute-done.2), channel_id=1, source_target_pairs={{16,24},{17,25},{18,26},{19,27},{20,28},{21,29},{22,30},{23,31}} | collective-permute-start | bytes 1351688 | tf_op jit(solution)/shard_map/ppermute | solution.py:1244
  51.0 34.6 %collective-permute-start.5 = (bf16[1760,128]{1,0:T(8,128)(2,1)}, bf16[1760,128]{1,0:T(8,128)(2,1)S(1)}, u32[]{:S(2)}, u32[]{:S(2)}) collective-permute-start(bf16[1760,128]{1,0:T(8,128)(2,1)} %collective-permute-done.4), channel_id=1, source_target_pairs={{8,0},{9,1},{10,2},{11,3},{12,4},{13,5},{14,6},{15,7}} | collective-permute-start | bytes 1351688 | tf_op jit(solution)/shard_map/ppermute | solution.py:1244
  89.1 44.8 %collective-permute-start.6 = (bf16[4,880,128]{2,1,0:T(8,128)(2,1)}, bf16[4,880,128]{2,1,0:T(8,128)(2,1)S(1)}, u32[]{:S(2)}, u32[]{:S(2)}) collective-permute-start(bf16[4,880,128]{2,1,0:T(8,128)(2,1)} %get-tuple-element.149), channel_id=1, source_target_pairs={{0,2},{1,3},{2,0},{3,1},{4,6},{5,7},{6,4},{7,5},{8,10},{9,11},{10,... | collective-permute-start | bytes 2703368 | tf_op jit(solution)/shard_map/ppermute | solution.py:1210
  91.1 45.7 %collective-permute-start.8 = (bf16[4,880,128]{2,1,0:T(8,128)(2,1)}, bf16[4,880,128]{2,1,0:T(8,128)(2,1)}, u32[]{:S(2)}, u32[]{:S(2)}) collective-permute-start(bf16[4,880,128]{2,1,0:T(8,128)(2,1)} %get-tuple-element.148), channel_id=1, source_target_pairs={{0,4},{1,5},{2,6},{3,7},{4,0},{5,1},{6,2},{7,3},{8,12},{9,13},{10,... | collective-permute-start | bytes 2703368 | tf_op jit(solution)/shard_map/ppermute | solution.py:1210
  95.4 24.6 %collective-permute-start.17 = (bf16[4,512,128]{2,1,0:T(8,128)(2,1)}, bf16[4,512,128]{2,1,0:T(8,128)(2,1)S(1)}, u32[]{:S(2)}, u32[]{:S(2)}) collective-permute-start(bf16[4,512,128]{2,1,0:T(8,128)(2,1)} %gate.7), channel_id=1, source_target_pairs={{0,8},{1,9},{2,10},{3,11},{4,12},{5,13},{6,14},{7,15},{8,16},{9,17... | collective-permute-start | bytes 1572872 | tf_op jit(solution)/shard_map/ppermute | solution.py:1244
  97.0 35.6 %collective-permute-start.20 = (bf16[4,512,128]{2,1,0:T(8,128)(2,1)}, bf16[4,512,128]{2,1,0:T(8,128)(2,1)S(1)}, u32[]{:S(2)}, u32[]{:S(2)}) collective-permute-start(bf16[4,512,128]{2,1,0:T(8,128)(2,1)} %gate.7), channel_id=1, source_target_pairs={{24,16},{25,17},{26,18},{27,19},{28,20},{29,21},{30,22},{31,23},{1... | collective-permute-start | bytes 1572872 | tf_op jit(solution)/shard_map/ppermute | solution.py:1244
  120.0 21.4 %collective-permute-start.18 = (bf16[4,512,128]{2,1,0:T(8,128)(2,1)S(1)}, bf16[4,512,128]{2,1,0:T(8,128)(2,1)S(1)}, u32[]{:S(2)}, u32[]{:S(2)}) collective-permute-start(bf16[4,512,128]{2,1,0:T(8,128)(2,1)S(1)} %collective-permute-done.17), channel_id=1, source_target_pairs={{8,16},{9,17},{10,18},{11,19},{12,20},{13,21},{14,22},{15,23},{16,... | collective-permute-start | bytes 1572872 | tf_op jit(solution)/shard_map/ppermute | solution.py:1244
  132.6 24.1 %collective-permute-start.21 = (bf16[4,512,128]{2,1,0:T(8,128)(2,1)S(1)}, bf16[4,512,128]{2,1,0:T(8,128)(2,1)S(1)}, u32[]{:S(2)}, u32[]{:S(2)}) collective-permute-start(bf16[4,512,128]{2,1,0:T(8,128)(2,1)S(1)} %collective-permute-done.20), channel_id=1, source_target_pairs={{16,8},{17,9},{18,10},{19,11},{20,12},{21,13},{22,14},{23,15},{8,0... | collective-permute-start | bytes 1572872 | tf_op jit(solution)/shard_map/ppermute | solution.py:1244
  135.3 48.8 %collective-permute-start.7 = (bf16[2,4,880,128]{3,2,1,0:T(8,128)(2,1)}, bf16[2,4,880,128]{3,2,1,0:T(8,128)(2,1)}, u32[]{:S(2)}, u32[]{:S(2)}) collective-permute-start(bf16[2,4,880,128]{3,2,1,0:T(8,128)(2,1)} %pad_maximum_fusion.2.refs_10_), channel_id=1, source_target_pairs={{0,4},{1,5},{2,6},{3,7},{4,0},{5,1},{6,2},{7,3},{8,12},{9,13},{10,... | collective-permute-start | bytes 5406728 | tf_op jit(solution)/shard_map/ppermute | solution.py:1210
  139.4 44.7 %collective-permute-start.9 = (bf16[2,4,880,128]{3,2,1,0:T(8,128)(2,1)}, bf16[2,4,880,128]{3,2,1,0:T(8,128)(2,1)}, u32[]{:S(2)}, u32[]{:S(2)}) collective-permute-start(bf16[2,4,880,128]{3,2,1,0:T(8,128)(2,1)} %pad_maximum_fusion.3.refs_12_), channel_id=1, source_target_pairs={{0,2},{1,3},{2,0},{3,1},{4,6},{5,7},{6,4},{7,5},{8,10},{9,11},{10,... | collective-permute-start | bytes 5406728 | tf_op jit(solution)/shard_map/ppermute | solution.py:1210
  156.8 22.1 %collective-permute-start.22 = (bf16[4,512,128]{2,1,0:T(8,128)(2,1)S(1)}, bf16[4,512,128]{2,1,0:T(8,128)(2,1)S(1)}, u32[]{:S(2)}, u32[]{:S(2)}) collective-permute-start(bf16[4,512,128]{2,1,0:T(8,128)(2,1)S(1)} %collective-permute-done.21), channel_id=1, source_target_pairs={{8,0},{9,1},{10,2},{11,3},{12,4},{13,5},{14,6},{15,7}} | collective-permute-start | bytes 1572872 | tf_op jit(solution)/shard_map/ppermute | solution.py:1244
  356.8 23.4 %collective-permute-start.30 = (bf16[2,1136,128]{2,1,0:T(8,128)(2,1)}, bf16[2,1136,128]{2,1,0:T(8,128)(2,1)}, u32[]{:S(2)}, u32[]{:S(2)}) collective-permute-start(bf16[2,1136,128]{2,1,0:T(8,128)(2,1)} %pad_maximum_fusion.9.refs_2_), channel_id=1, source_target_pairs={{0,4},{1,5},{2,6},{3,7},{4,0},{5,1},{6,2},{7,3},{8,12},{9,13},{10,... | collective-permute-start | bytes 1744904 | tf_op jit(solution)/shard_map/ppermute | solution.py:1210
  358.5 21.7 %collective-permute-start.29 = (bf16[2,1136,128]{2,1,0:T(8,128)(2,1)}, bf16[2,1136,128]{2,1,0:T(8,128)(2,1)}, u32[]{:S(2)}, u32[]{:S(2)}) collective-permute-start(bf16[2,1136,128]{2,1,0:T(8,128)(2,1)} %pad_maximum_fusion.8.refs_1_), channel_id=1, source_target_pairs={{0,2},{1,3},{2,0},{3,1},{4,6},{5,7},{6,4},{7,5},{8,10},{9,11},{10,... | collective-permute-start | bytes 1744904 | tf_op jit(solution)/shard_map/ppermute | solution.py:1210
  363.5 33.6 %collective-permute-start.53 = (bf16[2,1136,128]{2,1,0:T(8,128)(2,1)S(1)}, bf16[2,1136,128]{2,1,0:T(8,128)(2,1)}, u32[]{:S(2)}, u32[]{:S(2)}) collective-permute-start(bf16[2,1136,128]{2,1,0:T(8,128)(2,1)S(1)} %pad_maximum_fusion.11.refs_4_), channel_id=1, source_target_pairs={{0,4},{1,5},{2,6},{3,7},{4,0},{5,1},{6,2},{7,3},{8,12},{9,13},{10,... | collective-permute-start | bytes 1744904 | tf_op jit(solution)/shard_map/ppermute | solution.py:1210
  363.7 33.6 %collective-permute-start.51 = (bf16[2,1136,128]{2,1,0:T(8,128)(2,1)S(1)}, bf16[2,1136,128]{2,1,0:T(8,128)(2,1)}, u32[]{:S(2)}, u32[]{:S(2)}) collective-permute-start(bf16[2,1136,128]{2,1,0:T(8,128)(2,1)S(1)} %pad_maximum_fusion.10.refs_3_), channel_id=1, source_target_pairs={{0,2},{1,3},{2,0},{3,1},{4,6},{5,7},{6,4},{7,5},{8,10},{9,11},{10,... | collective-permute-start | bytes 1744904 | tf_op jit(solution)/shard_map/ppermute | solution.py:1210
  380.1 29.9 %collective-permute-start.42 = (bf16[4,2272,128]{2,1,0:T(8,128)(2,1)}, bf16[4,2272,128]{2,1,0:T(8,128)(2,1)}, u32[]{:S(2)}, u32[]{:S(2)}) collective-permute-start(bf16[4,2272,128]{2,1,0:T(8,128)(2,1)} %get-tuple-element.96), channel_id=1, source_target_pairs={{0,1},{1,0},{2,3},{3,2},{4,5},{5,4},{6,7},{7,6},{8,9},{9,8},{10,11... | collective-permute-start | bytes 6979592 | tf_op jit(solution)/shard_map/ppermute | solution.py:1210
  397.1 18.5 %collective-permute-start.32 = (bf16[4,2272,128]{2,1,0:T(8,128)(2,1)}, bf16[4,2272,128]{2,1,0:T(8,128)(2,1)S(1)}, u32[]{:S(2)}, u32[]{:S(2)}) collective-permute-start(bf16[4,2272,128]{2,1,0:T(8,128)(2,1)} %get-tuple-element.94), channel_id=1, source_target_pairs={{0,1},{1,0},{2,3},{3,2},{4,5},{5,4},{6,7},{7,6},{8,9},{9,8},{10,11... | collective-permute-start | bytes 6979592 | tf_op jit(solution)/shard_map/ppermute | solution.py:1210
  419.4 39.4 %collective-permute-start.38 = (bf16[2,1136,128]{2,1,0:T(8,128)(2,1)S(1)}, bf16[2,1136,128]{2,1,0:T(8,128)(2,1)S(1)}, u32[]{:S(2)}, u32[]{:S(2)}) collective-permute-start(bf16[2,1136,128]{2,1,0:T(8,128)(2,1)S(1)} %copy-done.19), channel_id=1, source_target_pairs={{0,2},{1,3},{2,0},{3,1},{4,6},{5,7},{6,4},{7,5},{8,10},{9,11},{10,... | collective-permute-start | bytes 1744904 | tf_op jit(solution)/shard_map/ppermute | solution.py:1210
  419.9 38.9 %collective-permute-start.40 = (bf16[2,1136,128]{2,1,0:T(8,128)(2,1)S(1)}, bf16[2,1136,128]{2,1,0:T(8,128)(2,1)S(1)}, u32[]{:S(2)}, u32[]{:S(2)}) collective-permute-start(bf16[2,1136,128]{2,1,0:T(8,128)(2,1)S(1)} %copy-done.20), channel_id=1, source_target_pairs={{0,4},{1,5},{2,6},{3,7},{4,0},{5,1},{6,2},{7,3},{8,12},{9,13},{10,... | collective-permute-start | bytes 1744904 | tf_op jit(solution)/shard_map/ppermute | solution.py:1210
  452.2 45.0 %collective-permute-start.60 = (bf16[2272,128]{1,0:T(8,128)(2,1)}, bf16[2272,128]{1,0:T(8,128)(2,1)}, u32[]{:S(2)}, u32[]{:S(2)}) collective-permute-start(bf16[2272,128]{1,0:T(8,128)(2,1)} %get-tuple-element.145), channel_id=1, source_target_pairs={{24,16},{25,17},{26,18},{27,19},{28,20},{29,21},{30,22},{31,23}} | collective-permute-start | bytes 1744904 | tf_op jit(solution)/shard_map/ppermute | solution.py:1350
  (91 other events, 1403.4 us)
Sparse Core Ops, SparseCore 0:
  10.9 165.6 all-gather.1

commit v4 on v3

--- a/solution.py
+++ b/solution.py
@@ -35,7 +35,7 @@
 PIX = HALF * HALF
 ROWS = MB_DEV * PIX
 GROUP_SIZE = PIX * (CH_MID // GROUPS)
-CHUNK = 64
+CHUNK = 128
 PADDED = 16 + MB_DEV * (PIX + 16)
 NN = (((1,), (0,)), ((), ()))
 NT = (((1,), (1,)), ((), ()))
@@ -213,19 +213,29 @@
     return jnp.broadcast_to(v, (8, v.shape[1]))
 
 
-def group_mean(v, gm_ref):
-    return dot3(eight(v), gm_ref[...])[:1] * (1.0 / GROUP_SIZE)
-
-
-def group_stats(x_ref, img, gm_ref):
-    mean = group_mean(colsum(x_ref, img * PIX), gm_ref)
-
-    def body(c, acc):
-        gap = x_ref[pl.ds(pl.multiple_of(img * PIX + c * CHUNK, 8), CHUNK), :] - mean
-        return acc + jnp.sum(gap * gap, 0, keepdims=True)
-
-    square = lax.fori_loop(0, PIX // CHUNK, body, jnp.zeros((1, CH_MID), F32))
-    return mean, lax.rsqrt(group_mean(square, gm_ref) + EPSILON)
+def group_means(rows, gm_ref):
+    rows = rows + [jnp.zeros((8 - len(rows), CH_MID), F32)]
+    means = dot3(jnp.concatenate(rows, 0), gm_ref[...]) * (1.0 / GROUP_SIZE)
+    return [means[n : n + 1] for n in range(len(rows) - 1)]
+
+
+def all_stats(x_ref, gm_ref):
+    def total(c, acc):
+        at = lambda img: pl.ds(pl.multiple_of(img * PIX + c * CHUNK, 8), CHUNK)
+        return tuple(acc[img] + jnp.sum(x_ref[at(img), :], 0, keepdims=True) for img in range(MB_DEV))
+
+    zero = (jnp.zeros((1, CH_MID), F32),) * MB_DEV
+    means = group_means(list(lax.fori_loop(0, PIX // CHUNK, total, zero, unroll=2)), gm_ref)
+
+    def square(c, acc):
+        out = []
+        for img in range(MB_DEV):
+            gap = x_ref[pl.ds(pl.multiple_of(img * PIX + c * CHUNK, 8), CHUNK), :] - means[img]
+            out.append(acc[img] + jnp.sum(gap * gap, 0, keepdims=True))
+        return tuple(out)
+
+    spreads = group_means(list(lax.fori_loop(0, PIX // CHUNK, square, zero, unroll=2)), gm_ref)
+    return [(mean, lax.rsqrt(spread + EPSILON)) for mean, spread in zip(means, spreads)]
 
 
 def norm_to(pbuf, x_ref, stats, scales, act):
@@ -238,26 +248,29 @@
             pbuf[pl.ds(r + 8, CHUNK), :] = silu(z) if act else z
             return carry
 
-        lax.fori_loop(0, PIX // CHUNK, body, 0)
+        lax.fori_loop(0, PIX // CHUNK, body, 0, unroll=2)
 
 
 def norm_back(x_ref, d_ref, stats, scales, act, gm_ref, emit):
-    sums = []
-    for img in range(MB_DEV):
-        (mean, rstd), (k, o) = stats[img], scales[img]
-
-        def one(c, carry):
+    def one(c, carry):
+        out = []
+        for img in range(MB_DEV):
+            (mean, rstd), (k, o) = stats[img], scales[img]
             r = pl.multiple_of(img * PIX + c * CHUNK, 8)
             xhat = (x_ref[pl.ds(r, CHUNK), :] - mean) * rstd
             dz = d_ref[pl.ds(r, CHUNK), :]
             if act:
                 dz = dz * silu_slope(xhat * k + o)
                 d_ref[pl.ds(r, CHUNK), :] = dz
-            return (carry[0] + jnp.sum(dz, 0, keepdims=True), carry[1] + jnp.sum(dz * xhat, 0, keepdims=True))
-
-        zero = jnp.zeros((1, CH_MID), F32)
-        a, b = lax.fori_loop(0, PIX // CHUNK, one, (zero, zero))
-        m1, m2 = group_mean(a * k, gm_ref), group_mean(b * k, gm_ref)
+            out.append(carry[2 * img] + jnp.sum(dz, 0, keepdims=True))
+            out.append(carry[2 * img + 1] + jnp.sum(dz * xhat, 0, keepdims=True))
+        return tuple(out)
+
+    sums = lax.fori_loop(0, PIX // CHUNK, one, (jnp.zeros((1, CH_MID), F32),) * (2 * MB_DEV), unroll=2)
+    means = group_means([v * scales[n // 2][0] for n, v in enumerate(sums)], gm_ref)
+    for img in range(MB_DEV):
+        (mean, rstd), (k, o) = stats[img], scales[img]
+        m1, m2 = means[2 * img], means[2 * img + 1]
 
         def two(c, carry):
             r = pl.multiple_of(img * PIX + c * CHUNK, 8)
@@ -265,15 +278,13 @@
             emit(r, rstd * (d_ref[pl.ds(r, CHUNK), :] * k - m1 - xhat * m2))
             return carry
 
-        lax.fori_loop(0, PIX // CHUNK, two, 0)
-        sums.append((a, b))
-    return sums
+        lax.fori_loop(0, PIX // CHUNK, two, 0, unroll=2)
+    return [(sums[2 * img], sums[2 * img + 1]) for img in range(MB_DEV)]
 
 
 def clear_pads(sbuf):
-    for k in range(3):
-        for r in range(0, PADDED, PIX + 16):
-            sbuf[k, pl.ds(r, 16), :] = jnp.zeros((16, sbuf.shape[2]), BF16)
+    for r in range(0, PADDED, PIX + 16):
+        sbuf[r : r + 16, :] = jnp.zeros((16, sbuf.shape[1]), BF16)
 
 
 def shift_to(sbuf, pbuf):
@@ -286,22 +297,24 @@
             if k == 2:
                 v = jnp.where(column == HALF - 1, 0.0, v)
             start = r + 16 * (r // PIX + 1)
-            sbuf[k, start : start + CHUNK, :] = v.astype(BF16)
-
-
-def shifted(sbuf, k, row):
-    first = sbuf[k, pl.ds(pl.multiple_of(row, 16), PIX), :]
-    second = sbuf[k, pl.ds(pl.multiple_of(row + PIX + 16, 16), PIX), :]
+            sbuf[start : start + CHUNK, k * CH_MID : (k + 1) * CH_MID] = v.astype(BF16)
+
+
+def shifted(sbuf, row, cols=slice(None)):
+    first = sbuf[pl.ds(pl.multiple_of(row, 16), PIX), cols]
+    second = sbuf[pl.ds(pl.multiple_of(row + PIX + 16, 16), PIX), cols]
     return jnp.concatenate([first, second], 0)
 
 
 def conv_forward(sbuf, w_ref, out_ref):
-    def body(t, carry):
-        lhs = shifted(sbuf, lax.rem(t, 3), lax.div(t, 3) * 16)
-        out_ref[...] += dot(lhs, w_ref[pl.ds(pl.multiple_of(t * CH_MID, CH_MID), CH_MID), :])
+    depth = 3 * CH_MID
+
+    def body(ky, carry):
+        w = w_ref[pl.ds(pl.multiple_of(ky * depth, depth), depth), :]
+        out_ref[...] += dot(shifted(sbuf, ky * 16), w)
         return carry
 
-    lax.fori_loop(0, 9, body, 0)
+    lax.fori_loop(0, 3, body, 0, unroll=3)
 
 
 def put_lines(g_ref, at, value, step, more=None):
@@ -320,16 +333,21 @@
 
 def conv_back(sbuf, at_ref, w_ref, dx_ref, g_ref, at):
     dx_ref[...] = jnp.zeros_like(dx_ref)
+    depth = 3 * CH_MID
 
     def body(s, carry):
-        t = 8 - s
-        d = shifted(sbuf, lax.rem(s, 3), lax.div(s, 3) * 16)
-        w = w_ref[pl.ds(pl.multiple_of(t * CH_MID, CH_MID), CH_MID), :]
-        dx_ref[...] += dot(d, w, NT)
-        put_lines(g_ref, at, dot(at_ref[...], d), 3, t * (3 * CH_MID))
+        d = shifted(sbuf, s * 16)
+        dw = dot(at_ref[...], d)
+        dx = dx_ref[...]
+        for k in range(3):
+            part = slice(k * CH_MID, (k + 1) * CH_MID)
+            tap = (2 - s) * depth + (2 - k) * CH_MID
+            dx = dx + dot(d[:, part], w_ref[pl.ds(pl.multiple_of(tap, CH_MID), CH_MID), :], NT)
+            put_lines(g_ref, at, dw[:, part], 3, 3 * tap)
+        dx_ref[...] = dx
         return carry
 
-    lax.fori_loop(0, 9, body, 0)
+    lax.fori_loop(0, 3, body, 0, unroll=3)
 
 
 def transpose_to(at_ref, pbuf):
@@ -358,7 +376,7 @@
                 ].astype(F32)
                 return carry
 
-            lax.fori_loop(0, whole, body, 0)
+            lax.fori_loop(0, whole, body, 0, unroll=2)
             if rest:
                 done = whole * 256
                 self.wide[to + done : to + count, :] = block[start + done : start + count, :].astype(F32)
@@ -383,7 +401,7 @@
                 w_ref[pl.ds(r, block), j * LINE : (j + 1) * LINE] = v.astype(BF16)
             return carry
 
-        lax.fori_loop(0, rows // block, body, 0)
+        lax.fori_loop(0, rows // block, body, 0, unroll=3 if (rows // block) % 3 == 0 else 2)
 
     def row(self, at, step):
         base = at - self.low
@@ -545,7 +563,7 @@
     def half_block(x_ref, scales, bias_row, add_ref, out_ref, at, target):
         src.matrix(w_ref, at, 9 * CH_MID, 3)
         keep(w_ref, target)
-        stats = [group_stats(x_ref, img, gm) for img in range(MB_DEV)]
+        stats = all_stats(x_ref, gm)
         norm_to(pbuf, x_ref, stats, scales, True)
         shift_to(sbuf, pbuf)
         bias = jnp.broadcast_to(vec[bias_row : bias_row + 1, :], (ROWS, CH_MID))
@@ -589,7 +607,7 @@
             w_ref[part * CH_MID : (part + 1) * CH_MID, j * LINE : (j + 1) * LINE] = v.astype(BF16)
     src.matrix(w_ref.at[pl.ds(3 * CH_MID, CH_MID), :], AT.attn_out, CH_MID, 3)
     keep(w_ref.at[pl.ds(0, 4 * CH_MID), :], sw_attn if save else None)
-    stats = [group_stats(h2, img, gm) for img in range(MB_DEV)]
+    stats = all_stats(h2, gm)
     norm_to(pbuf, h2, stats, block_scales(vec, V_AG), False)
     n_low = pbuf[8 : 8 + ROWS, :].astype(BF16)
     for part in range(3):
@@ -611,7 +629,7 @@
             ).astype(BF16)
         return carry
 
-    lax.fori_loop(0, MB_DEV, heads, 0)
+    lax.fori_loop(0, MB_DEV, heads, 0, unroll=2)
     h3[...] = h2[...] + dot(mixed[...], w_ref[3 * CH_MID : 4 * CH_MID, :]) + vec[V_AB : V_AB + 1, :]
 
     src.take(SPAN_EMB2)
@@ -622,7 +640,7 @@
     keep(w_sq.at[1], sw_emb2 if save else None)
     block(h3, u2, h4, AT.second, V_G2, V_B21, V_B22, 2, (SPAN_ONE2, SPAN_TWO2), saved[2:])
 
-    stats = [group_stats(h4, img, gm) for img in range(MB_DEV)]
+    stats = all_stats(h4, gm)
     norm_to(pbuf, h4, stats, block_scales(vec, V_FG), True)
     z = dot(pbuf[8 : 8 + ROWS, :].astype(BF16), wz[...], NT)
     t_all = dot3(z, sel[...])
@@ -684,7 +702,7 @@
         vmem((10432, LINE), F32),
         vmem((9 * CH_MID, CH_MID), BF16),
         vmem((2, EMB_DIM, EMB_DIM), BF16),
-        vmem((3, PADDED, CH_MID), BF16),
+        vmem((PADDED, 3 * CH_MID), BF16),
         vmem((ROWS + 16, CH_MID), F32),
         vmem((ROWS + 48, 256), F32),
         vmem((16, LINE), F32),
@@ -724,7 +742,7 @@
     g_row, b1_row, b2_row = rows
     sbuf, pbuf, dx, at_ref, gm = tools
     put_row(g, at.bias_two - base, colsum(dh, 0, ROWS))
-    u_stats = [group_stats(u_ref, img, gm) for img in range(MB_DEV)]
+    u_stats = all_stats(u_ref, gm)
     scales = block_scales(vec, g_row + 2, mod, mod_row)
     norm_to(pbuf, u_ref, u_stats, scales, True)
     transpose_to(at_ref, pbuf)
@@ -753,7 +771,7 @@
     sbuf, pbuf, dx, at_ref, gm = tools
     put_row(g, at.bias_one - base, column_sum(pbuf))
     shift_to(sbuf, pbuf)
-    stats = [group_stats(x_ref, img, gm) for img in range(MB_DEV)]
+    stats = all_stats(x_ref, gm)
     scales = block_scales(vec, g_row)
     norm_to(pbuf, x_ref, stats, scales, True)
     transpose_to(at_ref, pbuf)
@@ -861,7 +879,7 @@
     clear_lines(g, TAIL - base, g.shape[0] - (TAIL - base))
     tools = (sbuf, pbuf, dx, at_ref, gm)
 
-    stats = [group_stats(h4, img, gm) for img in range(MB_DEV)]
+    stats = all_stats(h4, gm)
     scales = block_scales(vec, V_FG)
     norm_to(pbuf, h4, stats, scales, True)
     transpose_to(at_ref, pbuf)
@@ -935,8 +953,8 @@
                 dqkv[rows, part * CH_MID + pair * LINE : part * CH_MID + (pair + 1) * LINE] = value.astype(BF16)
         return carry
 
-    lax.fori_loop(0, MB_DEV, heads, 0)
-    stats = [group_stats(h2, img, gm) for img in range(MB_DEV)]
+    lax.fori_loop(0, MB_DEV, heads, 0, unroll=2)
+    stats = all_stats(h2, gm)
     scales = block_scales(vec, V_AG)
     norm_to(pbuf, h2, stats, scales, False)
     transpose_to(at_ref, pbuf)
@@ -1066,7 +1084,8 @@
         d0 = jnp.zeros((ROWS, CH_BASE), F32)
         for ky in ((0, 2) if ph // 2 else (1,)):
             for kx in ((0, 2) if ph % 2 else (1,)):
-                d = shifted(sbuf, 2 if kx == 0 else 1, 32 if ky == 0 else 16)
+                side = 2 if kx == 0 else 1
+                d = shifted(sbuf, 32 if ky == 0 else 16, slice(side * CH_MID, (side + 1) * CH_MID))
                 t = 3 * ky + kx
                 d0 = d0 + dot(d, w[t * CH_BASE : (t + 1) * CH_BASE, :], NT)
                 put_lines(g, AT.conv_down + t * CH_BASE * 3, dot(h0t[0:CH_BASE, :], d), 3)
@@ -1097,7 +1116,7 @@
     common = [
         vmem((lines + 8, LINE), F32),
         vmem((slots, 9 * CH_MID, CH_MID), BF16),
-        vmem((3, PADDED, CH_MID), BF16),
+        vmem((PADDED, 3 * CH_MID), BF16),
         vmem((ROWS + 16, CH_MID), F32),
     ]
     if norms:

time: 528 us -> 484 us (0.917)
  Pallas kernels: 179 us -> 136 us
    pallas_call x2, Pallas kernels: 92.7 us -> 65.9 us  [forward_call(): pl.pallas_call(body, out_shape=outs, in_specs=[SM] * 2 + [VM] * 8 + [HB]...]
    pallas_call x4, Pallas kernels: 86.3 us -> 69.8 us  [back_call(): pl.pallas_call(kernel, out_shape=[plane, plane, *rest, *(sds(*o) for o in...]
  transfers between devices with their start and end apart: 62 -> 62, of which waited for: 27 -> 27; matrix products, arithmetic and copies ran while one was open for 13% -> 15% of each run, Pallas kernels for 18% -> 15%
where the time goes in v4:
time: 484 us; the launch traced here: 476 us
  waiting for transfers between devices  160 us (33%)
  Pallas kernels  136 us (28%)
  starting transfers between devices  75.1 us (16%)
  other arithmetic  61.1 us (13%)
  local copies, waits for them, and re-layouts  24.6 us (5%)
  between operations  19.1 us (4%)
    ppermute x12, waiting for transfers between devices, climb(): return lax.ppermute(values, AXIS, pairs)  100 us
    pallas_call x4, Pallas kernels, back_call(): pl.pallas_call(kernel, out_shape=[plane, plane, *rest, *(sds(*o) for o in...  69.8 us
    pallas_call x2, Pallas kernels, forward_call(): pl.pallas_call(body, out_shape=outs, in_specs=[SM] * 2 + [VM] * 8 + [HB]...  65.9 us
    ppermute x31, waiting for transfers between devices, swap(): return lax.ppermute(values, AXIS, [(i, i ^ hop) for i in range(SHARDS)])  31.1 us
    ppermute x31, starting transfers between devices, swap(): return lax.ppermute(values, AXIS, [(i, i ^ hop) for i in range(SHARDS)])  29.3 us
    ppermute x8, starting transfers between devices, column_sums(): run = wide(lax.ppermute(low(value), AXIS, pairs))  18.2 us
    ppermute x12, starting transfers between devices, climb(): return lax.ppermute(values, AXIS, pairs)  17.7 us
    ppermute x8, waiting for transfers between devices, column_sums(): run = wide(lax.ppermute(low(value), AXIS, pairs))  14.8 us
  transfers between devices with their start and end apart: 62, of which 27 were waited for; matrix products, arithmetic and copies ran while one was open for 15% of the time, Pallas kernels for 15%

profile of v4, /device:TPU:0, one launch (start us, length us, event | category | flops | bytes accessed | tf_op | source)
XLA Modules:
  0.0 475.9 jit_solution(546904381261245322)
XLA Ops:
  10.1 5.0 %collective-permute-start = (bf16[1760,128]{1,0:T(8,128)(2,1)S(1)}, bf16[1760,128]{1,0:T(8,128)(2,1)S(1)}, u32[]{:S(2)}, u32[]{:S(2)}) collective-permute-start(bf16[1760,128]{1,0:T(8,128)(2,1)S(1)} %slice_bitcast_fusion), channel_id=1, source_target_pairs={{0,8},{1,9},{2,10},{3,11},{4,12},{5,13},{6,14},{7,15},{8,16},{9,17... | collective-permute-start | bytes 1351688 | tf_op jit(solution)/shard_map/ppermute | solution.py:1263
  28.6 7.5 %collective-permute-done.1.refs_3_ = bf16[1760,128]{1,0:T(8,128)(2,1)S(1)} collective-permute-done((bf16[1760,128]{1,0:T(8,128)(2,1)S(1)}, bf16[1760,128]{1,0:T(8,128)(2,1)S(1)}, u32[]{:S(2)}, u32[]{:S(2)}) %collective-permute-start.1) | collective-permute-done | bytes 450592 | tf_op jit(solution)/shard_map/ppermute | solution.py:1263
  44.4 6.6 %collective-permute-done.4 = bf16[1760,128]{1,0:T(8,128)(2,1)} collective-permute-done((bf16[1760,128]{1,0:T(8,128)(2,1)S(1)}, bf16[1760,128]{1,0:T(8,128)(2,1)}, u32[]{:S(2)}, u32[]{:S(2)}) %collective-permute-start.4) | collective-permute-done | bytes 450592 | tf_op jit(solution)/shard_map/ppermute | solution.py:1263
  69.3 16.3 %collective-permute-done.5.refs_2_ = bf16[1760,128]{1,0:T(8,128)(2,1)S(1)} collective-permute-done((bf16[1760,128]{1,0:T(8,128)(2,1)}, bf16[1760,128]{1,0:T(8,128)(2,1)S(1)}, u32[]{:S(2)}, u32[]{:S(2)}) %collective-permute-start.5) | collective-permute-done | bytes 450592 | tf_op jit(solution)/shard_map/ppermute | solution.py:1263
  98.3 21.7 %collective-permute-done.17 = bf16[4,512,128]{2,1,0:T(8,128)(2,1)S(1)} collective-permute-done((bf16[4,512,128]{2,1,0:T(8,128)(2,1)}, bf16[4,512,128]{2,1,0:T(8,128)(2,1)S(1)}, u32[]{:S(2)}, u32[]{:S(2)}) %collective-permute-start.17) | collective-permute-done | bytes 524320 | tf_op jit(solution)/shard_map/ppermute | solution.py:1263
  120.7 12.0 %collective-permute-done.20 = bf16[4,512,128]{2,1,0:T(8,128)(2,1)S(1)} collective-permute-done((bf16[4,512,128]{2,1,0:T(8,128)(2,1)}, bf16[4,512,128]{2,1,0:T(8,128)(2,1)S(1)}, u32[]{:S(2)}, u32[]{:S(2)}) %collective-permute-start.20) | collective-permute-done | bytes 524320 | tf_op jit(solution)/shard_map/ppermute | solution.py:1263
  142.1 14.7 %collective-permute-done.21 = bf16[4,512,128]{2,1,0:T(8,128)(2,1)S(1)} collective-permute-done((bf16[4,512,128]{2,1,0:T(8,128)(2,1)S(1)}, bf16[4,512,128]{2,1,0:T(8,128)(2,1)S(1)}, u32[]{:S(2)}, u32[]{:S(2)}) %collective-permute-start.21) | collective-permute-done | bytes 524320 | tf_op jit(solution)/shard_map/ppermute | solution.py:1263
  158.1 20.8 %collective-permute-done.22 = bf16[4,512,128]{2,1,0:T(8,128)(2,1)S(1)} collective-permute-done((bf16[4,512,128]{2,1,0:T(8,128)(2,1)S(1)}, bf16[4,512,128]{2,1,0:T(8,128)(2,1)S(1)}, u32[]{:S(2)}, u32[]{:S(2)}) %collective-permute-start.22) | collective-permute-done | bytes 524320 | tf_op jit(solution)/shard_map/ppermute | solution.py:1263
  180.1 4.0 collective-permute-done.7.refs_11_
  194.3 34.3 %forward_save.1 = (f32[512,128]{1,0:T(8,128)}, bf16[2048,256]{1,0:T(8,128)(2,1)}, f32[512,384]{1,0:T(8,128)}, f32[512,384]{1,0:T(8,128)}, f32[512,384]{1,0:T(8,1...) custom-call(s32[1]{0:T(128)} %bitcast.7.refs_0_, ...), custom_call_target="tpu_custom_call" | custom-call | flops 8000000000 | bytes 40000000 | tf_op jit(solution)/shard_map/forward_save/pallas_call | solution.py:718
  228.8 31.6 %forward_plain.1 = f32[512,128]{1,0:T(8,128)} custom-call(s32[1]{0:T(128)} %constant.137.clone.1.refs_0_, s32[2]{0:T(128)} %refs_1_.6, bf16[512,128]{1,0:T(8,128)(2,1)} %pad.28.refs_4_.refs_2_, f32[8,192]{1,0:T(8,128)} %select_maximum_fusion.refs_5_.refs_3_, bf16[384,384]{1,0:T(8,128)(2,1)} %constant.145.clone.refs_4_.refs_3_.refs_2_.refs_6_, ...), custom_call_target="tpu_custom_call" | custom-call | flops 8000000000 | bytes 40000000 | tf_op jit(solution)/shard_map/forward_plain/pallas_call | solution.py:718
  260.4 3.8 select_reduce_fusion
  266.9 32.0 %back_top.1 = (bf16[4,2272,128]{2,1,0:T(8,128)(2,1)}, bf16[4,2272,128]{2,1,0:T(8,128)(2,1)}, f32[11968,128]{1,0:T(8,128)}, f32[512,384]{1,0:T(8,128)}, f32[8,768]{1,0:T(8,128)}) custom-call(s32[1]{0:T(128)} %bitcast.7.refs_0_, f32[512,128]{1,0:T(8,128)} %pad.31.refs_1_, bf16[128,384]{1,0:T(8,128)(2,1)} %get-tuple-element.55.refs_2_, ...), custom_call_target="tpu_custom_call" | custom-call | flops 8000000000 | bytes 40000000 | tf_op jit(solution)/shard_map/back_top/pallas_call | solution.py:1131
  299.1 14.2 %back_b.1 = (bf16[4,2272,128]{2,1,0:T(8,128)(2,1)}, bf16[4,2272,128]{2,1,0:T(8,128)(2,1)}, f32[4240,128]{1,0:T(8,128)}, f32[512,384]{1,0:T(8,128)}, f32[8,768]{1,0:T(8,128)}, /*index=5*/f32[8,384]{1,0:T(8,128)}) custom-call(s32[1]{0:T(128)} %bitcast.7.refs_0_, f32[512,384]{1,0:T(8,128)} %get-tuple-element.69.refs_1_, ...), custom_call_target="tpu_custom_call" | custom-call | flops 8000000000 | bytes 40000000 | tf_op jit(solution)/shard_map/back_b/pallas_call | solution.py:1131
  324.3 13.0 %back_c.1 = (bf16[4,2272,128]{2,1,0:T(8,128)(2,1)}, bf16[4,2272,128]{2,1,0:T(8,128)(2,1)}, f32[1120,128]{1,0:T(8,128)}, f32[512,384]{1,0:T(8,128)}, f32[8,768]{1,0:T(8,128)}) custom-call(s32[1]{0:T(128)} %bitcast.7.refs_0_, f32[512,384]{1,0:T(8,128)} %get-tuple-element.69.refs_1_, f32[512,384]{1,0:T(8,128)} %gate.8.refs_2_, ...), custom_call_target="tpu_custom_call" | custom-call | flops 8000000000 | bytes 40000000 | tf_op jit(solution)/shard_map/back_c/pallas_call | solution.py:1131
  343.4 10.6 %back_low.1 = (bf16[4,2272,128]{2,1,0:T(8,128)(2,1)}, bf16[4,2272,128]{2,1,0:T(8,128)(2,1)}) custom-call(s32[1]{0:T(128)} %bitcast.7.refs_0_, s32[2]{0:T(128)} %refs_1_.6, f32[512,384]{1,0:T(8,128)} %gate.9.refs_2_, f32[8,768]{1,0:T(8,128)} %get-tuple-element.86.refs_3_, f32[8,768]{1,0:T(8,128)} %get-tuple-element.58.refs_10_.refs_8_.refs_4_, ...), custom_call_target="tpu_custom_call" | custom-call | flops 8000000000 | bytes 40000000 | tf_op jit(solution)/shard_map/back_low/pallas_call | solution.py:1131
  358.0 7.1 %collective-permute-done.54 = bf16[1136,128]{1,0:T(8,128)(2,1)S(1)} collective-permute-done((bf16[1136,128]{1,0:T(8,128)(2,1)S(1)}, bf16[1136,128]{1,0:T(8,128)(2,1)S(1)}, u32[]{:S(2)}, u32[]{:S(2)}) %collective-permute-start.54) | collective-permute-done | bytes 290848 | tf_op jit(solution)/shard_map/ppermute | solution.py:1229
  380.7 5.4 %collective-permute-done.43 = bf16[2,1136,128]{2,1,0:T(8,128)(2,1)} collective-permute-done((bf16[2,1136,128]{2,1,0:T(8,128)(2,1)}, bf16[2,1136,128]{2,1,0:T(8,128)(2,1)}, u32[]{:S(2)}, u32[]{:S(2)}) %collective-permute-start.43) | collective-permute-done | bytes 581664 | tf_op jit(solution)/shard_map/ppermute | solution.py:1229
  390.3 6.9 %collective-permute-done.34 = f32[8,4]{1,0:T(8,128)S(1)} collective-permute-done((f32[8,4]{1,0:T(8,128)S(1)}, f32[8,4]{1,0:T(8,128)S(1)}, u32[]{:S(2)}, u32[]{:S(2)}) %collective-permute-start.34) | collective-permute-done | bytes 160 | tf_op jit(solution)/shard_map/ppermute | solution.py:1235
  418.9 3.8 collective-permute-done.39
  431.3 6.5 %collective-permute-done.58 = bf16[2272,128]{1,0:T(8,128)(2,1)S(1)} collective-permute-done((bf16[2272,128]{1,0:T(8,128)(2,1)S(1)}, bf16[2272,128]{1,0:T(8,128)(2,1)S(1)}, u32[]{:S(2)}, u32[]{:S(2)}) %collective-permute-start.58) | collective-permute-done | bytes 581664 | tf_op jit(solution)/shard_map/ppermute | solution.py:1369
  440.3 8.3 %collective-permute-start.47 = (bf16[2272,128]{1,0:T(8,128)(2,1)}, bf16[2272,128]{1,0:T(8,128)(2,1)}, u32[]{:S(2)}, u32[]{:S(2)}) collective-permute-start(bf16[2272,128]{1,0:T(8,128)(2,1)} %get-tuple-element.142), channel_id=1, source_target_pairs={{0,8},{1,9},{2,10},{3,11},{4,12},{5,13},{6,14},{7,15}} | collective-permute-start | bytes 1744904 | tf_op jit(solution)/shard_map/ppermute | solution.py:1369
  455.4 6.9 %collective-permute-done.50 = bf16[2272,128]{1,0:T(8,128)(2,1)} collective-permute-done((bf16[2272,128]{1,0:T(8,128)(2,1)}, bf16[2272,128]{1,0:T(8,128)(2,1)}, u32[]{:S(2)}, u32[]{:S(2)}) %collective-permute-start.50) | collective-permute-done | bytes 581664 | tf_op jit(solution)/shard_map/ppermute | solution.py:1369
  462.3 5.4 %multiply_add_fusion = (f32[289792]{0:T(1024)}, f32[289792]{0:T(1024)}, f32[289792]{0:T(1024)}) fusion(f32[289792]{0:T(1024)} %param.23, f32[289792]{0:T(1024)} %param.21, f32[289792]{0:T(1024)} %param.22, f32[1136,128]{1,0:T(8,128)S(1)} %get-tuple-element.126, f32[1136,128]{1,0:T(8,128)S(1)} %get-tuple-element.127, f32[1136,128]{1,0:T(8,128)} %copy-done.2, ...), kind=kLoop, calls=%fused_computation.27 | loop fusion | flops 6375424 | bytes 13918211 | tf_op jit(solution)/shard_map/add | solution.py:1467
  (326 shorter events, 158.4 us)
Async XLA Ops:
  7.2 221.5 %all-gather.2.cloned.1.call-start = ((), (), s32[]{:S(2)}) async-start(), calls=%async_computation | async-start | bytes 19193856 | tf_op jit(solution)/shard_map/all_gather | solution.py:1313
  15.1 21.0 %collective-permute-start.1 = (bf16[1760,128]{1,0:T(8,128)(2,1)S(1)}, bf16[1760,128]{1,0:T(8,128)(2,1)S(1)}, u32[]{:S(2)}, u32[]{:S(2)}) collective-permute-start(bf16[1760,128]{1,0:T(8,128)(2,1)S(1)} %slice_bitcast_fusion), channel_id=1, source_target_pairs={{24,16},{25,17},{26,18},{27,19},{28,20},{29,21},{30,22},{31,23},{1... | collective-permute-start | bytes 1351688 | tf_op jit(solution)/shard_map/ppermute | solution.py:1263
  18.5 20.5 %collective-permute-start.10 = (bf16[512,128]{1,0:T(8,128)(2,1)S(1)}, bf16[512,128]{1,0:T(8,128)(2,1)S(1)}, u32[]{:S(2)}, u32[]{:S(2)}) collective-permute-start(bf16[512,128]{1,0:T(8,128)(2,1)S(1)} %get-tuple-element.159), channel_id=1, source_target_pairs={{0,4},{1,5},{2,6},{3,7},{4,0},{5,1},{6,2},{7,3},{8,12},{9,13},{10,... | collective-permute-start | bytes 393224 | tf_op jit(solution)/shard_map/ppermute | solution.py:1229
  39.1 23.8 %collective-permute-start.11 = (bf16[2,512,128]{2,1,0:T(8,128)(2,1)S(1)}, bf16[2,512,128]{2,1,0:T(8,128)(2,1)S(1)}, u32[]{:S(2)}, u32[]{:S(2)}) collective-permute-start(bf16[2,512,128]{2,1,0:T(8,128)(2,1)S(1)} %pad_maximum_fusion.17), channel_id=1, source_target_pairs={{0,2},{1,3},{2,0},{3,1},{4,6},{5,7},{6,4},{7,5},{8,10},{9,11},{10,... | collective-permute-start | bytes 786440 | tf_op jit(solution)/shard_map/ppermute | solution.py:1229
  43.8 25.5 %collective-permute-start.3 = (bf16[1760,128]{1,0:T(8,128)(2,1)}, bf16[1760,128]{1,0:T(8,128)(2,1)S(1)}, u32[]{:S(2)}, u32[]{:S(2)}) collective-permute-start(bf16[1760,128]{1,0:T(8,128)(2,1)} %collective-permute-done.2), channel_id=1, source_target_pairs={{16,24},{17,25},{18,26},{19,27},{20,28},{21,29},{22,30},{23,31}} | collective-permute-start | bytes 1351688 | tf_op jit(solution)/shard_map/ppermute | solution.py:1263
  51.0 34.6 %collective-permute-start.5 = (bf16[1760,128]{1,0:T(8,128)(2,1)}, bf16[1760,128]{1,0:T(8,128)(2,1)S(1)}, u32[]{:S(2)}, u32[]{:S(2)}) collective-permute-start(bf16[1760,128]{1,0:T(8,128)(2,1)} %collective-permute-done.4), channel_id=1, source_target_pairs={{8,0},{9,1},{10,2},{11,3},{12,4},{13,5},{14,6},{15,7}} | collective-permute-start | bytes 1351688 | tf_op jit(solution)/shard_map/ppermute | solution.py:1263
  89.1 44.8 %collective-permute-start.6 = (bf16[4,880,128]{2,1,0:T(8,128)(2,1)}, bf16[4,880,128]{2,1,0:T(8,128)(2,1)S(1)}, u32[]{:S(2)}, u32[]{:S(2)}) collective-permute-start(bf16[4,880,128]{2,1,0:T(8,128)(2,1)} %get-tuple-element.149), channel_id=1, source_target_pairs={{0,2},{1,3},{2,0},{3,1},{4,6},{5,7},{6,4},{7,5},{8,10},{9,11},{10,... | collective-permute-start | bytes 2703368 | tf_op jit(solution)/shard_map/ppermute | solution.py:1229
  91.1 45.7 %collective-permute-start.8 = (bf16[4,880,128]{2,1,0:T(8,128)(2,1)}, bf16[4,880,128]{2,1,0:T(8,128)(2,1)}, u32[]{:S(2)}, u32[]{:S(2)}) collective-permute-start(bf16[4,880,128]{2,1,0:T(8,128)(2,1)} %get-tuple-element.148), channel_id=1, source_target_pairs={{0,4},{1,5},{2,6},{3,7},{4,0},{5,1},{6,2},{7,3},{8,12},{9,13},{10,... | collective-permute-start | bytes 2703368 | tf_op jit(solution)/shard_map/ppermute | solution.py:1229
  95.4 24.6 %collective-permute-start.17 = (bf16[4,512,128]{2,1,0:T(8,128)(2,1)}, bf16[4,512,128]{2,1,0:T(8,128)(2,1)S(1)}, u32[]{:S(2)}, u32[]{:S(2)}) collective-permute-start(bf16[4,512,128]{2,1,0:T(8,128)(2,1)} %gate.7), channel_id=1, source_target_pairs={{0,8},{1,9},{2,10},{3,11},{4,12},{5,13},{6,14},{7,15},{8,16},{9,17... | collective-permute-start | bytes 1572872 | tf_op jit(solution)/shard_map/ppermute | solution.py:1263
  97.0 35.6 %collective-permute-start.20 = (bf16[4,512,128]{2,1,0:T(8,128)(2,1)}, bf16[4,512,128]{2,1,0:T(8,128)(2,1)S(1)}, u32[]{:S(2)}, u32[]{:S(2)}) collective-permute-start(bf16[4,512,128]{2,1,0:T(8,128)(2,1)} %gate.7), channel_id=1, source_target_pairs={{24,16},{25,17},{26,18},{27,19},{28,20},{29,21},{30,22},{31,23},{1... | collective-permute-start | bytes 1572872 | tf_op jit(solution)/shard_map/ppermute | solution.py:1263
  120.0 21.4 %collective-permute-start.18 = (bf16[4,512,128]{2,1,0:T(8,128)(2,1)S(1)}, bf16[4,512,128]{2,1,0:T(8,128)(2,1)S(1)}, u32[]{:S(2)}, u32[]{:S(2)}) collective-permute-start(bf16[4,512,128]{2,1,0:T(8,128)(2,1)S(1)} %collective-permute-done.17), channel_id=1, source_target_pairs={{8,16},{9,17},{10,18},{11,19},{12,20},{13,21},{14,22},{15,23},{16,... | collective-permute-start | bytes 1572872 | tf_op jit(solution)/shard_map/ppermute | solution.py:1263
  132.6 24.1 %collective-permute-start.21 = (bf16[4,512,128]{2,1,0:T(8,128)(2,1)S(1)}, bf16[4,512,128]{2,1,0:T(8,128)(2,1)S(1)}, u32[]{:S(2)}, u32[]{:S(2)}) collective-permute-start(bf16[4,512,128]{2,1,0:T(8,128)(2,1)S(1)} %collective-permute-done.20), channel_id=1, source_target_pairs={{16,8},{17,9},{18,10},{19,11},{20,12},{21,13},{22,14},{23,15},{8,0... | collective-permute-start | bytes 1572872 | tf_op jit(solution)/shard_map/ppermute | solution.py:1263
  135.3 48.8 %collective-permute-start.7 = (bf16[2,4,880,128]{3,2,1,0:T(8,128)(2,1)}, bf16[2,4,880,128]{3,2,1,0:T(8,128)(2,1)}, u32[]{:S(2)}, u32[]{:S(2)}) collective-permute-start(bf16[2,4,880,128]{3,2,1,0:T(8,128)(2,1)} %pad_maximum_fusion.2.refs_10_), channel_id=1, source_target_pairs={{0,4},{1,5},{2,6},{3,7},{4,0},{5,1},{6,2},{7,3},{8,12},{9,13},{10,... | collective-permute-start | bytes 5406728 | tf_op jit(solution)/shard_map/ppermute | solution.py:1229
  139.4 44.7 %collective-permute-start.9 = (bf16[2,4,880,128]{3,2,1,0:T(8,128)(2,1)}, bf16[2,4,880,128]{3,2,1,0:T(8,128)(2,1)}, u32[]{:S(2)}, u32[]{:S(2)}) collective-permute-start(bf16[2,4,880,128]{3,2,1,0:T(8,128)(2,1)} %pad_maximum_fusion.3.refs_12_), channel_id=1, source_target_pairs={{0,2},{1,3},{2,0},{3,1},{4,6},{5,7},{6,4},{7,5},{8,10},{9,11},{10,... | collective-permute-start | bytes 5406728 | tf_op jit(solution)/shard_map/ppermute | solution.py:1229
  156.8 22.1 %collective-permute-start.22 = (bf16[4,512,128]{2,1,0:T(8,128)(2,1)S(1)}, bf16[4,512,128]{2,1,0:T(8,128)(2,1)S(1)}, u32[]{:S(2)}, u32[]{:S(2)}) collective-permute-start(bf16[4,512,128]{2,1,0:T(8,128)(2,1)S(1)} %collective-permute-done.21), channel_id=1, source_target_pairs={{8,0},{9,1},{10,2},{11,3},{12,4},{13,5},{14,6},{15,7}} | collective-permute-start | bytes 1572872 | tf_op jit(solution)/shard_map/ppermute | solution.py:1263
  317.0 20.3 %collective-permute-start.30 = (bf16[2,1136,128]{2,1,0:T(8,128)(2,1)}, bf16[2,1136,128]{2,1,0:T(8,128)(2,1)}, u32[]{:S(2)}, u32[]{:S(2)}) collective-permute-start(bf16[2,1136,128]{2,1,0:T(8,128)(2,1)} %pad_maximum_fusion.9.refs_2_), channel_id=1, source_target_pairs={{0,4},{1,5},{2,6},{3,7},{4,0},{5,1},{6,2},{7,3},{8,12},{9,13},{10,... | collective-permute-start | bytes 1744904 | tf_op jit(solution)/shard_map/ppermute | solution.py:1229
  318.8 18.6 %collective-permute-start.29 = (bf16[2,1136,128]{2,1,0:T(8,128)(2,1)}, bf16[2,1136,128]{2,1,0:T(8,128)(2,1)}, u32[]{:S(2)}, u32[]{:S(2)}) collective-permute-start(bf16[2,1136,128]{2,1,0:T(8,128)(2,1)} %pad_maximum_fusion.8.refs_1_), channel_id=1, source_target_pairs={{0,2},{1,3},{2,0},{3,1},{4,6},{5,7},{6,4},{7,5},{8,10},{9,11},{10,... | collective-permute-start | bytes 1744904 | tf_op jit(solution)/shard_map/ppermute | solution.py:1229
  323.8 30.2 %collective-permute-start.53 = (bf16[2,1136,128]{2,1,0:T(8,128)(2,1)S(1)}, bf16[2,1136,128]{2,1,0:T(8,128)(2,1)}, u32[]{:S(2)}, u32[]{:S(2)}) collective-permute-start(bf16[2,1136,128]{2,1,0:T(8,128)(2,1)S(1)} %pad_maximum_fusion.11.refs_4_), channel_id=1, source_target_pairs={{0,4},{1,5},{2,6},{3,7},{4,0},{5,1},{6,2},{7,3},{8,12},{9,13},{10,... | collective-permute-start | bytes 1744904 | tf_op jit(solution)/shard_map/ppermute | solution.py:1229
  323.9 30.2 %collective-permute-start.51 = (bf16[2,1136,128]{2,1,0:T(8,128)(2,1)S(1)}, bf16[2,1136,128]{2,1,0:T(8,128)(2,1)}, u32[]{:S(2)}, u32[]{:S(2)}) collective-permute-start(bf16[2,1136,128]{2,1,0:T(8,128)(2,1)S(1)} %pad_maximum_fusion.10.refs_3_), channel_id=1, source_target_pairs={{0,2},{1,3},{2,0},{3,1},{4,6},{5,7},{6,4},{7,5},{8,10},{9,11},{10,... | collective-permute-start | bytes 1744904 | tf_op jit(solution)/shard_map/ppermute | solution.py:1229
  337.3 29.6 %collective-permute-start.42 = (bf16[4,2272,128]{2,1,0:T(8,128)(2,1)}, bf16[4,2272,128]{2,1,0:T(8,128)(2,1)}, u32[]{:S(2)}, u32[]{:S(2)}) collective-permute-start(bf16[4,2272,128]{2,1,0:T(8,128)(2,1)} %get-tuple-element.96), channel_id=1, source_target_pairs={{0,1},{1,0},{2,3},{3,2},{4,5},{5,4},{6,7},{7,6},{8,9},{9,8},{10,11... | collective-permute-start | bytes 6979592 | tf_op jit(solution)/shard_map/ppermute | solution.py:1229
  354.0 18.5 %collective-permute-start.32 = (bf16[4,2272,128]{2,1,0:T(8,128)(2,1)}, bf16[4,2272,128]{2,1,0:T(8,128)(2,1)S(1)}, u32[]{:S(2)}, u32[]{:S(2)}) collective-permute-start(bf16[4,2272,128]{2,1,0:T(8,128)(2,1)} %get-tuple-element.94), channel_id=1, source_target_pairs={{0,1},{1,0},{2,3},{3,2},{4,5},{5,4},{6,7},{7,6},{8,9},{9,8},{10,11... | collective-permute-start | bytes 6979592 | tf_op jit(solution)/shard_map/ppermute | solution.py:1229
  376.2 39.4 %collective-permute-start.38 = (bf16[2,1136,128]{2,1,0:T(8,128)(2,1)S(1)}, bf16[2,1136,128]{2,1,0:T(8,128)(2,1)S(1)}, u32[]{:S(2)}, u32[]{:S(2)}) collective-permute-start(bf16[2,1136,128]{2,1,0:T(8,128)(2,1)S(1)} %copy-done.19), channel_id=1, source_target_pairs={{0,2},{1,3},{2,0},{3,1},{4,6},{5,7},{6,4},{7,5},{8,10},{9,11},{10,... | collective-permute-start | bytes 1744904 | tf_op jit(solution)/shard_map/ppermute | solution.py:1229
  376.8 38.9 %collective-permute-start.40 = (bf16[2,1136,128]{2,1,0:T(8,128)(2,1)S(1)}, bf16[2,1136,128]{2,1,0:T(8,128)(2,1)S(1)}, u32[]{:S(2)}, u32[]{:S(2)}) collective-permute-start(bf16[2,1136,128]{2,1,0:T(8,128)(2,1)S(1)} %copy-done.20), channel_id=1, source_target_pairs={{0,4},{1,5},{2,6},{3,7},{4,0},{5,1},{6,2},{7,3},{8,12},{9,13},{10,... | collective-permute-start | bytes 1744904 | tf_op jit(solution)/shard_map/ppermute | solution.py:1229
  409.0 45.0 %collective-permute-start.60 = (bf16[2272,128]{1,0:T(8,128)(2,1)}, bf16[2272,128]{1,0:T(8,128)(2,1)}, u32[]{:S(2)}, u32[]{:S(2)}) collective-permute-start(bf16[2272,128]{1,0:T(8,128)(2,1)} %get-tuple-element.145), channel_id=1, source_target_pairs={{24,16},{25,17},{26,18},{27,19},{28,20},{29,21},{30,22},{31,23}} | collective-permute-start | bytes 1744904 | tf_op jit(solution)/shard_map/ppermute | solution.py:1369
  (91 other events, 1274.0 us)
Sparse Core Ops, SparseCore 0:
  10.9 165.6 all-gather.1

commit v5 on v4

--- a/solution.py
+++ b/solution.py
@@ -817,7 +817,8 @@
 
 
 class Leave:
-    def __init__(self, me, g, base, keep, send, stage, sems):
+    def __init__(self, me, g, base, keep, send, stage, sems, pad):
+        self.pad = pad
         self.core, self.place = lax.rem(me[0], 2), lax.div(me[0], 2)
         self.g, self.base, self.outs, self.stage, self.sems = g, base, (keep, send), stage, sems
         self.copies = []
@@ -838,8 +839,8 @@
                     return carry
 
                 lax.fori_loop(0, whole, body, 0)
-                lines = self.g[pl.ds(pl.multiple_of(start + whole * 288, 8), rest), :]
-                stage[whole * 288 :, :] = lines.astype(BF16)
+                lines = self.g[pl.ds(pl.multiple_of(start + whole * 288, 8), rest - 8), :]
+                stage[whole * 288 :, :] = jnp.concatenate([lines, self.pad[...]], 0).astype(BF16)
                 copy = pltpu.make_async_copy(stage, self.outs[side].at[at], self.sems.at[side])
                 copy.start()
                 self.copies.append(copy)
@@ -866,9 +867,9 @@
 
 
 def back_top_kernel(*refs):
-    me, df, wz, gm, sel, gat, tile, expand, vec, mod, emb, h4, u2, h3, qkv, mixed, h2, s22, s21, s_attn, s_emb = refs[:21]
-    keep, send, rest, dh, dse = refs[21:26]
-    g, slots, sbuf, pbuf, dx, at_ref, stage, sems, out_sems, w_sq, dqkv, dm, sq_sem = refs[26:]
+    me, pad, df, wz, gm, sel, gat, tile, expand, vec, mod, emb, h4, u2, h3, qkv, mixed, h2, s22, s21, s_attn, s_emb = refs[:22]
+    keep, send, rest, dh, dse = refs[22:27]
+    g, slots, sbuf, pbuf, dx, at_ref, stage, sems, out_sems, w_sq, dqkv, dm, sq_sem = refs[27:]
     base = BASE_ONE
     weights = Weights([s22, s21, s_attn], slots, sems)
     weights.begin()
@@ -974,16 +975,16 @@
     put_row(g, AT.attn_gains - base, sums[0][1] + sums[1][1])
     put_row(g, AT.attn_gains + 3 - base, sums[0][0] + sums[1][0])
 
-    leave = Leave(me, g, base, keep, send, stage, out_sems)
+    leave = Leave(me, g, base, keep, send, stage, out_sems, pad)
     leave.plane(3)
     leave.below(PLANES[3] - base, rest)
     leave.wait()
 
 
 def back_second_half_kernel(*refs):
-    me, dh, gm, vec, mod, u1, s12, rest_in = refs[:8]
-    keep, send, rest, du, dm, extra = refs[8:14]
-    g, slots, sbuf, pbuf, dx, at_ref, stage, sems, out_sems, in_sem = refs[14:]
+    me, pad, dh, gm, vec, mod, u1, s12, rest_in = refs[:9]
+    keep, send, rest, du, dm, extra = refs[9:15]
+    g, slots, sbuf, pbuf, dx, at_ref, stage, sems, out_sems, in_sem = refs[15:]
     base = BASE_TWO
     weights = Weights([s12], slots, sems)
     weights.begin()
@@ -1000,16 +1001,16 @@
     extra[1:2, :] = d_shift
     for c in range(0, ROWS, CHUNK):
         du[c : c + CHUNK, :] = pbuf[8 + c : 8 + c + CHUNK, :]
-    leave = Leave(me, g, base, keep, send, stage, out_sems)
+    leave = Leave(me, g, base, keep, send, stage, out_sems, pad)
     leave.plane(2)
     leave.below(PLANES[2] - base, rest)
     leave.wait()
 
 
 def back_first_half_kernel(*refs):
-    me, dh_in, du, dm, extra, dse_in, gm, vec, emb, h1, s11, s_emb, rest_in = refs[:13]
-    keep, send, rest, dh, dse = refs[13:18]
-    g, slots, sbuf, pbuf, dx, at_ref, stage, sems, out_sems, w_sq, in_sem, sq_sem = refs[18:]
+    me, pad, dh_in, du, dm, extra, dse_in, gm, vec, emb, h1, s11, s_emb, rest_in = refs[:14]
+    keep, send, rest, dh, dse = refs[14:19]
+    g, slots, sbuf, pbuf, dx, at_ref, stage, sems, out_sems, w_sq, in_sem, sq_sem = refs[19:]
     base = BASE_THREE
     weights = Weights([s11], slots, sems)
     weights.begin()
@@ -1029,7 +1030,7 @@
     block_back_one(dh, h1, AT.first, base, (V_G1, V_B11, V_B12), vec, weights, tools, g)
     put_row(g, AT.first.gains + 6 - base, extra[0:1, :])
     put_row(g, AT.first.gains + 9 - base, extra[1:2, :])
-    leave = Leave(me, g, base, keep, send, stage, out_sems)
+    leave = Leave(me, g, base, keep, send, stage, out_sems, pad)
     leave.plane(1)
     leave.below(PLANES[1] - base, rest)
     sq_copy.wait()
@@ -1038,9 +1039,9 @@
 
 
 def back_low_kernel(*refs):
-    me, labels, dh, dse, emb, pre, phi, h0s, xp, s_down, s_time, rest_in = refs[:12]
-    keep, send = refs[12:14]
-    g, slots, sbuf, pbuf, h0t, stage, sems, out_sems, w_sq, demb_ref, dwin, dbin, in_sem, sq_sem = refs[14:]
+    me, labels, pad, dh, dse, emb, pre, phi, h0s, xp, s_down, s_time, rest_in = refs[:13]
+    keep, send = refs[13:15]
+    g, slots, sbuf, pbuf, h0t, stage, sems, out_sems, w_sq, demb_ref, dwin, dbin, in_sem, sq_sem = refs[15:]
     weights = Weights([s_down], slots, sems)
     weights.begin()
     sq_copy = pltpu.make_async_copy(s_time, w_sq, sq_sem)
@@ -1097,7 +1098,7 @@
     g[pl.ds(0, 14, stride=3), :] = even[0:14, :LINE]
     g[pl.ds(1, 14, stride=3), :] = jnp.where(first_lanes(), even[:, LINE:], turned[0])[0:14]
     g[pl.ds(2, 14, stride=3), :] = jnp.where(first_lanes(), turned[0], turned[1])[0:14]
-    leave = Leave(me, g, 0, keep, send, stage, out_sems)
+    leave = Leave(me, g, 0, keep, send, stage, out_sems, pad)
     leave.plane(0)
     leave.wait()
 
@@ -1317,6 +1318,23 @@
     return [lines], [(0, r, r, 0, ROOM) for r in range(PLANE)], (True,)
 
 
+def digit_weights():
+    return np.array([8.0 ** (k - 40) if k < 82 else 0.0 for k in range(LINE)], np.float32)[None]
+
+
+def to_digits(values):
+    weights = digit_weights()
+    inverse = np.where(weights > 0, 1.0 / np.where(weights > 0, weights, 1.0), 0.0).astype(np.float32)
+    size = jnp.abs(values)[:, None] * inverse
+    digit = jnp.floor(size) - 8.0 * jnp.floor(size * 0.125)
+    digit = jnp.where(size < 2.0**27, digit, 0.0)
+    return jnp.where(values[:, None] < 0, -digit, digit)
+
+
+def from_digits(rows):
+    return jnp.sum(rows * digit_weights(), 1)
+
+
 def low(v):
     return v.astype(BF16)
 
@@ -1407,8 +1425,11 @@
     else:
         online, target = gather_plain(shards[0]), gather_plain(shards[1])
         in_lo, in_hi, mask = early(())[0]
+    model_t, _ = per_part(jnp.zeros_like(me), labels, target, in_lo, False, tables)
+    if direct:
+        (x_in,) = gate([in_hi[1]], [model_t])
+        in_hi = (in_hi[0], x_in, *in_hi[2:])
     model_o, saved = per_part(me, labels, online, in_hi, True, tables)
-    model_t, _ = per_part(jnp.zeros_like(me), labels, target, in_lo, False, tables)
     online_out = in_hi[0] + in_hi[3] * model_o[:, :12]
     target_out = in_lo[0] + in_lo[3] * model_t[:, :12]
     phi, out_scale = in_hi[2], in_hi[3]
@@ -1421,51 +1442,50 @@
     gm = tables[0]
     df = jnp.pad(grad_model, ((0, 0), (0, LINE - 12)))
     small = jnp.concatenate([local_loss[None], bias_out])
-    small = jnp.broadcast_to(small, (8, 4))
+    pad = jnp.pad(to_digits(small), ((0, 4), (0, 0)))
     keep3, send3, rest, dh, dse = back_top(
-        (me, df, wz, *tables[:5], vec, mod, emb, h4, u2, h3, qkv, mixed, h2, s22, s21, s_attn, s_emb2)
+        (me, pad, df, wz, *tables[:5], vec, mod, emb, h4, u2, h3, qkv, mixed, h2, s22, s21, s_attn, s_emb2)
     )
     if direct:
         three = PlaneSum(keep3, send3)
-    keep2, send2, rest, du, dm, extra = back_second_half((me, dh, gm, vec, mod, u1, s12, rest))
+    keep2, send2, rest, du, dm, extra = back_second_half((me, pad, dh, gm, vec, mod, u1, s12, rest))
     if direct:
         first3 = three.first()
         (du,) = gate([du], first3)
         three.send_first(*first3)
         two = PlaneSum(keep2, send2)
-    keep1, send1, rest, dh, dse = back_first_half((me, dh, du, dm, extra, dse, gm, vec, emb, h1, s11, s_emb1, rest))
+    keep1, send1, rest, dh, dse = back_first_half((me, pad, dh, du, dm, extra, dse, gm, vec, emb, h1, s11, s_emb1, rest))
     if direct:
         last3, first2 = three.last(), two.first()
         (dh,) = gate([dh], [*last3, *first2])
         three.send_last(*last3)
         two.send_first(*first2)
         one = PlaneSum(keep1, send1)
-    keep0, send0 = back_low((me, labels, dh, dse, emb, pre, phi, h0s, xp, s_down, s_time, rest))
+    keep0, send0 = back_low((me, labels, pad, dh, dse, emb, pre, phi, h0s, xp, s_down, s_time, rest))
     if direct:
         zero = PlaneSum(keep0, send0)
         one.send_first(*one.first())
         two.send_last(*two.last())
-        first0 = zero.first()
-        zero.send_first(*first0)
-        (small,) = gate([small], first0)
-        small = total_of(small, n)
+        zero.send_first(*zero.first())
         top = [two.total(), three.total()]
         high = column_sums(top, 2, z)
         one.send_last(*one.last())
         zero.send_last(*zero.last())
-        bottom = gate([zero.total(), one.total()], [small])
+        bottom = [zero.total(), one.total()]
         reduced = column_sums(bottom, 0, z) + high
         own = jnp.where(z < 2, jnp.where(z == 0, bottom[0], bottom[1]), jnp.where(z == 2, top[0], top[1]))
-        reduced = (reduced + own)[:SHARD].reshape(-1)
+        reduced = reduced + own
+        small = from_digits(reduced[SHARD : SHARD + 4])
+        reduced = reduced[:SHARD].reshape(-1)
     else:
-        small = total_of(small, n)
+        small = total_of(jnp.broadcast_to(small, (8, 4)), n)[0]
         both = [jnp.stack([wide(k), wide(s)], 1) for k, s in ((keep0, send0), (keep1, send1), (keep2, send2), (keep3, send3))]
         lines = jnp.stack(both).reshape(SHARDS, ROOM, LINE)[:, :SHARD].reshape(n, -1)
         reduced = lax.psum_scatter(lines, AXIS, scatter_dimension=0, tiled=True).reshape(-1)
     new_momentum = MOMENTUM * momentum + reduced
     new_master = master - LEARN_RATE * (reduced + MOMENTUM * new_momentum)
     new_ema = EMA_DECAY * ema + (1.0 - EMA_DECAY) * new_master
-    return (small[0, 0] / pixel_total, new_momentum, new_master, new_ema, small[0, 1:])
+    return (small[0] / pixel_total, new_momentum, new_master, new_ema, small[1:])
 
 
 def solution(mesh):

time: 484 us -> 464 us (0.959)
  other arithmetic: 61.1 us -> 52.2 us
  waiting for transfers between devices: 160 us -> 155 us
    ppermute x10 -> x5, waiting for transfers between devices: 14.5 us -> 0.03 us  [total_of(): lax.ppermute(values, AXIS, [(i, i ^ hop) for i in range(n)])]
    ppermute x31, waiting for transfers between devices: 31.1 us -> 36.6 us  [swap(): return lax.ppermute(values, AXIS, [(i, i ^ hop) for i in range(SHARDS)])]
    ppermute x10 -> x5, starting transfers between devices: 9.86 us -> 9.31 us  [total_of(): lax.ppermute(values, AXIS, [(i, i ^ hop) for i in range(n)])]
    unnamed x122 -> x112, local copies, waits for them, and re-layouts: 9.96 us -> 9.66 us
  transfers between devices with their start and end apart: 62 -> 57, of which waited for: 27 -> 19; matrix products, arithmetic and copies ran while one was open for 15% -> 12% of each run, Pallas kernels for 15% -> 15%
where the time goes in v5:
time: 464 us; the launch traced here: 457 us
  waiting for transfers between devices  155 us (33%)
  Pallas kernels  136 us (29%)
  starting transfers between devices  72.7 us (16%)
  other arithmetic  52.2 us (11%)
  local copies, waits for them, and re-layouts  22.4 us (5%)
  between operations  18.5 us (4%)
    ppermute x12, waiting for transfers between devices, climb(): return lax.ppermute(values, AXIS, pairs)  100 us
    pallas_call x4, Pallas kernels, back_call(): pl.pallas_call(kernel, out_shape=[plane, plane, *rest, *(sds(*o) for o in...  69.9 us
    pallas_call x2, Pallas kernels, forward_call(): pl.pallas_call(body, out_shape=outs, in_specs=[SM] * 2 + [VM] * 8 + [HB]...  66.4 us
    ppermute x31, waiting for transfers between devices, swap(): return lax.ppermute(values, AXIS, [(i, i ^ hop) for i in range(SHARDS)])  36.6 us
    ppermute x31, starting transfers between devices, swap(): return lax.ppermute(values, AXIS, [(i, i ^ hop) for i in range(SHARDS)])  28 us
    ppermute x8, waiting for transfers between devices, column_sums(): run = wide(lax.ppermute(low(value), AXIS, pairs))  18.1 us
    ppermute x12, starting transfers between devices, climb(): return lax.ppermute(values, AXIS, pairs)  17.7 us
    ppermute x8, starting transfers between devices, column_sums(): run = wide(lax.ppermute(low(value), AXIS, pairs))  17.6 us
  transfers between devices with their start and end apart: 57, of which 19 were waited for; matrix products, arithmetic and copies ran while one was open for 12% of the time, Pallas kernels for 15%

profile of v5, /device:TPU:0, one launch (start us, length us, event | category | flops | bytes accessed | tf_op | source)
XLA Modules:
  0.0 457.2 jit_solution(1531265420932334669)
XLA Ops:
  10.1 5.0 %collective-permute-start = (bf16[1760,128]{1,0:T(8,128)(2,1)S(1)}, bf16[1760,128]{1,0:T(8,128)(2,1)S(1)}, u32[]{:S(2)}, u32[]{:S(2)}) collective-permute-start(bf16[1760,128]{1,0:T(8,128)(2,1)S(1)} %slice_bitcast_fusion.1), channel_id=1, source_target_pairs={{0,8},{1,9},{2,10},{3,11},{4,12},{5,13},{6,14},{7,15},{8,16},{9,17... | collective-permute-start | bytes 1351688 | tf_op jit(solution)/shard_map/ppermute | solution.py:1264
  28.0 7.5 %collective-permute-done.1.refs_3_ = bf16[1760,128]{1,0:T(8,128)(2,1)S(1)} collective-permute-done((bf16[1760,128]{1,0:T(8,128)(2,1)S(1)}, bf16[1760,128]{1,0:T(8,128)(2,1)S(1)}, u32[]{:S(2)}, u32[]{:S(2)}) %collective-permute-start.1) | collective-permute-done | bytes 450592 | tf_op jit(solution)/shard_map/ppermute | solution.py:1264
  44.2 6.8 %collective-permute-done.4 = bf16[1760,128]{1,0:T(8,128)(2,1)} collective-permute-done((bf16[1760,128]{1,0:T(8,128)(2,1)S(1)}, bf16[1760,128]{1,0:T(8,128)(2,1)}, u32[]{:S(2)}, u32[]{:S(2)}) %collective-permute-start.4) | collective-permute-done | bytes 450592 | tf_op jit(solution)/shard_map/ppermute | solution.py:1264
  69.6 16.2 %collective-permute-done.5.refs_2_ = bf16[1760,128]{1,0:T(8,128)(2,1)S(1)} collective-permute-done((bf16[1760,128]{1,0:T(8,128)(2,1)}, bf16[1760,128]{1,0:T(8,128)(2,1)S(1)}, u32[]{:S(2)}, u32[]{:S(2)}) %collective-permute-start.5) | collective-permute-done | bytes 450592 | tf_op jit(solution)/shard_map/ppermute | solution.py:1264
  98.4 21.6 %collective-permute-done.17 = bf16[4,512,128]{2,1,0:T(8,128)(2,1)S(1)} collective-permute-done((bf16[4,512,128]{2,1,0:T(8,128)(2,1)}, bf16[4,512,128]{2,1,0:T(8,128)(2,1)S(1)}, u32[]{:S(2)}, u32[]{:S(2)}) %collective-permute-start.17) | collective-permute-done | bytes 524320 | tf_op jit(solution)/shard_map/ppermute | solution.py:1264
  120.8 12.6 %collective-permute-done.20 = bf16[4,512,128]{2,1,0:T(8,128)(2,1)S(1)} collective-permute-done((bf16[4,512,128]{2,1,0:T(8,128)(2,1)}, bf16[4,512,128]{2,1,0:T(8,128)(2,1)S(1)}, u32[]{:S(2)}, u32[]{:S(2)}) %collective-permute-start.20) | collective-permute-done | bytes 524320 | tf_op jit(solution)/shard_map/ppermute | solution.py:1264
  142.5 17.3 %collective-permute-done.21 = bf16[4,512,128]{2,1,0:T(8,128)(2,1)S(1)} collective-permute-done((bf16[4,512,128]{2,1,0:T(8,128)(2,1)S(1)}, bf16[4,512,128]{2,1,0:T(8,128)(2,1)S(1)}, u32[]{:S(2)}, u32[]{:S(2)}) %collective-permute-start.21) | collective-permute-done | bytes 524320 | tf_op jit(solution)/shard_map/ppermute | solution.py:1264
  161.1 18.3 %collective-permute-done.22 = bf16[4,512,128]{2,1,0:T(8,128)(2,1)S(1)} collective-permute-done((bf16[4,512,128]{2,1,0:T(8,128)(2,1)S(1)}, bf16[4,512,128]{2,1,0:T(8,128)(2,1)S(1)}, u32[]{:S(2)}, u32[]{:S(2)}) %collective-permute-start.22) | collective-permute-done | bytes 524320 | tf_op jit(solution)/shard_map/ppermute | solution.py:1264
  186.6 31.3 %forward_plain.1.refs_1_ = f32[512,128]{1,0:T(8,128)} custom-call(s32[1]{0:T(128)} %constant.141.clone.1.refs_0_, s32[2]{0:T(128)} %refs_1_.6, bf16[512,128]{1,0:T(8,128)(2,1)} %pad.30.refs_2_.refs_4_, f32[8,192]{1,0:T(8,128)} %select_maximum_fusion.1.refs_3_.refs_5_, bf16[384,384]{1,0:T(8,128)(2,1)} %constant.156.clone.refs_4_.refs_3_.refs_7_, ...), custom_call_target="tpu_custom_call" | custom-call | flops 8000000000 | bytes 40000000 | tf_op jit(solution)/shard_map/forward_plain/pallas_call | solution.py:718
  218.1 35.1 %forward_save.1 = (f32[512,128]{1,0:T(8,128)}, bf16[2048,256]{1,0:T(8,128)(2,1)}, f32[512,384]{1,0:T(8,128)}, f32[512,384]{1,0:T(8,128)}, f32[512,384]{1,0:T(8,1...) custom-call(s32[1]{0:T(128)} %bitcast.refs_0_, ...), custom_call_target="tpu_custom_call" | custom-call | flops 8000000000 | bytes 40000000 | tf_op jit(solution)/shard_map/forward_save/pallas_call | solution.py:718
  253.2 3.6 select_reduce_fusion
  261.6 32.1 %back_top.1 = (bf16[4,2272,128]{2,1,0:T(8,128)(2,1)}, bf16[4,2272,128]{2,1,0:T(8,128)(2,1)}, f32[11968,128]{1,0:T(8,128)}, f32[512,384]{1,0:T(8,128)}, f32[8,768]{1,0:T(8,128)}) custom-call(s32[1]{0:T(128)} %bitcast.refs_0_, f32[8,128]{1,0:T(8,128)} %pad.35.refs_1_.refs_2_, f32[512,128]{1,0:T(8,128)} %pad.36.refs_2_, ...), custom_call_target="tpu_custom_call" | custom-call | flops 8000000000 | bytes 40000000 | tf_op jit(solution)/shard_map/back_top/pallas_call | solution.py:1132
  293.8 14.4 %back_b.1 = (bf16[4,2272,128]{2,1,0:T(8,128)(2,1)}, bf16[4,2272,128]{2,1,0:T(8,128)(2,1)}, f32[4240,128]{1,0:T(8,128)}, f32[512,384]{1,0:T(8,128)}, f32[8,768]{1,0:T(8,128)}, /*index=5*/f32[8,384]{1,0:T(8,128)}) custom-call(s32[1]{0:T(128)} %bitcast.refs_0_, f32[8,128]{1,0:T(8,128)} %pad.35.refs_1_.refs_2_, f32[512,384]{1,0:T(8,128)} %get-tuple-element.67.refs_2_, ...), custom_call_target="tpu_custom_call" | custom-call | flops 8000000000 | bytes 40000000 | tf_op jit(solution)/shard_map/back_b/pallas_call | solution.py:1132
  317.9 12.9 %back_c.1 = (bf16[4,2272,128]{2,1,0:T(8,128)(2,1)}, bf16[4,2272,128]{2,1,0:T(8,128)(2,1)}, f32[1120,128]{1,0:T(8,128)}, f32[512,384]{1,0:T(8,128)}, f32[8,768]{1,0:T(8,128)}) custom-call(s32[1]{0:T(128)} %bitcast.refs_0_, f32[8,128]{1,0:T(8,128)} %pad.35.refs_1_.refs_2_, f32[512,384]{1,0:T(8,128)} %get-tuple-element.67.refs_2_, f32[512,384]{1,0:T(8,128)} %gate.8.refs_3_, ...), custom_call_target="tpu_custom_call" | custom-call | flops 8000000000 | bytes 40000000 | tf_op jit(solution)/shard_map/back_c/pallas_call | solution.py:1132
  335.2 10.5 %back_low.1 = (bf16[4,2272,128]{2,1,0:T(8,128)(2,1)}, bf16[4,2272,128]{2,1,0:T(8,128)(2,1)}) custom-call(s32[1]{0:T(128)} %bitcast.refs_0_, s32[2]{0:T(128)} %refs_1_.6, f32[8,128]{1,0:T(8,128)} %pad.35.refs_1_.refs_2_, f32[512,384]{1,0:T(8,128)} %gate.9.refs_3_, f32[8,768]{1,0:T(8,128)} %get-tuple-element.84.refs_4_, ...), custom_call_target="tpu_custom_call" | custom-call | flops 8000000000 | bytes 40000000 | tf_op jit(solution)/shard_map/back_low/pallas_call | solution.py:1132
  351.4 5.5 %collective-permute-done.47 = bf16[1136,128]{1,0:T(8,128)(2,1)S(1)} collective-permute-done((bf16[1136,128]{1,0:T(8,128)(2,1)S(1)}, bf16[1136,128]{1,0:T(8,128)(2,1)S(1)}, u32[]{:S(2)}, u32[]{:S(2)}) %collective-permute-start.47) | collective-permute-done | bytes 290848 | tf_op jit(solution)/shard_map/ppermute | solution.py:1230
  368.2 8.9 %collective-permute-done.38 = bf16[2,1136,128]{2,1,0:T(8,128)(2,1)S(1)} collective-permute-done((bf16[2,1136,128]{2,1,0:T(8,128)(2,1)S(1)}, bf16[2,1136,128]{2,1,0:T(8,128)(2,1)S(1)}, u32[]{:S(2)}, u32[]{:S(2)}) %collective-permute-start.38) | collective-permute-done | bytes 581664 | tf_op jit(solution)/shard_map/ppermute | solution.py:1230
  380.9 6.9 %collective-permute-done.33 = bf16[2,1136,128]{2,1,0:T(8,128)(2,1)S(1)} collective-permute-done((bf16[2,1136,128]{2,1,0:T(8,128)(2,1)S(1)}, bf16[2,1136,128]{2,1,0:T(8,128)(2,1)S(1)}, u32[]{:S(2)}, u32[]{:S(2)}) %collective-permute-start.33) | collective-permute-done | bytes 581664 | tf_op jit(solution)/shard_map/ppermute | solution.py:1230
  392.2 4.8 %collective-permute-done.39 = bf16[1136,128]{1,0:T(8,128)(2,1)S(1)} collective-permute-done((bf16[1136,128]{1,0:T(8,128)(2,1)S(1)}, bf16[1136,128]{1,0:T(8,128)(2,1)S(1)}, u32[]{:S(2)}, u32[]{:S(2)}) %collective-permute-start.39) | collective-permute-done | bytes 290848 | tf_op jit(solution)/shard_map/ppermute | solution.py:1230
  408.7 7.4 %collective-permute-done.53 = bf16[2272,128]{1,0:T(8,128)(2,1)S(1)} collective-permute-done((bf16[2272,128]{1,0:T(8,128)(2,1)S(1)}, bf16[2272,128]{1,0:T(8,128)(2,1)S(1)}, u32[]{:S(2)}, u32[]{:S(2)}) %collective-permute-start.53) | collective-permute-done | bytes 581664 | tf_op jit(solution)/shard_map/ppermute | solution.py:1387
  418.6 8.9 %collective-permute-start.42 = (bf16[2272,128]{1,0:T(8,128)(2,1)}, bf16[2272,128]{1,0:T(8,128)(2,1)}, u32[]{:S(2)}, u32[]{:S(2)}) collective-permute-start(bf16[2272,128]{1,0:T(8,128)(2,1)} %get-tuple-element.138), channel_id=1, source_target_pairs={{0,8},{1,9},{2,10},{3,11},{4,12},{5,13},{6,14},{7,15}} | collective-permute-start | bytes 1744904 | tf_op jit(solution)/shard_map/ppermute | solution.py:1387
  429.8 4.4 collective-permute-done.42
  434.2 6.2 %collective-permute-done.45 = bf16[2272,128]{1,0:T(8,128)(2,1)} collective-permute-done((bf16[2272,128]{1,0:T(8,128)(2,1)}, bf16[2272,128]{1,0:T(8,128)(2,1)}, u32[]{:S(2)}, u32[]{:S(2)}) %collective-permute-start.45) | collective-permute-done | bytes 581664 | tf_op jit(solution)/shard_map/ppermute | solution.py:1387
  444.6 4.4 multiply_add_fusion
  (301 shorter events, 136.3 us)
Async XLA Ops:
  7.2 179.4 %all-gather.2.cloned.1.call-start = ((), (), s32[]{:S(2)}) async-start(), calls=%async_computation | async-start | bytes 19193856 | tf_op jit(solution)/shard_map/all_gather | solution.py:1314
  39.3 23.9 %collective-permute-start.11 = (bf16[2,512,128]{2,1,0:T(8,128)(2,1)S(1)}, bf16[2,512,128]{2,1,0:T(8,128)(2,1)S(1)}, u32[]{:S(2)}, u32[]{:S(2)}) collective-permute-start(bf16[2,512,128]{2,1,0:T(8,128)(2,1)S(1)} %pad_maximum_fusion.17), channel_id=1, source_target_pairs={{0,2},{1,3},{2,0},{3,1},{4,6},{5,7},{6,4},{7,5},{8,10},{9,11},{10,... | collective-permute-start | bytes 786440 | tf_op jit(solution)/shard_map/ppermute | solution.py:1230
  43.6 26.0 %collective-permute-start.3 = (bf16[1760,128]{1,0:T(8,128)(2,1)}, bf16[1760,128]{1,0:T(8,128)(2,1)S(1)}, u32[]{:S(2)}, u32[]{:S(2)}) collective-permute-start(bf16[1760,128]{1,0:T(8,128)(2,1)} %collective-permute-done.2), channel_id=1, source_target_pairs={{16,24},{17,25},{18,26},{19,27},{20,28},{21,29},{22,30},{23,31}} | collective-permute-start | bytes 1351688 | tf_op jit(solution)/shard_map/ppermute | solution.py:1264
  51.0 34.7 %collective-permute-start.5 = (bf16[1760,128]{1,0:T(8,128)(2,1)}, bf16[1760,128]{1,0:T(8,128)(2,1)S(1)}, u32[]{:S(2)}, u32[]{:S(2)}) collective-permute-start(bf16[1760,128]{1,0:T(8,128)(2,1)} %collective-permute-done.4), channel_id=1, source_target_pairs={{8,0},{9,1},{10,2},{11,3},{12,4},{13,5},{14,6},{15,7}} | collective-permute-start | bytes 1351688 | tf_op jit(solution)/shard_map/ppermute | solution.py:1264
  89.2 45.4 %collective-permute-start.6 = (bf16[4,880,128]{2,1,0:T(8,128)(2,1)}, bf16[4,880,128]{2,1,0:T(8,128)(2,1)S(1)}, u32[]{:S(2)}, u32[]{:S(2)}) collective-permute-start(bf16[4,880,128]{2,1,0:T(8,128)(2,1)} %get-tuple-element.145), channel_id=1, source_target_pairs={{0,2},{1,3},{2,0},{3,1},{4,6},{5,7},{6,4},{7,5},{8,10},{9,11},{10,... | collective-permute-start | bytes 2703368 | tf_op jit(solution)/shard_map/ppermute | solution.py:1230
  91.3 46.2 %collective-permute-start.8 = (bf16[4,880,128]{2,1,0:T(8,128)(2,1)}, bf16[4,880,128]{2,1,0:T(8,128)(2,1)}, u32[]{:S(2)}, u32[]{:S(2)}) collective-permute-start(bf16[4,880,128]{2,1,0:T(8,128)(2,1)} %get-tuple-element.144), channel_id=1, source_target_pairs={{0,4},{1,5},{2,6},{3,7},{4,0},{5,1},{6,2},{7,3},{8,12},{9,13},{10,... | collective-permute-start | bytes 2703368 | tf_op jit(solution)/shard_map/ppermute | solution.py:1230
  95.6 24.5 %collective-permute-start.17 = (bf16[4,512,128]{2,1,0:T(8,128)(2,1)}, bf16[4,512,128]{2,1,0:T(8,128)(2,1)S(1)}, u32[]{:S(2)}, u32[]{:S(2)}) collective-permute-start(bf16[4,512,128]{2,1,0:T(8,128)(2,1)} %gate.7), channel_id=1, source_target_pairs={{0,8},{1,9},{2,10},{3,11},{4,12},{5,13},{6,14},{7,15},{8,16},{9,17... | collective-permute-start | bytes 1572872 | tf_op jit(solution)/shard_map/ppermute | solution.py:1264
  97.1 36.2 %collective-permute-start.20 = (bf16[4,512,128]{2,1,0:T(8,128)(2,1)}, bf16[4,512,128]{2,1,0:T(8,128)(2,1)S(1)}, u32[]{:S(2)}, u32[]{:S(2)}) collective-permute-start(bf16[4,512,128]{2,1,0:T(8,128)(2,1)} %gate.7), channel_id=1, source_target_pairs={{24,16},{25,17},{26,18},{27,19},{28,20},{29,21},{30,22},{31,23},{1... | collective-permute-start | bytes 1572872 | tf_op jit(solution)/shard_map/ppermute | solution.py:1264
  120.1 21.7 %collective-permute-start.18 = (bf16[4,512,128]{2,1,0:T(8,128)(2,1)S(1)}, bf16[4,512,128]{2,1,0:T(8,128)(2,1)S(1)}, u32[]{:S(2)}, u32[]{:S(2)}) collective-permute-start(bf16[4,512,128]{2,1,0:T(8,128)(2,1)S(1)} %collective-permute-done.17), channel_id=1, source_target_pairs={{8,16},{9,17},{10,18},{11,19},{12,20},{13,21},{14,22},{15,23},{16,... | collective-permute-start | bytes 1572872 | tf_op jit(solution)/shard_map/ppermute | solution.py:1264
  133.4 26.4 %collective-permute-start.21 = (bf16[4,512,128]{2,1,0:T(8,128)(2,1)S(1)}, bf16[4,512,128]{2,1,0:T(8,128)(2,1)S(1)}, u32[]{:S(2)}, u32[]{:S(2)}) collective-permute-start(bf16[4,512,128]{2,1,0:T(8,128)(2,1)S(1)} %collective-permute-done.20), channel_id=1, source_target_pairs={{16,8},{17,9},{18,10},{19,11},{20,12},{21,13},{22,14},{23,15},{8,0... | collective-permute-start | bytes 1572872 | tf_op jit(solution)/shard_map/ppermute | solution.py:1264
  136.1 48.0 %collective-permute-start.7 = (bf16[2,4,880,128]{3,2,1,0:T(8,128)(2,1)}, bf16[2,4,880,128]{3,2,1,0:T(8,128)(2,1)}, u32[]{:S(2)}, u32[]{:S(2)}) collective-permute-start(bf16[2,4,880,128]{3,2,1,0:T(8,128)(2,1)} %pad_maximum_fusion.2.refs_10_), channel_id=1, source_target_pairs={{0,4},{1,5},{2,6},{3,7},{4,0},{5,1},{6,2},{7,3},{8,12},{9,13},{10,... | collective-permute-start | bytes 5406728 | tf_op jit(solution)/shard_map/ppermute | solution.py:1230
  140.3 43.9 %collective-permute-start.9 = (bf16[2,4,880,128]{3,2,1,0:T(8,128)(2,1)}, bf16[2,4,880,128]{3,2,1,0:T(8,128)(2,1)}, u32[]{:S(2)}, u32[]{:S(2)}) collective-permute-start(bf16[2,4,880,128]{3,2,1,0:T(8,128)(2,1)} %pad_maximum_fusion.3.refs_12_), channel_id=1, source_target_pairs={{0,2},{1,3},{2,0},{3,1},{4,6},{5,7},{6,4},{7,5},{8,10},{9,11},{10,... | collective-permute-start | bytes 5406728 | tf_op jit(solution)/shard_map/ppermute | solution.py:1230
  180.0 38.0 %collective-permute-start.27 = (bf16[4,4,512,128]{3,2,1,0:T(8,128)(2,1)S(1)}, bf16[4,4,512,128]{3,2,1,0:T(8,128)(2,1)}, u32[]{:S(2)}, u32[]{:S(2)}) collective-permute-start(bf16[4,4,512,128]{3,2,1,0:T(8,128)(2,1)S(1)} %pad_maximum_fusion.refs_14_), channel_id=1, source_target_pairs={{0,1},{1,0},{2,3},{3,2},{4,5},{5,4},{6,7},{7,6},{8,9},{9,8},{10,11... | collective-permute-start | bytes 6291464 | tf_op jit(solution)/shard_map/ppermute | solution.py:1230
  180.0 37.9 %collective-permute-start.23 = (bf16[2,4,880,128]{3,2,1,0:T(8,128)(2,1)}, bf16[2,4,880,128]{3,2,1,0:T(8,128)(2,1)}, u32[]{:S(2)}, u32[]{:S(2)}) collective-permute-start(bf16[2,4,880,128]{3,2,1,0:T(8,128)(2,1)} %pad_maximum_fusion.2.refs_10_), channel_id=1, source_target_pairs={{0,1},{1,0},{2,3},{3,2},{4,5},{5,4},{6,7},{7,6},{8,9},{9,8},{10,11... | collective-permute-start | bytes 5406728 | tf_op jit(solution)/shard_map/ppermute | solution.py:1230
  180.5 37.4 %collective-permute-start.25 = (bf16[2,4,880,128]{3,2,1,0:T(8,128)(2,1)}, bf16[2,4,880,128]{3,2,1,0:T(8,128)(2,1)}, u32[]{:S(2)}, u32[]{:S(2)}) collective-permute-start(bf16[2,4,880,128]{3,2,1,0:T(8,128)(2,1)} %pad_maximum_fusion.3.refs_12_), channel_id=1, source_target_pairs={{0,1},{1,0},{2,3},{3,2},{4,5},{5,4},{6,7},{7,6},{8,9},{9,8},{10,11... | collective-permute-start | bytes 5406728 | tf_op jit(solution)/shard_map/ppermute | solution.py:1230
  184.2 33.8 %collective-permute-start.24 = (bf16[2,4,880,128]{3,2,1,0:T(8,128)(2,1)}, bf16[2,4,880,128]{3,2,1,0:T(8,128)(2,1)}, u32[]{:S(2)}, u32[]{:S(2)}) collective-permute-start(bf16[2,4,880,128]{3,2,1,0:T(8,128)(2,1)} %collective-permute-done.7.refs_11_), channel_id=1, source_target_pairs={{0,1},{1,0},{2,3},{3,2},{4,5},{5,4},{6,7},{7,6},{8,9},{9,8},{10,11... | collective-permute-start | bytes 5406728 | tf_op jit(solution)/shard_map/ppermute | solution.py:1230
  184.2 33.8 %collective-permute-start.26 = (bf16[2,4,880,128]{3,2,1,0:T(8,128)(2,1)}, bf16[2,4,880,128]{3,2,1,0:T(8,128)(2,1)}, u32[]{:S(2)}, u32[]{:S(2)}) collective-permute-start(bf16[2,4,880,128]{3,2,1,0:T(8,128)(2,1)} %collective-permute-done.9.refs_13_), channel_id=1, source_target_pairs={{0,1},{1,0},{2,3},{3,2},{4,5},{5,4},{6,7},{7,6},{8,9},{9,8},{10,11... | collective-permute-start | bytes 5406728 | tf_op jit(solution)/shard_map/ppermute | solution.py:1230
  315.6 30.1 %collective-permute-start.46 = (bf16[2,1136,128]{2,1,0:T(8,128)(2,1)S(1)}, bf16[2,1136,128]{2,1,0:T(8,128)(2,1)}, u32[]{:S(2)}, u32[]{:S(2)}) collective-permute-start(bf16[2,1136,128]{2,1,0:T(8,128)(2,1)S(1)} %pad_maximum_fusion.10.refs_3_), channel_id=1, source_target_pairs={{0,2},{1,3},{2,0},{3,1},{4,6},{5,7},{6,4},{7,5},{8,10},{9,11},{10,... | collective-permute-start | bytes 1744904 | tf_op jit(solution)/shard_map/ppermute | solution.py:1230
  317.0 28.8 %collective-permute-start.48 = (bf16[2,1136,128]{2,1,0:T(8,128)(2,1)S(1)}, bf16[2,1136,128]{2,1,0:T(8,128)(2,1)}, u32[]{:S(2)}, u32[]{:S(2)}) collective-permute-start(bf16[2,1136,128]{2,1,0:T(8,128)(2,1)S(1)} %pad_maximum_fusion.11.refs_4_), channel_id=1, source_target_pairs={{0,4},{1,5},{2,6},{3,7},{4,0},{5,1},{6,2},{7,3},{8,12},{9,13},{10,... | collective-permute-start | bytes 1744904 | tf_op jit(solution)/shard_map/ppermute | solution.py:1230
  330.8 28.4 %collective-permute-start.37 = (bf16[4,2272,128]{2,1,0:T(8,128)(2,1)}, bf16[4,2272,128]{2,1,0:T(8,128)(2,1)}, u32[]{:S(2)}, u32[]{:S(2)}) collective-permute-start(bf16[4,2272,128]{2,1,0:T(8,128)(2,1)} %get-tuple-element.94), channel_id=1, source_target_pairs={{0,1},{1,0},{2,3},{3,2},{4,5},{5,4},{6,7},{7,6},{8,9},{9,8},{10,11... | collective-permute-start | bytes 6979592 | tf_op jit(solution)/shard_map/ppermute | solution.py:1230
  363.7 24.1 %collective-permute-start.33 = (bf16[2,1136,128]{2,1,0:T(8,128)(2,1)S(1)}, bf16[2,1136,128]{2,1,0:T(8,128)(2,1)S(1)}, u32[]{:S(2)}, u32[]{:S(2)}) collective-permute-start(bf16[2,1136,128]{2,1,0:T(8,128)(2,1)S(1)} %pad_maximum_fusion.12), channel_id=1, source_target_pairs={{0,2},{1,3},{2,0},{3,1},{4,6},{5,7},{6,4},{7,5},{8,10},{9,11},{10,... | collective-permute-start | bytes 1744904 | tf_op jit(solution)/shard_map/ppermute | solution.py:1230
  364.6 26.1 %collective-permute-start.35 = (bf16[2,1136,128]{2,1,0:T(8,128)(2,1)S(1)}, bf16[2,1136,128]{2,1,0:T(8,128)(2,1)S(1)}, u32[]{:S(2)}, u32[]{:S(2)}) collective-permute-start(bf16[2,1136,128]{2,1,0:T(8,128)(2,1)S(1)} %pad_maximum_fusion.13), channel_id=1, source_target_pairs={{0,4},{1,5},{2,6},{3,7},{4,0},{5,1},{6,2},{7,3},{8,12},{9,13},{10,... | collective-permute-start | bytes 1744904 | tf_op jit(solution)/shard_map/ppermute | solution.py:1230
  366.7 63.1 %collective-permute-start.55 = (bf16[2272,128]{1,0:T(8,128)(2,1)}, bf16[2272,128]{1,0:T(8,128)(2,1)}, u32[]{:S(2)}, u32[]{:S(2)}) collective-permute-start(bf16[2272,128]{1,0:T(8,128)(2,1)} %get-tuple-element.141), channel_id=1, source_target_pairs={{24,16},{25,17},{26,18},{27,19},{28,20},{29,21},{30,22},{31,23}} | collective-permute-start | bytes 1744904 | tf_op jit(solution)/shard_map/ppermute | solution.py:1387
  377.0 28.8 %collective-permute-start.52 = (bf16[2272,128]{1,0:T(8,128)(2,1)S(1)}, bf16[2272,128]{1,0:T(8,128)(2,1)S(1)}, u32[]{:S(2)}, u32[]{:S(2)}) collective-permute-start(bf16[2272,128]{1,0:T(8,128)(2,1)S(1)} %get-tuple-element.140), channel_id=1, source_target_pairs={{0,8},{1,9},{2,10},{3,11},{4,12},{5,13},{6,14},{7,15}} | collective-permute-start | bytes 1744904 | tf_op jit(solution)/shard_map/ppermute | solution.py:1387
  (81 other events, 1292.4 us)
Sparse Core Ops, SparseCore 0:
  11.4 165.0 all-gather.1

commit v6 on v5

--- a/solution.py
+++ b/solution.py
@@ -464,20 +464,21 @@
     held, wide, w_ref, w_sq, sbuf, pbuf, h0p, table, w_in, b_out, sems, save_sem = refs[25 if save else 16 :]
     src = Lines(held, wide)
     arriving = []
-    for plane in range(SHARDS // PLANE):
+    for plane in range(TALL):
         copies = []
         for n, lead, r, row, rows in moves:
             target = held.at[plane, r ^ me[0], pl.ds(row, rows), :]
             source = pieces[n].at[plane, lead] if flip[n] else pieces[n].at[lead, plane]
             copies.append(pltpu.make_async_copy(source, target, sems.at[plane]))
-        for copy in copies:
-            copy.start()
         arriving.append(copies)
 
     def arrive(plane):
         for copy in arriving[plane]:
             copy.wait()
 
+    for plane in range(TALL):
+        for copy in arriving[plane]:
+            copy.start()
     pending = []
 
     def keep(source, target):
@@ -867,9 +868,9 @@
 
 
 def back_top_kernel(*refs):
-    me, pad, df, wz, gm, sel, gat, tile, expand, vec, mod, emb, h4, u2, h3, qkv, mixed, h2, s22, s21, s_attn, s_emb = refs[:22]
-    keep, send, rest, dh, dse = refs[22:27]
-    g, slots, sbuf, pbuf, dx, at_ref, stage, sems, out_sems, w_sq, dqkv, dm, sq_sem = refs[27:]
+    me, total, f_o, f_t, base_o, base_t, out_o, out_t, mask, inverse, wz, gm, sel, gat, tile, expand, vec, mod, emb, h4, u2, h3, qkv, mixed, h2, s22, s21, s_attn, s_emb = refs[:29]
+    keep, send, rest, dh, dse, pad = refs[29:35]
+    g, slots, sbuf, pbuf, dx, at_ref, stage, sems, out_sems, w_sq, dqkv, dm, sq_sem = refs[35:]
     base = BASE_ONE
     weights = Weights([s22, s21, s_attn], slots, sems)
     weights.begin()
@@ -884,7 +885,10 @@
     scales = block_scales(vec, V_FG)
     norm_to(pbuf, h4, stats, scales, True)
     transpose_to(at_ref, pbuf)
-    spread = dot(df[...].astype(BF16), gat[...], NT)
+    gap = (base_o[...] + out_o[...] * f_o[:, :12]) - (base_t[...] + out_t[...] * f_t[:, :12])
+    loss = jnp.sum(mask[...] * (gap * gap))
+    df = jnp.pad(out_o[...] * 2.0 * mask[...] * gap / total[0], ((0, 0), (0, LINE - 12)))
+    spread = dot(df.astype(BF16), gat[...], NT)
     dt = jnp.zeros((ROWS, LINE), F32)
     for shift in range(9):
         inside, by = upsample_masks(shift)
@@ -901,7 +905,14 @@
     for j in range(9):
         g[pl.ds(TAIL - base + j, 9, stride=9), :] = d_taps[0:9, j * LINE : (j + 1) * LINE]
     b_row = AT.bias_out - base
-    g[b_row : b_row + 1, :] = dot3(eight(colsum(df, 0, ROWS)), tile[...], NT)[0:1]
+    bias = dot3(eight(rowsum(df)), tile[...], NT)[0:1]
+    g[b_row : b_row + 1, :] = bias
+    row = lax.broadcasted_iota(jnp.int32, (8, 1), 0)
+    lane = lax.broadcasted_iota(jnp.int32, (1, LINE), 1)
+    values = jnp.where(row == 0, loss, 0.0)
+    for c in range(3):
+        values = values + jnp.where(row == c + 1, jnp.sum(jnp.where(lane == c, bias, 0.0)), 0.0)
+    pad[...] = to_digits(values, inverse[...])
 
     def emit_first(r, v):
         dh[pl.ds(r, CHUNK), :] = v
@@ -1149,7 +1160,7 @@
     scratch = [vmem((EMB_DIM, EMB_DIM), BF16), vmem((ROWS, 3 * CH_MID), BF16), vmem(*WIDE_ROW), DMA]
     lines = ALL_LINES - BASE_ONE
     return back_call(
-        back_top_kernel, "back_top", lines, 2, args, 1, 4, PLANES[3] - BASE_ONE, [ACT, WIDE_ROW], scratch
+        back_top_kernel, "back_top", lines, 2, args, 2, 4, PLANES[3] - BASE_ONE, [ACT, WIDE_ROW, ((8, LINE), F32)], scratch
     )
 
 
@@ -1322,13 +1333,16 @@
     return np.array([8.0 ** (k - 40) if k < 82 else 0.0 for k in range(LINE)], np.float32)[None]
 
 
-def to_digits(values):
+def inverse_weights():
     weights = digit_weights()
-    inverse = np.where(weights > 0, 1.0 / np.where(weights > 0, weights, 1.0), 0.0).astype(np.float32)
-    size = jnp.abs(values)[:, None] * inverse
+    return np.where(weights > 0, 1.0 / np.where(weights > 0, weights, 1.0), 0.0).astype(np.float32)
+
+
+def to_digits(values, inverse):
+    size = jnp.abs(values) * inverse
     digit = jnp.floor(size) - 8.0 * jnp.floor(size * 0.125)
     digit = jnp.where(size < 2.0**27, digit, 0.0)
-    return jnp.where(values[:, None] < 0, -digit, digit)
+    return jnp.where(values < 0, -digit, digit)
 
 
 def from_digits(rows):
@@ -1430,21 +1444,14 @@
         (x_in,) = gate([in_hi[1]], [model_t])
         in_hi = (in_hi[0], x_in, *in_hi[2:])
     model_o, saved = per_part(me, labels, online, in_hi, True, tables)
-    online_out = in_hi[0] + in_hi[3] * model_o[:, :12]
-    target_out = in_lo[0] + in_lo[3] * model_t[:, :12]
-    phi, out_scale = in_hi[2], in_hi[3]
-    gap = online_out - target_out
-    local_loss = jnp.sum(mask * jnp.square(gap))
-    grad_model = out_scale * 2.0 * mask * gap / pixel_total
-    bias_out = jnp.sum(grad_model.reshape(ROWS, 4, 3), axis=(0, 1))
+    phi = in_hi[2]
     (h0s, h1, u1, h2, qkv, mixed, h3, u2, h4, vec, mod, emb, pre, wz, xp) = saved[:15]
     s_time, s_emb1, s_emb2, s_down, s11, s12, s_attn, s21, s22 = saved[15:]
     gm = tables[0]
-    df = jnp.pad(grad_model, ((0, 0), (0, LINE - 12)))
-    small = jnp.concatenate([local_loss[None], bias_out])
-    pad = jnp.pad(to_digits(small), ((0, 4), (0, 0)))
-    keep3, send3, rest, dh, dse = back_top(
-        (me, pad, df, wz, *tables[:5], vec, mod, emb, h4, u2, h3, qkv, mixed, h2, s22, s21, s_attn, s_emb2)
+    inverse = jnp.asarray(inverse_weights())
+    losses = (model_o, model_t, in_hi[0], in_lo[0], in_hi[3], in_lo[3], mask, inverse)
+    keep3, send3, rest, dh, dse, pad = back_top(
+        (me, pixel_total[None], *losses, wz, *tables[:5], vec, mod, emb, h4, u2, h3, qkv, mixed, h2, s22, s21, s_attn, s_emb2)
     )
     if direct:
         three = PlaneSum(keep3, send3)
@@ -1478,7 +1485,7 @@
         small = from_digits(reduced[SHARD : SHARD + 4])
         reduced = reduced[:SHARD].reshape(-1)
     else:
-        small = total_of(jnp.broadcast_to(small, (8, 4)), n)[0]
+        small = from_digits(total_of(pad, n)[:4])
         both = [jnp.stack([wide(k), wide(s)], 1) for k, s in ((keep0, send0), (keep1, send1), (keep2, send2), (keep3, send3))]
         lines = jnp.stack(both).reshape(SHARDS, ROOM, LINE)[:, :SHARD].reshape(n, -1)
         reduced = lax.psum_scatter(lines, AXIS, scatter_dimension=0, tiled=True).reshape(-1)

time: 464 us -> 453 us (0.976)
  other arithmetic: 52.2 us -> 43.6 us
    reduce_sum x3 -> x0, other arithmetic: 5.38 us -> none  [the longest x1 3.57 us: per_device(): local_loss = jnp.sum(mask * jnp.square(gap))]
    unnamed x112 -> x80, local copies, waits for them, and re-layouts: 9.66 us -> 7.49 us
  transfers between devices with their start and end apart: 57 -> 57, of which waited for: 19 -> 21; matrix products, arithmetic and copies ran while one was open for 12% -> 12% of each run, Pallas kernels for 15% -> 15%
where the time goes in v6:
time: 453 us; the launch traced here: 446 us
  waiting for transfers between devices  158 us (35%)
  Pallas kernels  136 us (30%)
  starting transfers between devices  71.8 us (16%)
  other arithmetic  43.6 us (10%)
  local copies, waits for them, and re-layouts  18.8 us (4%)
  between operations  18.3 us (4%)
    ppermute x12, waiting for transfers between devices, climb(): return lax.ppermute(values, AXIS, pairs)  103 us
    pallas_call x4, Pallas kernels, back_call(): pl.pallas_call(kernel, out_shape=[plane, plane, *rest, *(sds(*o) for o in...  69.4 us
    pallas_call x2, Pallas kernels, forward_call(): pl.pallas_call(body, out_shape=outs, in_specs=[SM] * 2 + [VM] * 8 + [HB]...  66.3 us
    ppermute x31, waiting for transfers between devices, swap(): return lax.ppermute(values, AXIS, [(i, i ^ hop) for i in range(SHARDS)])  36.5 us
    ppermute x31, starting transfers between devices, swap(): return lax.ppermute(values, AXIS, [(i, i ^ hop) for i in range(SHARDS)])  28.5 us
    ppermute x8, waiting for transfers between devices, column_sums(): run = wide(lax.ppermute(low(value), AXIS, pairs))  18 us
    ppermute x12, starting transfers between devices, climb(): return lax.ppermute(values, AXIS, pairs)  17.7 us
    ppermute x8, starting transfers between devices, column_sums(): run = wide(lax.ppermute(low(value), AXIS, pairs))  17.5 us
  transfers between devices with their start and end apart: 57, of which 21 were waited for; matrix products, arithmetic and copies ran while one was open for 12% of the time, Pallas kernels for 15%

profile of v6, /device:TPU:0, one launch (start us, length us, event | category | flops | bytes accessed | tf_op | source)
XLA Modules:
  0.0 446.4 jit_solution(11895200852550062652)
XLA Ops:
  10.1 5.0 %collective-permute-start.5 = (bf16[1760,128]{1,0:T(8,128)(2,1)S(1)}, bf16[1760,128]{1,0:T(8,128)(2,1)S(1)}, u32[]{:S(2)}, u32[]{:S(2)}) collective-permute-start(bf16[1760,128]{1,0:T(8,128)(2,1)S(1)} %slice_bitcast_fusion.1), channel_id=1, source_target_pairs={{0,8},{1,9},{2,10},{3,11},{4,12},{5,13},{6,14},{7,15},{8,16},{9,17... | collective-permute-start | bytes 1351688 | tf_op jit(solution)/shard_map/ppermute | solution.py:1275
  27.8 8.6 %collective-permute-done.6.refs_3_ = bf16[1760,128]{1,0:T(8,128)(2,1)S(1)} collective-permute-done((bf16[1760,128]{1,0:T(8,128)(2,1)S(1)}, bf16[1760,128]{1,0:T(8,128)(2,1)S(1)}, u32[]{:S(2)}, u32[]{:S(2)}) %collective-permute-start.6) | collective-permute-done | bytes 450592 | tf_op jit(solution)/shard_map/ppermute | solution.py:1275
  44.6 6.4 %collective-permute-done.9 = bf16[1760,128]{1,0:T(8,128)(2,1)} collective-permute-done((bf16[1760,128]{1,0:T(8,128)(2,1)S(1)}, bf16[1760,128]{1,0:T(8,128)(2,1)}, u32[]{:S(2)}, u32[]{:S(2)}) %collective-permute-start.9) | collective-permute-done | bytes 450592 | tf_op jit(solution)/shard_map/ppermute | solution.py:1275
  62.2 2.7 copy.45
  67.7 18.0 %collective-permute-done.10.refs_2_ = bf16[1760,128]{1,0:T(8,128)(2,1)S(1)} collective-permute-done((bf16[1760,128]{1,0:T(8,128)(2,1)}, bf16[1760,128]{1,0:T(8,128)(2,1)S(1)}, u32[]{:S(2)}, u32[]{:S(2)}) %collective-permute-start.10) | collective-permute-done | bytes 450592 | tf_op jit(solution)/shard_map/ppermute | solution.py:1275
  98.4 21.6 %collective-permute-done.17 = bf16[4,512,128]{2,1,0:T(8,128)(2,1)S(1)} collective-permute-done((bf16[4,512,128]{2,1,0:T(8,128)(2,1)}, bf16[4,512,128]{2,1,0:T(8,128)(2,1)S(1)}, u32[]{:S(2)}, u32[]{:S(2)}) %collective-permute-start.17) | collective-permute-done | bytes 524320 | tf_op jit(solution)/shard_map/ppermute | solution.py:1275
  120.7 12.6 %collective-permute-done.20 = bf16[4,512,128]{2,1,0:T(8,128)(2,1)S(1)} collective-permute-done((bf16[4,512,128]{2,1,0:T(8,128)(2,1)}, bf16[4,512,128]{2,1,0:T(8,128)(2,1)S(1)}, u32[]{:S(2)}, u32[]{:S(2)}) %collective-permute-start.20) | collective-permute-done | bytes 524320 | tf_op jit(solution)/shard_map/ppermute | solution.py:1275
  142.4 15.9 %collective-permute-done.21 = bf16[4,512,128]{2,1,0:T(8,128)(2,1)S(1)} collective-permute-done((bf16[4,512,128]{2,1,0:T(8,128)(2,1)S(1)}, bf16[4,512,128]{2,1,0:T(8,128)(2,1)S(1)}, u32[]{:S(2)}, u32[]{:S(2)}) %collective-permute-start.21) | collective-permute-done | bytes 524320 | tf_op jit(solution)/shard_map/ppermute | solution.py:1275
  159.6 19.6 %collective-permute-done.22 = bf16[4,512,128]{2,1,0:T(8,128)(2,1)S(1)} collective-permute-done((bf16[4,512,128]{2,1,0:T(8,128)(2,1)S(1)}, bf16[4,512,128]{2,1,0:T(8,128)(2,1)S(1)}, u32[]{:S(2)}, u32[]{:S(2)}) %collective-permute-start.22) | collective-permute-done | bytes 524320 | tf_op jit(solution)/shard_map/ppermute | solution.py:1275
  180.4 3.7 collective-permute-done.12.refs_11_
  188.3 31.3 %forward_plain.1.refs_1_.refs_3_ = f32[512,128]{1,0:T(8,128)} custom-call(s32[1]{0:T(128)} %constant.126.clone.1.refs_0_, s32[2]{0:T(128)} %refs_1_.6, bf16[512,128]{1,0:T(8,128)(2,1)} %pad.22.refs_2_.refs_4_, f32[8,192]{1,0:T(8,128)} %select_maximum_fusion.1.refs_3_.refs_5_, bf16[384,384]{1,0:T(8,128)(2,1)} %constant.145.clone.refs_4_.refs_11_.refs_3_.refs_7_, ...), custom_call_target="tpu_custom_call" | custom-call | flops 8000000000 | bytes 40000000 | tf_op jit(solution)/shard_map/forward_plain/pallas_call | solution.py:719
  219.7 35.0 %forward_save.1 = (f32[512,128]{1,0:T(8,128)}, bf16[2048,256]{1,0:T(8,128)(2,1)}, f32[512,384]{1,0:T(8,128)}, f32[512,384]{1,0:T(8,128)}, f32[512,384]{1,0:T(8,1...) custom-call(s32[1]{0:T(128)} %bitcast.refs_0_, ...), custom_call_target="tpu_custom_call" | custom-call | flops 8000000000 | bytes 40000000 | tf_op jit(solution)/shard_map/forward_save/pallas_call | solution.py:719
  254.7 31.6 %back_top.1 = (bf16[4,2272,128]{2,1,0:T(8,128)(2,1)}, bf16[4,2272,128]{2,1,0:T(8,128)(2,1)}, f32[11968,128]{1,0:T(8,128)}, f32[512,384]{1,0:T(8,128)}, f32[8,768]{1,0:T(8,128)}, /*index=5*/f32[8,128]{1,0:T(8,128)}) custom-call(s32[1]{0:T(128)} %bitcast.refs_0_, f32[1]{0:T(128)} %bitcast.2.refs_1_, f32[512,128]{1,0:T(8,128)} %get-tuple-element.53.refs_2_, ...), custom_call_target="tpu_custom_call" | custom-call | flops 8000000000 | bytes 40000000 | tf_op jit(solution)/shard_map/back_top/pallas_call | solution.py:1143
  286.4 14.2 %back_b.1 = (bf16[4,2272,128]{2,1,0:T(8,128)(2,1)}, bf16[4,2272,128]{2,1,0:T(8,128)(2,1)}, f32[4240,128]{1,0:T(8,128)}, f32[512,384]{1,0:T(8,128)}, f32[8,768]{1,0:T(8,128)}, /*index=5*/f32[8,384]{1,0:T(8,128)}) custom-call(s32[1]{0:T(128)} %bitcast.refs_0_, f32[8,128]{1,0:T(8,128)} %get-tuple-element.68.refs_1_.refs_2_, ...), custom_call_target="tpu_custom_call" | custom-call | flops 8000000000 | bytes 40000000 | tf_op jit(solution)/shard_map/back_b/pallas_call | solution.py:1143
  310.4 13.0 %back_c.1 = (bf16[4,2272,128]{2,1,0:T(8,128)(2,1)}, bf16[4,2272,128]{2,1,0:T(8,128)(2,1)}, f32[1120,128]{1,0:T(8,128)}, f32[512,384]{1,0:T(8,128)}, f32[8,768]{1,0:T(8,128)}) custom-call(s32[1]{0:T(128)} %bitcast.refs_0_, f32[8,128]{1,0:T(8,128)} %get-tuple-element.68.refs_1_.refs_2_, f32[512,384]{1,0:T(8,128)} %get-tuple-element.69.refs_2_, ...), custom_call_target="tpu_custom_call" | custom-call | flops 8000000000 | bytes 40000000 | tf_op jit(solution)/shard_map/back_c/pallas_call | solution.py:1143
  327.9 10.6 %back_low.1 = (bf16[4,2272,128]{2,1,0:T(8,128)(2,1)}, bf16[4,2272,128]{2,1,0:T(8,128)(2,1)}) custom-call(s32[1]{0:T(128)} %bitcast.refs_0_, s32[2]{0:T(128)} %refs_1_.6, f32[8,128]{1,0:T(8,128)} %get-tuple-element.68.refs_1_.refs_2_, f32[512,384]{1,0:T(8,128)} %gate.9.refs_3_, f32[8,768]{1,0:T(8,128)} %get-tuple-element.86.refs_4_, ...), custom_call_target="tpu_custom_call" | custom-call | flops 8000000000 | bytes 40000000 | tf_op jit(solution)/shard_map/back_low/pallas_call | solution.py:1143
  343.9 5.7 %collective-permute-done.47 = bf16[1136,128]{1,0:T(8,128)(2,1)S(1)} collective-permute-done((bf16[1136,128]{1,0:T(8,128)(2,1)S(1)}, bf16[1136,128]{1,0:T(8,128)(2,1)S(1)}, u32[]{:S(2)}, u32[]{:S(2)}) %collective-permute-start.47) | collective-permute-done | bytes 290848 | tf_op jit(solution)/shard_map/ppermute | solution.py:1241
  360.6 8.9 %collective-permute-done.38 = bf16[2,1136,128]{2,1,0:T(8,128)(2,1)S(1)} collective-permute-done((bf16[2,1136,128]{2,1,0:T(8,128)(2,1)S(1)}, bf16[2,1136,128]{2,1,0:T(8,128)(2,1)S(1)}, u32[]{:S(2)}, u32[]{:S(2)}) %collective-permute-start.38) | collective-permute-done | bytes 581664 | tf_op jit(solution)/shard_map/ppermute | solution.py:1241
  373.6 6.7 %collective-permute-done.33 = bf16[2,1136,128]{2,1,0:T(8,128)(2,1)S(1)} collective-permute-done((bf16[2,1136,128]{2,1,0:T(8,128)(2,1)S(1)}, bf16[2,1136,128]{2,1,0:T(8,128)(2,1)S(1)}, u32[]{:S(2)}, u32[]{:S(2)}) %collective-permute-start.33) | collective-permute-done | bytes 581664 | tf_op jit(solution)/shard_map/ppermute | solution.py:1241
  384.8 4.7 %collective-permute-done.39 = bf16[1136,128]{1,0:T(8,128)(2,1)S(1)} collective-permute-done((bf16[1136,128]{1,0:T(8,128)(2,1)S(1)}, bf16[1136,128]{1,0:T(8,128)(2,1)S(1)}, u32[]{:S(2)}, u32[]{:S(2)}) %collective-permute-start.39) | collective-permute-done | bytes 290848 | tf_op jit(solution)/shard_map/ppermute | solution.py:1241
  401.2 7.4 %collective-permute-done.53 = bf16[2272,128]{1,0:T(8,128)(2,1)S(1)} collective-permute-done((bf16[2272,128]{1,0:T(8,128)(2,1)S(1)}, bf16[2272,128]{1,0:T(8,128)(2,1)S(1)}, u32[]{:S(2)}, u32[]{:S(2)}) %collective-permute-start.53) | collective-permute-done | bytes 581664 | tf_op jit(solution)/shard_map/ppermute | solution.py:1401
  411.1 8.8 %collective-permute-start.42 = (bf16[2272,128]{1,0:T(8,128)(2,1)}, bf16[2272,128]{1,0:T(8,128)(2,1)}, u32[]{:S(2)}, u32[]{:S(2)}) collective-permute-start(bf16[2272,128]{1,0:T(8,128)(2,1)} %get-tuple-element.136), channel_id=1, source_target_pairs={{0,8},{1,9},{2,10},{3,11},{4,12},{5,13},{6,14},{7,15}} | collective-permute-start | bytes 1744904 | tf_op jit(solution)/shard_map/ppermute | solution.py:1401
  422.3 4.4 collective-permute-done.42
  426.7 6.2 %collective-permute-done.45 = bf16[2272,128]{1,0:T(8,128)(2,1)} collective-permute-done((bf16[2272,128]{1,0:T(8,128)(2,1)}, bf16[2272,128]{1,0:T(8,128)(2,1)}, u32[]{:S(2)}, u32[]{:S(2)}) %collective-permute-start.45) | collective-permute-done | bytes 581664 | tf_op jit(solution)/shard_map/ppermute | solution.py:1401
  (259 shorter events, 125.6 us)
Async XLA Ops:
  7.2 181.2 %all-gather.2.cloned.1.call-start = ((), (), s32[]{:S(2)}) async-start(), calls=%async_computation | async-start | bytes 19193856 | tf_op jit(solution)/shard_map/all_gather | solution.py:1325
  39.2 22.1 %collective-permute-start.16 = (bf16[2,512,128]{2,1,0:T(8,128)(2,1)S(1)}, bf16[2,512,128]{2,1,0:T(8,128)(2,1)S(1)}, u32[]{:S(2)}, u32[]{:S(2)}) collective-permute-start(bf16[2,512,128]{2,1,0:T(8,128)(2,1)S(1)} %pad_maximum_fusion.17), channel_id=1, source_target_pairs={{0,2},{1,3},{2,0},{3,1},{4,6},{5,7},{6,4},{7,5},{8,10},{9,11},{10,... | collective-permute-start | bytes 786440 | tf_op jit(solution)/shard_map/ppermute | solution.py:1241
  44.0 23.7 %collective-permute-start.8 = (bf16[1760,128]{1,0:T(8,128)(2,1)}, bf16[1760,128]{1,0:T(8,128)(2,1)S(1)}, u32[]{:S(2)}, u32[]{:S(2)}) collective-permute-start(bf16[1760,128]{1,0:T(8,128)(2,1)} %collective-permute-done.7), channel_id=1, source_target_pairs={{16,24},{17,25},{18,26},{19,27},{20,28},{21,29},{22,30},{23,31}} | collective-permute-start | bytes 1351688 | tf_op jit(solution)/shard_map/ppermute | solution.py:1275
  51.0 34.7 %collective-permute-start.10 = (bf16[1760,128]{1,0:T(8,128)(2,1)}, bf16[1760,128]{1,0:T(8,128)(2,1)S(1)}, u32[]{:S(2)}, u32[]{:S(2)}) collective-permute-start(bf16[1760,128]{1,0:T(8,128)(2,1)} %collective-permute-done.9), channel_id=1, source_target_pairs={{8,0},{9,1},{10,2},{11,3},{12,4},{13,5},{14,6},{15,7}} | collective-permute-start | bytes 1351688 | tf_op jit(solution)/shard_map/ppermute | solution.py:1275
  89.2 45.4 %collective-permute-start.11 = (bf16[4,880,128]{2,1,0:T(8,128)(2,1)}, bf16[4,880,128]{2,1,0:T(8,128)(2,1)S(1)}, u32[]{:S(2)}, u32[]{:S(2)}) collective-permute-start(bf16[4,880,128]{2,1,0:T(8,128)(2,1)} %get-tuple-element.143), channel_id=1, source_target_pairs={{0,2},{1,3},{2,0},{3,1},{4,6},{5,7},{6,4},{7,5},{8,10},{9,11},{10,... | collective-permute-start | bytes 2703368 | tf_op jit(solution)/shard_map/ppermute | solution.py:1241
  91.3 46.2 %collective-permute-start.13 = (bf16[4,880,128]{2,1,0:T(8,128)(2,1)}, bf16[4,880,128]{2,1,0:T(8,128)(2,1)}, u32[]{:S(2)}, u32[]{:S(2)}) collective-permute-start(bf16[4,880,128]{2,1,0:T(8,128)(2,1)} %get-tuple-element.142), channel_id=1, source_target_pairs={{0,4},{1,5},{2,6},{3,7},{4,0},{5,1},{6,2},{7,3},{8,12},{9,13},{10,... | collective-permute-start | bytes 2703368 | tf_op jit(solution)/shard_map/ppermute | solution.py:1241
  95.5 24.5 %collective-permute-start.17 = (bf16[4,512,128]{2,1,0:T(8,128)(2,1)}, bf16[4,512,128]{2,1,0:T(8,128)(2,1)S(1)}, u32[]{:S(2)}, u32[]{:S(2)}) collective-permute-start(bf16[4,512,128]{2,1,0:T(8,128)(2,1)} %gate.7), channel_id=1, source_target_pairs={{0,8},{1,9},{2,10},{3,11},{4,12},{5,13},{6,14},{7,15},{8,16},{9,17... | collective-permute-start | bytes 1572872 | tf_op jit(solution)/shard_map/ppermute | solution.py:1275
  97.1 36.3 %collective-permute-start.20 = (bf16[4,512,128]{2,1,0:T(8,128)(2,1)}, bf16[4,512,128]{2,1,0:T(8,128)(2,1)S(1)}, u32[]{:S(2)}, u32[]{:S(2)}) collective-permute-start(bf16[4,512,128]{2,1,0:T(8,128)(2,1)} %gate.7), channel_id=1, source_target_pairs={{24,16},{25,17},{26,18},{27,19},{28,20},{29,21},{30,22},{31,23},{1... | collective-permute-start | bytes 1572872 | tf_op jit(solution)/shard_map/ppermute | solution.py:1275
  120.0 21.7 %collective-permute-start.18 = (bf16[4,512,128]{2,1,0:T(8,128)(2,1)S(1)}, bf16[4,512,128]{2,1,0:T(8,128)(2,1)S(1)}, u32[]{:S(2)}, u32[]{:S(2)}) collective-permute-start(bf16[4,512,128]{2,1,0:T(8,128)(2,1)S(1)} %collective-permute-done.17), channel_id=1, source_target_pairs={{8,16},{9,17},{10,18},{11,19},{12,20},{13,21},{14,22},{15,23},{16,... | collective-permute-start | bytes 1572872 | tf_op jit(solution)/shard_map/ppermute | solution.py:1275
  133.4 25.0 %collective-permute-start.21 = (bf16[4,512,128]{2,1,0:T(8,128)(2,1)S(1)}, bf16[4,512,128]{2,1,0:T(8,128)(2,1)S(1)}, u32[]{:S(2)}, u32[]{:S(2)}) collective-permute-start(bf16[4,512,128]{2,1,0:T(8,128)(2,1)S(1)} %collective-permute-done.20), channel_id=1, source_target_pairs={{16,8},{17,9},{18,10},{19,11},{20,12},{21,13},{22,14},{23,15},{8,0... | collective-permute-start | bytes 1572872 | tf_op jit(solution)/shard_map/ppermute | solution.py:1275
  136.0 48.1 %collective-permute-start.12 = (bf16[2,4,880,128]{3,2,1,0:T(8,128)(2,1)}, bf16[2,4,880,128]{3,2,1,0:T(8,128)(2,1)}, u32[]{:S(2)}, u32[]{:S(2)}) collective-permute-start(bf16[2,4,880,128]{3,2,1,0:T(8,128)(2,1)} %pad_maximum_fusion.2.refs_10_), channel_id=1, source_target_pairs={{0,4},{1,5},{2,6},{3,7},{4,0},{5,1},{6,2},{7,3},{8,12},{9,13},{10,... | collective-permute-start | bytes 5406728 | tf_op jit(solution)/shard_map/ppermute | solution.py:1241
  140.1 44.0 %collective-permute-start.14 = (bf16[2,4,880,128]{3,2,1,0:T(8,128)(2,1)}, bf16[2,4,880,128]{3,2,1,0:T(8,128)(2,1)}, u32[]{:S(2)}, u32[]{:S(2)}) collective-permute-start(bf16[2,4,880,128]{3,2,1,0:T(8,128)(2,1)} %pad_maximum_fusion.3.refs_12_), channel_id=1, source_target_pairs={{0,2},{1,3},{2,0},{3,1},{4,6},{5,7},{6,4},{7,5},{8,10},{9,11},{10,... | collective-permute-start | bytes 5406728 | tf_op jit(solution)/shard_map/ppermute | solution.py:1241
  179.8 39.9 %collective-permute-start.27 = (bf16[4,4,512,128]{3,2,1,0:T(8,128)(2,1)S(1)}, bf16[4,4,512,128]{3,2,1,0:T(8,128)(2,1)}, u32[]{:S(2)}, u32[]{:S(2)}) collective-permute-start(bf16[4,4,512,128]{3,2,1,0:T(8,128)(2,1)S(1)} %pad_maximum_fusion.refs_14_), channel_id=1, source_target_pairs={{0,1},{1,0},{2,3},{3,2},{4,5},{5,4},{6,7},{7,6},{8,9},{9,8},{10,11... | collective-permute-start | bytes 6291464 | tf_op jit(solution)/shard_map/ppermute | solution.py:1241
  179.9 39.8 %collective-permute-start.23 = (bf16[2,4,880,128]{3,2,1,0:T(8,128)(2,1)}, bf16[2,4,880,128]{3,2,1,0:T(8,128)(2,1)}, u32[]{:S(2)}, u32[]{:S(2)}) collective-permute-start(bf16[2,4,880,128]{3,2,1,0:T(8,128)(2,1)} %pad_maximum_fusion.2.refs_10_), channel_id=1, source_target_pairs={{0,1},{1,0},{2,3},{3,2},{4,5},{5,4},{6,7},{7,6},{8,9},{9,8},{10,11... | collective-permute-start | bytes 5406728 | tf_op jit(solution)/shard_map/ppermute | solution.py:1241
  180.4 39.3 %collective-permute-start.25 = (bf16[2,4,880,128]{3,2,1,0:T(8,128)(2,1)}, bf16[2,4,880,128]{3,2,1,0:T(8,128)(2,1)}, u32[]{:S(2)}, u32[]{:S(2)}) collective-permute-start(bf16[2,4,880,128]{3,2,1,0:T(8,128)(2,1)} %pad_maximum_fusion.3.refs_12_), channel_id=1, source_target_pairs={{0,1},{1,0},{2,3},{3,2},{4,5},{5,4},{6,7},{7,6},{8,9},{9,8},{10,11... | collective-permute-start | bytes 5406728 | tf_op jit(solution)/shard_map/ppermute | solution.py:1241
  184.2 35.5 %collective-permute-start.24 = (bf16[2,4,880,128]{3,2,1,0:T(8,128)(2,1)}, bf16[2,4,880,128]{3,2,1,0:T(8,128)(2,1)}, u32[]{:S(2)}, u32[]{:S(2)}) collective-permute-start(bf16[2,4,880,128]{3,2,1,0:T(8,128)(2,1)} %collective-permute-done.12.refs_11_), channel_id=1, source_target_pairs={{0,1},{1,0},{2,3},{3,2},{4,5},{5,4},{6,7},{7,6},{8,9},{9,8},{10,11... | collective-permute-start | bytes 5406728 | tf_op jit(solution)/shard_map/ppermute | solution.py:1241
  184.2 35.5 %collective-permute-start.26 = (bf16[2,4,880,128]{3,2,1,0:T(8,128)(2,1)}, bf16[2,4,880,128]{3,2,1,0:T(8,128)(2,1)}, u32[]{:S(2)}, u32[]{:S(2)}) collective-permute-start(bf16[2,4,880,128]{3,2,1,0:T(8,128)(2,1)} %collective-permute-done.14.refs_13_), channel_id=1, source_target_pairs={{0,1},{1,0},{2,3},{3,2},{4,5},{5,4},{6,7},{7,6},{8,9},{9,8},{10,11... | collective-permute-start | bytes 5406728 | tf_op jit(solution)/shard_map/ppermute | solution.py:1241
  308.2 30.3 %collective-permute-start.46 = (bf16[2,1136,128]{2,1,0:T(8,128)(2,1)S(1)}, bf16[2,1136,128]{2,1,0:T(8,128)(2,1)}, u32[]{:S(2)}, u32[]{:S(2)}) collective-permute-start(bf16[2,1136,128]{2,1,0:T(8,128)(2,1)S(1)} %pad_maximum_fusion.10.refs_3_), channel_id=1, source_target_pairs={{0,2},{1,3},{2,0},{3,1},{4,6},{5,7},{6,4},{7,5},{8,10},{9,11},{10,... | collective-permute-start | bytes 1744904 | tf_op jit(solution)/shard_map/ppermute | solution.py:1241
  309.6 29.0 %collective-permute-start.48 = (bf16[2,1136,128]{2,1,0:T(8,128)(2,1)S(1)}, bf16[2,1136,128]{2,1,0:T(8,128)(2,1)}, u32[]{:S(2)}, u32[]{:S(2)}) collective-permute-start(bf16[2,1136,128]{2,1,0:T(8,128)(2,1)S(1)} %pad_maximum_fusion.11.refs_4_), channel_id=1, source_target_pairs={{0,4},{1,5},{2,6},{3,7},{4,0},{5,1},{6,2},{7,3},{8,12},{9,13},{10,... | collective-permute-start | bytes 1744904 | tf_op jit(solution)/shard_map/ppermute | solution.py:1241
  323.4 28.3 %collective-permute-start.37 = (bf16[4,2272,128]{2,1,0:T(8,128)(2,1)}, bf16[4,2272,128]{2,1,0:T(8,128)(2,1)}, u32[]{:S(2)}, u32[]{:S(2)}) collective-permute-start(bf16[4,2272,128]{2,1,0:T(8,128)(2,1)} %get-tuple-element.96), channel_id=1, source_target_pairs={{0,1},{1,0},{2,3},{3,2},{4,5},{5,4},{6,7},{7,6},{8,9},{9,8},{10,11... | collective-permute-start | bytes 6979592 | tf_op jit(solution)/shard_map/ppermute | solution.py:1241
  356.3 23.9 %collective-permute-start.33 = (bf16[2,1136,128]{2,1,0:T(8,128)(2,1)S(1)}, bf16[2,1136,128]{2,1,0:T(8,128)(2,1)S(1)}, u32[]{:S(2)}, u32[]{:S(2)}) collective-permute-start(bf16[2,1136,128]{2,1,0:T(8,128)(2,1)S(1)} %pad_maximum_fusion.12), channel_id=1, source_target_pairs={{0,2},{1,3},{2,0},{3,1},{4,6},{5,7},{6,4},{7,5},{8,10},{9,11},{10,... | collective-permute-start | bytes 1744904 | tf_op jit(solution)/shard_map/ppermute | solution.py:1241
  357.3 26.0 %collective-permute-start.35 = (bf16[2,1136,128]{2,1,0:T(8,128)(2,1)S(1)}, bf16[2,1136,128]{2,1,0:T(8,128)(2,1)S(1)}, u32[]{:S(2)}, u32[]{:S(2)}) collective-permute-start(bf16[2,1136,128]{2,1,0:T(8,128)(2,1)S(1)} %pad_maximum_fusion.13), channel_id=1, source_target_pairs={{0,4},{1,5},{2,6},{3,7},{4,0},{5,1},{6,2},{7,3},{8,12},{9,13},{10,... | collective-permute-start | bytes 1744904 | tf_op jit(solution)/shard_map/ppermute | solution.py:1241
  359.1 63.1 %collective-permute-start.55 = (bf16[2272,128]{1,0:T(8,128)(2,1)}, bf16[2272,128]{1,0:T(8,128)(2,1)}, u32[]{:S(2)}, u32[]{:S(2)}) collective-permute-start(bf16[2272,128]{1,0:T(8,128)(2,1)} %get-tuple-element.139), channel_id=1, source_target_pairs={{24,16},{25,17},{26,18},{27,19},{28,20},{29,21},{30,22},{31,23}} | collective-permute-start | bytes 1744904 | tf_op jit(solution)/shard_map/ppermute | solution.py:1401
  369.5 28.9 %collective-permute-start.52 = (bf16[2272,128]{1,0:T(8,128)(2,1)S(1)}, bf16[2272,128]{1,0:T(8,128)(2,1)S(1)}, u32[]{:S(2)}, u32[]{:S(2)}) collective-permute-start(bf16[2272,128]{1,0:T(8,128)(2,1)S(1)} %get-tuple-element.138), channel_id=1, source_target_pairs={{0,8},{1,9},{2,10},{3,11},{4,12},{5,13},{6,14},{7,15}} | collective-permute-start | bytes 1744904 | tf_op jit(solution)/shard_map/ppermute | solution.py:1401
  (64 other events, 888.5 us)
Sparse Core Ops, SparseCore 0:
  11.4 165.2 all-gather.1

commit v7 on v6

--- a/solution.py
+++ b/solution.py
@@ -376,7 +376,7 @@
                 ].astype(F32)
                 return carry
 
-            lax.fori_loop(0, whole, body, 0, unroll=2)
+            lax.fori_loop(0, whole, body, 0, unroll=4)
             if rest:
                 done = whole * 256
                 self.wide[to + done : to + count, :] = block[start + done : start + count, :].astype(F32)
@@ -401,7 +401,7 @@
                 w_ref[pl.ds(r, block), j * LINE : (j + 1) * LINE] = v.astype(BF16)
             return carry
 
-        lax.fori_loop(0, rows // block, body, 0, unroll=3 if (rows // block) % 3 == 0 else 2)
+        lax.fori_loop(0, rows // block, body, 0, unroll=6 if (rows // block) % 6 == 0 else 3 if (rows // block) % 3 == 0 else 2)
 
     def row(self, at, step):
         base = at - self.low
@@ -839,7 +839,7 @@
                     stage[pl.ds(pl.multiple_of(c * 288, 16), 288), :] = lines.astype(BF16)
                     return carry
 
-                lax.fori_loop(0, whole, body, 0)
+                lax.fori_loop(0, whole, body, 0, unroll=7)
                 lines = self.g[pl.ds(pl.multiple_of(start + whole * 288, 8), rest - 8), :]
                 stage[whole * 288 :, :] = jnp.concatenate([lines, self.pad[...]], 0).astype(BF16)
                 copy = pltpu.make_async_copy(stage, self.outs[side].at[at], self.sems.at[side])

time: 453 us -> 453 us (level)
  no operation moved by 1% of the time
where the time goes in v7:
time: 453 us; the launch traced here: 445 us
  waiting for transfers between devices  158 us (35%)
  Pallas kernels  135 us (30%)
  starting transfers between devices  71.8 us (16%)
  other arithmetic  43.6 us (10%)
  local copies, waits for them, and re-layouts  18.8 us (4%)
  between operations  18.3 us (4%)
    ppermute x12, waiting for transfers between devices, climb(): return lax.ppermute(values, AXIS, pairs)  103 us
    pallas_call x4, Pallas kernels, back_call(): pl.pallas_call(kernel, out_shape=[plane, plane, *rest, *(sds(*o) for o in...  69 us
    pallas_call x2, Pallas kernels, forward_call(): pl.pallas_call(body, out_shape=outs, in_specs=[SM] * 2 + [VM] * 8 + [HB]...  65.7 us
    ppermute x31, waiting for transfers between devices, swap(): return lax.ppermute(values, AXIS, [(i, i ^ hop) for i in range(SHARDS)])  36.4 us
    ppermute x31, starting transfers between devices, swap(): return lax.ppermute(values, AXIS, [(i, i ^ hop) for i in range(SHARDS)])  28.5 us
    ppermute x8, waiting for transfers between devices, column_sums(): run = wide(lax.ppermute(low(value), AXIS, pairs))  18 us
    ppermute x12, starting transfers between devices, climb(): return lax.ppermute(values, AXIS, pairs)  17.7 us
    ppermute x8, starting transfers between devices, column_sums(): run = wide(lax.ppermute(low(value), AXIS, pairs))  17.5 us
  transfers between devices with their start and end apart: 57, of which 21 were waited for; matrix products, arithmetic and copies ran while one was open for 12% of the time, Pallas kernels for 15%

profile of v7, /device:TPU:0, one launch (start us, length us, event | category | flops | bytes accessed | tf_op | source)
XLA Modules:
  0.0 445.4 jit_solution(17509002165143201775)
XLA Ops:
  10.1 5.0 %collective-permute-start.5 = (bf16[1760,128]{1,0:T(8,128)(2,1)S(1)}, bf16[1760,128]{1,0:T(8,128)(2,1)S(1)}, u32[]{:S(2)}, u32[]{:S(2)}) collective-permute-start(bf16[1760,128]{1,0:T(8,128)(2,1)S(1)} %slice_bitcast_fusion.1), channel_id=1, source_target_pairs={{0,8},{1,9},{2,10},{3,11},{4,12},{5,13},{6,14},{7,15},{8,16},{9,17... | collective-permute-start | bytes 1351688 | tf_op jit(solution)/shard_map/ppermute | solution.py:1275
  27.8 8.6 %collective-permute-done.6.refs_3_ = bf16[1760,128]{1,0:T(8,128)(2,1)S(1)} collective-permute-done((bf16[1760,128]{1,0:T(8,128)(2,1)S(1)}, bf16[1760,128]{1,0:T(8,128)(2,1)S(1)}, u32[]{:S(2)}, u32[]{:S(2)}) %collective-permute-start.6) | collective-permute-done | bytes 450592 | tf_op jit(solution)/shard_map/ppermute | solution.py:1275
  44.6 6.4 %collective-permute-done.9 = bf16[1760,128]{1,0:T(8,128)(2,1)} collective-permute-done((bf16[1760,128]{1,0:T(8,128)(2,1)S(1)}, bf16[1760,128]{1,0:T(8,128)(2,1)}, u32[]{:S(2)}, u32[]{:S(2)}) %collective-permute-start.9) | collective-permute-done | bytes 450592 | tf_op jit(solution)/shard_map/ppermute | solution.py:1275
  62.2 2.7 copy.45
  67.7 18.0 %collective-permute-done.10.refs_2_ = bf16[1760,128]{1,0:T(8,128)(2,1)S(1)} collective-permute-done((bf16[1760,128]{1,0:T(8,128)(2,1)}, bf16[1760,128]{1,0:T(8,128)(2,1)S(1)}, u32[]{:S(2)}, u32[]{:S(2)}) %collective-permute-start.10) | collective-permute-done | bytes 450592 | tf_op jit(solution)/shard_map/ppermute | solution.py:1275
  98.4 21.6 %collective-permute-done.17 = bf16[4,512,128]{2,1,0:T(8,128)(2,1)S(1)} collective-permute-done((bf16[4,512,128]{2,1,0:T(8,128)(2,1)}, bf16[4,512,128]{2,1,0:T(8,128)(2,1)S(1)}, u32[]{:S(2)}, u32[]{:S(2)}) %collective-permute-start.17) | collective-permute-done | bytes 524320 | tf_op jit(solution)/shard_map/ppermute | solution.py:1275
  120.7 12.6 %collective-permute-done.20 = bf16[4,512,128]{2,1,0:T(8,128)(2,1)S(1)} collective-permute-done((bf16[4,512,128]{2,1,0:T(8,128)(2,1)}, bf16[4,512,128]{2,1,0:T(8,128)(2,1)S(1)}, u32[]{:S(2)}, u32[]{:S(2)}) %collective-permute-start.20) | collective-permute-done | bytes 524320 | tf_op jit(solution)/shard_map/ppermute | solution.py:1275
  142.4 15.9 %collective-permute-done.21 = bf16[4,512,128]{2,1,0:T(8,128)(2,1)S(1)} collective-permute-done((bf16[4,512,128]{2,1,0:T(8,128)(2,1)S(1)}, bf16[4,512,128]{2,1,0:T(8,128)(2,1)S(1)}, u32[]{:S(2)}, u32[]{:S(2)}) %collective-permute-start.21) | collective-permute-done | bytes 524320 | tf_op jit(solution)/shard_map/ppermute | solution.py:1275
  159.6 19.6 %collective-permute-done.22 = bf16[4,512,128]{2,1,0:T(8,128)(2,1)S(1)} collective-permute-done((bf16[4,512,128]{2,1,0:T(8,128)(2,1)S(1)}, bf16[4,512,128]{2,1,0:T(8,128)(2,1)S(1)}, u32[]{:S(2)}, u32[]{:S(2)}) %collective-permute-start.22) | collective-permute-done | bytes 524320 | tf_op jit(solution)/shard_map/ppermute | solution.py:1275
  180.4 3.7 collective-permute-done.12.refs_11_
  188.3 31.0 %forward_plain.1.refs_1_.refs_3_ = f32[512,128]{1,0:T(8,128)} custom-call(s32[1]{0:T(128)} %constant.126.clone.1.refs_0_, s32[2]{0:T(128)} %refs_1_.6, bf16[512,128]{1,0:T(8,128)(2,1)} %pad.22.refs_2_.refs_4_, f32[8,192]{1,0:T(8,128)} %select_maximum_fusion.1.refs_3_.refs_5_, bf16[384,384]{1,0:T(8,128)(2,1)} %constant.145.clone.refs_4_.refs_11_.refs_3_.refs_7_, ...), custom_call_target="tpu_custom_call" | custom-call | flops 8000000000 | bytes 40000000 | tf_op jit(solution)/shard_map/forward_plain/pallas_call | solution.py:719
  219.4 34.7 %forward_save.1 = (f32[512,128]{1,0:T(8,128)}, bf16[2048,256]{1,0:T(8,128)(2,1)}, f32[512,384]{1,0:T(8,128)}, f32[512,384]{1,0:T(8,128)}, f32[512,384]{1,0:T(8,1...) custom-call(s32[1]{0:T(128)} %bitcast.refs_0_, ...), custom_call_target="tpu_custom_call" | custom-call | flops 8000000000 | bytes 40000000 | tf_op jit(solution)/shard_map/forward_save/pallas_call | solution.py:719
  254.1 31.0 %back_top.1 = (bf16[4,2272,128]{2,1,0:T(8,128)(2,1)}, bf16[4,2272,128]{2,1,0:T(8,128)(2,1)}, f32[11968,128]{1,0:T(8,128)}, f32[512,384]{1,0:T(8,128)}, f32[8,768]{1,0:T(8,128)}, /*index=5*/f32[8,128]{1,0:T(8,128)}) custom-call(s32[1]{0:T(128)} %bitcast.refs_0_, f32[1]{0:T(128)} %bitcast.2.refs_1_, f32[512,128]{1,0:T(8,128)} %get-tuple-element.53.refs_2_, ...), custom_call_target="tpu_custom_call" | custom-call | flops 8000000000 | bytes 40000000 | tf_op jit(solution)/shard_map/back_top/pallas_call | solution.py:1143
  285.2 14.1 %back_b.1 = (bf16[4,2272,128]{2,1,0:T(8,128)(2,1)}, bf16[4,2272,128]{2,1,0:T(8,128)(2,1)}, f32[4240,128]{1,0:T(8,128)}, f32[512,384]{1,0:T(8,128)}, f32[8,768]{1,0:T(8,128)}, /*index=5*/f32[8,384]{1,0:T(8,128)}) custom-call(s32[1]{0:T(128)} %bitcast.refs_0_, f32[8,128]{1,0:T(8,128)} %get-tuple-element.68.refs_1_.refs_2_, ...), custom_call_target="tpu_custom_call" | custom-call | flops 8000000000 | bytes 40000000 | tf_op jit(solution)/shard_map/back_b/pallas_call | solution.py:1143
  309.1 12.9 %back_c.1 = (bf16[4,2272,128]{2,1,0:T(8,128)(2,1)}, bf16[4,2272,128]{2,1,0:T(8,128)(2,1)}, f32[1120,128]{1,0:T(8,128)}, f32[512,384]{1,0:T(8,128)}, f32[8,768]{1,0:T(8,128)}) custom-call(s32[1]{0:T(128)} %bitcast.refs_0_, f32[8,128]{1,0:T(8,128)} %get-tuple-element.68.refs_1_.refs_2_, f32[512,384]{1,0:T(8,128)} %get-tuple-element.69.refs_2_, ...), custom_call_target="tpu_custom_call" | custom-call | flops 8000000000 | bytes 40000000 | tf_op jit(solution)/shard_map/back_c/pallas_call | solution.py:1143
  326.5 11.0 %back_low.1 = (bf16[4,2272,128]{2,1,0:T(8,128)(2,1)}, bf16[4,2272,128]{2,1,0:T(8,128)(2,1)}) custom-call(s32[1]{0:T(128)} %bitcast.refs_0_, s32[2]{0:T(128)} %refs_1_.6, f32[8,128]{1,0:T(8,128)} %get-tuple-element.68.refs_1_.refs_2_, f32[512,384]{1,0:T(8,128)} %gate.9.refs_3_, f32[8,768]{1,0:T(8,128)} %get-tuple-element.86.refs_4_, ...), custom_call_target="tpu_custom_call" | custom-call | flops 8000000000 | bytes 40000000 | tf_op jit(solution)/shard_map/back_low/pallas_call | solution.py:1143
  342.9 5.7 %collective-permute-done.47 = bf16[1136,128]{1,0:T(8,128)(2,1)S(1)} collective-permute-done((bf16[1136,128]{1,0:T(8,128)(2,1)S(1)}, bf16[1136,128]{1,0:T(8,128)(2,1)S(1)}, u32[]{:S(2)}, u32[]{:S(2)}) %collective-permute-start.47) | collective-permute-done | bytes 290848 | tf_op jit(solution)/shard_map/ppermute | solution.py:1241
  359.6 8.9 %collective-permute-done.38 = bf16[2,1136,128]{2,1,0:T(8,128)(2,1)S(1)} collective-permute-done((bf16[2,1136,128]{2,1,0:T(8,128)(2,1)S(1)}, bf16[2,1136,128]{2,1,0:T(8,128)(2,1)S(1)}, u32[]{:S(2)}, u32[]{:S(2)}) %collective-permute-start.38) | collective-permute-done | bytes 581664 | tf_op jit(solution)/shard_map/ppermute | solution.py:1241
  372.7 6.6 %collective-permute-done.33 = bf16[2,1136,128]{2,1,0:T(8,128)(2,1)S(1)} collective-permute-done((bf16[2,1136,128]{2,1,0:T(8,128)(2,1)S(1)}, bf16[2,1136,128]{2,1,0:T(8,128)(2,1)S(1)}, u32[]{:S(2)}, u32[]{:S(2)}) %collective-permute-start.33) | collective-permute-done | bytes 581664 | tf_op jit(solution)/shard_map/ppermute | solution.py:1241
  383.9 4.7 %collective-permute-done.39 = bf16[1136,128]{1,0:T(8,128)(2,1)S(1)} collective-permute-done((bf16[1136,128]{1,0:T(8,128)(2,1)S(1)}, bf16[1136,128]{1,0:T(8,128)(2,1)S(1)}, u32[]{:S(2)}, u32[]{:S(2)}) %collective-permute-start.39) | collective-permute-done | bytes 290848 | tf_op jit(solution)/shard_map/ppermute | solution.py:1241
  400.2 7.4 %collective-permute-done.53 = bf16[2272,128]{1,0:T(8,128)(2,1)S(1)} collective-permute-done((bf16[2272,128]{1,0:T(8,128)(2,1)S(1)}, bf16[2272,128]{1,0:T(8,128)(2,1)S(1)}, u32[]{:S(2)}, u32[]{:S(2)}) %collective-permute-start.53) | collective-permute-done | bytes 581664 | tf_op jit(solution)/shard_map/ppermute | solution.py:1401
  410.1 8.8 %collective-permute-start.42 = (bf16[2272,128]{1,0:T(8,128)(2,1)}, bf16[2272,128]{1,0:T(8,128)(2,1)}, u32[]{:S(2)}, u32[]{:S(2)}) collective-permute-start(bf16[2272,128]{1,0:T(8,128)(2,1)} %get-tuple-element.136), channel_id=1, source_target_pairs={{0,8},{1,9},{2,10},{3,11},{4,12},{5,13},{6,14},{7,15}} | collective-permute-start | bytes 1744904 | tf_op jit(solution)/shard_map/ppermute | solution.py:1401
  421.3 4.4 collective-permute-done.42
  425.7 6.2 %collective-permute-done.45 = bf16[2272,128]{1,0:T(8,128)(2,1)} collective-permute-done((bf16[2272,128]{1,0:T(8,128)(2,1)}, bf16[2272,128]{1,0:T(8,128)(2,1)}, u32[]{:S(2)}, u32[]{:S(2)}) %collective-permute-start.45) | collective-permute-done | bytes 581664 | tf_op jit(solution)/shard_map/ppermute | solution.py:1401
  (259 shorter events, 125.6 us)
Async XLA Ops:
  7.2 181.2 %all-gather.2.cloned.1.call-start = ((), (), s32[]{:S(2)}) async-start(), calls=%async_computation | async-start | bytes 19193856 | tf_op jit(solution)/shard_map/all_gather | solution.py:1325
  39.2 22.1 %collective-permute-start.16 = (bf16[2,512,128]{2,1,0:T(8,128)(2,1)S(1)}, bf16[2,512,128]{2,1,0:T(8,128)(2,1)S(1)}, u32[]{:S(2)}, u32[]{:S(2)}) collective-permute-start(bf16[2,512,128]{2,1,0:T(8,128)(2,1)S(1)} %pad_maximum_fusion.17), channel_id=1, source_target_pairs={{0,2},{1,3},{2,0},{3,1},{4,6},{5,7},{6,4},{7,5},{8,10},{9,11},{10,... | collective-permute-start | bytes 786440 | tf_op jit(solution)/shard_map/ppermute | solution.py:1241
  44.0 23.7 %collective-permute-start.8 = (bf16[1760,128]{1,0:T(8,128)(2,1)}, bf16[1760,128]{1,0:T(8,128)(2,1)S(1)}, u32[]{:S(2)}, u32[]{:S(2)}) collective-permute-start(bf16[1760,128]{1,0:T(8,128)(2,1)} %collective-permute-done.7), channel_id=1, source_target_pairs={{16,24},{17,25},{18,26},{19,27},{20,28},{21,29},{22,30},{23,31}} | collective-permute-start | bytes 1351688 | tf_op jit(solution)/shard_map/ppermute | solution.py:1275
  51.0 34.7 %collective-permute-start.10 = (bf16[1760,128]{1,0:T(8,128)(2,1)}, bf16[1760,128]{1,0:T(8,128)(2,1)S(1)}, u32[]{:S(2)}, u32[]{:S(2)}) collective-permute-start(bf16[1760,128]{1,0:T(8,128)(2,1)} %collective-permute-done.9), channel_id=1, source_target_pairs={{8,0},{9,1},{10,2},{11,3},{12,4},{13,5},{14,6},{15,7}} | collective-permute-start | bytes 1351688 | tf_op jit(solution)/shard_map/ppermute | solution.py:1275
  89.2 45.4 %collective-permute-start.11 = (bf16[4,880,128]{2,1,0:T(8,128)(2,1)}, bf16[4,880,128]{2,1,0:T(8,128)(2,1)S(1)}, u32[]{:S(2)}, u32[]{:S(2)}) collective-permute-start(bf16[4,880,128]{2,1,0:T(8,128)(2,1)} %get-tuple-element.143), channel_id=1, source_target_pairs={{0,2},{1,3},{2,0},{3,1},{4,6},{5,7},{6,4},{7,5},{8,10},{9,11},{10,... | collective-permute-start | bytes 2703368 | tf_op jit(solution)/shard_map/ppermute | solution.py:1241
  91.3 46.2 %collective-permute-start.13 = (bf16[4,880,128]{2,1,0:T(8,128)(2,1)}, bf16[4,880,128]{2,1,0:T(8,128)(2,1)}, u32[]{:S(2)}, u32[]{:S(2)}) collective-permute-start(bf16[4,880,128]{2,1,0:T(8,128)(2,1)} %get-tuple-element.142), channel_id=1, source_target_pairs={{0,4},{1,5},{2,6},{3,7},{4,0},{5,1},{6,2},{7,3},{8,12},{9,13},{10,... | collective-permute-start | bytes 2703368 | tf_op jit(solution)/shard_map/ppermute | solution.py:1241
  95.5 24.5 %collective-permute-start.17 = (bf16[4,512,128]{2,1,0:T(8,128)(2,1)}, bf16[4,512,128]{2,1,0:T(8,128)(2,1)S(1)}, u32[]{:S(2)}, u32[]{:S(2)}) collective-permute-start(bf16[4,512,128]{2,1,0:T(8,128)(2,1)} %gate.7), channel_id=1, source_target_pairs={{0,8},{1,9},{2,10},{3,11},{4,12},{5,13},{6,14},{7,15},{8,16},{9,17... | collective-permute-start | bytes 1572872 | tf_op jit(solution)/shard_map/ppermute | solution.py:1275
  97.1 36.3 %collective-permute-start.20 = (bf16[4,512,128]{2,1,0:T(8,128)(2,1)}, bf16[4,512,128]{2,1,0:T(8,128)(2,1)S(1)}, u32[]{:S(2)}, u32[]{:S(2)}) collective-permute-start(bf16[4,512,128]{2,1,0:T(8,128)(2,1)} %gate.7), channel_id=1, source_target_pairs={{24,16},{25,17},{26,18},{27,19},{28,20},{29,21},{30,22},{31,23},{1... | collective-permute-start | bytes 1572872 | tf_op jit(solution)/shard_map/ppermute | solution.py:1275
  120.0 21.7 %collective-permute-start.18 = (bf16[4,512,128]{2,1,0:T(8,128)(2,1)S(1)}, bf16[4,512,128]{2,1,0:T(8,128)(2,1)S(1)}, u32[]{:S(2)}, u32[]{:S(2)}) collective-permute-start(bf16[4,512,128]{2,1,0:T(8,128)(2,1)S(1)} %collective-permute-done.17), channel_id=1, source_target_pairs={{8,16},{9,17},{10,18},{11,19},{12,20},{13,21},{14,22},{15,23},{16,... | collective-permute-start | bytes 1572872 | tf_op jit(solution)/shard_map/ppermute | solution.py:1275
  133.4 25.0 %collective-permute-start.21 = (bf16[4,512,128]{2,1,0:T(8,128)(2,1)S(1)}, bf16[4,512,128]{2,1,0:T(8,128)(2,1)S(1)}, u32[]{:S(2)}, u32[]{:S(2)}) collective-permute-start(bf16[4,512,128]{2,1,0:T(8,128)(2,1)S(1)} %collective-permute-done.20), channel_id=1, source_target_pairs={{16,8},{17,9},{18,10},{19,11},{20,12},{21,13},{22,14},{23,15},{8,0... | collective-permute-start | bytes 1572872 | tf_op jit(solution)/shard_map/ppermute | solution.py:1275
  136.0 48.1 %collective-permute-start.12 = (bf16[2,4,880,128]{3,2,1,0:T(8,128)(2,1)}, bf16[2,4,880,128]{3,2,1,0:T(8,128)(2,1)}, u32[]{:S(2)}, u32[]{:S(2)}) collective-permute-start(bf16[2,4,880,128]{3,2,1,0:T(8,128)(2,1)} %pad_maximum_fusion.2.refs_10_), channel_id=1, source_target_pairs={{0,4},{1,5},{2,6},{3,7},{4,0},{5,1},{6,2},{7,3},{8,12},{9,13},{10,... | collective-permute-start | bytes 5406728 | tf_op jit(solution)/shard_map/ppermute | solution.py:1241
  140.1 44.0 %collective-permute-start.14 = (bf16[2,4,880,128]{3,2,1,0:T(8,128)(2,1)}, bf16[2,4,880,128]{3,2,1,0:T(8,128)(2,1)}, u32[]{:S(2)}, u32[]{:S(2)}) collective-permute-start(bf16[2,4,880,128]{3,2,1,0:T(8,128)(2,1)} %pad_maximum_fusion.3.refs_12_), channel_id=1, source_target_pairs={{0,2},{1,3},{2,0},{3,1},{4,6},{5,7},{6,4},{7,5},{8,10},{9,11},{10,... | collective-permute-start | bytes 5406728 | tf_op jit(solution)/shard_map/ppermute | solution.py:1241
  179.8 39.6 %collective-permute-start.27 = (bf16[4,4,512,128]{3,2,1,0:T(8,128)(2,1)S(1)}, bf16[4,4,512,128]{3,2,1,0:T(8,128)(2,1)}, u32[]{:S(2)}, u32[]{:S(2)}) collective-permute-start(bf16[4,4,512,128]{3,2,1,0:T(8,128)(2,1)S(1)} %pad_maximum_fusion.refs_14_), channel_id=1, source_target_pairs={{0,1},{1,0},{2,3},{3,2},{4,5},{5,4},{6,7},{7,6},{8,9},{9,8},{10,11... | collective-permute-start | bytes 6291464 | tf_op jit(solution)/shard_map/ppermute | solution.py:1241
  179.9 39.5 %collective-permute-start.23 = (bf16[2,4,880,128]{3,2,1,0:T(8,128)(2,1)}, bf16[2,4,880,128]{3,2,1,0:T(8,128)(2,1)}, u32[]{:S(2)}, u32[]{:S(2)}) collective-permute-start(bf16[2,4,880,128]{3,2,1,0:T(8,128)(2,1)} %pad_maximum_fusion.2.refs_10_), channel_id=1, source_target_pairs={{0,1},{1,0},{2,3},{3,2},{4,5},{5,4},{6,7},{7,6},{8,9},{9,8},{10,11... | collective-permute-start | bytes 5406728 | tf_op jit(solution)/shard_map/ppermute | solution.py:1241
  180.4 39.0 %collective-permute-start.25 = (bf16[2,4,880,128]{3,2,1,0:T(8,128)(2,1)}, bf16[2,4,880,128]{3,2,1,0:T(8,128)(2,1)}, u32[]{:S(2)}, u32[]{:S(2)}) collective-permute-start(bf16[2,4,880,128]{3,2,1,0:T(8,128)(2,1)} %pad_maximum_fusion.3.refs_12_), channel_id=1, source_target_pairs={{0,1},{1,0},{2,3},{3,2},{4,5},{5,4},{6,7},{7,6},{8,9},{9,8},{10,11... | collective-permute-start | bytes 5406728 | tf_op jit(solution)/shard_map/ppermute | solution.py:1241
  184.2 35.2 %collective-permute-start.24 = (bf16[2,4,880,128]{3,2,1,0:T(8,128)(2,1)}, bf16[2,4,880,128]{3,2,1,0:T(8,128)(2,1)}, u32[]{:S(2)}, u32[]{:S(2)}) collective-permute-start(bf16[2,4,880,128]{3,2,1,0:T(8,128)(2,1)} %collective-permute-done.12.refs_11_), channel_id=1, source_target_pairs={{0,1},{1,0},{2,3},{3,2},{4,5},{5,4},{6,7},{7,6},{8,9},{9,8},{10,11... | collective-permute-start | bytes 5406728 | tf_op jit(solution)/shard_map/ppermute | solution.py:1241
  184.2 35.2 %collective-permute-start.26 = (bf16[2,4,880,128]{3,2,1,0:T(8,128)(2,1)}, bf16[2,4,880,128]{3,2,1,0:T(8,128)(2,1)}, u32[]{:S(2)}, u32[]{:S(2)}) collective-permute-start(bf16[2,4,880,128]{3,2,1,0:T(8,128)(2,1)} %collective-permute-done.14.refs_13_), channel_id=1, source_target_pairs={{0,1},{1,0},{2,3},{3,2},{4,5},{5,4},{6,7},{7,6},{8,9},{9,8},{10,11... | collective-permute-start | bytes 5406728 | tf_op jit(solution)/shard_map/ppermute | solution.py:1241
  306.9 30.6 %collective-permute-start.46 = (bf16[2,1136,128]{2,1,0:T(8,128)(2,1)S(1)}, bf16[2,1136,128]{2,1,0:T(8,128)(2,1)}, u32[]{:S(2)}, u32[]{:S(2)}) collective-permute-start(bf16[2,1136,128]{2,1,0:T(8,128)(2,1)S(1)} %pad_maximum_fusion.10.refs_3_), channel_id=1, source_target_pairs={{0,2},{1,3},{2,0},{3,1},{4,6},{5,7},{6,4},{7,5},{8,10},{9,11},{10,... | collective-permute-start | bytes 1744904 | tf_op jit(solution)/shard_map/ppermute | solution.py:1241
  308.3 29.3 %collective-permute-start.48 = (bf16[2,1136,128]{2,1,0:T(8,128)(2,1)S(1)}, bf16[2,1136,128]{2,1,0:T(8,128)(2,1)}, u32[]{:S(2)}, u32[]{:S(2)}) collective-permute-start(bf16[2,1136,128]{2,1,0:T(8,128)(2,1)S(1)} %pad_maximum_fusion.11.refs_4_), channel_id=1, source_target_pairs={{0,4},{1,5},{2,6},{3,7},{4,0},{5,1},{6,2},{7,3},{8,12},{9,13},{10,... | collective-permute-start | bytes 1744904 | tf_op jit(solution)/shard_map/ppermute | solution.py:1241
  322.0 28.7 %collective-permute-start.37 = (bf16[4,2272,128]{2,1,0:T(8,128)(2,1)}, bf16[4,2272,128]{2,1,0:T(8,128)(2,1)}, u32[]{:S(2)}, u32[]{:S(2)}) collective-permute-start(bf16[4,2272,128]{2,1,0:T(8,128)(2,1)} %get-tuple-element.96), channel_id=1, source_target_pairs={{0,1},{1,0},{2,3},{3,2},{4,5},{5,4},{6,7},{7,6},{8,9},{9,8},{10,11... | collective-permute-start | bytes 6979592 | tf_op jit(solution)/shard_map/ppermute | solution.py:1241
  355.4 23.9 %collective-permute-start.33 = (bf16[2,1136,128]{2,1,0:T(8,128)(2,1)S(1)}, bf16[2,1136,128]{2,1,0:T(8,128)(2,1)S(1)}, u32[]{:S(2)}, u32[]{:S(2)}) collective-permute-start(bf16[2,1136,128]{2,1,0:T(8,128)(2,1)S(1)} %pad_maximum_fusion.12), channel_id=1, source_target_pairs={{0,2},{1,3},{2,0},{3,1},{4,6},{5,7},{6,4},{7,5},{8,10},{9,11},{10,... | collective-permute-start | bytes 1744904 | tf_op jit(solution)/shard_map/ppermute | solution.py:1241
  356.4 26.0 %collective-permute-start.35 = (bf16[2,1136,128]{2,1,0:T(8,128)(2,1)S(1)}, bf16[2,1136,128]{2,1,0:T(8,128)(2,1)S(1)}, u32[]{:S(2)}, u32[]{:S(2)}) collective-permute-start(bf16[2,1136,128]{2,1,0:T(8,128)(2,1)S(1)} %pad_maximum_fusion.13), channel_id=1, source_target_pairs={{0,4},{1,5},{2,6},{3,7},{4,0},{5,1},{6,2},{7,3},{8,12},{9,13},{10,... | collective-permute-start | bytes 1744904 | tf_op jit(solution)/shard_map/ppermute | solution.py:1241
  358.2 63.1 %collective-permute-start.55 = (bf16[2272,128]{1,0:T(8,128)(2,1)}, bf16[2272,128]{1,0:T(8,128)(2,1)}, u32[]{:S(2)}, u32[]{:S(2)}) collective-permute-start(bf16[2272,128]{1,0:T(8,128)(2,1)} %get-tuple-element.139), channel_id=1, source_target_pairs={{24,16},{25,17},{26,18},{27,19},{28,20},{29,21},{30,22},{31,23}} | collective-permute-start | bytes 1744904 | tf_op jit(solution)/shard_map/ppermute | solution.py:1401
  368.5 28.9 %collective-permute-start.52 = (bf16[2272,128]{1,0:T(8,128)(2,1)S(1)}, bf16[2272,128]{1,0:T(8,128)(2,1)S(1)}, u32[]{:S(2)}, u32[]{:S(2)}) collective-permute-start(bf16[2272,128]{1,0:T(8,128)(2,1)S(1)} %get-tuple-element.138), channel_id=1, source_target_pairs={{0,8},{1,9},{2,10},{3,11},{4,12},{5,13},{6,14},{7,15}} | collective-permute-start | bytes 1744904 | tf_op jit(solution)/shard_map/ppermute | solution.py:1401
  (64 other events, 888.7 us)
Sparse Core Ops, SparseCore 0:
  11.4 165.2 all-gather.1
